TPU v7x, 32 devices: a whole 2x2x4 slice. The times are simulated.
32 devices in a mesh: seg: 4 (over z), sec: 8 (over y, x, core).
Axes of the slice: x: 2, y: 2, z: 4, core: 2. Of those that a mesh axis runs over, the one named last changes fastest.
Arguments:
- left_env: bfloat16 [4, 8, 34, 128, 128], P('seg', 'sec'), as said below
- right_env: bfloat16 [4, 8, 34, 128, 128], P('seg', 'sec')
- site_tensors: bfloat16 [4, 1, 4, 8, 128, 128], P('seg', None, None, 'sec'), may hold values from -0.5 to 0.5
- mpo: float32 [4, 1, 34, 34, 4], P('seg'), may hold values from -0.5 to 0.5
- boundary_mpo: float32 [4, 34, 34, 4], P('seg'), may hold values from -1 to 1
- guess: float32 [4, 4, 8, 128, 128], P('seg', None, 'sec'), may hold values from -6 to 6
- sector_dims: int32 [8], replicated, may hold values from 16 to 128, as said below
Outputs:
- new_env: bfloat16 [4, 8, 34, 128, 128], P('seg', 'sec')
- lanczos_vector: float32 [4, 4, 8, 128, 128], P('seg', None, 'sec')
- coefficients: float32 [4, 4, 2], P('seg')
Inputs may be any that keep to these rules, and one draw needn't show every extreme that they name: sector_dims[q] counts the live rows and columns of sector q within its 128 padded ones; some sector has exactly 128. Every block of left_env and right_env is symmetric.
All inputs are finite; a program needn't handle non-finite values.
Results may differ from a plain program's by a relative error of at most 0.01.
Values may be sent and summed in bfloat16 or wider, within the bound.
No kernel may reach another device: no remote copies, remote signals or barrier semaphores. Data moves between devices by JAX's collectives and lax.ppermute only.
A program may use at most 128 MiB of HBM per device.

v0:
```python
import functools

import jax
import jax.numpy as jnp
from jax import lax
from jax.experimental import pallas as pl
from jax.experimental.pallas import tpu as pltpu
from jax.sharding import PartitionSpec as P

LANCZOS = 4
CHARGES = (0, 1, 1, 2)
F32 = jnp.float32
BF16 = jnp.bfloat16
VMEM_LIMIT = 56 * 1024 * 1024


def params():
    return pltpu.CompilerParams(vmem_limit_bytes=VMEM_LIMIT)


def padded(count):
    return -(-count // 8) * 8


def packed_rows(width, tile):
    return -(-(width * tile // 2 + padded(width)) // 16) * 16


def iotas(shape):
    return lax.broadcasted_iota(jnp.int32, shape, 0), lax.broadcasted_iota(jnp.int32, shape, 1)


def pack_block(block):
    tile = block.shape[0]
    half = tile // 2
    top, low = block[:half], block[half:]
    row, lane = iotas((half, tile))
    turned = pltpu.roll(low, half, 1)
    folded = jnp.where((lane < half) & (row > lane), turned, top)
    diagonal = jnp.sum(jnp.where(lane == row + half, low, 0.0), axis=0, keepdims=True)
    return folded, diagonal


def unpack_block(folded, diagonal):
    half, tile = folded.shape
    row, lane = iotas((half, tile))
    rolled = pltpu.roll(folded, half, 1)
    turned = jnp.transpose(jnp.concatenate([folded, rolled], axis=0))
    top = jnp.where((lane < half) & (row > lane), turned[:half], folded)
    low = jnp.where((lane >= half) & (row > lane - half), rolled, turned[half:])
    low = jnp.where(lane == row + half, diagonal, low)
    return jnp.concatenate([top, low], axis=0)


def live_limits(dims_ref, sector):
    count = dims_ref.shape[0]
    rows = dims_ref[sector]
    columns = []
    for charge in CHARGES:
        target = sector + charge
        columns.append(jnp.where(target < count, dims_ref[jnp.minimum(target, count - 1)], 0))
    return rows, columns


def pack_kernel(width, tile, source_ref, out_ref, diag):
    half = tile // 2
    diag[...] = jnp.zeros_like(diag)

    def one(w, carry):
        block = source_ref[pl.ds(pl.multiple_of(w * tile, tile), tile), :].astype(F32)
        folded, diagonal = pack_block(block)
        out_ref[pl.ds(pl.multiple_of(w * half, half), half), :] = folded.astype(BF16)
        diag[pl.ds(w, 1), :] = diagonal
        return carry

    lax.fori_loop(0, width, one, 0, unroll=2)
    out_ref[width * half :, :] = diag[...].astype(BF16)


def unpack_kernel(width, tile, source_ref, out_ref, diag):
    half = tile // 2
    diag[...] = source_ref[width * half :, :].astype(F32)

    def one(w, carry):
        folded = source_ref[pl.ds(pl.multiple_of(w * half, half), half), :].astype(F32)
        block = unpack_block(folded, diag[pl.ds(w, 1), :])
        out_ref[pl.ds(pl.multiple_of(w * tile, tile), tile), :] = block.astype(BF16)
        return carry

    lax.fori_loop(0, width, one, 0, unroll=2)


def fold_kernel(
    width, tile, place_ref, dims_ref, environ_ref, site_ref, weight_ref,
    own_ref, one_ref, two_ref, half_s, turned_s, diag_s, sums_s, diag_sums_s,
):
    half = tile // 2
    wide = padded(width)
    states = len(CHARGES)
    rows, columns = live_limits(dims_ref, place_ref[0])
    row, lane = iotas((tile, tile))
    blocks = []
    for p in range(states):
        live = (row < rows) & (lane < columns[p])
        blocks.append(jnp.where(live, site_ref[p].astype(F32), 0.0))
    turned_blocks = [jnp.transpose(block).astype(BF16) for block in blocks]
    joined = jnp.concatenate(blocks, axis=1).astype(BF16)

    def first(w, carry):
        at = pl.ds(pl.multiple_of(w * tile, tile), tile)
        half_s[at, :] = jnp.dot(environ_ref[at, :], joined, preferred_element_type=F32).astype(BF16)
        return carry

    lax.fori_loop(0, width, first, 0, unroll=2)
    for p in range(states):
        turned_s[p, width * half :, :] = jnp.zeros(((wide - width) * half, tile), F32)
        diag_s[p] = jnp.zeros_like(diag_s[p])

    def second(w, carry):
        at = pl.ds(pl.multiple_of(w * tile, tile), tile)
        for p in range(states):
            block = jnp.dot(
                turned_blocks[p], half_s[at, p * tile : (p + 1) * tile], preferred_element_type=F32
            )
            folded, diagonal = pack_block(block)
            turned_s[p, pl.ds(pl.multiple_of(w * half, half), half), :] = folded
            diag_s[p, pl.ds(w, 1), :] = diagonal
        return carry

    lax.fori_loop(0, width, second, 0, unroll=2)

    def mixed(inputs):
        products = []
        for p in range(states):
            value = inputs[p]
            value = jnp.concatenate([value, value], axis=0).astype(BF16)
            products.append(jnp.dot(weight_ref[p], value, preferred_element_type=F32)[:wide])
        return products[0], products[1] + products[2], products[3]

    def mix(step, carry):
        at = step * 2
        inputs = [
            jnp.concatenate(
                [turned_s[p, pl.ds(at + k, wide, stride=half), :] for k in range(2)], axis=1
            )
            for p in range(states)
        ]
        for index, value in enumerate(mixed(inputs)):
            for k in range(2):
                sums_s[index, pl.ds(at + k, wide, stride=half), :] = value[:, k * tile : (k + 1) * tile]
        return carry

    lax.fori_loop(0, half // 2, mix, 0, unroll=2)
    diag_sums_s[...] = jnp.zeros_like(diag_sums_s)
    for index, value in enumerate(mixed([diag_s[p, :wide] for p in range(states)])):
        diag_sums_s[index, :wide, :] = value
    for index, ref in enumerate((own_ref, one_ref, two_ref)):
        ref[: width * half, :] = sums_s[index, : width * half, :].astype(ref.dtype)
        ref[width * half :, :] = diag_sums_s[index].astype(ref.dtype)


def mix_into(width, tile, weight, wide_s, sums_s, out_ref, base):
    wide = padded(width)

    def mix(step, carry):
        at = step * 2
        value = jnp.concatenate(
            [wide_s[pl.ds(at + k, wide, stride=tile), :] for k in range(2)], axis=1
        )
        value = jnp.concatenate([value, value], axis=0).astype(BF16)
        value = jnp.dot(weight, value, preferred_element_type=F32)[:wide]
        for k in range(2):
            sums_s[pl.ds(at + k, wide, stride=tile), :] = value[:, k * tile : (k + 1) * tile]
        return carry

    lax.fori_loop(0, tile // 2, mix, 0, unroll=4)
    out_ref[pl.ds(base * tile, width * tile), :] = sums_s[: width * tile, :].astype(BF16)


def mix_own_kernel(width, tile, source_ref, weight_ref, out_ref, wide_s, sums_s):
    wide_s[: width * tile, :] = source_ref[...].astype(F32)
    wide_s[width * tile :, :] = jnp.zeros_like(wide_s[width * tile :, :])
    mix_into(width, tile, weight_ref[0], wide_s, sums_s, out_ref, 0)


def mix_far_kernel(
    width, tile, near_ref, relay_ref, far_ref, weight_ref, out_ref, diag, wide_s, sums_s
):
    half = tile // 2
    wide_s[width * tile :, :] = jnp.zeros_like(wide_s[width * tile :, :])

    def unpacked(read):
        diag[...] = read(pl.ds(width * half, diag.shape[0]))

        def one(w, carry):
            folded = read(pl.ds(pl.multiple_of(w * half, half), half))
            wide_s[pl.ds(pl.multiple_of(w * tile, tile), tile), :] = unpack_block(
                folded, diag[pl.ds(w, 1), :]
            )
            return carry

        lax.fori_loop(0, width, one, 0, unroll=2)

    unpacked(lambda at: near_ref[at, :].astype(F32) + relay_ref[at, :].astype(F32))
    mix_into(width, tile, weight_ref[1], wide_s, sums_s, out_ref, 0)
    mix_into(width, tile, weight_ref[2], wide_s, sums_s, out_ref, width)
    unpacked(lambda at: far_ref[at, :].astype(F32))
    mix_into(width, tile, weight_ref[3], wide_s, sums_s, out_ref, 2 * width)


def total(value):
    return jnp.sum(jnp.sum(value, axis=0, keepdims=True), axis=1, keepdims=True)


def lanczos_kernel(
    width, tile, place_ref, dims_ref, packed_ref, environ_ref, own_ref, far_ref, guess_ref,
    basis_ref, stats_ref, bound_s, first_s, diag,
):
    half = tile // 2
    states = len(CHARGES)
    sector = place_ref[0]

    @pl.when(place_ref[1] == 0)
    def _():
        bound_s[...] = environ_ref[...]

    @pl.when(place_ref[1] != 0)
    def _():
        diag[...] = packed_ref[width * half :, :].astype(F32)

        def one(w, carry):
            folded = packed_ref[pl.ds(pl.multiple_of(w * half, half), half), :].astype(F32)
            bound_s[pl.ds(pl.multiple_of(w * tile, tile), tile), :] = unpack_block(
                folded, diag[pl.ds(w, 1), :]
            ).astype(BF16)
            return carry

        lax.fori_loop(0, width, one, 0, unroll=2)

    rows, columns = live_limits(dims_ref, sector)
    row, lane = iotas((tile, tile))
    stat_row, stat_lane = iotas(stats_ref.shape)
    stats = jnp.zeros(stats_ref.shape, F32)

    def put(stats, kind, p, value):
        here = (stat_row == kind) & (stat_lane == sector * states + p)
        return jnp.where(here, value, stats)

    def scaled(value):
        square = total(value * value)
        inverse = jnp.where(square > 0.0, lax.rsqrt(square), 0.0)
        return value * inverse, square * inverse

    for p in range(states):
        live = (row < rows) & (lane < columns[p])
        vector, norm = scaled(jnp.where(live, guess_ref[p], 0.0))
        basis_ref[0, p] = vector
        stats = put(stats, 0, p, norm)

    betas = [jnp.zeros((1, 1), F32)] * states
    for j in range(LANCZOS):
        field = jnp.concatenate([basis_ref[j, p] for p in range(states)], axis=1).astype(BF16)
        for w in range(width):
            first = jnp.dot(
                bound_s[w * tile : (w + 1) * tile, :], field, preferred_element_type=F32
            ).astype(BF16)
            for p in range(states):
                first_s[p, :, w * tile : (w + 1) * tile] = first[:, p * tile : (p + 1) * tile]
        for p in range(states):
            live = (row < rows) & (lane < columns[p])
            if p == 0:
                right = own_ref[...]
            else:
                right = far_ref[(p - 1) * width * tile : p * width * tile, :]
            image = jnp.dot(first_s[p], right, preferred_element_type=F32)
            image = jnp.where(live, image, 0.0)
            vector = basis_ref[j, p]
            alpha = total(vector * image)
            image = image - alpha * vector
            if j > 0:
                image = image - betas[p] * basis_ref[j - 1, p]
            following, beta = scaled(image)
            basis_ref[j + 1, p] = following
            betas[p] = beta
            stats = put(stats, 1 + 2 * j, p, alpha)
            stats = put(stats, 2 + 2 * j, p, beta)
    stats_ref[...] = stats


def finish_kernel(entries, place_ref, stats_ref, basis_ref, vector_ref, table_ref):
    states = len(CHARGES)
    sector = place_ref[0]
    stats = stats_ref[...]
    alphas = [stats[1 + 2 * j : 2 + 2 * j, :] for j in range(LANCZOS)]
    betas = [stats[2 + 2 * j : 3 + 2 * j, :] for j in range(LANCZOS)]

    def mean(left, right):
        products = left[0] * right[0]
        for x, y in zip(left[1:], right[1:]):
            products = products + x * y
        return jnp.sum(products, axis=1, keepdims=True) / entries

    start = [stats[0:1, :]]
    vector = [start[0] / jnp.sqrt(mean(start, start) + 1e-06)]
    previous = []
    beta = jnp.zeros((1, 1), F32)
    table_row, table_column = iotas(table_ref.shape)
    table = jnp.zeros(table_ref.shape, F32)
    for j in range(LANCZOS):
        image = []
        for k in range(j + 2):
            term = None
            if k > 0:
                term = betas[k - 1] * vector[k - 1]
            if k <= j:
                more = alphas[k] * vector[k]
                term = more if term is None else term + more
            if k + 1 <= j:
                term = term + betas[k] * vector[k + 1]
            image.append(term)
        alpha = mean(vector, image[: j + 1])
        for k in range(j + 1):
            image[k] = image[k] - alpha * vector[k]
        for k in range(j):
            image[k] = image[k] - beta * previous[k]
        beta = jnp.sqrt(mean(image, image) + 1e-06)
        previous = vector
        vector = [value / beta for value in image]
        table = jnp.where((table_row == j) & (table_column == 0), alpha, table)
        table = jnp.where((table_row == j) & (table_column == 1), beta, table)
    table_ref[...] = table
    lane = lax.broadcasted_iota(jnp.int32, (1, stats.shape[1]), 1)
    for p in range(states):
        value = None
        here = lane == sector * states + p
        for k in range(LANCZOS + 1):
            weight = jnp.sum(jnp.where(here, vector[k], 0.0), axis=1, keepdims=True)
            term = weight * basis_ref[k, p]
            value = term if value is None else value + term
        vector_ref[p] = value


def smem():
    return pl.BlockSpec(memory_space=pltpu.SMEM)


def vmem():
    return pl.BlockSpec(memory_space=pltpu.VMEM)


def call(kernel, scalars, arrays, outs, scratch, flops=0, name=None):
    many = isinstance(outs, (tuple, list))
    return pl.pallas_call(
        kernel,
        out_shape=outs,
        in_specs=[smem()] * len(scalars) + [vmem()] * len(arrays),
        out_specs=[vmem()] * len(outs) if many else vmem(),
        scratch_shapes=scratch,
        compiler_params=params(),
        name=name,
        cost_estimate=pl.CostEstimate(flops=flops, bytes_accessed=4 * 1024 * 1024, transcendentals=0),
    )(*scalars, *arrays)


def split_weights(weights, rows):
    states, out_count, in_count = weights.shape
    wide = padded(in_count)
    high = weights.astype(BF16)
    low = (weights - high.astype(F32)).astype(BF16)
    gap = ((0, 0), (0, rows - out_count), (0, wide - in_count))
    return jnp.concatenate([jnp.pad(high, gap), jnp.pad(low, gap)], axis=2)


def pairs_of(count, pick):
    return [(source, target) for source in range(count) for target in pick(source) if 0 <= target < count]


def on_device(left_env, right_env, site_tensors, mpo, boundary_mpo, guess, sector_dims):
    width, tile = left_env.shape[2], left_env.shape[-1]
    half = tile // 2
    wide = padded(width)
    states = len(CHARGES)
    sector_count = sector_dims.shape[0]
    sectors = lax.axis_size("sec")
    segments = lax.axis_size("seg")
    prows = packed_rows(width, tile)
    drows = prows - width * half
    sector = lax.axis_index("sec")
    place = jnp.stack([sector, lax.axis_index("seg")]).astype(jnp.int32)
    odd = lax.rem(sector, 2) == 1
    packed = jax.ShapeDtypeStruct((prows, tile), BF16)
    packed32 = jax.ShapeDtypeStruct((prows, tile), F32)
    product = 2 * width * tile**3

    environ = left_env.reshape(width * tile, tile)
    right = right_env.reshape(width * tile, tile)
    site = site_tensors[0, 0, :, 0]
    mrows = -(-width // 16) * 16
    site_weights = split_weights(jnp.transpose(mpo[0, 0], (2, 1, 0)), mrows)
    bound_weights = split_weights(jnp.transpose(boundary_mpo[0], (2, 0, 1)), mrows)

    swap = pairs_of(sectors, lambda q: [q ^ 1])
    down = pairs_of(sectors, lambda q: [q - 1] if q % 2 else [])
    across = pairs_of(sectors, lambda q: [q + 1] if q % 2 == 0 else [])
    up_two = pairs_of(sectors, lambda q: [q + 2])
    down_two = pairs_of(sectors, lambda q: [q - 2])
    onward = pairs_of(segments, lambda s: [s + 1])

    right_packed = call(
        functools.partial(pack_kernel, width, tile), [], [right], packed,
        [pltpu.VMEM((drows, tile), F32)], name="pack_right",
    )
    right_far = lax.ppermute(right_packed, "sec", down_two)
    right_near = lax.ppermute(right_packed, "sec", down)

    own, one, two = call(
        functools.partial(fold_kernel, width, tile),
        [place, sector_dims], [environ, site, site_weights],
        (packed32, packed, packed32),
        [
            pltpu.VMEM((width * tile, states * tile), BF16),
            pltpu.VMEM((states, wide * half, tile), F32),
            pltpu.VMEM((states, drows, tile), F32),
            pltpu.VMEM((3, wide * half, tile), F32),
            pltpu.VMEM((3, drows, tile), F32),
        ],
        flops=2 * states * product, name="fold",
    )
    partner = lax.ppermute(one, "sec", swap)
    outgoing = jnp.where(odd, two, two + partner.astype(F32)).astype(BF16)
    arrived = lax.ppermute(outgoing, "sec", up_two)
    own_mixed = call(
        functools.partial(mix_own_kernel, width, tile), [], [right, bound_weights],
        jax.ShapeDtypeStruct((width * tile, tile), BF16),
        [pltpu.VMEM((wide * tile, tile), F32)] * 2,
        flops=product, name="mix_own",
    )
    right_relay = lax.ppermute(right_far, "sec", across)
    fresh = own + arrived.astype(F32) + jnp.where(odd, partner.astype(F32), 0.0)
    fresh = fresh.astype(BF16)
    received = lax.ppermute(fresh, "seg", onward)
    far_mixed = call(
        functools.partial(mix_far_kernel, width, tile), [],
        [right_near, right_relay, right_far, bound_weights],
        jax.ShapeDtypeStruct((3 * width * tile, tile), BF16),
        [pltpu.VMEM((drows, tile), F32)] + [pltpu.VMEM((wide * tile, tile), F32)] * 2,
        flops=3 * product, name="mix_far",
    )
    new_env = call(
        functools.partial(unpack_kernel, width, tile), [], [fresh],
        jax.ShapeDtypeStruct((width * tile, tile), BF16),
        [pltpu.VMEM((drows, tile), F32)], name="unpack_env",
    )
    basis, stats = call(
        functools.partial(lanczos_kernel, width, tile),
        [place, sector_dims], [received, environ, own_mixed, far_mixed, guess[0, :, 0]],
        (
            jax.ShapeDtypeStruct((LANCZOS + 1, states, tile, tile), F32),
            jax.ShapeDtypeStruct((16, 128), F32),
        ),
        [
            pltpu.VMEM((width * tile, tile), BF16),
            pltpu.VMEM((states, tile, width * tile), BF16),
            pltpu.VMEM((drows, tile), F32),
        ],
        flops=8 * states * product, name="lanczos",
    )
    stats = lax.psum(stats, "sec")
    entries = float(states * sector_count * tile * tile)
    vector, table = call(
        functools.partial(finish_kernel, entries), [place], [stats, basis],
        (
            jax.ShapeDtypeStruct((states, tile, tile), F32),
            jax.ShapeDtypeStruct((LANCZOS, 2), F32),
        ),
        [], name="finish",
    )
    return new_env.reshape(left_env.shape), vector[None, :, None], table[None]


def solution(mesh):
    placed = (
        P("seg", "sec", None, None, None),
        P("seg", "sec", None, None, None),
        P("seg", None, None, "sec", None, None),
        P("seg", None, None, None, None),
        P("seg", None, None, None),
        P("seg", None, "sec", None, None),
        P(),
    )
    return jax.shard_map(
        on_device,
        mesh=mesh,
        in_specs=placed,
        out_specs=(
            P("seg", "sec", None, None, None),
            P("seg", None, "sec", None, None),
            P("seg", None, None),
        ),
        check_vma=False,
    )
```

profile of v0, /device:TPU:0, one launch (start us, length us, event | category | flops | bytes accessed | tf_op | source)
XLA Modules:
  0.0 129.8 jit_solution(9498755296799090930)
XLA Ops:
  0.6 1.0 copy.10
  1.6 0.6 pad_add_fusion.place_ref
  2.3 0.7 fusion.9.weight_ref
  3.0 18.1 %fold.1 = (f32[2224,128]{1,0:T(8,128)}, bf16[2224,128]{1,0:T(8,128)(2,1)}, f32[2224,128]{1,0:T(8,128)}) custom-call(s32[2]{0:T(128)} %pad_add_fusion.place_ref, s32[8]{0:T(128)} %dims_ref.3, bf16[4352,128]{1,0:T(8,128)(2,1)} %bitcast.31, bf16[4,128,128]{2,1,0:T(8,128)(2,1)} %bitcast.35, bf16[4,48,80]{2,1,0:T(8,128)(2,1)} %fusion.9.weight_ref), custom_call_target="tpu_custom_call" | custom-call | flops 1140850688 | bytes 4194304 | tf_op jit(solution)/shard_map/fold/pallas_call | solution.py:353
  21.1 0.0 copy-start.2
  21.1 0.5 collective-permute-start
  21.5 3.5 %pack_right.1 = bf16[2224,128]{1,0:T(8,128)(2,1)} custom-call(bf16[4352,128]{1,0:T(8,128)(2,1)} %bitcast.27), custom_call_target="tpu_custom_call" | custom-call | bytes 4194304 | tf_op jit(solution)/shard_map/pack_right/pallas_call | solution.py:353
  25.0 1.3 collective-permute-start.4
  26.3 0.0 collective-permute-done
  26.3 0.0 copy-done.2
  26.3 0.0 copy-start.3
  26.3 0.0 copy-start.1
  26.3 0.2 fusion.2
  26.5 5.3 %collective-permute-start.1 = (bf16[2224,128]{1,0:T(8,128)(2,1)S(1)}, bf16[2224,128]{1,0:T(8,128)(2,1)S(1)}, u32[]{:S(2)}, u32[]{:S(2)}) collective-permute-start(bf16[2224,128]{1,0:T(8,128)(2,1)S(1)} %fusion.2), channel_id=1, source_target_pairs={{0,2},{1,3},{2,4},{3,5},{4,6},{5,7},{8,10},{9,11},{10,12},{11,13},... | collective-permute-start | bytes 1708040 | tf_op jit(solution)/shard_map/ppermute | solution.py:431
  31.8 0.0 copy-done.3
  31.8 1.3 collective-permute-start.3
  33.1 10.3 %collective-permute-done.4.far_ref = bf16[2224,128]{1,0:T(8,128)(2,1)S(1)} collective-permute-done((bf16[2224,128]{1,0:T(8,128)(2,1)}, bf16[2224,128]{1,0:T(8,128)(2,1)S(1)}, u32[]{:S(2)}, u32[]{:S(2)}) %collective-permute-start.4) | collective-permute-done | bytes 569376 | tf_op jit(solution)/shard_map/ppermute | solution.py:413
  43.4 0.0 copy-start.4
  43.4 1.5 %collective-permute-start.5 = (bf16[2224,128]{1,0:T(8,128)(2,1)S(1)}, bf16[2224,128]{1,0:T(8,128)(2,1)S(1)}, u32[]{:S(2)}, u32[]{:S(2)}) collective-permute-start(bf16[2224,128]{1,0:T(8,128)(2,1)S(1)} %collective-permute-done.4.far_ref), channel_id=1, source_target_pairs={{0,1},{2,3},{4,5},{6,7},{8,9},{10,11},{12,13},{14,15},{16,17},{18,... | collective-permute-start | bytes 1708040 | tf_op jit(solution)/shard_map/ppermute | solution.py:438
  44.9 0.0 collective-permute-done.1
  45.0 0.0 copy-done.1
  45.0 0.0 copy-start.7
  45.0 0.3 fusion.1.source_ref
  45.3 0.0 copy-done.4
  45.3 0.0 copy-start
  45.3 3.8 %collective-permute-start.2 = (bf16[2224,128]{1,0:T(8,128)(2,1)S(1)}, bf16[2224,128]{1,0:T(8,128)(2,1)S(1)}, u32[]{:S(2)}, u32[]{:S(2)}) collective-permute-start(bf16[2224,128]{1,0:T(8,128)(2,1)S(1)} %fusion.1.source_ref), channel_id=1, source_target_pairs={{0,8},{8,16},{16,24},{1,9},{9,17},{17,25},{2,10},{10,18},{18,26},{... | collective-permute-start | bytes 1708040 | tf_op jit(solution)/shard_map/ppermute | solution.py:441
  49.1 0.0 copy-done.7
  49.1 0.7 fusion.10.weight_ref
  49.8 6.9 %mix_own.1.own_ref = bf16[4352,128]{1,0:T(8,128)(2,1)} custom-call(bf16[4352,128]{1,0:T(8,128)(2,1)} %bitcast.28, bf16[4,48,80]{2,1,0:T(8,128)(2,1)} %fusion.10.weight_ref), custom_call_target="tpu_custom_call" | custom-call | flops 142606336 | bytes 4194304 | tf_op jit(solution)/shard_map/mix_own/pallas_call | solution.py:353
  56.8 0.0 copy-done
  56.8 4.8 %unpack_env.1 = bf16[4352,128]{1,0:T(8,128)(2,1)} custom-call(bf16[2224,128]{1,0:T(8,128)(2,1)} %copy-done), custom_call_target="tpu_custom_call" | custom-call | bytes 4194304 | tf_op jit(solution)/shard_map/unpack_env/pallas_call | solution.py:353
  61.6 0.0 collective-permute-done.3.near_ref
  61.6 0.0 copy-start.5
  61.6 0.0 collective-permute-done.5.relay_ref
  61.6 0.8 copy-done.5
  62.4 0.0 copy-start.6
  62.4 0.8 copy-done.6
  63.2 22.1 %mix_far.1.far_ref = bf16[13056,128]{1,0:T(8,128)(2,1)} custom-call(bf16[2224,128]{1,0:T(8,128)(2,1)} %copy-done.5, bf16[2224,128]{1,0:T(8,128)(2,1)} %copy-done.6, bf16[2224,128]{1,0:T(8,128)(2,1)} %copy-done.4, bf16[4,48,80]{2,1,0:T(8,128)(2,1)} %fusion.10.weight_ref), custom_call_target="tpu_custom_call" | custom-call | flops 427819008 | bytes 4194304 | tf_op jit(solution)/shard_map/mix_far/pallas_call | solution.py:353
  85.2 0.0 collective-permute-done.2.packed_ref
  85.2 0.0 copy-start.8
  85.2 0.8 copy-done.8
  86.0 14.9 %lanczos.1 = (f32[5,4,128,128]{3,2,1,0:T(8,128)}, f32[16,128]{1,0:T(8,128)}) custom-call(s32[2]{0:T(128)} %pad_add_fusion.place_ref, s32[8]{0:T(128)} %dims_ref.3, bf16[2224,128]{1,0:T(8,128)(2,1)} %copy-done.8, bf16[4352,128]{1,0:T(8,128)(2,1)} %bitcast.32, bf16[4352,128]{1,0:T(8,128)(2,1)} %mix_own.1.own_ref, bf16[13056,128]{1,0:T(8,128)(2,1)} %mix_far.1.far_ref, ...), custom_call_target="tpu_custom_call" | custom-call | flops 4563402752 | bytes 4194304 | tf_op jit(solution)/shard_map/lanczos/pallas_call | solution.py:353
  101.0 24.5 %psum.7.stats_ref = f32[16,128]{1,0:T(8,128)} all-reduce(f32[16,128]{1,0:T(8,128)} %get-tuple-element.13), channel_id=1, replica_groups=mesh['seg'=4,'sec'=8] {'sec'}, use_global_device_ids=true, to_apply=%region_0.1 | all-reduce | flops 2048 | bytes 16384 | tf_op jit(solution)/shard_map/psum | solution.py:468
  125.4 3.1 %finish.1 = (f32[4,128,128]{2,1,0:T(8,128)}, f32[4,2]{1,0:T(4,128)}) custom-call(s32[2]{0:T(128)} %pad_add_fusion.place_ref, f32[16,128]{1,0:T(8,128)} %psum.7.stats_ref, f32[5,4,128,128]{3,2,1,0:T(8,128)} %get-tuple-element.14.basis_ref), custom_call_target="tpu_custom_call" | custom-call | bytes 4194304 | tf_op jit(solution)/shard_map/finish/pallas_call | solution.py:353
  128.5 1.3 %copy.12 = f32[4,2]{0,1:T(2,128)} copy(f32[4,2]{1,0:T(4,128)} %get-tuple-element.16) | data formatting | bytes 64 | tf_op jit(solution)/shard_map/finish/pallas_call | solution.py:353
  (2 shorter events, 0.0 us)
Async XLA Ops:
  21.1 5.3 %copy-start.2 = (f32[2224,128]{1,0:T(8,128)S(1)}, f32[2224,128]{1,0:T(8,128)}, u32[]{:S(2)}) copy-start(f32[2224,128]{1,0:T(8,128)} %get-tuple-element.11) | copy-start | bytes 3416068
  21.1 5.2 %collective-permute-start = (bf16[2224,128]{1,0:T(8,128)(2,1)}, bf16[2224,128]{1,0:T(8,128)(2,1)S(1)}, u32[]{:S(2)}, u32[]{:S(2)}) collective-permute-start(bf16[2224,128]{1,0:T(8,128)(2,1)} %get-tuple-element.12), channel_id=1, source_target_pairs={{0,1},{1,0},{2,3},{3,2},{4,5},{5,4},{6,7},{7,6},{8,9},{9,8},{10,11... | collective-permute-start | bytes 1708040 | tf_op jit(solution)/shard_map/ppermute | solution.py:429
  25.0 18.4 %collective-permute-start.4 = (bf16[2224,128]{1,0:T(8,128)(2,1)}, bf16[2224,128]{1,0:T(8,128)(2,1)S(1)}, u32[]{:S(2)}, u32[]{:S(2)}) collective-permute-start(bf16[2224,128]{1,0:T(8,128)(2,1)} %pack_right.1), channel_id=1, source_target_pairs={{2,0},{3,1},{4,2},{5,3},{6,4},{7,5},{10,8},{11,9},{12,10},{13,11},... | collective-permute-start | bytes 1708040 | tf_op jit(solution)/shard_map/ppermute | solution.py:413
  26.3 5.5 %copy-start.3 = (bf16[2224,128]{1,0:T(8,128)(2,1)S(1)}, bf16[2224,128]{1,0:T(8,128)(2,1)}, u32[]{:S(2)}) copy-start(bf16[2224,128]{1,0:T(8,128)(2,1)} %pack_right.1) | copy-start | bytes 1708036
  26.3 18.6 %copy-start.1 = (f32[2224,128]{1,0:T(8,128)S(1)}, f32[2224,128]{1,0:T(8,128)}, u32[]{:S(2)}) copy-start(f32[2224,128]{1,0:T(8,128)} %get-tuple-element.10) | copy-start | bytes 3416068
  26.5 18.4 %collective-permute-start.1 = (bf16[2224,128]{1,0:T(8,128)(2,1)S(1)}, bf16[2224,128]{1,0:T(8,128)(2,1)S(1)}, u32[]{:S(2)}, u32[]{:S(2)}) collective-permute-start(bf16[2224,128]{1,0:T(8,128)(2,1)S(1)} %fusion.2), channel_id=1, source_target_pairs={{0,2},{1,3},{2,4},{3,5},{4,6},{5,7},{8,10},{9,11},{10,12},{11,13},... | collective-permute-start | bytes 1708040 | tf_op jit(solution)/shard_map/ppermute | solution.py:431
  31.8 29.7 %collective-permute-start.3 = (bf16[2224,128]{1,0:T(8,128)(2,1)S(1)}, bf16[2224,128]{1,0:T(8,128)(2,1)S(1)}, u32[]{:S(2)}, u32[]{:S(2)}) collective-permute-start(bf16[2224,128]{1,0:T(8,128)(2,1)S(1)} %copy-done.3), channel_id=1, source_target_pairs={{1,0},{3,2},{5,4},{7,6},{9,8},{11,10},{13,12},{15,14},{17,16},{19,... | collective-permute-start | bytes 1708040 | tf_op jit(solution)/shard_map/ppermute | solution.py:414
  43.4 1.8 %copy-start.4 = (bf16[2224,128]{1,0:T(8,128)(2,1)}, bf16[2224,128]{1,0:T(8,128)(2,1)S(1)}, u32[]{:S(2)}) copy-start(bf16[2224,128]{1,0:T(8,128)(2,1)S(1)} %collective-permute-done.4.far_ref) | copy-start | bytes 1708036
  43.4 18.1 %collective-permute-start.5 = (bf16[2224,128]{1,0:T(8,128)(2,1)S(1)}, bf16[2224,128]{1,0:T(8,128)(2,1)S(1)}, u32[]{:S(2)}, u32[]{:S(2)}) collective-permute-start(bf16[2224,128]{1,0:T(8,128)(2,1)S(1)} %collective-permute-done.4.far_ref), channel_id=1, source_target_pairs={{0,1},{2,3},{4,5},{6,7},{8,9},{10,11},{12,13},{14,15},{16,17},{18,... | collective-permute-start | bytes 1708040 | tf_op jit(solution)/shard_map/ppermute | solution.py:438
  45.0 4.1 %copy-start.7 = (f32[1,34,34,4]{2,3,1,0:T(4,128)S(1)}, f32[1,34,34,4]{2,3,1,0:T(4,128)}, u32[]{:S(2)}) copy-start(f32[1,34,34,4]{2,3,1,0:T(4,128)} %param.11) | copy-start | bytes 55492
  45.3 11.5 %copy-start = (bf16[2224,128]{1,0:T(8,128)(2,1)}, bf16[2224,128]{1,0:T(8,128)(2,1)S(1)}, u32[]{:S(2)}) copy-start(bf16[2224,128]{1,0:T(8,128)(2,1)S(1)} %fusion.1.source_ref) | copy-start | bytes 1708036
  45.3 39.9 %collective-permute-start.2 = (bf16[2224,128]{1,0:T(8,128)(2,1)S(1)}, bf16[2224,128]{1,0:T(8,128)(2,1)S(1)}, u32[]{:S(2)}, u32[]{:S(2)}) collective-permute-start(bf16[2224,128]{1,0:T(8,128)(2,1)S(1)} %fusion.1.source_ref), channel_id=1, source_target_pairs={{0,8},{8,16},{16,24},{1,9},{9,17},{17,25},{2,10},{10,18},{18,26},{... | collective-permute-start | bytes 1708040 | tf_op jit(solution)/shard_map/ppermute | solution.py:441
  61.6 0.8 copy-start.5
  62.4 0.8 copy-start.6
  85.2 0.8 copy-start.8
where the time goes:
time: 132 us; the launch traced here: 130 us
  Pallas kernels  73.4 us (56%)
  blocking collectives  24.5 us (19%)
  starting transfers between devices  13.6 us (10%)
  waiting for transfers between devices  10.3 us (8%)
  local copies, waits for them, and re-layouts  4.77 us (4%)
  other arithmetic  2.52 us (2%)
    pallas_call x7, Pallas kernels, call(): pl.pallas_call(kernel, out_shape=outs, in_specs=[smem()] * len(scalars) +...  73.4 us
    psum x1, blocking collectives, on_device(): stats = lax.psum(stats, 'sec')  24.5 us
    ppermute x1, waiting for transfers between devices, on_device(): right_far = lax.ppermute(right_packed, 'sec', down_two)  10.3 us
    ppermute x1, starting transfers between devices, on_device(): arrived = lax.ppermute(outgoing, 'sec', up_two)  5.28 us
    ppermute x1, starting transfers between devices, on_device(): received = lax.ppermute(fresh, 'seg', onward)  3.79 us
    unnamed x19, local copies, waits for them, and re-layouts  3.45 us
  transfers between devices with their start and end apart: 6, of which 1 were waited for; matrix products, arithmetic and copies ran while one was open for 1% of the time, Pallas kernels for 29%

commit v1 on v0

v1 whole, which is shorter than its diff:
```python
import functools

import jax
import jax.numpy as jnp
from jax import lax
from jax.experimental import pallas as pl
from jax.experimental.pallas import tpu as pltpu
from jax.sharding import PartitionSpec as P

LANCZOS = 4
CHARGES = (0, 1, 1, 2)
F32 = jnp.float32
BF16 = jnp.bfloat16
MIB = 1024 * 1024


def padded(count):
    return -(-count // 8) * 8


def packed_height(count):
    return -(-count // 16) * 16


def packed_rows(width, tile):
    return -(-(width * tile // 2 + padded(width)) // 16) * 16


def iotas(shape):
    return lax.broadcasted_iota(jnp.int32, shape, 0), lax.broadcasted_iota(jnp.int32, shape, 1)


def pack_block(block):
    tile = block.shape[0]
    half = tile // 2
    top, low = block[:half], block[half:]
    row, lane = iotas((half, tile))
    turned = pltpu.roll(low, half, 1)
    folded = jnp.where((lane < half) & (row > lane), turned, top)
    diagonal = jnp.sum(jnp.where(lane == row + half, low, 0.0), axis=0, keepdims=True)
    return folded, diagonal


def unpack_block(folded, diagonal):
    half, tile = folded.shape
    row, lane = iotas((half, tile))
    rolled = pltpu.roll(folded, half, 1)
    turned = jnp.transpose(jnp.concatenate([folded, rolled], axis=0))
    top = jnp.where((lane < half) & (row > lane), turned[:half], folded)
    low = jnp.where((lane >= half) & (row > lane - half), rolled, turned[half:])
    low = jnp.where(lane == row + half, diagonal, low)
    return jnp.concatenate([top, low], axis=0)


def live_limits(dims_ref):
    sector = lax.axis_index("sec")
    count = dims_ref.shape[0]
    rows = dims_ref[sector]
    columns = []
    for charge in CHARGES:
        target = sector + charge
        columns.append(jnp.where(target < count, dims_ref[jnp.minimum(target, count - 1)], 0))
    return rows, columns


def aligned(index, size):
    return pl.ds(pl.multiple_of(index * size, size), size)


def weight_rows(weight_ref, width, p, square, turned):
    wide = padded(width)
    square[...] = jnp.zeros_like(square)
    square[:width, :width] = weight_ref[pl.ds(p, width, stride=len(CHARGES)), :]
    value = square[...]
    if turned:
        value = jnp.transpose(value)
    high = value.astype(BF16).astype(F32)
    joined = (high + pltpu.roll(value - high, wide, 1)).astype(BF16)
    return joined[: packed_height(width), : 2 * wide]


def doubled(value):
    return jnp.concatenate([value, value], axis=0).astype(BF16)


def pack_kernel(width, tile, source_ref, out_ref, diag):
    half = tile // 2
    diag[...] = jnp.zeros_like(diag)
    for w in range(width):
        folded, diagonal = pack_block(source_ref[w * tile : (w + 1) * tile, :].astype(F32))
        out_ref[w * half : (w + 1) * half, :] = folded.astype(BF16)
        diag[w : w + 1, :] = diagonal
    out_ref[width * half :, :] = diag[...].astype(BF16)


def unpack_into(width, tile, pitch, read, out_ref, diag):
    half = tile // 2
    diag[...] = read(width * half, diag.shape[0])
    for w in range(width):
        block = unpack_block(read(w * half, half), diag[w : w + 1, :])
        out_ref[w * pitch : w * pitch + tile, :] = block.astype(out_ref.dtype)


def unpack_kernel(width, tile, source_ref, out_ref, diag):
    unpack_into(
        width, tile, tile, lambda at, size: source_ref[at : at + size, :].astype(F32), out_ref, diag
    )


def fold_kernel(
    width, tile, dims_ref, environ_ref, site_ref, weight_ref, own_ref, one_ref, two_ref,
    joined_s, turned_s, square_s, weight_s, half_s, packed_s, diag_s, sums_s, diag_sums_s,
):
    half = tile // 2
    pitch = half + 8
    wide = padded(width)
    states = len(CHARGES)
    rows, columns = live_limits(dims_ref)
    row, lane = iotas((tile, tile))
    for p in range(states):
        live = (row < rows) & (lane < columns[p])
        block = jnp.where(live, site_ref[p].astype(F32), 0.0)
        joined_s[:, p * tile : (p + 1) * tile] = block.astype(BF16)
        turned_s[p] = jnp.transpose(block).astype(BF16)
        weight_s[p] = weight_rows(weight_ref, width, p, square_s, True)
        packed_s[p, width * pitch :, :] = jnp.zeros(((wide - width) * pitch, tile), F32)
        diag_s[p] = jnp.zeros_like(diag_s[p])

    def first(pair, carry):
        for k in range(2):
            block = environ_ref[aligned(pair * 2 + k, tile), :]
            block = jnp.dot(block, joined_s[...], preferred_element_type=F32).astype(BF16)
            for p in range(states):
                half_s[p, aligned(pair, tile), k * tile : (k + 1) * tile] = block[
                    :, p * tile : (p + 1) * tile
                ]
        return carry

    lax.fori_loop(0, width // 2, first, 0, unroll=2)

    def second(pair, carry):
        for p in range(states):
            both = jnp.dot(turned_s[p], half_s[p, aligned(pair, tile), :], preferred_element_type=F32)
            for k in range(2):
                folded, diagonal = pack_block(both[:, k * tile : (k + 1) * tile])
                at = pl.multiple_of((pair * 2 + k) * pitch, 8)
                packed_s[p, pl.ds(at, half), :] = folded
                diag_s[p, pl.ds(pair * 2 + k, 1), :] = diagonal
        return carry

    lax.fori_loop(0, width // 2, second, 0, unroll=2)

    def mixed(inputs):
        products = [
            jnp.dot(weight_s[p], doubled(inputs[p]), preferred_element_type=F32)[:wide]
            for p in range(states)
        ]
        return products[0], products[1] + products[2], products[3]

    def mix(step, carry):
        at = step * 2
        inputs = [
            jnp.concatenate(
                [packed_s[p, pl.ds(at + k, wide, stride=pitch), :] for k in range(2)], axis=1
            )
            for p in range(states)
        ]
        for index, value in enumerate(mixed(inputs)):
            for k in range(2):
                sums_s[index, pl.ds(at + k, wide, stride=pitch), :] = value[:, k * tile : (k + 1) * tile]
        return carry

    lax.fori_loop(0, half // 2, mix, 0, unroll=4)
    diag_sums_s[...] = jnp.zeros_like(diag_sums_s)
    for index, value in enumerate(mixed([diag_s[p, :wide] for p in range(states)])):
        diag_sums_s[index, :wide, :] = value
    for index, ref in enumerate((own_ref, one_ref, two_ref)):
        for w in range(width):
            ref[w * half : (w + 1) * half, :] = sums_s[index, w * pitch : w * pitch + half, :].astype(
                ref.dtype
            )
        ref[width * half :, :] = diag_sums_s[index].astype(ref.dtype)


def mix_into(width, tile, weights, wide_s, sums_s, out_ref):
    wide = padded(width)
    pitch = tile + 8
    wide_s[width * pitch :, :] = jnp.zeros_like(wide_s[width * pitch :, :])

    def mix(step, carry):
        at = step * 2
        value = doubled(
            jnp.concatenate(
                [wide_s[pl.ds(at + k, wide, stride=pitch), :] for k in range(2)], axis=1
            )
        )
        for index, weight in enumerate(weights):
            mixed = jnp.dot(weight[...], value, preferred_element_type=F32)[:wide]
            for k in range(2):
                sums_s[index, pl.ds(at + k, wide, stride=pitch), :] = mixed[:, k * tile : (k + 1) * tile]
        return carry

    lax.fori_loop(0, tile // 2, mix, 0, unroll=4)
    for index in range(len(weights)):
        for w in range(width):
            out = (index * width + w) * tile
            out_ref[out : out + tile, :] = sums_s[index, w * pitch : w * pitch + tile, :].astype(BF16)


def mix_own_kernel(width, tile, source_ref, weight_ref, out_ref, square_s, weight_s, wide_s, sums_s):
    pitch = tile + 8
    weight_s[0] = weight_rows(weight_ref, width, 0, square_s, False)
    for w in range(width):
        wide_s[w * pitch : w * pitch + tile, :] = source_ref[w * tile : (w + 1) * tile, :].astype(F32)
    mix_into(width, tile, [weight_s.at[0]], wide_s, sums_s, out_ref)


def mix_next_kernel(
    width, tile, near_ref, relay_ref, weight_ref, out_ref, square_s, weight_s, wide_s, sums_s, diag
):
    for k in range(2):
        weight_s[k] = weight_rows(weight_ref, width, k + 1, square_s, False)

    def read(at, size):
        return near_ref[at : at + size, :].astype(F32) + relay_ref[at : at + size, :].astype(F32)

    unpack_into(width, tile, tile + 8, read, wide_s, diag)
    mix_into(width, tile, [weight_s.at[k] for k in range(2)], wide_s, sums_s, out_ref)


def mix_after_kernel(
    width, tile, far_ref, weight_ref, out_ref, square_s, weight_s, wide_s, sums_s, diag
):
    weight_s[0] = weight_rows(weight_ref, width, 3, square_s, False)

    def read(at, size):
        return far_ref[at : at + size, :].astype(F32)

    unpack_into(width, tile, tile + 8, read, wide_s, diag)
    mix_into(width, tile, [weight_s.at[0]], wide_s, sums_s, out_ref)


def total(value):
    return jnp.sum(jnp.sum(value, axis=0, keepdims=True), axis=1, keepdims=True)


def lanczos_kernel(
    width, tile, dims_ref, packed_ref, environ_ref, own_ref, next_ref, after_ref, guess_ref,
    basis_ref, stats_ref, bound_s, first_s, diag,
):
    states = len(CHARGES)
    sector = lax.axis_index("sec")
    segment = lax.axis_index("seg")

    @pl.when(segment == 0)
    def _():
        bound_s[...] = environ_ref[...]

    @pl.when(segment != 0)
    def _():
        unpack_into(
            width, tile, tile, lambda at, size: packed_ref[at : at + size, :].astype(F32), bound_s, diag
        )

    rows, columns = live_limits(dims_ref)
    row, lane = iotas((tile, tile))
    stat_row, stat_lane = iotas(stats_ref.shape)
    stats = jnp.zeros(stats_ref.shape, F32)

    def put(stats, kind, p, value):
        here = (stat_row == kind) & (stat_lane == sector * states + p)
        return jnp.where(here, value, stats)

    def scaled(value):
        square = total(value * value)
        inverse = jnp.where(square > 0.0, lax.rsqrt(square), 0.0)
        return value * inverse, square * inverse

    for p in range(states):
        live = (row < rows) & (lane < columns[p])
        vector, norm = scaled(jnp.where(live, guess_ref[p], 0.0))
        basis_ref[0, p] = vector
        stats = put(stats, 0, p, norm)

    size = width * tile
    rights = [own_ref, next_ref.at[:size, :], next_ref.at[size:, :], after_ref]
    betas = [jnp.zeros((1, 1), F32)] * states
    for j in range(LANCZOS):
        field = jnp.concatenate([basis_ref[j, p] for p in range(states)], axis=1).astype(BF16)
        for w in range(width):
            first = jnp.dot(
                bound_s[w * tile : (w + 1) * tile, :], field, preferred_element_type=F32
            ).astype(BF16)
            for p in range(states):
                first_s[p, :, w * tile : (w + 1) * tile] = first[:, p * tile : (p + 1) * tile]
        for p in range(states):
            live = (row < rows) & (lane < columns[p])
            right = rights[p][...]
            image = jnp.dot(first_s[p], right, preferred_element_type=F32)
            image = jnp.where(live, image, 0.0)
            vector = basis_ref[j, p]
            alpha = total(vector * image)
            image = image - alpha * vector
            if j > 0:
                image = image - betas[p] * basis_ref[j - 1, p]
            following, beta = scaled(image)
            basis_ref[j + 1, p] = following
            betas[p] = beta
            stats = put(stats, 1 + 2 * j, p, alpha)
            stats = put(stats, 2 + 2 * j, p, beta)
    stats_ref[...] = stats


def finish_kernel(entries, stats_ref, basis_ref, vector_ref, table_ref):
    states = len(CHARGES)
    sector = lax.axis_index("sec")
    stats = stats_ref[...]
    alphas = [stats[1 + 2 * j : 2 + 2 * j, :] for j in range(LANCZOS)]
    betas = [stats[2 + 2 * j : 3 + 2 * j, :] for j in range(LANCZOS)]

    def mean(left, right):
        products = left[0] * right[0]
        for x, y in zip(left[1:], right[1:]):
            products = products + x * y
        return jnp.sum(products, axis=1, keepdims=True) / entries

    start = [stats[0:1, :]]
    vector = [start[0] / jnp.sqrt(mean(start, start) + 1e-06)]
    previous = []
    beta = jnp.zeros((1, 1), F32)
    table_row, table_column = iotas(table_ref.shape)
    table = jnp.zeros(table_ref.shape, F32)
    for j in range(LANCZOS):
        image = []
        for k in range(j + 2):
            term = None
            if k > 0:
                term = betas[k - 1] * vector[k - 1]
            if k <= j:
                more = alphas[k] * vector[k]
                term = more if term is None else term + more
            if k + 1 <= j:
                term = term + betas[k] * vector[k + 1]
            image.append(term)
        alpha = mean(vector, image[: j + 1])
        for k in range(j + 1):
            image[k] = image[k] - alpha * vector[k]
        for k in range(j):
            image[k] = image[k] - beta * previous[k]
        beta = jnp.sqrt(mean(image, image) + 1e-06)
        previous = vector
        vector = [value / beta for value in image]
        table = jnp.where((table_row == 0) & (table_column == j), alpha, table)
        table = jnp.where((table_row == 1) & (table_column == j), beta, table)
    table_ref[...] = table
    lane = lax.broadcasted_iota(jnp.int32, (1, stats.shape[1]), 1)
    for p in range(states):
        value = None
        here = lane == sector * states + p
        for k in range(LANCZOS + 1):
            weight = jnp.sum(jnp.where(here, vector[k], 0.0), axis=1, keepdims=True)
            term = weight * basis_ref[k, p]
            value = term if value is None else value + term
        vector_ref[p] = value


def smem():
    return pl.BlockSpec(memory_space=pltpu.SMEM)


def vmem():
    return pl.BlockSpec(memory_space=pltpu.VMEM)


def call(name, kernel, scalars, arrays, outs, scratch, limit, micros):
    many = isinstance(outs, (tuple, list))
    return pl.pallas_call(
        kernel,
        out_shape=outs,
        in_specs=[smem()] * len(scalars) + [vmem()] * len(arrays),
        out_specs=[vmem()] * len(outs) if many else vmem(),
        scratch_shapes=scratch,
        compiler_params=pltpu.CompilerParams(vmem_limit_bytes=limit * MIB),
        name=name,
        cost_estimate=pl.CostEstimate(
            flops=int(micros * 1.1e9), bytes_accessed=0, transcendentals=0
        ),
    )(*scalars, *arrays)


def pairs_of(count, pick):
    return [(source, target) for source in range(count) for target in pick(source) if 0 <= target < count]


def on_device(left_env, right_env, site_tensors, mpo, boundary_mpo, guess, sector_dims):
    width, tile = left_env.shape[2], left_env.shape[-1]
    half = tile // 2
    wide = padded(width)
    states = len(CHARGES)
    sector_count = sector_dims.shape[0]
    sectors = lax.axis_size("sec")
    segments = lax.axis_size("seg")
    prows = packed_rows(width, tile)
    drows = prows - width * half
    odd = lax.rem(lax.axis_index("sec"), 2) == 1
    packed = jax.ShapeDtypeStruct((prows, tile), BF16)
    packed32 = jax.ShapeDtypeStruct((prows, tile), F32)

    def blocks(count):
        return jax.ShapeDtypeStruct((count * width * tile, tile), BF16)

    environ = left_env.reshape(width * tile, tile)
    right = right_env.reshape(width * tile, tile)
    site = site_tensors[0, 0, :, 0]
    site_weights = jnp.transpose(mpo[0, 0], (0, 2, 1)).reshape(width * states, width)
    bound_weights = jnp.transpose(boundary_mpo[0], (0, 2, 1)).reshape(width * states, width)

    swap = pairs_of(sectors, lambda q: [q ^ 1])
    down = pairs_of(sectors, lambda q: [q - 1] if q % 2 else [])
    across = pairs_of(sectors, lambda q: [q + 1] if q % 2 == 0 else [])
    up_two = pairs_of(sectors, lambda q: [q + 2])
    down_two = pairs_of(sectors, lambda q: [q - 2])
    onward = pairs_of(segments, lambda s: [s + 1])
    diag = pltpu.VMEM((drows, tile), F32)

    def mix_scratch(count):
        return [
            pltpu.VMEM((tile, tile), F32),
            pltpu.VMEM((count, packed_height(width), 2 * wide), BF16),
            pltpu.VMEM((wide * (tile + 8), tile), F32),
            pltpu.VMEM((count, wide * (tile + 8), tile), F32),
        ]

    right_packed = call(
        "pack_right", functools.partial(pack_kernel, width, tile), [], [right], packed, [diag], 6, 2
    )
    right_far = lax.ppermute(right_packed, "sec", down_two)
    right_near = lax.ppermute(right_packed, "sec", down)
    environ, right_packed = lax.optimization_barrier((environ, right_packed))
    own, one, two = call(
        "fold", functools.partial(fold_kernel, width, tile),
        [sector_dims], [environ, site, site_weights], (packed32, packed, packed32),
        [
            pltpu.VMEM((tile, states * tile), BF16),
            pltpu.VMEM((states, tile, tile), BF16),
            pltpu.VMEM((tile, tile), F32),
            pltpu.VMEM((states, packed_height(width), 2 * wide), BF16),
            pltpu.VMEM((states, width // 2 * tile, 2 * tile), BF16),
            pltpu.VMEM((states, wide * (half + 8), tile), F32),
            pltpu.VMEM((states, drows, tile), F32),
            pltpu.VMEM((3, wide * (half + 8), tile), F32),
            pltpu.VMEM((3, drows, tile), F32),
        ],
        26, 12,
    )
    one, right_far = lax.optimization_barrier((one, right_far))
    partner = lax.ppermute(one, "sec", swap)
    outgoing = jnp.where(odd, two, two + partner.astype(F32)).astype(BF16)
    right, outgoing = lax.optimization_barrier((right, outgoing))
    arrived = lax.ppermute(outgoing, "sec", up_two)
    right_relay = lax.ppermute(right_far, "sec", across)
    own_mixed = call(
        "mix_own", functools.partial(mix_own_kernel, width, tile), [], [right, bound_weights],
        blocks(1), mix_scratch(1), 12, 5,
    )
    after_mixed = call(
        "mix_after", functools.partial(mix_after_kernel, width, tile), [],
        [right_far, bound_weights], blocks(1), mix_scratch(1) + [diag], 12, 6,
    )
    arrived, own_mixed, after_mixed = lax.optimization_barrier((arrived, own_mixed, after_mixed))
    fresh = own + arrived.astype(F32) + jnp.where(odd, partner.astype(F32), 0.0)
    fresh = fresh.astype(BF16)
    received = lax.ppermute(fresh, "seg", onward)
    next_mixed = call(
        "mix_next", functools.partial(mix_next_kernel, width, tile), [],
        [right_near, right_relay, bound_weights], blocks(2), mix_scratch(2) + [diag], 16, 7,
    )
    new_env = call(
        "unpack_env", functools.partial(unpack_kernel, width, tile), [], [fresh], blocks(1), [diag],
        6, 3,
    )
    received, next_mixed, new_env = lax.optimization_barrier((received, next_mixed, new_env))
    basis, stats = call(
        "lanczos", functools.partial(lanczos_kernel, width, tile),
        [sector_dims], [received, environ, own_mixed, next_mixed, after_mixed, guess[0, :, 0]],
        (
            jax.ShapeDtypeStruct((LANCZOS + 1, states, tile, tile), F32),
            jax.ShapeDtypeStruct((16, 128), F32),
        ),
        [
            pltpu.VMEM((width * tile, tile), BF16),
            pltpu.VMEM((states, tile, width * tile), BF16),
            diag,
        ],
        18, 15,
    )
    stats = lax.psum(stats, "sec")
    entries = float(states * sector_count * tile * tile)
    vector, table = call(
        "finish", functools.partial(finish_kernel, entries), [], [stats, basis],
        (
            jax.ShapeDtypeStruct((states, tile, tile), F32),
            jax.ShapeDtypeStruct((2, LANCZOS), F32),
        ),
        [], 6, 2,
    )
    return new_env.reshape(left_env.shape), vector[None, :, None], jnp.transpose(table)[None]


def solution(mesh):
    placed = (
        P("seg", "sec", None, None, None),
        P("seg", "sec", None, None, None),
        P("seg", None, None, "sec", None, None),
        P("seg", None, None, None, None),
        P("seg", None, None, None),
        P("seg", None, "sec", None, None),
        P(),
    )
    return jax.shard_map(
        on_device,
        mesh=mesh,
        in_specs=placed,
        out_specs=(
            P("seg", "sec", None, None, None),
            P("seg", None, "sec", None, None),
            P("seg", None, None),
        ),
        check_vma=False,
    )
```

time: 132 us -> 86.5 us (0.66)
  Pallas kernels: 73.4 us -> 39.7 us
  blocking collectives: 24.5 us -> 12 us
  waiting for transfers between devices: 10.3 us -> 14 us
  local copies, waits for them, and re-layouts: 4.77 us -> 1.28 us
    pallas_call x7 -> x8, Pallas kernels: 73.4 us -> 39.7 us  [call(): pl.pallas_call(kernel, out_shape=outs, in_specs=[smem()] * len(scalars) +...]
    psum x1, blocking collectives: 24.5 us -> 12 us  [on_device(): stats = lax.psum(stats, 'sec')]
    ppermute x1, waiting for transfers between devices: 0.01 us -> 3.74 us  [on_device(): arrived = lax.ppermute(outgoing, 'sec', up_two)]
    ppermute x1, waiting for transfers between devices: 10.3 us -> 6.92 us  [on_device(): right_far = lax.ppermute(right_packed, 'sec', down_two)]
    ppermute x1, waiting for transfers between devices: 0.01 us -> 3.32 us  [on_device(): received = lax.ppermute(fresh, 'seg', onward)]
    ppermute x1, starting transfers between devices: 1.49 us -> 3.87 us  [on_device(): right_relay = lax.ppermute(right_far, 'sec', across)]
    unnamed x19 -> x16, local copies, waits for them, and re-layouts: 3.45 us -> 1.28 us
    concatenate x2 -> x0, other arithmetic: 1.41 us -> none  [split_weights(): return jnp.concatenate([jnp.pad(high, gap), jnp.pad(low, gap)], axis=2)]
  transfers between devices with their start and end apart: 6 -> 6, of which waited for: 1 -> 3; matrix products, arithmetic and copies ran while one was open for 1% -> 3% of each run, Pallas kernels for 29% -> 29%
where the time goes in v1:
time: 86.5 us; the launch traced here: 84.8 us
  Pallas kernels  39.7 us (46%)
  starting transfers between devices  14.5 us (17%)
  waiting for transfers between devices  14 us (16%)
  blocking collectives  12 us (14%)
  other arithmetic  2.53 us (3%)
  local copies, waits for them, and re-layouts  1.28 us (1%)
    pallas_call x8, Pallas kernels, call(): pl.pallas_call(kernel, out_shape=outs, in_specs=[smem()] * len(scalars) +...  39.7 us
    psum x1, blocking collectives, on_device(): stats = lax.psum(stats, 'sec')  12 us
    ppermute x1, waiting for transfers between devices, on_device(): right_far = lax.ppermute(right_packed, 'sec', down_two)  6.92 us
    ppermute x1, starting transfers between devices, on_device(): arrived = lax.ppermute(outgoing, 'sec', up_two)  4.57 us
    ppermute x1, starting transfers between devices, on_device(): right_relay = lax.ppermute(right_far, 'sec', across)  3.87 us
    ppermute x1, waiting for transfers between devices, on_device(): arrived = lax.ppermute(outgoing, 'sec', up_two)  3.74 us
    ppermute x1, starting transfers between devices, on_device(): received = lax.ppermute(fresh, 'seg', onward)  3.52 us
    ppermute x1, waiting for transfers between devices, on_device(): received = lax.ppermute(fresh, 'seg', onward)  3.32 us
  transfers between devices with their start and end apart: 6, of which 3 were waited for; matrix products, arithmetic and copies ran while one was open for 3% of the time, Pallas kernels for 29%

profile of v1, /device:TPU:0, one launch (start us, length us, event | category | flops | bytes accessed | tf_op | source)
XLA Modules:
  0.0 84.8 jit_solution(10931548130969114718)
XLA Ops:
  0.6 0.0 copy-start
  0.6 1.2 %copy-done = bf16[1,1,34,128,128]{4,3,2,1,0:T(8,128)(2,1)S(1)} copy-done((bf16[1,1,34,128,128]{4,3,2,1,0:T(8,128)(2,1)S(1)}, bf16[1,1,34,128,128]{4,3,2,1,0:T(8,128)(2,1)}, u32[]{:S(2)}) %copy-start) | copy-done | bytes 1114136
  1.9 0.0 copy-start.2
  1.9 0.0 copy-start.4
  1.9 0.0 copy-start.5
  1.9 0.0 copy-start.7
  1.9 1.1 %pack_right.1 = bf16[2224,128]{1,0:T(8,128)(2,1)} custom-call(bf16[4352,128]{1,0:T(8,128)(2,1)S(1)} %bitcast.21), custom_call_target="tpu_custom_call" | custom-call | flops 2200000000 | tf_op jit(solution)/shard_map/pack_right/pallas_call | solution.py:377
  3.0 1.3 %collective-permute-start = (bf16[2224,128]{1,0:T(8,128)(2,1)}, bf16[2224,128]{1,0:T(8,128)(2,1)}, u32[]{:S(2)}, u32[]{:S(2)}) collective-permute-start(bf16[2224,128]{1,0:T(8,128)(2,1)} %pack_right.1), channel_id=1, source_target_pairs={{2,0},{3,1},{4,2},{5,3},{6,4},{7,5},{10,8},{11,9},{12,10},{13,11},... | collective-permute-start | bytes 1708040 | tf_op jit(solution)/shard_map/ppermute | solution.py:437
  4.3 0.0 copy-done.2
  4.3 0.0 copy-done.4
  4.3 0.0 copy-done.5
  4.3 0.0 copy-done.7
  4.3 9.8 %fold.1 = (f32[2224,128]{1,0:T(8,128)S(1)}, bf16[2224,128]{1,0:T(8,128)(2,1)}, f32[2224,128]{1,0:T(8,128)S(1)}) custom-call(s32[8]{0:T(128)S(1)} %copy-done.7, bf16[4352,128]{1,0:T(8,128)(2,1)S(1)} %bitcast.23, bf16[4,128,128]{2,1,0:T(8,128)(2,1)S(1)} %bitcast.26, f32[136,34]{1,0:T(8,128)S(1)} %bitcast.27), custom_call_target="tpu_custom_call" | custom-call | flops 13200000000 | tf_op jit(solution)/shard_map/fold/pallas_call | solution.py:377
  14.1 6.9 %collective-permute-done.far_ref = bf16[2224,128]{1,0:T(8,128)(2,1)} collective-permute-done((bf16[2224,128]{1,0:T(8,128)(2,1)}, bf16[2224,128]{1,0:T(8,128)(2,1)}, u32[]{:S(2)}, u32[]{:S(2)}) %collective-permute-start) | collective-permute-done | bytes 569376 | tf_op jit(solution)/shard_map/ppermute | solution.py:437
  21.0 0.0 collective-permute-start.1
  21.0 1.3 %collective-permute-start.4 = (bf16[2224,128]{1,0:T(8,128)(2,1)}, bf16[2224,128]{1,0:T(8,128)(2,1)}, u32[]{:S(2)}, u32[]{:S(2)}) collective-permute-start(bf16[2224,128]{1,0:T(8,128)(2,1)} %pack_right.1), channel_id=1, source_target_pairs={{1,0},{3,2},{5,4},{7,6},{9,8},{11,10},{13,12},{15,14},{17,16},{19,... | collective-permute-start | bytes 1708040 | tf_op jit(solution)/shard_map/ppermute | solution.py:438
  22.3 3.9 %collective-permute-start.5 = (bf16[2224,128]{1,0:T(8,128)(2,1)}, bf16[2224,128]{1,0:T(8,128)(2,1)S(1)}, u32[]{:S(2)}, u32[]{:S(2)}) collective-permute-start(bf16[2224,128]{1,0:T(8,128)(2,1)} %collective-permute-done.far_ref), channel_id=1, source_target_pairs={{0,1},{2,3},{4,5},{6,7},{8,9},{10,11},{12,13},{14,15},{16,17},{18,... | collective-permute-start | bytes 1708040 | tf_op jit(solution)/shard_map/ppermute | solution.py:461
  26.2 0.0 collective-permute-done.1
  26.2 0.0 copy-start.6
  26.2 1.2 %fusion.2 = bf16[2224,128]{1,0:T(8,128)(2,1)S(1)} fusion(f32[2224,128]{1,0:T(8,128)S(1)} %get-tuple-element.23, bf16[2224,128]{1,0:T(8,128)(2,1)} %collective-permute-done.1, pred[]{:T(512)S(6)} %eq.3), kind=kLoop, calls=%fused_computation.4 | loop fusion | flops 1138688 | bytes 2277377 | tf_op jit(solution)/shard_map/convert_element_type | solution.py:458
  27.5 4.6 %collective-permute-start.2 = (bf16[2224,128]{1,0:T(8,128)(2,1)S(1)}, bf16[2224,128]{1,0:T(8,128)(2,1)S(1)}, u32[]{:S(2)}, u32[]{:S(2)}) collective-permute-start(bf16[2224,128]{1,0:T(8,128)(2,1)S(1)} %fusion.2), channel_id=1, source_target_pairs={{0,2},{1,3},{2,4},{3,5},{4,6},{5,7},{8,10},{9,11},{10,12},{11,13},... | collective-permute-start | bytes 1708040 | tf_op jit(solution)/shard_map/ppermute | solution.py:460
  32.1 0.0 copy-done.6
  32.1 0.0 copy-start.1
  32.1 4.8 %mix_after.1.after_ref = bf16[4352,128]{1,0:T(8,128)(2,1)S(1)} custom-call(bf16[2224,128]{1,0:T(8,128)(2,1)} %collective-permute-done.far_ref, f32[136,34]{1,0:T(8,128)S(1)} %bitcast.28), custom_call_target="tpu_custom_call" | custom-call | flops 6600000000 | tf_op jit(solution)/shard_map/mix_after/pallas_call | solution.py:377
  36.9 0.0 copy-done.1
  36.9 3.0 %mix_own.1.own_ref = bf16[4352,128]{1,0:T(8,128)(2,1)S(1)} custom-call(bf16[4352,128]{1,0:T(8,128)(2,1)S(1)} %bitcast.22, f32[136,34]{1,0:T(8,128)S(1)} %bitcast.29), custom_call_target="tpu_custom_call" | custom-call | flops 5500000256 | tf_op jit(solution)/shard_map/mix_own/pallas_call | solution.py:377
  39.9 3.7 %collective-permute-done.2 = bf16[2224,128]{1,0:T(8,128)(2,1)S(1)} collective-permute-done((bf16[2224,128]{1,0:T(8,128)(2,1)S(1)}, bf16[2224,128]{1,0:T(8,128)(2,1)S(1)}, u32[]{:S(2)}, u32[]{:S(2)}) %collective-permute-start.2) | collective-permute-done | bytes 569376 | tf_op jit(solution)/shard_map/ppermute | solution.py:460
  43.7 1.3 %fusion.1.source_ref = bf16[2224,128]{1,0:T(8,128)(2,1)S(1)} fusion(bf16[2224,128]{1,0:T(8,128)(2,1)} %collective-permute-done.1, f32[2224,128]{1,0:T(8,128)S(1)} %get-tuple-element.22, bf16[2224,128]{1,0:T(8,128)(2,1)S(1)} %collective-permute-done.2, pred[]{:T(512)S(6)} %eq.3), kind=kLoop, calls=%fused_computation.3 | loop fusion | flops 1708032 | bytes 2846721 | tf_op jit(solution)/shard_map/convert_element_type | solution.py:472
  44.9 3.5 %collective-permute-start.3 = (bf16[2224,128]{1,0:T(8,128)(2,1)S(1)}, bf16[2224,128]{1,0:T(8,128)(2,1)S(1)}, u32[]{:S(2)}, u32[]{:S(2)}) collective-permute-start(bf16[2224,128]{1,0:T(8,128)(2,1)S(1)} %fusion.1.source_ref), channel_id=1, source_target_pairs={{0,8},{8,16},{16,24},{1,9},{9,17},{17,25},{2,10},{10,18},{18,26},{... | collective-permute-start | bytes 1708040 | tf_op jit(solution)/shard_map/ppermute | solution.py:473
  48.5 0.0 collective-permute-done.4.near_ref
  48.5 0.0 collective-permute-done.5.relay_ref
  48.5 5.5 %mix_next.1.next_ref = bf16[8704,128]{1,0:T(8,128)(2,1)S(1)} custom-call(bf16[2224,128]{1,0:T(8,128)(2,1)} %collective-permute-done.4.near_ref, bf16[2224,128]{1,0:T(8,128)(2,1)S(1)} %collective-permute-done.5.relay_ref, f32[136,34]{1,0:T(8,128)S(1)} %bitcast.30), custom_call_target="tpu_custom_call" | custom-call | flops 7699999744 | tf_op jit(solution)/shard_map/mix_next/pallas_call | solution.py:377
  54.0 0.0 copy-start.3
  54.0 1.8 %unpack_env.1 = bf16[4352,128]{1,0:T(8,128)(2,1)} custom-call(bf16[2224,128]{1,0:T(8,128)(2,1)S(1)} %fusion.1.source_ref), custom_call_target="tpu_custom_call" | custom-call | flops 3300000000 | tf_op jit(solution)/shard_map/unpack_env/pallas_call | solution.py:377
  55.8 3.3 %collective-permute-done.3.packed_ref = bf16[2224,128]{1,0:T(8,128)(2,1)S(1)} collective-permute-done((bf16[2224,128]{1,0:T(8,128)(2,1)S(1)}, bf16[2224,128]{1,0:T(8,128)(2,1)S(1)}, u32[]{:S(2)}, u32[]{:S(2)}) %collective-permute-start.3) | collective-permute-done | bytes 569376 | tf_op jit(solution)/shard_map/ppermute | solution.py:473
  59.2 0.0 copy-done.3
  59.2 11.9 %lanczos.1 = (f32[5,4,128,128]{3,2,1,0:T(8,128)S(1)}, f32[16,128]{1,0:T(8,128)S(1)}) custom-call(s32[8]{0:T(128)S(1)} %copy-done.7, bf16[2224,128]{1,0:T(8,128)(2,1)S(1)} %collective-permute-done.3.packed_ref, bf16[4352,128]{1,0:T(8,128)(2,1)S(1)} %bitcast.24, bf16[4352,128]{1,0:T(8,128)(2,1)S(1)} %mix_own.1.own_ref, ...), custom_call_target="tpu_custom_call" | custom-call | flops 16499999744 | tf_op jit(solution)/shard_map/lanczos/pallas_call | solution.py:377
  71.1 12.0 %psum.7.stats_ref = f32[16,128]{1,0:T(8,128)S(1)} all-reduce(f32[16,128]{1,0:T(8,128)S(1)} %get-tuple-element.35), channel_id=1, replica_groups=mesh['seg'=4,'sec'=8] {'sec'}, use_global_device_ids=true, to_apply=%region_0.1 | all-reduce | flops 2048 | bytes 16384 | tf_op jit(solution)/shard_map/psum | solution.py:497
  83.1 1.7 %finish.1 = (f32[4,128,128]{2,1,0:T(8,128)}, f32[2,4]{1,0:T(2,128)}) custom-call(f32[16,128]{1,0:T(8,128)S(1)} %psum.7.stats_ref, f32[5,4,128,128]{3,2,1,0:T(8,128)S(1)} %get-tuple-element.36.basis_ref), custom_call_target="tpu_custom_call" | custom-call | flops 2200000000 | tf_op jit(solution)/shard_map/finish/pallas_call | solution.py:377
Async XLA Ops:
  0.6 1.3 %copy-start = (bf16[1,1,34,128,128]{4,3,2,1,0:T(8,128)(2,1)S(1)}, bf16[1,1,34,128,128]{4,3,2,1,0:T(8,128)(2,1)}, u32[]{:S(2)}) copy-start(bf16[1,1,34,128,128]{4,3,2,1,0:T(8,128)(2,1)} %param.8) | copy-start | bytes 3342340
  1.9 2.4 %copy-start.2 = (bf16[1,1,34,128,128]{4,3,2,1,0:T(8,128)(2,1)S(1)}, bf16[1,1,34,128,128]{4,3,2,1,0:T(8,128)(2,1)}, u32[]{:S(2)}) copy-start(bf16[1,1,34,128,128]{4,3,2,1,0:T(8,128)(2,1)} %param.7) | copy-start | bytes 3342340
  1.9 2.4 %copy-start.4 = (bf16[1,1,4,1,128,128]{5,4,3,2,1,0:T(8,128)(2,1)S(1)}, bf16[1,1,4,1,128,128]{5,4,3,2,1,0:T(8,128)(2,1)}, u32[]{:S(2)}) copy-start(bf16[1,1,4,1,128,128]{5,4,3,2,1,0:T(8,128)(2,1)} %param.9) | copy-start | bytes 393220
  1.9 2.4 %copy-start.5 = (f32[1,1,34,34,4]{3,4,2,1,0:T(4,128)S(1)}, f32[1,1,34,34,4]{3,4,2,1,0:T(4,128)}, u32[]{:S(2)}) copy-start(f32[1,1,34,34,4]{3,4,2,1,0:T(4,128)} %param.10) | copy-start | bytes 55492
  1.9 2.4 %copy-start.7 = (s32[8]{0:T(128)S(1)}, s32[8]{0:T(128)}, u32[]{:S(2)}) copy-start(s32[8]{0:T(128)} %dims_ref.3) | copy-start | bytes 100
  3.0 18.0 %collective-permute-start = (bf16[2224,128]{1,0:T(8,128)(2,1)}, bf16[2224,128]{1,0:T(8,128)(2,1)}, u32[]{:S(2)}, u32[]{:S(2)}) collective-permute-start(bf16[2224,128]{1,0:T(8,128)(2,1)} %pack_right.1), channel_id=1, source_target_pairs={{2,0},{3,1},{4,2},{5,3},{6,4},{7,5},{10,8},{11,9},{12,10},{13,11},... | collective-permute-start | bytes 1708040 | tf_op jit(solution)/shard_map/ppermute | solution.py:437
  21.0 5.2 %collective-permute-start.1 = (bf16[2224,128]{1,0:T(8,128)(2,1)}, bf16[2224,128]{1,0:T(8,128)(2,1)}, u32[]{:S(2)}, u32[]{:S(2)}) collective-permute-start(bf16[2224,128]{1,0:T(8,128)(2,1)} %get-tuple-element.25), channel_id=1, source_target_pairs={{0,1},{1,0},{2,3},{3,2},{4,5},{5,4},{6,7},{7,6},{8,9},{9,8},{10,11... | collective-permute-start | bytes 1708040 | tf_op jit(solution)/shard_map/ppermute | solution.py:457
  21.0 27.4 %collective-permute-start.4 = (bf16[2224,128]{1,0:T(8,128)(2,1)}, bf16[2224,128]{1,0:T(8,128)(2,1)}, u32[]{:S(2)}, u32[]{:S(2)}) collective-permute-start(bf16[2224,128]{1,0:T(8,128)(2,1)} %pack_right.1), channel_id=1, source_target_pairs={{1,0},{3,2},{5,4},{7,6},{9,8},{11,10},{13,12},{15,14},{17,16},{19,... | collective-permute-start | bytes 1708040 | tf_op jit(solution)/shard_map/ppermute | solution.py:438
  22.3 26.2 %collective-permute-start.5 = (bf16[2224,128]{1,0:T(8,128)(2,1)}, bf16[2224,128]{1,0:T(8,128)(2,1)S(1)}, u32[]{:S(2)}, u32[]{:S(2)}) collective-permute-start(bf16[2224,128]{1,0:T(8,128)(2,1)} %collective-permute-done.far_ref), channel_id=1, source_target_pairs={{0,1},{2,3},{4,5},{6,7},{8,9},{10,11},{12,13},{14,15},{16,17},{18,... | collective-permute-start | bytes 1708040 | tf_op jit(solution)/shard_map/ppermute | solution.py:461
  26.2 5.8 %copy-start.6 = (f32[1,34,34,4]{2,3,1,0:T(4,128)S(1)}, f32[1,34,34,4]{2,3,1,0:T(4,128)}, u32[]{:S(2)}) copy-start(f32[1,34,34,4]{2,3,1,0:T(4,128)} %param.11) | copy-start | bytes 55492
  27.5 16.2 %collective-permute-start.2 = (bf16[2224,128]{1,0:T(8,128)(2,1)S(1)}, bf16[2224,128]{1,0:T(8,128)(2,1)S(1)}, u32[]{:S(2)}, u32[]{:S(2)}) collective-permute-start(bf16[2224,128]{1,0:T(8,128)(2,1)S(1)} %fusion.2), channel_id=1, source_target_pairs={{0,2},{1,3},{2,4},{3,5},{4,6},{5,7},{8,10},{9,11},{10,12},{11,13},... | collective-permute-start | bytes 1708040 | tf_op jit(solution)/shard_map/ppermute | solution.py:460
  32.1 4.9 %copy-start.1 = (bf16[1,1,34,128,128]{4,3,2,1,0:T(8,128)(2,1)S(1)}, bf16[1,1,34,128,128]{4,3,2,1,0:T(8,128)(2,1)}, u32[]{:S(2)}) copy-start(bf16[1,1,34,128,128]{4,3,2,1,0:T(8,128)(2,1)} %param.8) | copy-start | bytes 3342340
  44.9 14.2 %collective-permute-start.3 = (bf16[2224,128]{1,0:T(8,128)(2,1)S(1)}, bf16[2224,128]{1,0:T(8,128)(2,1)S(1)}, u32[]{:S(2)}, u32[]{:S(2)}) collective-permute-start(bf16[2224,128]{1,0:T(8,128)(2,1)S(1)} %fusion.1.source_ref), channel_id=1, source_target_pairs={{0,8},{8,16},{16,24},{1,9},{9,17},{17,25},{2,10},{10,18},{18,26},{... | collective-permute-start | bytes 1708040 | tf_op jit(solution)/shard_map/ppermute | solution.py:473
  54.0 5.2 %copy-start.3 = (f32[1,4,1,128,128]{4,3,2,1,0:T(8,128)S(1)}, f32[1,4,1,128,128]{4,3,2,1,0:T(8,128)}, u32[]{:S(2)}) copy-start(f32[1,4,1,128,128]{4,3,2,1,0:T(8,128)} %param.12) | copy-start | bytes 786436

commit v2 on v1

--- a/solution.py
+++ b/solution.py
@@ -52,8 +52,11 @@
     return jnp.concatenate([top, low], axis=0)
 
 
-def live_limits(dims_ref):
-    sector = lax.axis_index("sec")
+def partner_of(sector):
+    return sector + 1 - 2 * lax.rem(sector, 2)
+
+
+def live_limits(dims_ref, sector):
     count = dims_ref.shape[0]
     rows = dims_ref[sector]
     columns = []
@@ -83,14 +86,23 @@
     return jnp.concatenate([value, value], axis=0).astype(BF16)
 
 
-def pack_kernel(width, tile, source_ref, out_ref, diag):
+def prepare_kernel(width, tile, right_ref, environ_ref, site_ref, packed_ref, bundle_ref, diag):
     half = tile // 2
+    size = width * tile
     diag[...] = jnp.zeros_like(diag)
+    bundle_ref[:size, :] = environ_ref[...]
+    for k in range(2):
+        bundle_ref[size + k * tile : size + (k + 1) * tile, :] = site_ref[k + 1]
+    base = size + 2 * tile
     for w in range(width):
-        folded, diagonal = pack_block(source_ref[w * tile : (w + 1) * tile, :].astype(F32))
-        out_ref[w * half : (w + 1) * half, :] = folded.astype(BF16)
+        folded, diagonal = pack_block(right_ref[w * tile : (w + 1) * tile, :].astype(F32))
+        folded = folded.astype(BF16)
+        packed_ref[w * half : (w + 1) * half, :] = folded
+        bundle_ref[base + w * half : base + (w + 1) * half, :] = folded
         diag[w : w + 1, :] = diagonal
-    out_ref[width * half :, :] = diag[...].astype(BF16)
+    rows = diag[...].astype(BF16)
+    packed_ref[width * half :, :] = rows
+    bundle_ref[base + width * half :, :] = rows
 
 
 def unpack_into(width, tile, pitch, read, out_ref, diag):
@@ -108,78 +120,106 @@
 
 
 def fold_kernel(
-    width, tile, dims_ref, environ_ref, site_ref, weight_ref, own_ref, one_ref, two_ref,
+    width, tile, travels, dims_ref, environ_ref, site_ref, bundle_ref, weight_ref, out_ref,
     joined_s, turned_s, square_s, weight_s, half_s, packed_s, diag_s, sums_s, diag_sums_s,
 ):
     half = tile // 2
     pitch = half + 8
     wide = padded(width)
-    states = len(CHARGES)
-    rows, columns = live_limits(dims_ref)
+    size = width * tile
+    sector = lax.axis_index("sec")
+    partner = partner_of(sector)
     row, lane = iotas((tile, tile))
-    for p in range(states):
-        live = (row < rows) & (lane < columns[p])
-        block = jnp.where(live, site_ref[p].astype(F32), 0.0)
-        joined_s[:, p * tile : (p + 1) * tile] = block.astype(BF16)
-        turned_s[p] = jnp.transpose(block).astype(BF16)
-        weight_s[p] = weight_rows(weight_ref, width, p, square_s, True)
-        packed_s[p, width * pitch :, :] = jnp.zeros(((wide - width) * pitch, tile), F32)
-        diag_s[p] = jnp.zeros_like(diag_s[p])
-
-    def first(pair, carry):
-        for k in range(2):
-            block = environ_ref[aligned(pair * 2 + k, tile), :]
-            block = jnp.dot(block, joined_s[...], preferred_element_type=F32).astype(BF16)
-            for p in range(states):
-                half_s[p, aligned(pair, tile), k * tile : (k + 1) * tile] = block[
-                    :, p * tile : (p + 1) * tile
+
+    def run(own_state, with_partner):
+        rows, columns = live_limits(dims_ref, sector)
+        live = (row < rows) & (lane < columns[own_state])
+        sites = [jnp.where(live, site_ref[own_state].astype(F32), 0.0)]
+        states = [own_state]
+        if with_partner:
+            rows, columns = live_limits(dims_ref, partner)
+            for k in range(2):
+                live = (row < rows) & (lane < columns[k + 1])
+                block = bundle_ref[size + k * tile : size + (k + 1) * tile, :].astype(F32)
+                sites.append(jnp.where(live, block, 0.0))
+                states.append(k + 1)
+        parts = len(states)
+        for n in range(parts):
+            joined_s[:, n * tile : (n + 1) * tile] = sites[n].astype(BF16)
+            turned_s[n] = jnp.transpose(sites[n]).astype(BF16)
+            weight_s[n] = weight_rows(weight_ref, width, states[n], square_s, True)
+            packed_s[n, width * pitch :, :] = jnp.zeros(((wide - width) * pitch, tile), F32)
+            diag_s[n] = jnp.zeros_like(diag_s[n])
+
+        def first(pair, carry):
+            for k in range(2):
+                at = aligned(pair * 2 + k, tile)
+                blocks = [
+                    jnp.dot(environ_ref[at, :], joined_s[:, :tile], preferred_element_type=F32)
                 ]
-        return carry
-
-    lax.fori_loop(0, width // 2, first, 0, unroll=2)
-
-    def second(pair, carry):
-        for p in range(states):
-            both = jnp.dot(turned_s[p], half_s[p, aligned(pair, tile), :], preferred_element_type=F32)
+                if with_partner:
+                    both = jnp.dot(
+                        bundle_ref[at, :], joined_s[:, tile:], preferred_element_type=F32
+                    )
+                    blocks += [both[:, :tile], both[:, tile:]]
+                for n in range(parts):
+                    half_s[n, aligned(pair, tile), k * tile : (k + 1) * tile] = blocks[n].astype(BF16)
+            return carry
+
+        lax.fori_loop(0, width // 2, first, 0, unroll=2)
+
+        def second(pair, carry):
+            for n in range(parts):
+                both = jnp.dot(
+                    turned_s[n], half_s[n, aligned(pair, tile), :], preferred_element_type=F32
+                )
+                for k in range(2):
+                    folded, diagonal = pack_block(both[:, k * tile : (k + 1) * tile])
+                    at = pl.multiple_of((pair * 2 + k) * pitch, 8)
+                    packed_s[n, pl.ds(at, half), :] = folded
+                    diag_s[n, pl.ds(pair * 2 + k, 1), :] = diagonal
+            return carry
+
+        lax.fori_loop(0, width // 2, second, 0, unroll=2)
+
+        def mixed(inputs):
+            value = None
+            for n in range(parts):
+                term = jnp.dot(weight_s[n], doubled(inputs[n]), preferred_element_type=F32)
+                value = term if value is None else value + term
+            return value[:wide]
+
+        def mix(step, carry):
+            at = step * 2
+            value = mixed([
+                jnp.concatenate(
+                    [packed_s[n, pl.ds(at + k, wide, stride=pitch), :] for k in range(2)], axis=1
+                )
+                for n in range(parts)
+            ])
             for k in range(2):
-                folded, diagonal = pack_block(both[:, k * tile : (k + 1) * tile])
-                at = pl.multiple_of((pair * 2 + k) * pitch, 8)
-                packed_s[p, pl.ds(at, half), :] = folded
-                diag_s[p, pl.ds(pair * 2 + k, 1), :] = diagonal
-        return carry
-
-    lax.fori_loop(0, width // 2, second, 0, unroll=2)
-
-    def mixed(inputs):
-        products = [
-            jnp.dot(weight_s[p], doubled(inputs[p]), preferred_element_type=F32)[:wide]
-            for p in range(states)
-        ]
-        return products[0], products[1] + products[2], products[3]
-
-    def mix(step, carry):
-        at = step * 2
-        inputs = [
-            jnp.concatenate(
-                [packed_s[p, pl.ds(at + k, wide, stride=pitch), :] for k in range(2)], axis=1
+                sums_s[pl.ds(at + k, wide, stride=pitch), :] = value[:, k * tile : (k + 1) * tile]
+            return carry
+
+        lax.fori_loop(0, half // 2, mix, 0, unroll=4)
+        diag_sums_s[...] = jnp.zeros_like(diag_sums_s)
+        diag_sums_s[:wide, :] = mixed([diag_s[n, :wide] for n in range(parts)])
+        for w in range(width):
+            out_ref[w * half : (w + 1) * half, :] = sums_s[w * pitch : w * pitch + half, :].astype(
+                out_ref.dtype
             )
-            for p in range(states)
-        ]
-        for index, value in enumerate(mixed(inputs)):
-            for k in range(2):
-                sums_s[index, pl.ds(at + k, wide, stride=pitch), :] = value[:, k * tile : (k + 1) * tile]
-        return carry
-
-    lax.fori_loop(0, half // 2, mix, 0, unroll=4)
-    diag_sums_s[...] = jnp.zeros_like(diag_sums_s)
-    for index, value in enumerate(mixed([diag_s[p, :wide] for p in range(states)])):
-        diag_sums_s[index, :wide, :] = value
-    for index, ref in enumerate((own_ref, one_ref, two_ref)):
-        for w in range(width):
-            ref[w * half : (w + 1) * half, :] = sums_s[index, w * pitch : w * pitch + half, :].astype(
-                ref.dtype
-            )
-        ref[width * half :, :] = diag_sums_s[index].astype(ref.dtype)
+        out_ref[width * half :, :] = diag_sums_s[...].astype(out_ref.dtype)
+
+    even = lax.rem(sector, 2) == 0
+    own_state = len(CHARGES) - 1 if travels else 0
+
+    @pl.when(even)
+    def _():
+        run(own_state, travels)
+
+    @pl.when(jnp.logical_not(even))
+    def _():
+        run(own_state, not travels)
 
 
 def mix_into(width, tile, weights, wide_s, sums_s, out_ref):
@@ -216,13 +256,16 @@
 
 
 def mix_next_kernel(
-    width, tile, near_ref, relay_ref, weight_ref, out_ref, square_s, weight_s, wide_s, sums_s, diag
+    width, tile, bundle_ref, relay_ref, weight_ref, out_ref, square_s, weight_s, wide_s, sums_s, diag
 ):
+    base = (width + 2) * tile
+    even = lax.rem(lax.axis_index("sec"), 2) == 0
     for k in range(2):
         weight_s[k] = weight_rows(weight_ref, width, k + 1, square_s, False)
 
     def read(at, size):
-        return near_ref[at : at + size, :].astype(F32) + relay_ref[at : at + size, :].astype(F32)
+        near = bundle_ref[base + at : base + at + size, :].astype(F32)
+        return jnp.where(even, near, relay_ref[at : at + size, :].astype(F32))
 
     unpack_into(width, tile, tile + 8, read, wide_s, diag)
     mix_into(width, tile, [weight_s.at[k] for k in range(2)], wide_s, sums_s, out_ref)
@@ -262,7 +305,7 @@
             width, tile, tile, lambda at, size: packed_ref[at : at + size, :].astype(F32), bound_s, diag
         )
 
-    rows, columns = live_limits(dims_ref)
+    rows, columns = live_limits(dims_ref, sector)
     row, lane = iotas((tile, tile))
     stat_row, stat_lane = iotas(stats_ref.shape)
     stats = jnp.zeros(stats_ref.shape, F32)
@@ -392,6 +435,17 @@
     return [(source, target) for source in range(count) for target in pick(source) if 0 <= target < count]
 
 
+def sum_over(value, axis):
+    count = lax.axis_size(axis)
+    if count & (count - 1):
+        return lax.psum(value, axis)
+    step = 1
+    while step < count:
+        value = value + lax.ppermute(value, axis, [(q, q ^ step) for q in range(count)])
+        step *= 2
+    return value
+
+
 def on_device(left_env, right_env, site_tensors, mpo, boundary_mpo, guess, sector_dims):
     width, tile = left_env.shape[2], left_env.shape[-1]
     half = tile // 2
@@ -402,7 +456,6 @@
     segments = lax.axis_size("seg")
     prows = packed_rows(width, tile)
     drows = prows - width * half
-    odd = lax.rem(lax.axis_index("sec"), 2) == 1
     packed = jax.ShapeDtypeStruct((prows, tile), BF16)
     packed32 = jax.ShapeDtypeStruct((prows, tile), F32)
 
@@ -416,7 +469,6 @@
     bound_weights = jnp.transpose(boundary_mpo[0], (0, 2, 1)).reshape(width * states, width)
 
     swap = pairs_of(sectors, lambda q: [q ^ 1])
-    down = pairs_of(sectors, lambda q: [q - 1] if q % 2 else [])
     across = pairs_of(sectors, lambda q: [q + 1] if q % 2 == 0 else [])
     up_two = pairs_of(sectors, lambda q: [q + 2])
     down_two = pairs_of(sectors, lambda q: [q - 2])
@@ -431,33 +483,34 @@
             pltpu.VMEM((count, wide * (tile + 8), tile), F32),
         ]
 
-    right_packed = call(
-        "pack_right", functools.partial(pack_kernel, width, tile), [], [right], packed, [diag], 6, 2
-    )
+    right_packed, bundle = call(
+        "prepare", functools.partial(prepare_kernel, width, tile), [], [right, environ, site],
+        (packed, jax.ShapeDtypeStruct((width * tile + 2 * tile + prows, tile), BF16)), [diag], 10, 2,
+    )
+    bundle = lax.ppermute(bundle, "sec", swap)
     right_far = lax.ppermute(right_packed, "sec", down_two)
-    right_near = lax.ppermute(right_packed, "sec", down)
-    environ, right_packed = lax.optimization_barrier((environ, right_packed))
-    own, one, two = call(
-        "fold", functools.partial(fold_kernel, width, tile),
-        [sector_dims], [environ, site, site_weights], (packed32, packed, packed32),
-        [
-            pltpu.VMEM((tile, states * tile), BF16),
-            pltpu.VMEM((states, tile, tile), BF16),
-            pltpu.VMEM((tile, tile), F32),
-            pltpu.VMEM((states, packed_height(width), 2 * wide), BF16),
-            pltpu.VMEM((states, width // 2 * tile, 2 * tile), BF16),
-            pltpu.VMEM((states, wide * (half + 8), tile), F32),
-            pltpu.VMEM((states, drows, tile), F32),
-            pltpu.VMEM((3, wide * (half + 8), tile), F32),
-            pltpu.VMEM((3, drows, tile), F32),
-        ],
-        26, 12,
-    )
-    one, right_far = lax.optimization_barrier((one, right_far))
-    partner = lax.ppermute(one, "sec", swap)
-    outgoing = jnp.where(odd, two, two + partner.astype(F32)).astype(BF16)
-    right, outgoing = lax.optimization_barrier((right, outgoing))
+    fold_scratch = [
+        pltpu.VMEM((tile, 3 * tile), BF16),
+        pltpu.VMEM((3, tile, tile), BF16),
+        pltpu.VMEM((tile, tile), F32),
+        pltpu.VMEM((3, packed_height(width), 2 * wide), BF16),
+        pltpu.VMEM((3, width // 2 * tile, 2 * tile), BF16),
+        pltpu.VMEM((3, wide * (half + 8), tile), F32),
+        pltpu.VMEM((3, drows, tile), F32),
+        pltpu.VMEM((wide * (half + 8), tile), F32),
+        pltpu.VMEM((drows, tile), F32),
+    ]
+    outgoing = call(
+        "fold_up", functools.partial(fold_kernel, width, tile, True),
+        [sector_dims], [environ, site, bundle, site_weights], packed, fold_scratch, 20, 12,
+    )
+    outgoing, right_far, right = lax.optimization_barrier((outgoing, right_far, right))
     arrived = lax.ppermute(outgoing, "sec", up_two)
+    kept = call(
+        "fold_own", functools.partial(fold_kernel, width, tile, False),
+        [sector_dims], [environ, site, bundle, site_weights], packed32, fold_scratch, 20, 8,
+    )
+    kept, right_far, right = lax.optimization_barrier((kept, right_far, right))
     right_relay = lax.ppermute(right_far, "sec", across)
     own_mixed = call(
         "mix_own", functools.partial(mix_own_kernel, width, tile), [], [right, bound_weights],
@@ -468,12 +521,11 @@
         [right_far, bound_weights], blocks(1), mix_scratch(1) + [diag], 12, 6,
     )
     arrived, own_mixed, after_mixed = lax.optimization_barrier((arrived, own_mixed, after_mixed))
-    fresh = own + arrived.astype(F32) + jnp.where(odd, partner.astype(F32), 0.0)
-    fresh = fresh.astype(BF16)
+    fresh = (kept + arrived.astype(F32)).astype(BF16)
     received = lax.ppermute(fresh, "seg", onward)
     next_mixed = call(
         "mix_next", functools.partial(mix_next_kernel, width, tile), [],
-        [right_near, right_relay, bound_weights], blocks(2), mix_scratch(2) + [diag], 16, 7,
+        [bundle, right_relay, bound_weights], blocks(2), mix_scratch(2) + [diag], 16, 7,
     )
     new_env = call(
         "unpack_env", functools.partial(unpack_kernel, width, tile), [], [fresh], blocks(1), [diag],
@@ -494,7 +546,7 @@
         ],
         18, 15,
     )
-    stats = lax.psum(stats, "sec")
+    stats = sum_over(stats, "sec")
     entries = float(states * sector_count * tile * tile)
     vector, table = call(
         "finish", functools.partial(finish_kernel, entries), [], [stats, basis],

time: 86.5 us -> 81.8 us (0.946); the launches traced: 84.8 us -> 81.2 us
  blocking collectives: 12 us -> 0 us
  waiting for transfers between devices: 14 us -> 21.9 us
  other arithmetic: 2.53 us -> 0.16 us
  local copies, waits for them, and re-layouts: 1.28 us -> 3.42 us
  Pallas kernels: 39.7 us -> 41.1 us
    psum x1 -> x0, blocking collectives: 12 us -> none  [on_device(): stats = lax.psum(stats, 'sec')]
    ppermute x2 -> x4, waiting for transfers between devices: 0.01 us -> 9.9 us  [the longest x3 7.9 us: sum_over(): lax.ppermute(value, axis, [(q, q ^ step) for q in range(count)])]
    ppermute x1, waiting for transfers between devices: 3.74 us -> 0.01 us  [on_device(): arrived = lax.ppermute(outgoing, 'sec', up_two)]
    convert_element_type x2 -> x1, other arithmetic: 2.53 us -> 0.15 us  [on_device(): fresh = (kept + arrived.astype(F32)).astype(BF16)]
    unnamed x16 -> x20, local copies, waits for them, and re-layouts: 1.28 us -> 3.42 us
    ppermute x1, waiting for transfers between devices: 3.32 us -> 5.43 us  [on_device(): received = lax.ppermute(fresh, 'seg', onward)]
    pallas_call x8 -> x9, Pallas kernels: 39.7 us -> 41.1 us  [call(): pl.pallas_call(kernel, out_shape=outs, in_specs=[smem()] * len(scalars) +...]
  transfers between devices with their start and end apart: 6 -> 8, of which waited for: 3 -> 6; matrix products, arithmetic and copies ran while one was open for 3% -> 0% of each run, Pallas kernels for 29% -> 33%
where the time goes in v2:
time: 81.8 us; the launch traced here: 81.2 us
  Pallas kernels  41.1 us (50%)
  waiting for transfers between devices  21.9 us (27%)
  starting transfers between devices  13.9 us (17%)
  local copies, waits for them, and re-layouts  3.42 us (4%)
    pallas_call x9, Pallas kernels, call(): pl.pallas_call(kernel, out_shape=outs, in_specs=[smem()] * len(scalars) +...  41.1 us
    ppermute x3, waiting for transfers between devices, sum_over(): lax.ppermute(value, axis, [(q, q ^ step) for q in range(count)])  7.9 us
    ppermute x1, waiting for transfers between devices, on_device(): right_far = lax.ppermute(right_packed, 'sec', down_two)  6.51 us
    ppermute x1, waiting for transfers between devices, on_device(): received = lax.ppermute(fresh, 'seg', onward)  5.43 us
    ppermute x1, starting transfers between devices, on_device(): arrived = lax.ppermute(outgoing, 'sec', up_two)  4.56 us
    ppermute x1, starting transfers between devices, on_device(): received = lax.ppermute(fresh, 'seg', onward)  3.51 us
    ppermute x1, starting transfers between devices, on_device(): right_relay = lax.ppermute(right_far, 'sec', across)  3.43 us
    unnamed x20, local copies, waits for them, and re-layouts  3.42 us
  transfers between devices with their start and end apart: 8, of which 6 were waited for; matrix products, arithmetic and copies ran while one was open for 0% of the time, Pallas kernels for 33%

profile of v2, /device:TPU:0, one launch (start us, length us, event | category | flops | bytes accessed | tf_op | source)
XLA Modules:
  0.0 81.2 jit_solution(18240493440710407968)
XLA Ops:
  0.6 0.0 copy-start
  0.6 1.2 %copy-done = bf16[1,1,34,128,128]{4,3,2,1,0:T(8,128)(2,1)S(1)} copy-done((bf16[1,1,34,128,128]{4,3,2,1,0:T(8,128)(2,1)S(1)}, bf16[1,1,34,128,128]{4,3,2,1,0:T(8,128)(2,1)}, u32[]{:S(2)}) %copy-start) | copy-done | bytes 1114136
  1.9 0.0 copy-start.2
  1.9 1.2 %copy-done.2 = bf16[1,1,34,128,128]{4,3,2,1,0:T(8,128)(2,1)S(1)} copy-done((bf16[1,1,34,128,128]{4,3,2,1,0:T(8,128)(2,1)S(1)}, bf16[1,1,34,128,128]{4,3,2,1,0:T(8,128)(2,1)}, u32[]{:S(2)}) %copy-start.2) | copy-done | bytes 1114136
  3.1 0.0 copy-start.5
  3.1 0.9 %copy-done.5 = bf16[1,1,4,1,128,128]{5,4,3,2,1,0:T(8,128)(2,1)S(1)} copy-done((bf16[1,1,4,1,128,128]{5,4,3,2,1,0:T(8,128)(2,1)S(1)}, bf16[1,1,4,1,128,128]{5,4,3,2,1,0:T(8,128)(2,1)}, u32[]{:S(2)}) %copy-start.5) | copy-done | bytes 131096
  4.0 0.0 copy-start.3
  4.0 0.0 copy-start.6
  4.0 0.0 copy-start.7
  4.0 0.0 copy-start.9
  4.0 0.3 prepare.1
  4.4 0.5 collective-permute-start
  4.9 1.3 %collective-permute-start.1 = (bf16[2224,128]{1,0:T(8,128)(2,1)S(1)}, bf16[2224,128]{1,0:T(8,128)(2,1)S(1)}, u32[]{:S(2)}, u32[]{:S(2)}) collective-permute-start(bf16[2224,128]{1,0:T(8,128)(2,1)S(1)} %get-tuple-element.22), channel_id=1, source_target_pairs={{2,0},{3,1},{4,2},{5,3},{6,4},{7,5},{10,8},{11,9},{12,10},{13,11},... | collective-permute-start | bytes 1708040 | tf_op jit(solution)/shard_map/ppermute | solution.py:491
  6.2 2.0 %collective-permute-done.bundle_ref = bf16[6832,128]{1,0:T(8,128)(2,1)S(1)} collective-permute-done((bf16[6832,128]{1,0:T(8,128)(2,1)S(1)}, bf16[6832,128]{1,0:T(8,128)(2,1)S(1)}, u32[]{:S(2)}, u32[]{:S(2)}) %collective-permute-start) | collective-permute-done | bytes 1749024 | tf_op jit(solution)/shard_map/ppermute | solution.py:490
  8.2 0.0 copy-done.3
  8.2 0.0 copy-done.6
  8.2 0.0 copy-done.7
  8.2 0.0 copy-done.9
  8.2 8.1 %fold_up.1 = bf16[2224,128]{1,0:T(8,128)(2,1)S(1)} custom-call(s32[8]{0:T(128)S(1)} %copy-done.9, bf16[4352,128]{1,0:T(8,128)(2,1)S(1)} %bitcast.24, bf16[4,128,128]{2,1,0:T(8,128)(2,1)S(1)} %bitcast.29, bf16[6832,128]{1,0:T(8,128)(2,1)S(1)} %collective-permute-done.bundle_ref, f32[136,34]{1,0:T(8,128)S(1)} %bitcast.31), custom_call_target="tpu_custom_call" | custom-call | flops 13200000000 | tf_op jit(solution)/shard_map/fold_up/pallas_call | solution.py:420
  16.3 0.0 copy-start.1
  16.3 0.0 copy-start.8
  16.3 6.5 %collective-permute-done.1.far_ref = bf16[2224,128]{1,0:T(8,128)(2,1)S(1)} collective-permute-done((bf16[2224,128]{1,0:T(8,128)(2,1)S(1)}, bf16[2224,128]{1,0:T(8,128)(2,1)S(1)}, u32[]{:S(2)}, u32[]{:S(2)}) %collective-permute-start.1) | collective-permute-done | bytes 569376 | tf_op jit(solution)/shard_map/ppermute | solution.py:491
  22.8 4.6 %collective-permute-start.2 = (bf16[2224,128]{1,0:T(8,128)(2,1)S(1)}, bf16[2224,128]{1,0:T(8,128)(2,1)S(1)}, u32[]{:S(2)}, u32[]{:S(2)}) collective-permute-start(bf16[2224,128]{1,0:T(8,128)(2,1)S(1)} %fold_up.1), channel_id=1, source_target_pairs={{0,2},{1,3},{2,4},{3,5},{4,6},{5,7},{8,10},{9,11},{10,12},{11,13},... | collective-permute-start | bytes 1708040 | tf_op jit(solution)/shard_map/ppermute | solution.py:508
  27.4 6.0 %fold_own.1 = f32[2224,128]{1,0:T(8,128)S(1)} custom-call(s32[8]{0:T(128)S(1)} %copy-done.9, bf16[4352,128]{1,0:T(8,128)(2,1)S(1)} %bitcast.25, bf16[4,128,128]{2,1,0:T(8,128)(2,1)S(1)} %bitcast.30, bf16[6832,128]{1,0:T(8,128)(2,1)S(1)} %collective-permute-done.bundle_ref, f32[136,34]{1,0:T(8,128)S(1)} %bitcast.32), custom_call_target="tpu_custom_call" | custom-call | flops 8800000000 | tf_op jit(solution)/shard_map/fold_own/pallas_call | solution.py:420
  33.5 3.4 %collective-permute-start.4 = (bf16[2224,128]{1,0:T(8,128)(2,1)S(1)}, bf16[2224,128]{1,0:T(8,128)(2,1)S(1)}, u32[]{:S(2)}, u32[]{:S(2)}) collective-permute-start(bf16[2224,128]{1,0:T(8,128)(2,1)S(1)} %collective-permute-done.1.far_ref), channel_id=1, source_target_pairs={{0,1},{2,3},{4,5},{6,7},{8,9},{10,11},{12,13},{14,15},{16,17},{18,... | collective-permute-start | bytes 1708040 | tf_op jit(solution)/shard_map/ppermute | solution.py:514
  36.9 0.0 copy-done.1
  36.9 0.0 copy-done.8
  36.9 3.0 %mix_own.1.own_ref = bf16[4352,128]{1,0:T(8,128)(2,1)S(1)} custom-call(bf16[4352,128]{1,0:T(8,128)(2,1)S(1)} %bitcast.22, f32[136,34]{1,0:T(8,128)S(1)} %bitcast.33), custom_call_target="tpu_custom_call" | custom-call | flops 5500000256 | tf_op jit(solution)/shard_map/mix_own/pallas_call | solution.py:420
  39.9 3.7 %mix_after.1.after_ref = bf16[4352,128]{1,0:T(8,128)(2,1)S(1)} custom-call(bf16[2224,128]{1,0:T(8,128)(2,1)S(1)} %collective-permute-done.1.far_ref, f32[136,34]{1,0:T(8,128)S(1)} %bitcast.34), custom_call_target="tpu_custom_call" | custom-call | flops 6600000000 | tf_op jit(solution)/shard_map/mix_after/pallas_call | solution.py:420
  43.6 0.0 collective-permute-done.2
  43.6 0.1 add_convert_fusion.source_ref
  43.8 3.5 %collective-permute-start.3 = (bf16[2224,128]{1,0:T(8,128)(2,1)S(1)}, bf16[2224,128]{1,0:T(8,128)(2,1)S(1)}, u32[]{:S(2)}, u32[]{:S(2)}) collective-permute-start(bf16[2224,128]{1,0:T(8,128)(2,1)S(1)} %add_convert_fusion.source_ref), channel_id=1, source_target_pairs={{0,8},{8,16},{16,24},{1,9},{9,17},{17,25},{2,10},{10,18},{18,26},{... | collective-permute-start | bytes 1708040 | tf_op jit(solution)/shard_map/ppermute | solution.py:525
  47.3 1.8 %unpack_env.1 = bf16[4352,128]{1,0:T(8,128)(2,1)} custom-call(bf16[2224,128]{1,0:T(8,128)(2,1)S(1)} %add_convert_fusion.source_ref), custom_call_target="tpu_custom_call" | custom-call | flops 3300000000 | tf_op jit(solution)/shard_map/unpack_env/pallas_call | solution.py:420
  49.1 0.0 copy-start.4
  49.1 0.0 collective-permute-done.4.relay_ref
  49.1 4.3 %mix_next.1.next_ref = bf16[8704,128]{1,0:T(8,128)(2,1)S(1)} custom-call(bf16[6832,128]{1,0:T(8,128)(2,1)S(1)} %collective-permute-done.bundle_ref, bf16[2224,128]{1,0:T(8,128)(2,1)S(1)} %collective-permute-done.4.relay_ref, f32[136,34]{1,0:T(8,128)S(1)} %bitcast.35), custom_call_target="tpu_custom_call" | custom-call | flops 7699999744 | tf_op jit(solution)/shard_map/mix_next/pallas_call | solution.py:420
  53.5 5.4 %collective-permute-done.3.packed_ref = bf16[2224,128]{1,0:T(8,128)(2,1)S(1)} collective-permute-done((bf16[2224,128]{1,0:T(8,128)(2,1)S(1)}, bf16[2224,128]{1,0:T(8,128)(2,1)S(1)}, u32[]{:S(2)}, u32[]{:S(2)}) %collective-permute-start.3) | collective-permute-done | bytes 569376 | tf_op jit(solution)/shard_map/ppermute | solution.py:525
  58.9 0.0 copy-done.4
  58.9 12.1 %lanczos.1 = (f32[5,4,128,128]{3,2,1,0:T(8,128)S(1)}, f32[16,128]{1,0:T(8,128)S(1)}) custom-call(s32[8]{0:T(128)S(1)} %copy-done.9, bf16[2224,128]{1,0:T(8,128)(2,1)S(1)} %collective-permute-done.3.packed_ref, bf16[4352,128]{1,0:T(8,128)(2,1)S(1)} %bitcast.26, bf16[4352,128]{1,0:T(8,128)(2,1)S(1)} %mix_own.1.own_ref, ...), custom_call_target="tpu_custom_call" | custom-call | flops 16499999744 | tf_op jit(solution)/shard_map/lanczos/pallas_call | solution.py:420
  71.0 0.0 collective-permute-start.5
  71.0 1.2 %collective-permute-done.5 = f32[16,128]{1,0:T(8,128)S(1)} collective-permute-done((f32[16,128]{1,0:T(8,128)S(1)}, f32[16,128]{1,0:T(8,128)S(1)}, u32[]{:S(2)}, u32[]{:S(2)}) %collective-permute-start.5) | collective-permute-done | bytes 8224 | tf_op jit(solution)/shard_map/ppermute | solution.py:444
  72.2 0.6 collective-permute-start.6
  72.8 3.1 %collective-permute-done.6 = f32[16,128]{1,0:T(8,128)S(1)} collective-permute-done((f32[16,128]{1,0:T(8,128)S(1)}, f32[16,128]{1,0:T(8,128)S(1)}, u32[]{:S(2)}, u32[]{:S(2)}) %collective-permute-start.6) | collective-permute-done | bytes 8224 | tf_op jit(solution)/shard_map/ppermute | solution.py:444
  75.9 0.0 collective-permute-start.7
  75.9 3.6 %collective-permute-done.7 = f32[16,128]{1,0:T(8,128)S(1)} collective-permute-done((f32[16,128]{1,0:T(8,128)S(1)}, f32[16,128]{1,0:T(8,128)S(1)}, u32[]{:S(2)}, u32[]{:S(2)}) %collective-permute-start.7) | collective-permute-done | bytes 8224 | tf_op jit(solution)/shard_map/ppermute | solution.py:444
  79.5 1.7 %finish.1 = (f32[4,128,128]{2,1,0:T(8,128)}, f32[2,4]{1,0:T(2,128)}) custom-call(f32[16,128]{1,0:T(8,128)S(1)} %add.15.stats_ref, f32[5,4,128,128]{3,2,1,0:T(8,128)S(1)} %get-tuple-element.36.basis_ref), custom_call_target="tpu_custom_call" | custom-call | flops 2200000000 | tf_op jit(solution)/shard_map/finish/pallas_call | solution.py:420
  (3 shorter events, 0.0 us)
Async XLA Ops:
  0.6 1.3 %copy-start = (bf16[1,1,34,128,128]{4,3,2,1,0:T(8,128)(2,1)S(1)}, bf16[1,1,34,128,128]{4,3,2,1,0:T(8,128)(2,1)}, u32[]{:S(2)}) copy-start(bf16[1,1,34,128,128]{4,3,2,1,0:T(8,128)(2,1)} %param.8) | copy-start | bytes 3342340
  1.9 1.2 %copy-start.2 = (bf16[1,1,34,128,128]{4,3,2,1,0:T(8,128)(2,1)S(1)}, bf16[1,1,34,128,128]{4,3,2,1,0:T(8,128)(2,1)}, u32[]{:S(2)}) copy-start(bf16[1,1,34,128,128]{4,3,2,1,0:T(8,128)(2,1)} %param.7) | copy-start | bytes 3342340
  3.1 0.9 %copy-start.5 = (bf16[1,1,4,1,128,128]{5,4,3,2,1,0:T(8,128)(2,1)S(1)}, bf16[1,1,4,1,128,128]{5,4,3,2,1,0:T(8,128)(2,1)}, u32[]{:S(2)}) copy-start(bf16[1,1,4,1,128,128]{5,4,3,2,1,0:T(8,128)(2,1)} %param.9) | copy-start | bytes 393220
  4.0 4.2 %copy-start.3 = (bf16[1,1,34,128,128]{4,3,2,1,0:T(8,128)(2,1)S(1)}, bf16[1,1,34,128,128]{4,3,2,1,0:T(8,128)(2,1)}, u32[]{:S(2)}) copy-start(bf16[1,1,34,128,128]{4,3,2,1,0:T(8,128)(2,1)} %param.7) | copy-start | bytes 3342340
  4.0 4.2 %copy-start.6 = (bf16[1,1,4,1,128,128]{5,4,3,2,1,0:T(8,128)(2,1)S(1)}, bf16[1,1,4,1,128,128]{5,4,3,2,1,0:T(8,128)(2,1)}, u32[]{:S(2)}) copy-start(bf16[1,1,4,1,128,128]{5,4,3,2,1,0:T(8,128)(2,1)} %param.9) | copy-start | bytes 393220
  4.0 4.2 %copy-start.7 = (f32[1,1,34,34,4]{3,4,2,1,0:T(4,128)S(1)}, f32[1,1,34,34,4]{3,4,2,1,0:T(4,128)}, u32[]{:S(2)}) copy-start(f32[1,1,34,34,4]{3,4,2,1,0:T(4,128)} %param.10) | copy-start | bytes 55492
  4.0 4.2 %copy-start.9 = (s32[8]{0:T(128)S(1)}, s32[8]{0:T(128)}, u32[]{:S(2)}) copy-start(s32[8]{0:T(128)} %dims_ref.5) | copy-start | bytes 100
  4.4 3.8 %collective-permute-start = (bf16[6832,128]{1,0:T(8,128)(2,1)S(1)}, bf16[6832,128]{1,0:T(8,128)(2,1)S(1)}, u32[]{:S(2)}, u32[]{:S(2)}) collective-permute-start(bf16[6832,128]{1,0:T(8,128)(2,1)S(1)} %get-tuple-element.21), channel_id=1, source_target_pairs={{0,1},{1,0},{2,3},{3,2},{4,5},{5,4},{6,7},{7,6},{8,9},{9,8},{10,11... | collective-permute-start | bytes 5246984 | tf_op jit(solution)/shard_map/ppermute | solution.py:490
  4.9 17.9 %collective-permute-start.1 = (bf16[2224,128]{1,0:T(8,128)(2,1)S(1)}, bf16[2224,128]{1,0:T(8,128)(2,1)S(1)}, u32[]{:S(2)}, u32[]{:S(2)}) collective-permute-start(bf16[2224,128]{1,0:T(8,128)(2,1)S(1)} %get-tuple-element.22), channel_id=1, source_target_pairs={{2,0},{3,1},{4,2},{5,3},{6,4},{7,5},{10,8},{11,9},{12,10},{13,11},... | collective-permute-start | bytes 1708040 | tf_op jit(solution)/shard_map/ppermute | solution.py:491
  16.3 20.6 %copy-start.1 = (bf16[1,1,34,128,128]{4,3,2,1,0:T(8,128)(2,1)S(1)}, bf16[1,1,34,128,128]{4,3,2,1,0:T(8,128)(2,1)}, u32[]{:S(2)}) copy-start(bf16[1,1,34,128,128]{4,3,2,1,0:T(8,128)(2,1)} %param.8) | copy-start | bytes 3342340
  16.3 20.6 %copy-start.8 = (f32[1,34,34,4]{2,3,1,0:T(4,128)S(1)}, f32[1,34,34,4]{2,3,1,0:T(4,128)}, u32[]{:S(2)}) copy-start(f32[1,34,34,4]{2,3,1,0:T(4,128)} %param.11) | copy-start | bytes 55492
  22.8 20.8 %collective-permute-start.2 = (bf16[2224,128]{1,0:T(8,128)(2,1)S(1)}, bf16[2224,128]{1,0:T(8,128)(2,1)S(1)}, u32[]{:S(2)}, u32[]{:S(2)}) collective-permute-start(bf16[2224,128]{1,0:T(8,128)(2,1)S(1)} %fold_up.1), channel_id=1, source_target_pairs={{0,2},{1,3},{2,4},{3,5},{4,6},{5,7},{8,10},{9,11},{10,12},{11,13},... | collective-permute-start | bytes 1708040 | tf_op jit(solution)/shard_map/ppermute | solution.py:508
  33.5 15.7 %collective-permute-start.4 = (bf16[2224,128]{1,0:T(8,128)(2,1)S(1)}, bf16[2224,128]{1,0:T(8,128)(2,1)S(1)}, u32[]{:S(2)}, u32[]{:S(2)}) collective-permute-start(bf16[2224,128]{1,0:T(8,128)(2,1)S(1)} %collective-permute-done.1.far_ref), channel_id=1, source_target_pairs={{0,1},{2,3},{4,5},{6,7},{8,9},{10,11},{12,13},{14,15},{16,17},{18,... | collective-permute-start | bytes 1708040 | tf_op jit(solution)/shard_map/ppermute | solution.py:514
  43.8 15.1 %collective-permute-start.3 = (bf16[2224,128]{1,0:T(8,128)(2,1)S(1)}, bf16[2224,128]{1,0:T(8,128)(2,1)S(1)}, u32[]{:S(2)}, u32[]{:S(2)}) collective-permute-start(bf16[2224,128]{1,0:T(8,128)(2,1)S(1)} %add_convert_fusion.source_ref), channel_id=1, source_target_pairs={{0,8},{8,16},{16,24},{1,9},{9,17},{17,25},{2,10},{10,18},{18,26},{... | collective-permute-start | bytes 1708040 | tf_op jit(solution)/shard_map/ppermute | solution.py:525
  49.1 9.8 %copy-start.4 = (f32[1,4,1,128,128]{4,3,2,1,0:T(8,128)S(1)}, f32[1,4,1,128,128]{4,3,2,1,0:T(8,128)}, u32[]{:S(2)}) copy-start(f32[1,4,1,128,128]{4,3,2,1,0:T(8,128)} %param.12) | copy-start | bytes 786436
  71.0 1.2 %collective-permute-start.5 = (f32[16,128]{1,0:T(8,128)S(1)}, f32[16,128]{1,0:T(8,128)S(1)}, u32[]{:S(2)}, u32[]{:S(2)}) collective-permute-start(f32[16,128]{1,0:T(8,128)S(1)} %get-tuple-element.35), channel_id=1, source_target_pairs={{0,1},{1,0},{2,3},{3,2},{4,5},{5,4},{6,7},{7,6},{8,9},{9,8},{10,11... | collective-permute-start | bytes 24584 | tf_op jit(solution)/shard_map/ppermute | solution.py:444
  72.2 3.7 %collective-permute-start.6 = (f32[16,128]{1,0:T(8,128)S(1)}, f32[16,128]{1,0:T(8,128)S(1)}, u32[]{:S(2)}, u32[]{:S(2)}) collective-permute-start(f32[16,128]{1,0:T(8,128)S(1)} %add.13), channel_id=1, source_target_pairs={{0,2},{1,3},{2,0},{3,1},{4,6},{5,7},{6,4},{7,5},{8,10},{9,11},{10,... | collective-permute-start | bytes 24584 | tf_op jit(solution)/shard_map/ppermute | solution.py:444
  75.9 3.7 %collective-permute-start.7 = (f32[16,128]{1,0:T(8,128)S(1)}, f32[16,128]{1,0:T(8,128)S(1)}, u32[]{:S(2)}, u32[]{:S(2)}) collective-permute-start(f32[16,128]{1,0:T(8,128)S(1)} %add.14), channel_id=1, source_target_pairs={{0,4},{1,5},{2,6},{3,7},{4,0},{5,1},{6,2},{7,3},{8,12},{9,13},{10,... | collective-permute-start | bytes 24584 | tf_op jit(solution)/shard_map/ppermute | solution.py:444

commit v3 on v2

--- a/solution.py
+++ b/solution.py
@@ -64,10 +64,6 @@
         target = sector + charge
         columns.append(jnp.where(target < count, dims_ref[jnp.minimum(target, count - 1)], 0))
     return rows, columns
-
-
-def aligned(index, size):
-    return pl.ds(pl.multiple_of(index * size, size), size)
 
 
 def weight_rows(weight_ref, width, p, square, turned):
@@ -86,23 +82,14 @@
     return jnp.concatenate([value, value], axis=0).astype(BF16)
 
 
-def prepare_kernel(width, tile, right_ref, environ_ref, site_ref, packed_ref, bundle_ref, diag):
+def pack_kernel(width, tile, source_ref, out_ref, diag):
     half = tile // 2
-    size = width * tile
     diag[...] = jnp.zeros_like(diag)
-    bundle_ref[:size, :] = environ_ref[...]
-    for k in range(2):
-        bundle_ref[size + k * tile : size + (k + 1) * tile, :] = site_ref[k + 1]
-    base = size + 2 * tile
     for w in range(width):
-        folded, diagonal = pack_block(right_ref[w * tile : (w + 1) * tile, :].astype(F32))
-        folded = folded.astype(BF16)
-        packed_ref[w * half : (w + 1) * half, :] = folded
-        bundle_ref[base + w * half : base + (w + 1) * half, :] = folded
+        folded, diagonal = pack_block(source_ref[w * tile : (w + 1) * tile, :].astype(F32))
+        out_ref[w * half : (w + 1) * half, :] = folded.astype(BF16)
         diag[w : w + 1, :] = diagonal
-    rows = diag[...].astype(BF16)
-    packed_ref[width * half :, :] = rows
-    bundle_ref[base + width * half :, :] = rows
+    out_ref[width * half :, :] = diag[...].astype(BF16)
 
 
 def unpack_into(width, tile, pitch, read, out_ref, diag):
@@ -120,13 +107,12 @@
 
 
 def fold_kernel(
-    width, tile, travels, dims_ref, environ_ref, site_ref, bundle_ref, weight_ref, out_ref,
+    width, tile, travels, dims_ref, environ_ref, site_ref, far_environ_ref, far_site_ref, weight_ref, out_ref,
     joined_s, turned_s, square_s, weight_s, half_s, packed_s, diag_s, sums_s, diag_sums_s,
 ):
     half = tile // 2
     pitch = half + 8
     wide = padded(width)
-    size = width * tile
     sector = lax.axis_index("sec")
     partner = partner_of(sector)
     row, lane = iotas((tile, tile))
@@ -140,8 +126,7 @@
             rows, columns = live_limits(dims_ref, partner)
             for k in range(2):
                 live = (row < rows) & (lane < columns[k + 1])
-                block = bundle_ref[size + k * tile : size + (k + 1) * tile, :].astype(F32)
-                sites.append(jnp.where(live, block, 0.0))
+                sites.append(jnp.where(live, far_site_ref[k + 1].astype(F32), 0.0))
                 states.append(k + 1)
         parts = len(states)
         for n in range(parts):
@@ -151,36 +136,27 @@
             packed_s[n, width * pitch :, :] = jnp.zeros(((wide - width) * pitch, tile), F32)
             diag_s[n] = jnp.zeros_like(diag_s[n])
 
-        def first(pair, carry):
+        for pair in range(width // 2):
+            at = slice(pair * tile, (pair + 1) * tile)
             for k in range(2):
-                at = aligned(pair * 2 + k, tile)
+                here = slice((pair * 2 + k) * tile, (pair * 2 + k + 1) * tile)
                 blocks = [
-                    jnp.dot(environ_ref[at, :], joined_s[:, :tile], preferred_element_type=F32)
+                    jnp.dot(environ_ref[here, :], joined_s[:, :tile], preferred_element_type=F32)
                 ]
                 if with_partner:
                     both = jnp.dot(
-                        bundle_ref[at, :], joined_s[:, tile:], preferred_element_type=F32
+                        far_environ_ref[here, :], joined_s[:, tile:], preferred_element_type=F32
                     )
                     blocks += [both[:, :tile], both[:, tile:]]
                 for n in range(parts):
-                    half_s[n, aligned(pair, tile), k * tile : (k + 1) * tile] = blocks[n].astype(BF16)
-            return carry
-
-        lax.fori_loop(0, width // 2, first, 0, unroll=2)
-
-        def second(pair, carry):
+                    half_s[n, at, k * tile : (k + 1) * tile] = blocks[n].astype(BF16)
             for n in range(parts):
-                both = jnp.dot(
-                    turned_s[n], half_s[n, aligned(pair, tile), :], preferred_element_type=F32
-                )
+                both = jnp.dot(turned_s[n], half_s[n, at, :], preferred_element_type=F32)
                 for k in range(2):
+                    w = pair * 2 + k
                     folded, diagonal = pack_block(both[:, k * tile : (k + 1) * tile])
-                    at = pl.multiple_of((pair * 2 + k) * pitch, 8)
-                    packed_s[n, pl.ds(at, half), :] = folded
-                    diag_s[n, pl.ds(pair * 2 + k, 1), :] = diagonal
-            return carry
-
-        lax.fori_loop(0, width // 2, second, 0, unroll=2)
+                    packed_s[n, w * pitch : w * pitch + half, :] = folded
+                    diag_s[n, w : w + 1, :] = diagonal
 
         def mixed(inputs):
             value = None
@@ -189,8 +165,7 @@
                 value = term if value is None else value + term
             return value[:wide]
 
-        def mix(step, carry):
-            at = step * 2
+        for at in range(0, half, 2):
             value = mixed([
                 jnp.concatenate(
                     [packed_s[n, pl.ds(at + k, wide, stride=pitch), :] for k in range(2)], axis=1
@@ -199,9 +174,6 @@
             ])
             for k in range(2):
                 sums_s[pl.ds(at + k, wide, stride=pitch), :] = value[:, k * tile : (k + 1) * tile]
-            return carry
-
-        lax.fori_loop(0, half // 2, mix, 0, unroll=4)
         diag_sums_s[...] = jnp.zeros_like(diag_sums_s)
         diag_sums_s[:wide, :] = mixed([diag_s[n, :wide] for n in range(parts)])
         for w in range(width):
@@ -227,8 +199,7 @@
     pitch = tile + 8
     wide_s[width * pitch :, :] = jnp.zeros_like(wide_s[width * pitch :, :])
 
-    def mix(step, carry):
-        at = step * 2
+    for at in range(0, tile, 2):
         value = doubled(
             jnp.concatenate(
                 [wide_s[pl.ds(at + k, wide, stride=pitch), :] for k in range(2)], axis=1
@@ -238,9 +209,6 @@
             mixed = jnp.dot(weight[...], value, preferred_element_type=F32)[:wide]
             for k in range(2):
                 sums_s[index, pl.ds(at + k, wide, stride=pitch), :] = mixed[:, k * tile : (k + 1) * tile]
-        return carry
-
-    lax.fori_loop(0, tile // 2, mix, 0, unroll=4)
     for index in range(len(weights)):
         for w in range(width):
             out = (index * width + w) * tile
@@ -256,15 +224,14 @@
 
 
 def mix_next_kernel(
-    width, tile, bundle_ref, relay_ref, weight_ref, out_ref, square_s, weight_s, wide_s, sums_s, diag
+    width, tile, near_ref, relay_ref, weight_ref, out_ref, square_s, weight_s, wide_s, sums_s, diag
 ):
-    base = (width + 2) * tile
     even = lax.rem(lax.axis_index("sec"), 2) == 0
     for k in range(2):
         weight_s[k] = weight_rows(weight_ref, width, k + 1, square_s, False)
 
     def read(at, size):
-        near = bundle_ref[base + at : base + at + size, :].astype(F32)
+        near = near_ref[at : at + size, :].astype(F32)
         return jnp.where(even, near, relay_ref[at : at + size, :].astype(F32))
 
     unpack_into(width, tile, tile + 8, read, wide_s, diag)
@@ -357,7 +324,9 @@
 def finish_kernel(entries, stats_ref, basis_ref, vector_ref, table_ref):
     states = len(CHARGES)
     sector = lax.axis_index("sec")
-    stats = stats_ref[...]
+    stats = stats_ref[0]
+    for q in range(1, stats_ref.shape[0]):
+        stats = stats + stats_ref[q]
     alphas = [stats[1 + 2 * j : 2 + 2 * j, :] for j in range(LANCZOS)]
     betas = [stats[2 + 2 * j : 3 + 2 * j, :] for j in range(LANCZOS)]
 
@@ -435,15 +404,9 @@
     return [(source, target) for source in range(count) for target in pick(source) if 0 <= target < count]
 
 
-def sum_over(value, axis):
+def gathered(value, axis):
     count = lax.axis_size(axis)
-    if count & (count - 1):
-        return lax.psum(value, axis)
-    step = 1
-    while step < count:
-        value = value + lax.ppermute(value, axis, [(q, q ^ step) for q in range(count)])
-        step *= 2
-    return value
+    return lax.all_to_all(jnp.broadcast_to(value, (count,) + value.shape), axis, 0, 0)
 
 
 def on_device(left_env, right_env, site_tensors, mpo, boundary_mpo, guess, sector_dims):
@@ -483,11 +446,11 @@
             pltpu.VMEM((count, wide * (tile + 8), tile), F32),
         ]
 
-    right_packed, bundle = call(
-        "prepare", functools.partial(prepare_kernel, width, tile), [], [right, environ, site],
-        (packed, jax.ShapeDtypeStruct((width * tile + 2 * tile + prows, tile), BF16)), [diag], 10, 2,
-    )
-    bundle = lax.ppermute(bundle, "sec", swap)
+    far_environ = lax.ppermute(environ, "sec", swap)
+    far_site = lax.ppermute(site, "sec", swap)
+    right_packed = call(
+        "pack_right", functools.partial(pack_kernel, width, tile), [], [right], packed, [diag], 6, 1
+    )
     right_far = lax.ppermute(right_packed, "sec", down_two)
     fold_scratch = [
         pltpu.VMEM((tile, 3 * tile), BF16),
@@ -502,15 +465,18 @@
     ]
     outgoing = call(
         "fold_up", functools.partial(fold_kernel, width, tile, True),
-        [sector_dims], [environ, site, bundle, site_weights], packed, fold_scratch, 20, 12,
-    )
-    outgoing, right_far, right = lax.optimization_barrier((outgoing, right_far, right))
+        [sector_dims], [environ, site, far_environ, far_site, site_weights], packed, fold_scratch, 20, 12,
+    )
     arrived = lax.ppermute(outgoing, "sec", up_two)
+    outgoing, right_far, far_environ = lax.optimization_barrier((outgoing, right_far, far_environ))
     kept = call(
         "fold_own", functools.partial(fold_kernel, width, tile, False),
-        [sector_dims], [environ, site, bundle, site_weights], packed32, fold_scratch, 20, 8,
-    )
-    kept, right_far, right = lax.optimization_barrier((kept, right_far, right))
+        [sector_dims], [environ, site, far_environ, far_site, site_weights], packed32, fold_scratch, 20, 8,
+    )
+    kept, right_far, right, right_packed = lax.optimization_barrier(
+        (kept, right_far, right, right_packed)
+    )
+    right_near = lax.ppermute(right_packed, "sec", swap)
     right_relay = lax.ppermute(right_far, "sec", across)
     own_mixed = call(
         "mix_own", functools.partial(mix_own_kernel, width, tile), [], [right, bound_weights],
@@ -525,7 +491,7 @@
     received = lax.ppermute(fresh, "seg", onward)
     next_mixed = call(
         "mix_next", functools.partial(mix_next_kernel, width, tile), [],
-        [bundle, right_relay, bound_weights], blocks(2), mix_scratch(2) + [diag], 16, 7,
+        [right_near, right_relay, bound_weights], blocks(2), mix_scratch(2) + [diag], 16, 7,
     )
     new_env = call(
         "unpack_env", functools.partial(unpack_kernel, width, tile), [], [fresh], blocks(1), [diag],
@@ -546,7 +512,7 @@
         ],
         18, 15,
     )
-    stats = sum_over(stats, "sec")
+    stats = gathered(stats, "sec")
     entries = float(states * sector_count * tile * tile)
     vector, table = call(
         "finish", functools.partial(finish_kernel, entries), [], [stats, basis],

time: 81.8 us -> 71.3 us (0.87)
  Pallas kernels: 41.1 us -> 29.8 us
  blocking collectives: 0 us -> 9.98 us
  waiting for transfers between devices: 21.9 us -> 12.8 us
  local copies, waits for them, and re-layouts: 3.42 us -> 1.29 us
  starting transfers between devices: 13.9 us -> 16 us
    pallas_call x9, Pallas kernels: 41.1 us -> 29.8 us  [call(): pl.pallas_call(kernel, out_shape=outs, in_specs=[smem()] * len(scalars) +...]
    all_to_all x0 -> x1, blocking collectives: none -> 9.98 us  [gathered(): lax.all_to_all(jnp.broadcast_to(value, (count,) + value.shape), axis, 0, 0)]
    ppermute x4 -> x3, waiting for transfers between devices: 9.9 us -> 0.01 us  [the longest x1 0.01 us: on_device(): far_site = lax.ppermute(site, 'sec', swap)]
    ppermute x4 -> x3, starting transfers between devices: 1.11 us -> 3.58 us  [the longest x1 2.99 us: on_device(): right_near = lax.ppermute(right_packed, 'sec', swap)]
    unnamed x20 -> x16, local copies, waits for them, and re-layouts: 3.42 us -> 1.28 us
    ppermute x1, waiting for transfers between devices: 5.43 us -> 7.44 us  [on_device(): received = lax.ppermute(fresh, 'seg', onward)]
    ppermute x1, starting transfers between devices: 3.43 us -> 1.95 us  [on_device(): right_relay = lax.ppermute(right_far, 'sec', across)]
    ppermute x1, waiting for transfers between devices: 6.51 us -> 5.39 us  [on_device(): right_far = lax.ppermute(right_packed, 'sec', down_two)]
  transfers between devices with their start and end apart: 8 -> 7, of which waited for: 6 -> 2; matrix products, arithmetic and copies ran while one was open for 0% -> 0% of each run, Pallas kernels for 33% -> 22%
where the time goes in v3:
time: 71.3 us; the launch traced here: 70.8 us
  Pallas kernels  29.8 us (42%)
  starting transfers between devices  16 us (22%)
  waiting for transfers between devices  12.8 us (18%)
  blocking collectives  9.98 us (14%)
  local copies, waits for them, and re-layouts  1.29 us (2%)
  between operations  0.82 us (1%)
    pallas_call x9, Pallas kernels, call(): pl.pallas_call(kernel, out_shape=outs, in_specs=[smem()] * len(scalars) +...  29.8 us
    all_to_all x1, blocking collectives, gathered(): lax.all_to_all(jnp.broadcast_to(value, (count,) + value.shape), axis, 0, 0)  9.98 us
    ppermute x1, waiting for transfers between devices, on_device(): received = lax.ppermute(fresh, 'seg', onward)  7.44 us
    ppermute x1, starting transfers between devices, on_device(): arrived = lax.ppermute(outgoing, 'sec', up_two)  5.62 us
    ppermute x1, waiting for transfers between devices, on_device(): right_far = lax.ppermute(right_packed, 'sec', down_two)  5.39 us
    ppermute x1, starting transfers between devices, on_device(): received = lax.ppermute(fresh, 'seg', onward)  3.43 us
    ppermute x1, starting transfers between devices, on_device(): right_near = lax.ppermute(right_packed, 'sec', swap)  2.99 us
    ppermute x1, starting transfers between devices, on_device(): right_relay = lax.ppermute(right_far, 'sec', across)  1.95 us
  transfers between devices with their start and end apart: 7, of which 2 were waited for; matrix products, arithmetic and copies ran while one was open for 0% of the time, Pallas kernels for 22%

profile of v3, /device:TPU:0, one launch (start us, length us, event | category | flops | bytes accessed | tf_op | source)
XLA Modules:
  0.0 70.8 jit_solution(4301994465218291284)
XLA Ops:
  0.6 0.5 collective-permute-start
  1.1 0.1 collective-permute-start.1
  1.2 0.0 copy-start
  1.2 1.2 %copy-done = bf16[1,1,34,128,128]{4,3,2,1,0:T(8,128)(2,1)S(1)} copy-done((bf16[1,1,34,128,128]{4,3,2,1,0:T(8,128)(2,1)S(1)}, bf16[1,1,34,128,128]{4,3,2,1,0:T(8,128)(2,1)}, u32[]{:S(2)}) %copy-start) | copy-done | bytes 1114136
  2.5 0.0 copy-start.2
  2.5 0.0 copy-start.4
  2.5 0.0 copy-start.5
  2.5 0.0 copy-start.7
  2.5 0.3 pack_right.1
  2.8 1.4 %collective-permute-start.2 = (bf16[2224,128]{1,0:T(8,128)(2,1)S(1)}, bf16[2224,128]{1,0:T(8,128)(2,1)S(1)}, u32[]{:S(2)}, u32[]{:S(2)}) collective-permute-start(bf16[2224,128]{1,0:T(8,128)(2,1)S(1)} %pack_right.1), channel_id=1, source_target_pairs={{2,0},{3,1},{4,2},{5,3},{6,4},{7,5},{10,8},{11,9},{12,10},{13,11},... | collective-permute-start | bytes 1708040 | tf_op jit(solution)/shard_map/ppermute | solution.py:454
  4.2 0.0 collective-permute-done.1.far_site_ref
  4.2 0.0 collective-permute-done.far_environ_ref
  4.2 0.0 copy-done.2
  4.2 0.0 copy-done.4
  4.3 0.0 copy-done.5
  4.3 0.0 copy-done.7
  4.3 6.1 %fold_up.1 = bf16[2224,128]{1,0:T(8,128)(2,1)S(1)} custom-call(s32[8]{0:T(128)S(1)} %copy-done.7, bf16[4352,128]{1,0:T(8,128)(2,1)S(1)} %bitcast.24, bf16[4,128,128]{2,1,0:T(8,128)(2,1)S(1)} %bitcast.29, bf16[4352,128]{1,0:T(8,128)(2,1)S(1)} %collective-permute-done.far_environ_ref, bf16[4,128,128]{2,1,0:T(8,128)(2,1)S(1)} %collective-permute-done.1.far_site_ref, ...), custom_call_target="tpu_custom_call" | custom-call | flops 13200000000 | tf_op jit(solution)/shard_map/fold_up/pallas_call | solution.py:389
  10.4 0.0 copy-start.1
  10.4 0.0 copy-start.6
  10.4 5.6 %collective-permute-start.3 = (bf16[2224,128]{1,0:T(8,128)(2,1)S(1)}, bf16[2224,128]{1,0:T(8,128)(2,1)S(1)}, u32[]{:S(2)}, u32[]{:S(2)}) collective-permute-start(bf16[2224,128]{1,0:T(8,128)(2,1)S(1)} %fold_up.1), channel_id=1, source_target_pairs={{0,2},{1,3},{2,4},{3,5},{4,6},{5,7},{8,10},{9,11},{10,12},{11,13},... | collective-permute-start | bytes 1708040 | tf_op jit(solution)/shard_map/ppermute | solution.py:470
  16.0 5.4 %collective-permute-done.2.far_ref = bf16[2224,128]{1,0:T(8,128)(2,1)S(1)} collective-permute-done((bf16[2224,128]{1,0:T(8,128)(2,1)S(1)}, bf16[2224,128]{1,0:T(8,128)(2,1)S(1)}, u32[]{:S(2)}, u32[]{:S(2)}) %collective-permute-start.2) | collective-permute-done | bytes 569376 | tf_op jit(solution)/shard_map/ppermute | solution.py:454
  21.4 2.4 %fold_own.1 = f32[2224,128]{1,0:T(8,128)S(1)} custom-call(s32[8]{0:T(128)S(1)} %copy-done.7, bf16[4352,128]{1,0:T(8,128)(2,1)S(1)} %bitcast.25, bf16[4,128,128]{2,1,0:T(8,128)(2,1)S(1)} %bitcast.30, bf16[4352,128]{1,0:T(8,128)(2,1)S(1)} %collective-permute-done.far_environ_ref, bf16[4,128,128]{2,1,0:T(8,128)(2,1)S(1)} %collective-permute-done.1.far_site_ref, ...), custom_call_target="tpu_custom_call" | custom-call | flops 8800000000 | tf_op jit(solution)/shard_map/fold_own/pallas_call | solution.py:389
  23.8 3.0 %collective-permute-start.5 = (bf16[2224,128]{1,0:T(8,128)(2,1)S(1)}, bf16[2224,128]{1,0:T(8,128)(2,1)S(1)}, u32[]{:S(2)}, u32[]{:S(2)}) collective-permute-start(bf16[2224,128]{1,0:T(8,128)(2,1)S(1)} %pack_right.1), channel_id=1, source_target_pairs={{0,1},{1,0},{2,3},{3,2},{4,5},{5,4},{6,7},{7,6},{8,9},{9,8},{10,11... | collective-permute-start | bytes 1708040 | tf_op jit(solution)/shard_map/ppermute | solution.py:479
  26.8 2.0 %collective-permute-start.6 = (bf16[2224,128]{1,0:T(8,128)(2,1)S(1)}, bf16[2224,128]{1,0:T(8,128)(2,1)S(1)}, u32[]{:S(2)}, u32[]{:S(2)}) collective-permute-start(bf16[2224,128]{1,0:T(8,128)(2,1)S(1)} %collective-permute-done.2.far_ref), channel_id=1, source_target_pairs={{0,1},{2,3},{4,5},{6,7},{8,9},{10,11},{12,13},{14,15},{16,17},{18,... | collective-permute-start | bytes 1708040 | tf_op jit(solution)/shard_map/ppermute | solution.py:480
  28.8 0.0 copy-done.1
  28.8 0.0 copy-done.6
  28.8 1.2 %mix_own.1.own_ref = bf16[4352,128]{1,0:T(8,128)(2,1)S(1)} custom-call(bf16[4352,128]{1,0:T(8,128)(2,1)S(1)} %bitcast.22, f32[136,34]{1,0:T(8,128)S(1)} %bitcast.33), custom_call_target="tpu_custom_call" | custom-call | flops 5500000256 | tf_op jit(solution)/shard_map/mix_own/pallas_call | solution.py:389
  30.0 1.7 %mix_after.1.after_ref = bf16[4352,128]{1,0:T(8,128)(2,1)S(1)} custom-call(bf16[2224,128]{1,0:T(8,128)(2,1)S(1)} %collective-permute-done.2.far_ref, f32[136,34]{1,0:T(8,128)S(1)} %bitcast.34), custom_call_target="tpu_custom_call" | custom-call | flops 6600000000 | tf_op jit(solution)/shard_map/mix_after/pallas_call | solution.py:389
  31.8 0.0 collective-permute-done.3
  31.8 0.1 add_convert_fusion.source_ref
  31.9 3.4 %collective-permute-start.4 = (bf16[2224,128]{1,0:T(8,128)(2,1)S(1)}, bf16[2224,128]{1,0:T(8,128)(2,1)S(1)}, u32[]{:S(2)}, u32[]{:S(2)}) collective-permute-start(bf16[2224,128]{1,0:T(8,128)(2,1)S(1)} %add_convert_fusion.source_ref), channel_id=1, source_target_pairs={{0,8},{8,16},{16,24},{1,9},{9,17},{17,25},{2,10},{10,18},{18,26},{... | collective-permute-start | bytes 1708040 | tf_op jit(solution)/shard_map/ppermute | solution.py:491
  35.3 1.8 %unpack_env.1 = bf16[4352,128]{1,0:T(8,128)(2,1)} custom-call(bf16[2224,128]{1,0:T(8,128)(2,1)S(1)} %add_convert_fusion.source_ref), custom_call_target="tpu_custom_call" | custom-call | flops 3300000000 | tf_op jit(solution)/shard_map/unpack_env/pallas_call | solution.py:389
  37.2 0.0 copy-start.3
  37.2 0.0 collective-permute-done.5.near_ref
  37.2 0.0 collective-permute-done.6.relay_ref
  37.2 2.3 %mix_next.1.next_ref = bf16[8704,128]{1,0:T(8,128)(2,1)S(1)} custom-call(bf16[2224,128]{1,0:T(8,128)(2,1)S(1)} %collective-permute-done.5.near_ref, bf16[2224,128]{1,0:T(8,128)(2,1)S(1)} %collective-permute-done.6.relay_ref, f32[136,34]{1,0:T(8,128)S(1)} %bitcast.35), custom_call_target="tpu_custom_call" | custom-call | flops 7699999744 | tf_op jit(solution)/shard_map/mix_next/pallas_call | solution.py:389
  39.5 7.4 %collective-permute-done.4.packed_ref = bf16[2224,128]{1,0:T(8,128)(2,1)S(1)} collective-permute-done((bf16[2224,128]{1,0:T(8,128)(2,1)S(1)}, bf16[2224,128]{1,0:T(8,128)(2,1)S(1)}, u32[]{:S(2)}, u32[]{:S(2)}) %collective-permute-start.4) | collective-permute-done | bytes 569376 | tf_op jit(solution)/shard_map/ppermute | solution.py:491
  46.9 0.0 copy-done.3
  47.0 12.1 %lanczos.1 = (f32[5,4,128,128]{3,2,1,0:T(8,128)S(1)}, f32[16,128]{1,0:T(8,128)S(1)}) custom-call(s32[8]{0:T(128)S(1)} %copy-done.7, bf16[2224,128]{1,0:T(8,128)(2,1)S(1)} %collective-permute-done.4.packed_ref, bf16[4352,128]{1,0:T(8,128)(2,1)S(1)} %bitcast.26, bf16[4352,128]{1,0:T(8,128)(2,1)S(1)} %mix_own.1.own_ref, ...), custom_call_target="tpu_custom_call" | custom-call | flops 16499999744 | tf_op jit(solution)/shard_map/lanczos/pallas_call | solution.py:389
  59.1 10.0 %all_to_all.5.stats_ref = f32[8,16,128]{2,1,0:T(8,128)S(1)} all-to-all(f32[8,16,128]{2,1,0:T(8,128)S(1)} %broadcast_in_dim.9), channel_id=1, replica_groups=mesh['seg'=4,'sec'=8] {'sec'}, dimensions={0} | all-to-all | bytes 131072 | tf_op jit(solution)/shard_map/all_to_all | solution.py:409
  69.1 1.7 %finish.1 = (f32[4,128,128]{2,1,0:T(8,128)}, f32[2,4]{1,0:T(2,128)}) custom-call(f32[8,16,128]{2,1,0:T(8,128)S(1)} %all_to_all.5.stats_ref, f32[5,4,128,128]{3,2,1,0:T(8,128)S(1)} %get-tuple-element.32.basis_ref), custom_call_target="tpu_custom_call" | custom-call | flops 2200000000 | tf_op jit(solution)/shard_map/finish/pallas_call | solution.py:389
  (1 shorter events, 0.0 us)
Async XLA Ops:
  0.6 3.6 %collective-permute-start = (bf16[4352,128]{1,0:T(8,128)(2,1)}, bf16[4352,128]{1,0:T(8,128)(2,1)S(1)}, u32[]{:S(2)}, u32[]{:S(2)}) collective-permute-start(bf16[4352,128]{1,0:T(8,128)(2,1)} %bitcast.23), channel_id=1, source_target_pairs={{0,1},{1,0},{2,3},{3,2},{4,5},{5,4},{6,7},{7,6},{8,9},{9,8},{10,11... | collective-permute-start | bytes 3342344 | tf_op jit(solution)/shard_map/ppermute | solution.py:449
  1.1 3.1 %collective-permute-start.1 = (bf16[4,128,128]{2,1,0:T(8,128)(2,1)}, bf16[4,128,128]{2,1,0:T(8,128)(2,1)S(1)}, u32[]{:S(2)}, u32[]{:S(2)}) collective-permute-start(bf16[4,128,128]{2,1,0:T(8,128)(2,1)} %bitcast.28), channel_id=1, source_target_pairs={{0,1},{1,0},{2,3},{3,2},{4,5},{5,4},{6,7},{7,6},{8,9},{9,8},{10,11... | collective-permute-start | bytes 393224 | tf_op jit(solution)/shard_map/ppermute | solution.py:450
  1.2 1.2 %copy-start = (bf16[1,1,34,128,128]{4,3,2,1,0:T(8,128)(2,1)S(1)}, bf16[1,1,34,128,128]{4,3,2,1,0:T(8,128)(2,1)}, u32[]{:S(2)}) copy-start(bf16[1,1,34,128,128]{4,3,2,1,0:T(8,128)(2,1)} %param.8) | copy-start | bytes 3342340
  2.5 1.8 %copy-start.2 = (bf16[1,1,34,128,128]{4,3,2,1,0:T(8,128)(2,1)S(1)}, bf16[1,1,34,128,128]{4,3,2,1,0:T(8,128)(2,1)}, u32[]{:S(2)}) copy-start(bf16[1,1,34,128,128]{4,3,2,1,0:T(8,128)(2,1)} %param.7) | copy-start | bytes 3342340
  2.5 1.8 %copy-start.4 = (bf16[1,1,4,1,128,128]{5,4,3,2,1,0:T(8,128)(2,1)S(1)}, bf16[1,1,4,1,128,128]{5,4,3,2,1,0:T(8,128)(2,1)}, u32[]{:S(2)}) copy-start(bf16[1,1,4,1,128,128]{5,4,3,2,1,0:T(8,128)(2,1)} %param.9) | copy-start | bytes 393220
  2.5 1.8 %copy-start.5 = (f32[1,1,34,34,4]{3,4,2,1,0:T(4,128)S(1)}, f32[1,1,34,34,4]{3,4,2,1,0:T(4,128)}, u32[]{:S(2)}) copy-start(f32[1,1,34,34,4]{3,4,2,1,0:T(4,128)} %param.10) | copy-start | bytes 55492
  2.5 1.8 %copy-start.7 = (s32[8]{0:T(128)S(1)}, s32[8]{0:T(128)}, u32[]{:S(2)}) copy-start(s32[8]{0:T(128)} %dims_ref.5) | copy-start | bytes 100
  2.8 18.6 %collective-permute-start.2 = (bf16[2224,128]{1,0:T(8,128)(2,1)S(1)}, bf16[2224,128]{1,0:T(8,128)(2,1)S(1)}, u32[]{:S(2)}, u32[]{:S(2)}) collective-permute-start(bf16[2224,128]{1,0:T(8,128)(2,1)S(1)} %pack_right.1), channel_id=1, source_target_pairs={{2,0},{3,1},{4,2},{5,3},{6,4},{7,5},{10,8},{11,9},{12,10},{13,11},... | collective-permute-start | bytes 1708040 | tf_op jit(solution)/shard_map/ppermute | solution.py:454
  10.4 18.4 %copy-start.1 = (bf16[1,1,34,128,128]{4,3,2,1,0:T(8,128)(2,1)S(1)}, bf16[1,1,34,128,128]{4,3,2,1,0:T(8,128)(2,1)}, u32[]{:S(2)}) copy-start(bf16[1,1,34,128,128]{4,3,2,1,0:T(8,128)(2,1)} %param.8) | copy-start | bytes 3342340
  10.4 18.4 %copy-start.6 = (f32[1,34,34,4]{2,3,1,0:T(4,128)S(1)}, f32[1,34,34,4]{2,3,1,0:T(4,128)}, u32[]{:S(2)}) copy-start(f32[1,34,34,4]{2,3,1,0:T(4,128)} %param.11) | copy-start | bytes 55492
  10.4 21.4 %collective-permute-start.3 = (bf16[2224,128]{1,0:T(8,128)(2,1)S(1)}, bf16[2224,128]{1,0:T(8,128)(2,1)S(1)}, u32[]{:S(2)}, u32[]{:S(2)}) collective-permute-start(bf16[2224,128]{1,0:T(8,128)(2,1)S(1)} %fold_up.1), channel_id=1, source_target_pairs={{0,2},{1,3},{2,4},{3,5},{4,6},{5,7},{8,10},{9,11},{10,12},{11,13},... | collective-permute-start | bytes 1708040 | tf_op jit(solution)/shard_map/ppermute | solution.py:470
  23.8 13.3 %collective-permute-start.5 = (bf16[2224,128]{1,0:T(8,128)(2,1)S(1)}, bf16[2224,128]{1,0:T(8,128)(2,1)S(1)}, u32[]{:S(2)}, u32[]{:S(2)}) collective-permute-start(bf16[2224,128]{1,0:T(8,128)(2,1)S(1)} %pack_right.1), channel_id=1, source_target_pairs={{0,1},{1,0},{2,3},{3,2},{4,5},{5,4},{6,7},{7,6},{8,9},{9,8},{10,11... | collective-permute-start | bytes 1708040 | tf_op jit(solution)/shard_map/ppermute | solution.py:479
  26.8 10.4 %collective-permute-start.6 = (bf16[2224,128]{1,0:T(8,128)(2,1)S(1)}, bf16[2224,128]{1,0:T(8,128)(2,1)S(1)}, u32[]{:S(2)}, u32[]{:S(2)}) collective-permute-start(bf16[2224,128]{1,0:T(8,128)(2,1)S(1)} %collective-permute-done.2.far_ref), channel_id=1, source_target_pairs={{0,1},{2,3},{4,5},{6,7},{8,9},{10,11},{12,13},{14,15},{16,17},{18,... | collective-permute-start | bytes 1708040 | tf_op jit(solution)/shard_map/ppermute | solution.py:480
  31.9 15.0 %collective-permute-start.4 = (bf16[2224,128]{1,0:T(8,128)(2,1)S(1)}, bf16[2224,128]{1,0:T(8,128)(2,1)S(1)}, u32[]{:S(2)}, u32[]{:S(2)}) collective-permute-start(bf16[2224,128]{1,0:T(8,128)(2,1)S(1)} %add_convert_fusion.source_ref), channel_id=1, source_target_pairs={{0,8},{8,16},{16,24},{1,9},{9,17},{17,25},{2,10},{10,18},{18,26},{... | collective-permute-start | bytes 1708040 | tf_op jit(solution)/shard_map/ppermute | solution.py:491
  37.2 9.8 %copy-start.3 = (f32[1,4,1,128,128]{4,3,2,1,0:T(8,128)S(1)}, f32[1,4,1,128,128]{4,3,2,1,0:T(8,128)}, u32[]{:S(2)}) copy-start(f32[1,4,1,128,128]{4,3,2,1,0:T(8,128)} %param.12) | copy-start | bytes 786436

commit v4 on v3

--- a/solution.py
+++ b/solution.py
@@ -22,8 +22,13 @@
     return -(-count // 16) * 16
 
 
-def packed_rows(width, tile):
-    return -(-(width * tile // 2 + padded(width)) // 16) * 16
+def packed_rows(count, tile):
+    return count * tile // 2 + packed_height(count)
+
+
+def chunks_of(width):
+    first = -(-width // 4) * 2
+    return (0, first), (first, width - first)
 
 
 def iotas(shape):
@@ -92,22 +97,29 @@
     out_ref[width * half :, :] = diag[...].astype(BF16)
 
 
-def unpack_into(width, tile, pitch, read, out_ref, diag):
+def unpack_into(count, tile, read, write, diag):
     half = tile // 2
-    diag[...] = read(width * half, diag.shape[0])
-    for w in range(width):
-        block = unpack_block(read(w * half, half), diag[w : w + 1, :])
-        out_ref[w * pitch : w * pitch + tile, :] = block.astype(out_ref.dtype)
-
-
-def unpack_kernel(width, tile, source_ref, out_ref, diag):
-    unpack_into(
-        width, tile, tile, lambda at, size: source_ref[at : at + size, :].astype(F32), out_ref, diag
-    )
+    size = packed_height(count)
+    diag[:size, :] = read(count * half, size)
+    for w in range(count):
+        write(w, unpack_block(read(w * half, half), diag[w : w + 1, :]))
+
+
+def reader(ref):
+    return lambda at, size: ref[at : at + size, :].astype(F32)
+
+
+def unpack_kernel(width, tile, early_ref, late_ref, out_ref, diag):
+    for (first, count), ref in zip(chunks_of(width), (early_ref, late_ref)):
+
+        def write(w, block, first=first):
+            out_ref[(first + w) * tile : (first + w + 1) * tile, :] = block.astype(BF16)
+
+        unpack_into(count, tile, reader(ref), write, diag)
 
 
 def fold_kernel(
-    width, tile, travels, dims_ref, environ_ref, site_ref, far_environ_ref, far_site_ref, weight_ref, out_ref,
+    width, tile, travels, dims_ref, environ_ref, site_ref, far_environ_ref, far_site_ref, weight_ref, early_ref, late_ref,
     joined_s, turned_s, square_s, weight_s, half_s, packed_s, diag_s, sums_s, diag_sums_s,
 ):
     half = tile // 2
@@ -176,11 +188,12 @@
                 sums_s[pl.ds(at + k, wide, stride=pitch), :] = value[:, k * tile : (k + 1) * tile]
         diag_sums_s[...] = jnp.zeros_like(diag_sums_s)
         diag_sums_s[:wide, :] = mixed([diag_s[n, :wide] for n in range(parts)])
-        for w in range(width):
-            out_ref[w * half : (w + 1) * half, :] = sums_s[w * pitch : w * pitch + half, :].astype(
-                out_ref.dtype
-            )
-        out_ref[width * half :, :] = diag_sums_s[...].astype(out_ref.dtype)
+        for (first, count), ref in zip(chunks_of(width), (early_ref, late_ref)):
+            for w in range(count):
+                at = (first + w) * pitch
+                ref[w * half : (w + 1) * half, :] = sums_s[at : at + half, :].astype(ref.dtype)
+            rows = packed_height(count)
+            ref[count * half :, :] = diag_sums_s[first : first + rows, :].astype(ref.dtype)
 
     even = lax.rem(sector, 2) == 0
     own_state = len(CHARGES) - 1 if travels else 0
@@ -211,8 +224,16 @@
                 sums_s[index, pl.ds(at + k, wide, stride=pitch), :] = mixed[:, k * tile : (k + 1) * tile]
     for index in range(len(weights)):
         for w in range(width):
-            out = (index * width + w) * tile
-            out_ref[out : out + tile, :] = sums_s[index, w * pitch : w * pitch + tile, :].astype(BF16)
+            out_ref[index, :, w * tile : (w + 1) * tile] = sums_s[
+                index, w * pitch : w * pitch + tile, :
+            ].astype(BF16)
+
+
+def unpack_wide(width, tile, read, wide_s, diag):
+    def write(w, block):
+        wide_s[w * (tile + 8) : w * (tile + 8) + tile, :] = block
+
+    unpack_into(width, tile, read, write, diag)
 
 
 def mix_own_kernel(width, tile, source_ref, weight_ref, out_ref, square_s, weight_s, wide_s, sums_s):
@@ -234,7 +255,7 @@
         near = near_ref[at : at + size, :].astype(F32)
         return jnp.where(even, near, relay_ref[at : at + size, :].astype(F32))
 
-    unpack_into(width, tile, tile + 8, read, wide_s, diag)
+    unpack_wide(width, tile, read, wide_s, diag)
     mix_into(width, tile, [weight_s.at[k] for k in range(2)], wide_s, sums_s, out_ref)
 
 
@@ -242,11 +263,7 @@
     width, tile, far_ref, weight_ref, out_ref, square_s, weight_s, wide_s, sums_s, diag
 ):
     weight_s[0] = weight_rows(weight_ref, width, 3, square_s, False)
-
-    def read(at, size):
-        return far_ref[at : at + size, :].astype(F32)
-
-    unpack_into(width, tile, tile + 8, read, wide_s, diag)
+    unpack_wide(width, tile, reader(far_ref), wide_s, diag)
     mix_into(width, tile, [weight_s.at[0]], wide_s, sums_s, out_ref)
 
 
@@ -254,74 +271,117 @@
     return jnp.sum(jnp.sum(value, axis=0, keepdims=True), axis=1, keepdims=True)
 
 
-def lanczos_kernel(
-    width, tile, dims_ref, packed_ref, environ_ref, own_ref, next_ref, after_ref, guess_ref,
-    basis_ref, stats_ref, bound_s, first_s, diag,
+def put(stats, kind, lane_at, value):
+    row, lane = iotas(stats.shape)
+    return jnp.where((row == kind) & (lane == lane_at), value, stats)
+
+
+def scaled(value):
+    square = total(value * value)
+    inverse = jnp.where(square > 0.0, lax.rsqrt(square), 0.0)
+    return value * inverse, square * inverse
+
+
+def right_products(width, tile, field, right_ref, out_ref, p):
+    group, lanes = p // 2, slice(p % 2 * tile, (p % 2 + 1) * tile)
+    for pair in range(width // 2):
+        at = pair * 2 * tile
+        both = jnp.dot(field, right_ref[:, at : at + 2 * tile], preferred_element_type=F32).astype(BF16)
+        for k in range(2):
+            out_ref[group, at + k * tile : at + (k + 1) * tile, lanes] = both[:, k * tile : (k + 1) * tile]
+
+
+def head_kernel(
+    width, tile, dims_ref, guess_ref, own_ref, next_ref, after_ref, vector_ref, stats_ref, product_ref
 ):
     states = len(CHARGES)
     sector = lax.axis_index("sec")
-    segment = lax.axis_index("seg")
-
-    @pl.when(segment == 0)
-    def _():
-        bound_s[...] = environ_ref[...]
-
-    @pl.when(segment != 0)
-    def _():
-        unpack_into(
-            width, tile, tile, lambda at, size: packed_ref[at : at + size, :].astype(F32), bound_s, diag
-        )
-
     rows, columns = live_limits(dims_ref, sector)
     row, lane = iotas((tile, tile))
-    stat_row, stat_lane = iotas(stats_ref.shape)
+    rights = [own_ref.at[0], next_ref.at[0], next_ref.at[1], after_ref.at[0]]
     stats = jnp.zeros(stats_ref.shape, F32)
-
-    def put(stats, kind, p, value):
-        here = (stat_row == kind) & (stat_lane == sector * states + p)
-        return jnp.where(here, value, stats)
-
-    def scaled(value):
-        square = total(value * value)
-        inverse = jnp.where(square > 0.0, lax.rsqrt(square), 0.0)
-        return value * inverse, square * inverse
-
     for p in range(states):
         live = (row < rows) & (lane < columns[p])
         vector, norm = scaled(jnp.where(live, guess_ref[p], 0.0))
-        basis_ref[0, p] = vector
-        stats = put(stats, 0, p, norm)
-
-    size = width * tile
-    rights = [own_ref, next_ref.at[:size, :], next_ref.at[size:, :], after_ref]
-    betas = [jnp.zeros((1, 1), F32)] * states
+        vector_ref[p] = vector
+        stats = put(stats, 0, sector * states + p, norm)
+        right_products(width, tile, vector.astype(BF16), rights[p], product_ref, p)
+    stats_ref[...] = stats
+
+
+def bound_blocks(first, count, tile, packed_ref, environ_ref, out_ref, diag):
+    segment = lax.axis_index("seg")
+
+    @pl.when(segment == 0)
+    def _():
+        for w in range(count):
+            out_ref[:, w * tile : (w + 1) * tile] = environ_ref[
+                (first + w) * tile : (first + w + 1) * tile, :
+            ]
+
+    @pl.when(segment != 0)
+    def _():
+        def write(w, block):
+            out_ref[:, w * tile : (w + 1) * tile] = block.astype(BF16)
+
+        unpack_into(count, tile, reader(packed_ref), write, diag)
+
+
+def open_kernel(width, tile, packed_ref, environ_ref, product_ref, bound_ref, image_ref, diag):
+    first, count = chunks_of(width)[0]
+    bound_blocks(first, count, tile, packed_ref, environ_ref, bound_ref, diag)
+    for group in range(len(CHARGES) // 2):
+        image_ref[group] = jnp.dot(
+            bound_ref[...], product_ref[group, : count * tile, :], preferred_element_type=F32
+        )
+
+
+def lanczos_kernel(
+    width, tile, dims_ref, packed_ref, environ_ref, early_ref, image_ref, own_ref, next_ref, after_ref,
+    start_ref, norm_ref, product_ref, basis_ref, stats_ref, late_s, product_s, diag,
+):
+    states = len(CHARGES)
+    sector = lax.axis_index("sec")
+    first, count = chunks_of(width)[1]
+    bound_blocks(first, count, tile, packed_ref, environ_ref, late_s, diag)
+    rows, columns = live_limits(dims_ref, sector)
+    row, lane = iotas((tile, tile))
+    rights = [own_ref.at[0], next_ref.at[0], next_ref.at[1], after_ref.at[0]]
+    stats = norm_ref[...]
+    split = first * tile
+    betas = [None] * states
     for j in range(LANCZOS):
-        field = jnp.concatenate([basis_ref[j, p] for p in range(states)], axis=1).astype(BF16)
-        for w in range(width):
-            first = jnp.dot(
-                bound_s[w * tile : (w + 1) * tile, :], field, preferred_element_type=F32
-            ).astype(BF16)
-            for p in range(states):
-                first_s[p, :, w * tile : (w + 1) * tile] = first[:, p * tile : (p + 1) * tile]
-        for p in range(states):
-            live = (row < rows) & (lane < columns[p])
-            right = rights[p][...]
-            image = jnp.dot(first_s[p], right, preferred_element_type=F32)
-            image = jnp.where(live, image, 0.0)
-            vector = basis_ref[j, p]
-            alpha = total(vector * image)
-            image = image - alpha * vector
-            if j > 0:
-                image = image - betas[p] * basis_ref[j - 1, p]
-            following, beta = scaled(image)
-            basis_ref[j + 1, p] = following
-            betas[p] = beta
-            stats = put(stats, 1 + 2 * j, p, alpha)
-            stats = put(stats, 2 + 2 * j, p, beta)
+        source = product_ref if j == 0 else product_s
+        for group in range(states // 2):
+            members = (2 * group, 2 * group + 1)
+            if j == 0:
+                images = image_ref[group]
+            else:
+                for p in members:
+                    field = basis_ref[j - 1, p].astype(BF16)
+                    right_products(width, tile, field, rights[p], product_s, p)
+                images = jnp.dot(early_ref[...], source[group, :split, :], preferred_element_type=F32)
+            images = images + jnp.dot(
+                late_s[...], source[group, split:, :], preferred_element_type=F32
+            )
+            for p in members:
+                live = (row < rows) & (lane < columns[p])
+                image = jnp.where(live, images[:, p % 2 * tile : (p % 2 + 1) * tile], 0.0)
+                vector = start_ref[p] if j == 0 else basis_ref[j - 1, p]
+                alpha = total(vector * image)
+                image = image - alpha * vector
+                if j > 0:
+                    before = start_ref[p] if j == 1 else basis_ref[j - 2, p]
+                    image = image - betas[p] * before
+                following, beta = scaled(image)
+                basis_ref[j, p] = following
+                betas[p] = beta
+                stats = put(stats, 1 + 2 * j, sector * states + p, alpha)
+                stats = put(stats, 2 + 2 * j, sector * states + p, beta)
     stats_ref[...] = stats
 
 
-def finish_kernel(entries, stats_ref, basis_ref, vector_ref, table_ref):
+def finish_kernel(entries, stats_ref, start_ref, basis_ref, vector_ref, table_ref):
     states = len(CHARGES)
     sector = lax.axis_index("sec")
     stats = stats_ref[0]
@@ -371,7 +431,7 @@
         here = lane == sector * states + p
         for k in range(LANCZOS + 1):
             weight = jnp.sum(jnp.where(here, vector[k], 0.0), axis=1, keepdims=True)
-            term = weight * basis_ref[k, p]
+            term = weight * (start_ref[p] if k == 0 else basis_ref[k - 1, p])
             value = term if value is None else value + term
         vector_ref[p] = value
 
@@ -420,10 +480,13 @@
     prows = packed_rows(width, tile)
     drows = prows - width * half
     packed = jax.ShapeDtypeStruct((prows, tile), BF16)
-    packed32 = jax.ShapeDtypeStruct((prows, tile), F32)
-
-    def blocks(count):
-        return jax.ShapeDtypeStruct((count * width * tile, tile), BF16)
+    parts = chunks_of(width)
+
+    def packed_parts(dtype):
+        return [jax.ShapeDtypeStruct((packed_rows(count, tile), tile), dtype) for _, count in parts]
+
+    def mixed(count):
+        return jax.ShapeDtypeStruct((count, tile, width * tile), BF16)
 
     environ = left_env.reshape(width * tile, tile)
     right = right_env.reshape(width * tile, tile)
@@ -465,57 +528,84 @@
     ]
     outgoing = call(
         "fold_up", functools.partial(fold_kernel, width, tile, True),
-        [sector_dims], [environ, site, far_environ, far_site, site_weights], packed, fold_scratch, 20, 12,
-    )
-    arrived = lax.ppermute(outgoing, "sec", up_two)
-    outgoing, right_far, far_environ = lax.optimization_barrier((outgoing, right_far, far_environ))
+        [sector_dims], [environ, site, far_environ, far_site, site_weights], packed_parts(BF16),
+        fold_scratch, 20, 12,
+    )
+    arrived = [lax.ppermute(part, "sec", up_two) for part in outgoing]
     kept = call(
         "fold_own", functools.partial(fold_kernel, width, tile, False),
-        [sector_dims], [environ, site, far_environ, far_site, site_weights], packed32, fold_scratch, 20, 8,
-    )
-    kept, right_far, right, right_packed = lax.optimization_barrier(
-        (kept, right_far, right, right_packed)
+        [sector_dims], [environ, site, far_environ, far_site, site_weights], packed_parts(F32),
+        fold_scratch, 20, 0.1,
+    )
+    kept, right_far = lax.optimization_barrier((kept, right_far))
+    early = (kept[0] + arrived[0].astype(F32)).astype(BF16)
+    early_bound = lax.ppermute(early, "seg", onward)
+    early, right_far, right, right_packed = lax.optimization_barrier(
+        (early, right_far, right, right_packed)
     )
     right_near = lax.ppermute(right_packed, "sec", swap)
     right_relay = lax.ppermute(right_far, "sec", across)
     own_mixed = call(
         "mix_own", functools.partial(mix_own_kernel, width, tile), [], [right, bound_weights],
-        blocks(1), mix_scratch(1), 12, 5,
+        mixed(1), mix_scratch(1), 12, 1,
     )
     after_mixed = call(
         "mix_after", functools.partial(mix_after_kernel, width, tile), [],
-        [right_far, bound_weights], blocks(1), mix_scratch(1) + [diag], 12, 6,
-    )
-    arrived, own_mixed, after_mixed = lax.optimization_barrier((arrived, own_mixed, after_mixed))
-    fresh = (kept + arrived.astype(F32)).astype(BF16)
-    received = lax.ppermute(fresh, "seg", onward)
+        [right_far, bound_weights], mixed(1), mix_scratch(1) + [diag], 12, 2,
+    )
+    late_arrived, own_mixed, after_mixed = lax.optimization_barrier(
+        (arrived[1], own_mixed, after_mixed)
+    )
+    late = (kept[1] + late_arrived.astype(F32)).astype(BF16)
+    late_bound = lax.ppermute(late, "seg", onward)
+    late, right_near, right_relay = lax.optimization_barrier((late, right_near, right_relay))
     next_mixed = call(
         "mix_next", functools.partial(mix_next_kernel, width, tile), [],
-        [right_near, right_relay, bound_weights], blocks(2), mix_scratch(2) + [diag], 16, 7,
+        [right_near, right_relay, bound_weights], mixed(2), mix_scratch(2) + [diag], 16, 3,
+    )
+    start, norms, products = call(
+        "head", functools.partial(head_kernel, width, tile),
+        [sector_dims], [guess[0, :, 0], own_mixed, next_mixed, after_mixed],
+        (
+            jax.ShapeDtypeStruct((states, tile, tile), F32),
+            jax.ShapeDtypeStruct((16, 128), F32),
+            jax.ShapeDtypeStruct((states // 2, width * tile, 2 * tile), BF16),
+        ),
+        [], 14, 2,
     )
     new_env = call(
-        "unpack_env", functools.partial(unpack_kernel, width, tile), [], [fresh], blocks(1), [diag],
-        6, 3,
-    )
-    received, next_mixed, new_env = lax.optimization_barrier((received, next_mixed, new_env))
+        "unpack_env", functools.partial(unpack_kernel, width, tile), [], [early, late],
+        jax.ShapeDtypeStruct((width * tile, tile), BF16), [diag], 6, 2,
+    )
+    early_bound, products, new_env = lax.optimization_barrier((early_bound, products, new_env))
+    bound, image = call(
+        "open", functools.partial(open_kernel, width, tile), [], [early_bound, environ, products],
+        (
+            jax.ShapeDtypeStruct((tile, parts[0][1] * tile), BF16),
+            jax.ShapeDtypeStruct((states // 2, tile, 2 * tile), F32),
+        ),
+        [diag], 12, 1,
+    )
+    late_bound, bound = lax.optimization_barrier((late_bound, bound))
     basis, stats = call(
         "lanczos", functools.partial(lanczos_kernel, width, tile),
-        [sector_dims], [received, environ, own_mixed, next_mixed, after_mixed, guess[0, :, 0]],
+        [sector_dims],
+        [late_bound, environ, bound, image, own_mixed, next_mixed, after_mixed, start, norms, products],
         (
-            jax.ShapeDtypeStruct((LANCZOS + 1, states, tile, tile), F32),
+            jax.ShapeDtypeStruct((LANCZOS, states, tile, tile), F32),
             jax.ShapeDtypeStruct((16, 128), F32),
         ),
         [
-            pltpu.VMEM((width * tile, tile), BF16),
-            pltpu.VMEM((states, tile, width * tile), BF16),
+            pltpu.VMEM((tile, parts[1][1] * tile), BF16),
+            pltpu.VMEM((states // 2, width * tile, 2 * tile), BF16),
             diag,
         ],
-        18, 15,
+        22, 12,
     )
     stats = gathered(stats, "sec")
     entries = float(states * sector_count * tile * tile)
     vector, table = call(
-        "finish", functools.partial(finish_kernel, entries), [], [stats, basis],
+        "finish", functools.partial(finish_kernel, entries), [], [stats, start, basis],
         (
             jax.ShapeDtypeStruct((states, tile, tile), F32),
             jax.ShapeDtypeStruct((2, LANCZOS), F32),

time: 71.3 us -> 66.7 us (0.935)
  waiting for transfers between devices: 12.8 us -> 3.13 us
  starting transfers between devices: 16 us -> 22 us
  Pallas kernels: 29.8 us -> 28.2 us
  blocking collectives: 9.98 us -> 10.7 us
    ppermute x2 -> x4, starting transfers between devices: 9.05 us -> 17.5 us  [the longest x2 10.3 us: on_device(): arrived = [lax.ppermute(part, 'sec', up_two) for part in outgoing]]
    ppermute x2 -> x4, waiting for transfers between devices: 7.44 us -> 0.01 us  [the longest x2 0.01 us: on_device(): arrived = [lax.ppermute(part, 'sec', up_two) for part in outgoing]]
    ppermute x1, starting transfers between devices: 2.99 us -> 0.07 us  [on_device(): right_near = lax.ppermute(right_packed, 'sec', swap)]
    ppermute x1, waiting for transfers between devices: 5.39 us -> 3.11 us  [on_device(): right_far = lax.ppermute(right_packed, 'sec', down_two)]
    pallas_call x9 -> x11, Pallas kernels: 29.8 us -> 28.2 us  [call(): pl.pallas_call(kernel, out_shape=outs, in_specs=[smem()] * len(scalars) +...]
  transfers between devices with their start and end apart: 7 -> 9, of which waited for: 2 -> 1; matrix products, arithmetic and copies ran while one was open for 0% -> 0% of each run, Pallas kernels for 22% -> 28%
where the time goes in v4:
time: 66.7 us; the launch traced here: 66.4 us
  Pallas kernels  28.2 us (42%)
  starting transfers between devices  22 us (33%)
  blocking collectives  10.7 us (16%)
  waiting for transfers between devices  3.13 us (5%)
  local copies, waits for them, and re-layouts  1.29 us (2%)
  between operations  0.91 us (1%)
    pallas_call x11, Pallas kernels, call(): pl.pallas_call(kernel, out_shape=outs, in_specs=[smem()] * len(scalars) +...  28.2 us
    all_to_all x1, blocking collectives, gathered(): lax.all_to_all(jnp.broadcast_to(value, (count,) + value.shape), axis, 0, 0)  10.7 us
    ppermute x2, starting transfers between devices, on_device(): arrived = [lax.ppermute(part, 'sec', up_two) for part in outgoing]  10.3 us
    ppermute x1, starting transfers between devices, on_device(): late_bound = lax.ppermute(late, 'seg', onward)  3.7 us
    ppermute x1, starting transfers between devices, on_device(): early_bound = lax.ppermute(early, 'seg', onward)  3.5 us
    ppermute x1, waiting for transfers between devices, on_device(): right_far = lax.ppermute(right_packed, 'sec', down_two)  3.11 us
    ppermute x1, starting transfers between devices, on_device(): right_relay = lax.ppermute(right_far, 'sec', across)  2.42 us
    ppermute x1, starting transfers between devices, on_device(): right_far = lax.ppermute(right_packed, 'sec', down_two)  1.42 us
  transfers between devices with their start and end apart: 9, of which 1 were waited for; matrix products, arithmetic and copies ran while one was open for 0% of the time, Pallas kernels for 28%

profile of v4, /device:TPU:0, one launch (start us, length us, event | category | flops | bytes accessed | tf_op | source)
XLA Modules:
  0.0 66.4 jit_solution(1014166895704742231)
XLA Ops:
  0.6 0.5 collective-permute-start
  1.1 0.1 collective-permute-start.1
  1.2 0.0 copy-start.4
  1.2 1.2 %copy-done.4 = bf16[1,1,34,128,128]{4,3,2,1,0:T(8,128)(2,1)S(1)} copy-done((bf16[1,1,34,128,128]{4,3,2,1,0:T(8,128)(2,1)S(1)}, bf16[1,1,34,128,128]{4,3,2,1,0:T(8,128)(2,1)}, u32[]{:S(2)}) %copy-start.4) | copy-done | bytes 1114136
  2.5 0.0 copy-start
  2.5 0.0 copy-start.1
  2.5 0.0 copy-start.2
  2.5 0.0 copy-start.3
  2.5 0.3 pack_right.1
  2.8 1.4 %collective-permute-start.2 = (bf16[2224,128]{1,0:T(8,128)(2,1)S(1)}, bf16[2224,128]{1,0:T(8,128)(2,1)S(1)}, u32[]{:S(2)}, u32[]{:S(2)}) collective-permute-start(bf16[2224,128]{1,0:T(8,128)(2,1)S(1)} %pack_right.1), channel_id=1, source_target_pairs={{2,0},{3,1},{4,2},{5,3},{6,4},{7,5},{10,8},{11,9},{12,10},{13,11},... | collective-permute-start | bytes 1708040 | tf_op jit(solution)/shard_map/ppermute | solution.py:517
  4.2 0.0 collective-permute-done.1.far_site_ref
  4.2 0.0 collective-permute-done.far_environ_ref
  4.2 0.0 copy-done
  4.2 0.0 copy-done.1
  4.3 0.0 copy-done.2
  4.3 0.0 copy-done.3
  4.3 6.1 %fold_up.1 = (bf16[1184,128]{1,0:T(8,128)(2,1)S(1)}, bf16[1040,128]{1,0:T(8,128)(2,1)S(1)}) custom-call(s32[8]{0:T(128)S(1)} %copy-done.3, bf16[4352,128]{1,0:T(8,128)(2,1)S(1)} %bitcast.22, bf16[4,128,128]{2,1,0:T(8,128)(2,1)S(1)} %bitcast.27, bf16[4352,128]{1,0:T(8,128)(2,1)S(1)} %collective-permute-done.far_environ_ref, ...), custom_call_target="tpu_custom_call" | custom-call | flops 13200000000 | tf_op jit(solution)/shard_map/fold_up/pallas_call | solution.py:449
  10.4 5.5 %collective-permute-start.3 = (bf16[1184,128]{1,0:T(8,128)(2,1)S(1)}, bf16[1184,128]{1,0:T(8,128)(2,1)S(1)}, u32[]{:S(2)}, u32[]{:S(2)}) collective-permute-start(bf16[1184,128]{1,0:T(8,128)(2,1)S(1)} %get-tuple-element.37), channel_id=1, source_target_pairs={{0,2},{1,3},{2,4},{3,5},{4,6},{5,7},{8,10},{9,11},{10,12},{11,13},... | collective-permute-start | bytes 909320 | tf_op jit(solution)/shard_map/ppermute | solution.py:534
  15.9 2.4 %fold_own.1 = (f32[1184,128]{1,0:T(8,128)S(1)}, f32[1040,128]{1,0:T(8,128)S(1)}) custom-call(s32[8]{0:T(128)S(1)} %copy-done.3, bf16[4352,128]{1,0:T(8,128)(2,1)S(1)} %bitcast.23, bf16[4,128,128]{2,1,0:T(8,128)(2,1)S(1)} %bitcast.28, bf16[4352,128]{1,0:T(8,128)(2,1)S(1)} %collective-permute-done.far_environ_ref, ...), custom_call_target="tpu_custom_call" | custom-call | flops 110000000 | tf_op jit(solution)/shard_map/fold_own/pallas_call | solution.py:449
  18.3 0.0 copy-start.7
  18.3 3.1 %collective-permute-done.2.far_ref = bf16[2224,128]{1,0:T(8,128)(2,1)S(1)} collective-permute-done((bf16[2224,128]{1,0:T(8,128)(2,1)S(1)}, bf16[2224,128]{1,0:T(8,128)(2,1)S(1)}, u32[]{:S(2)}, u32[]{:S(2)}) %collective-permute-start.2) | collective-permute-done | bytes 569376 | tf_op jit(solution)/shard_map/ppermute | solution.py:517
  21.4 4.9 %collective-permute-start.5 = (bf16[1040,128]{1,0:T(8,128)(2,1)S(1)}, bf16[1040,128]{1,0:T(8,128)(2,1)S(1)}, u32[]{:S(2)}, u32[]{:S(2)}) collective-permute-start(bf16[1040,128]{1,0:T(8,128)(2,1)S(1)} %get-tuple-element.38), channel_id=1, source_target_pairs={{0,2},{1,3},{2,4},{3,5},{4,6},{5,7},{8,10},{9,11},{10,12},{11,13},... | collective-permute-start | bytes 798728 | tf_op jit(solution)/shard_map/ppermute | solution.py:534
  26.3 0.0 collective-permute-done.3
  26.3 0.1 add_convert_fusion.early_ref
  26.4 3.5 %collective-permute-start.4 = (bf16[1184,128]{1,0:T(8,128)(2,1)S(1)}, bf16[1184,128]{1,0:T(8,128)(2,1)S(1)}, u32[]{:S(2)}, u32[]{:S(2)}) collective-permute-start(bf16[1184,128]{1,0:T(8,128)(2,1)S(1)} %add_convert_fusion.early_ref), channel_id=1, source_target_pairs={{0,8},{8,16},{16,24},{1,9},{9,17},{17,25},{2,10},{10,18},{18,26},{... | collective-permute-start | bytes 909320 | tf_op jit(solution)/shard_map/ppermute | solution.py:542
  29.9 0.1 collective-permute-start.6
  30.0 2.4 %collective-permute-start.7 = (bf16[2224,128]{1,0:T(8,128)(2,1)S(1)}, bf16[2224,128]{1,0:T(8,128)(2,1)S(1)}, u32[]{:S(2)}, u32[]{:S(2)}) collective-permute-start(bf16[2224,128]{1,0:T(8,128)(2,1)S(1)} %collective-permute-done.2.far_ref), channel_id=1, source_target_pairs={{0,1},{2,3},{4,5},{6,7},{8,9},{10,11},{12,13},{14,15},{16,17},{18,... | collective-permute-start | bytes 1708040 | tf_op jit(solution)/shard_map/ppermute | solution.py:547
  32.4 0.0 copy-done.7
  32.4 0.0 copy-start.5
  32.4 1.8 %mix_after.1.after_ref = bf16[1,128,4352]{2,1,0:T(8,128)(2,1)S(1)} custom-call(bf16[2224,128]{1,0:T(8,128)(2,1)S(1)} %collective-permute-done.2.far_ref, f32[136,34]{1,0:T(8,128)S(1)} %bitcast.34), custom_call_target="tpu_custom_call" | custom-call | flops 2200000000 | tf_op jit(solution)/shard_map/mix_after/pallas_call | solution.py:449
  34.2 0.0 copy-done.5
  34.2 1.3 %mix_own.1.own_ref = bf16[1,128,4352]{2,1,0:T(8,128)(2,1)S(1)} custom-call(bf16[4352,128]{1,0:T(8,128)(2,1)S(1)} %bitcast.32, f32[136,34]{1,0:T(8,128)S(1)} %bitcast.35), custom_call_target="tpu_custom_call" | custom-call | flops 1100000000 | tf_op jit(solution)/shard_map/mix_own/pallas_call | solution.py:449
  35.5 0.0 collective-permute-done.5
  35.5 0.1 add_convert_fusion.1.late_ref
  35.6 3.7 %collective-permute-start.8 = (bf16[1040,128]{1,0:T(8,128)(2,1)S(1)}, bf16[1040,128]{1,0:T(8,128)(2,1)S(1)}, u32[]{:S(2)}, u32[]{:S(2)}) collective-permute-start(bf16[1040,128]{1,0:T(8,128)(2,1)S(1)} %add_convert_fusion.1.late_ref), channel_id=1, source_target_pairs={{0,8},{8,16},{16,24},{1,9},{9,17},{17,25},{2,10},{10,18},{18,26},{... | collective-permute-start | bytes 798728 | tf_op jit(solution)/shard_map/ppermute | solution.py:560
  39.3 0.0 collective-permute-done.6.near_ref
  39.3 0.0 collective-permute-done.7.relay_ref
  39.3 2.4 %mix_next.1.next_ref = bf16[2,128,4352]{2,1,0:T(8,128)(2,1)S(1)} custom-call(bf16[2224,128]{1,0:T(8,128)(2,1)S(1)} %collective-permute-done.6.near_ref, bf16[2224,128]{1,0:T(8,128)(2,1)S(1)} %collective-permute-done.7.relay_ref, f32[136,34]{1,0:T(8,128)S(1)} %bitcast.36), custom_call_target="tpu_custom_call" | custom-call | flops 3300000000 | tf_op jit(solution)/shard_map/mix_next/pallas_call | solution.py:449
  41.8 0.0 copy-start.6
  41.8 1.8 %unpack_env.1 = bf16[4352,128]{1,0:T(8,128)(2,1)} custom-call(bf16[1184,128]{1,0:T(8,128)(2,1)S(1)} %add_convert_fusion.early_ref, bf16[1040,128]{1,0:T(8,128)(2,1)S(1)} %add_convert_fusion.1.late_ref), custom_call_target="tpu_custom_call" | custom-call | flops 2200000000 | tf_op jit(solution)/shard_map/unpack_env/pallas_call | solution.py:449
  43.6 0.0 copy-done.6
  43.6 2.0 %head.1 = (f32[4,128,128]{2,1,0:T(8,128)S(1)}, f32[16,128]{1,0:T(8,128)S(1)}, bf16[2,4352,256]{2,1,0:T(8,128)(2,1)S(1)}) custom-call(s32[8]{0:T(128)S(1)} %copy-done.3, f32[4,128,128]{2,1,0:T(8,128)S(1)} %bitcast.33, bf16[1,128,4352]{2,1,0:T(8,128)(2,1)S(1)} %mix_own.1.own_ref, bf16[2,128,4352]{2,1,0:T(8,128)(2,1)S(1)} %mix_next.1.next_ref, ...), custom_call_target="tpu_custom_call" | custom-call | flops 2200000000 | tf_op jit(solution)/shard_map/head/pallas_call | solution.py:449
  45.6 0.0 collective-permute-done.4.packed_ref
  45.6 0.6 open.1
  46.2 0.0 collective-permute-done.8.packed_ref
  46.2 7.8 %lanczos.1 = (f32[4,4,128,128]{3,2,1,0:T(8,128)S(1)}, f32[16,128]{1,0:T(8,128)S(1)}) custom-call(s32[8]{0:T(128)S(1)} %copy-done.3, bf16[1040,128]{1,0:T(8,128)(2,1)S(1)} %collective-permute-done.8.packed_ref, bf16[4352,128]{1,0:T(8,128)(2,1)S(1)} %bitcast.25, bf16[128,2304]{1,0:T(8,128)(2,1)S(1)} %get-tuple-element.57.early_ref, ...), custom_call_target="tpu_custom_call" | custom-call | flops 13200000000 | tf_op jit(solution)/shard_map/lanczos/pallas_call | solution.py:449
  54.0 10.7 %all_to_all.5.stats_ref = f32[8,16,128]{2,1,0:T(8,128)S(1)} all-to-all(f32[8,16,128]{2,1,0:T(8,128)S(1)} %broadcast_in_dim.9), channel_id=1, replica_groups=mesh['seg'=4,'sec'=8] {'sec'}, dimensions={0} | all-to-all | bytes 131072 | tf_op jit(solution)/shard_map/all_to_all | solution.py:469
  64.6 1.7 %finish.1 = (f32[4,128,128]{2,1,0:T(8,128)}, f32[2,4]{1,0:T(2,128)}) custom-call(f32[8,16,128]{2,1,0:T(8,128)S(1)} %all_to_all.5.stats_ref, f32[4,128,128]{2,1,0:T(8,128)S(1)} %get-tuple-element.59.start_ref, f32[4,4,128,128]{3,2,1,0:T(8,128)S(1)} %get-tuple-element.62.basis_ref), custom_call_target="tpu_custom_call" | custom-call | flops 2200000000 | tf_op jit(solution)/shard_map/finish/pallas_call | solution.py:449
  (1 shorter events, 0.0 us)
Async XLA Ops:
  0.6 3.6 %collective-permute-start = (bf16[4352,128]{1,0:T(8,128)(2,1)}, bf16[4352,128]{1,0:T(8,128)(2,1)S(1)}, u32[]{:S(2)}, u32[]{:S(2)}) collective-permute-start(bf16[4352,128]{1,0:T(8,128)(2,1)} %bitcast.21), channel_id=1, source_target_pairs={{0,1},{1,0},{2,3},{3,2},{4,5},{5,4},{6,7},{7,6},{8,9},{9,8},{10,11... | collective-permute-start | bytes 3342344 | tf_op jit(solution)/shard_map/ppermute | solution.py:512
  1.1 3.1 %collective-permute-start.1 = (bf16[4,128,128]{2,1,0:T(8,128)(2,1)}, bf16[4,128,128]{2,1,0:T(8,128)(2,1)S(1)}, u32[]{:S(2)}, u32[]{:S(2)}) collective-permute-start(bf16[4,128,128]{2,1,0:T(8,128)(2,1)} %bitcast.26), channel_id=1, source_target_pairs={{0,1},{1,0},{2,3},{3,2},{4,5},{5,4},{6,7},{7,6},{8,9},{9,8},{10,11... | collective-permute-start | bytes 393224 | tf_op jit(solution)/shard_map/ppermute | solution.py:513
  1.2 1.2 %copy-start.4 = (bf16[1,1,34,128,128]{4,3,2,1,0:T(8,128)(2,1)S(1)}, bf16[1,1,34,128,128]{4,3,2,1,0:T(8,128)(2,1)}, u32[]{:S(2)}) copy-start(bf16[1,1,34,128,128]{4,3,2,1,0:T(8,128)(2,1)} %param.8) | copy-start | bytes 3342340
  2.5 1.8 %copy-start = (bf16[1,1,34,128,128]{4,3,2,1,0:T(8,128)(2,1)S(1)}, bf16[1,1,34,128,128]{4,3,2,1,0:T(8,128)(2,1)}, u32[]{:S(2)}) copy-start(bf16[1,1,34,128,128]{4,3,2,1,0:T(8,128)(2,1)} %param.7) | copy-start | bytes 3342340
  2.5 1.8 %copy-start.1 = (bf16[1,1,4,1,128,128]{5,4,3,2,1,0:T(8,128)(2,1)S(1)}, bf16[1,1,4,1,128,128]{5,4,3,2,1,0:T(8,128)(2,1)}, u32[]{:S(2)}) copy-start(bf16[1,1,4,1,128,128]{5,4,3,2,1,0:T(8,128)(2,1)} %param.9) | copy-start | bytes 393220
  2.5 1.8 %copy-start.2 = (f32[1,1,34,34,4]{3,4,2,1,0:T(4,128)S(1)}, f32[1,1,34,34,4]{3,4,2,1,0:T(4,128)}, u32[]{:S(2)}) copy-start(f32[1,1,34,34,4]{3,4,2,1,0:T(4,128)} %param.10) | copy-start | bytes 55492
  2.5 1.8 %copy-start.3 = (s32[8]{0:T(128)S(1)}, s32[8]{0:T(128)}, u32[]{:S(2)}) copy-start(s32[8]{0:T(128)} %dims_ref.7) | copy-start | bytes 100
  2.8 18.6 %collective-permute-start.2 = (bf16[2224,128]{1,0:T(8,128)(2,1)S(1)}, bf16[2224,128]{1,0:T(8,128)(2,1)S(1)}, u32[]{:S(2)}, u32[]{:S(2)}) collective-permute-start(bf16[2224,128]{1,0:T(8,128)(2,1)S(1)} %pack_right.1), channel_id=1, source_target_pairs={{2,0},{3,1},{4,2},{5,3},{6,4},{7,5},{10,8},{11,9},{12,10},{13,11},... | collective-permute-start | bytes 1708040 | tf_op jit(solution)/shard_map/ppermute | solution.py:517
  10.4 15.9 %collective-permute-start.3 = (bf16[1184,128]{1,0:T(8,128)(2,1)S(1)}, bf16[1184,128]{1,0:T(8,128)(2,1)S(1)}, u32[]{:S(2)}, u32[]{:S(2)}) collective-permute-start(bf16[1184,128]{1,0:T(8,128)(2,1)S(1)} %get-tuple-element.37), channel_id=1, source_target_pairs={{0,2},{1,3},{2,4},{3,5},{4,6},{5,7},{8,10},{9,11},{10,12},{11,13},... | collective-permute-start | bytes 909320 | tf_op jit(solution)/shard_map/ppermute | solution.py:534
  18.3 14.1 %copy-start.7 = (f32[1,34,34,4]{2,3,1,0:T(4,128)S(1)}, f32[1,34,34,4]{2,3,1,0:T(4,128)}, u32[]{:S(2)}) copy-start(f32[1,34,34,4]{2,3,1,0:T(4,128)} %param.11) | copy-start | bytes 55492
  21.4 14.1 %collective-permute-start.5 = (bf16[1040,128]{1,0:T(8,128)(2,1)S(1)}, bf16[1040,128]{1,0:T(8,128)(2,1)S(1)}, u32[]{:S(2)}, u32[]{:S(2)}) collective-permute-start(bf16[1040,128]{1,0:T(8,128)(2,1)S(1)} %get-tuple-element.38), channel_id=1, source_target_pairs={{0,2},{1,3},{2,4},{3,5},{4,6},{5,7},{8,10},{9,11},{10,12},{11,13},... | collective-permute-start | bytes 798728 | tf_op jit(solution)/shard_map/ppermute | solution.py:534
  26.4 19.2 %collective-permute-start.4 = (bf16[1184,128]{1,0:T(8,128)(2,1)S(1)}, bf16[1184,128]{1,0:T(8,128)(2,1)S(1)}, u32[]{:S(2)}, u32[]{:S(2)}) collective-permute-start(bf16[1184,128]{1,0:T(8,128)(2,1)S(1)} %add_convert_fusion.early_ref), channel_id=1, source_target_pairs={{0,8},{8,16},{16,24},{1,9},{9,17},{17,25},{2,10},{10,18},{18,26},{... | collective-permute-start | bytes 909320 | tf_op jit(solution)/shard_map/ppermute | solution.py:542
  29.9 9.4 %collective-permute-start.6 = (bf16[2224,128]{1,0:T(8,128)(2,1)S(1)}, bf16[2224,128]{1,0:T(8,128)(2,1)S(1)}, u32[]{:S(2)}, u32[]{:S(2)}) collective-permute-start(bf16[2224,128]{1,0:T(8,128)(2,1)S(1)} %pack_right.1), channel_id=1, source_target_pairs={{0,1},{1,0},{2,3},{3,2},{4,5},{5,4},{6,7},{7,6},{8,9},{9,8},{10,11... | collective-permute-start | bytes 1708040 | tf_op jit(solution)/shard_map/ppermute | solution.py:546
  30.0 9.3 %collective-permute-start.7 = (bf16[2224,128]{1,0:T(8,128)(2,1)S(1)}, bf16[2224,128]{1,0:T(8,128)(2,1)S(1)}, u32[]{:S(2)}, u32[]{:S(2)}) collective-permute-start(bf16[2224,128]{1,0:T(8,128)(2,1)S(1)} %collective-permute-done.2.far_ref), channel_id=1, source_target_pairs={{0,1},{2,3},{4,5},{6,7},{8,9},{10,11},{12,13},{14,15},{16,17},{18,... | collective-permute-start | bytes 1708040 | tf_op jit(solution)/shard_map/ppermute | solution.py:547
  32.4 1.8 %copy-start.5 = (bf16[1,1,34,128,128]{4,3,2,1,0:T(8,128)(2,1)S(1)}, bf16[1,1,34,128,128]{4,3,2,1,0:T(8,128)(2,1)}, u32[]{:S(2)}) copy-start(bf16[1,1,34,128,128]{4,3,2,1,0:T(8,128)(2,1)} %param.8) | copy-start | bytes 3342340
  35.6 10.6 %collective-permute-start.8 = (bf16[1040,128]{1,0:T(8,128)(2,1)S(1)}, bf16[1040,128]{1,0:T(8,128)(2,1)S(1)}, u32[]{:S(2)}, u32[]{:S(2)}) collective-permute-start(bf16[1040,128]{1,0:T(8,128)(2,1)S(1)} %add_convert_fusion.1.late_ref), channel_id=1, source_target_pairs={{0,8},{8,16},{16,24},{1,9},{9,17},{17,25},{2,10},{10,18},{18,26},{... | collective-permute-start | bytes 798728 | tf_op jit(solution)/shard_map/ppermute | solution.py:560
  41.8 1.9 %copy-start.6 = (f32[1,4,1,128,128]{4,3,2,1,0:T(8,128)S(1)}, f32[1,4,1,128,128]{4,3,2,1,0:T(8,128)}, u32[]{:S(2)}) copy-start(f32[1,4,1,128,128]{4,3,2,1,0:T(8,128)} %param.12) | copy-start | bytes 786436

commit v5 on v4

--- a/solution.py
+++ b/solution.py
@@ -236,11 +236,15 @@
     unpack_into(width, tile, read, write, diag)
 
 
+def copy_wide(width, tile, source_ref, wide_s):
+    for w in range(width):
+        at = w * (tile + 8)
+        wide_s[at : at + tile, :] = source_ref[w * tile : (w + 1) * tile, :].astype(F32)
+
+
 def mix_own_kernel(width, tile, source_ref, weight_ref, out_ref, square_s, weight_s, wide_s, sums_s):
-    pitch = tile + 8
     weight_s[0] = weight_rows(weight_ref, width, 0, square_s, False)
-    for w in range(width):
-        wide_s[w * pitch : w * pitch + tile, :] = source_ref[w * tile : (w + 1) * tile, :].astype(F32)
+    copy_wide(width, tile, source_ref, wide_s)
     mix_into(width, tile, [weight_s.at[0]], wide_s, sums_s, out_ref)
 
 
@@ -251,11 +255,14 @@
     for k in range(2):
         weight_s[k] = weight_rows(weight_ref, width, k + 1, square_s, False)
 
-    def read(at, size):
-        near = near_ref[at : at + size, :].astype(F32)
-        return jnp.where(even, near, relay_ref[at : at + size, :].astype(F32))
-
-    unpack_wide(width, tile, read, wide_s, diag)
+    @pl.when(even)
+    def _():
+        copy_wide(width, tile, near_ref, wide_s)
+
+    @pl.when(jnp.logical_not(even))
+    def _():
+        unpack_wide(width, tile, reader(relay_ref), wide_s, diag)
+
     mix_into(width, tile, [weight_s.at[k] for k in range(2)], wide_s, sums_s, out_ref)
 
 
@@ -496,6 +503,7 @@
 
     swap = pairs_of(sectors, lambda q: [q ^ 1])
     across = pairs_of(sectors, lambda q: [q + 1] if q % 2 == 0 else [])
+    down = pairs_of(sectors, lambda q: [q - 1] if q % 2 else [])
     up_two = pairs_of(sectors, lambda q: [q + 2])
     down_two = pairs_of(sectors, lambda q: [q - 2])
     onward = pairs_of(segments, lambda s: [s + 1])
@@ -511,6 +519,7 @@
 
     far_environ = lax.ppermute(environ, "sec", swap)
     far_site = lax.ppermute(site, "sec", swap)
+    right_near = lax.ppermute(right, "sec", down)
     right_packed = call(
         "pack_right", functools.partial(pack_kernel, width, tile), [], [right], packed, [diag], 6, 1
     )
@@ -531,19 +540,16 @@
         [sector_dims], [environ, site, far_environ, far_site, site_weights], packed_parts(BF16),
         fold_scratch, 20, 12,
     )
-    arrived = [lax.ppermute(part, "sec", up_two) for part in outgoing]
+    early_arrived = lax.ppermute(outgoing[0], "sec", up_two)
+    far_environ, outgoing = lax.optimization_barrier((far_environ, outgoing))
     kept = call(
         "fold_own", functools.partial(fold_kernel, width, tile, False),
         [sector_dims], [environ, site, far_environ, far_site, site_weights], packed_parts(F32),
         fold_scratch, 20, 0.1,
     )
-    kept, right_far = lax.optimization_barrier((kept, right_far))
-    early = (kept[0] + arrived[0].astype(F32)).astype(BF16)
-    early_bound = lax.ppermute(early, "seg", onward)
-    early, right_far, right, right_packed = lax.optimization_barrier(
-        (early, right_far, right, right_packed)
-    )
-    right_near = lax.ppermute(right_packed, "sec", swap)
+    kept, late_outgoing = lax.optimization_barrier((kept, outgoing[1]))
+    late_arrived = lax.ppermute(late_outgoing, "sec", up_two)
+    kept, right_far, right = lax.optimization_barrier((kept, right_far, right))
     right_relay = lax.ppermute(right_far, "sec", across)
     own_mixed = call(
         "mix_own", functools.partial(mix_own_kernel, width, tile), [], [right, bound_weights],
@@ -553,9 +559,12 @@
         "mix_after", functools.partial(mix_after_kernel, width, tile), [],
         [right_far, bound_weights], mixed(1), mix_scratch(1) + [diag], 12, 2,
     )
-    late_arrived, own_mixed, after_mixed = lax.optimization_barrier(
-        (arrived[1], own_mixed, after_mixed)
-    )
+    early_arrived, own_mixed, after_mixed = lax.optimization_barrier(
+        (early_arrived, own_mixed, after_mixed)
+    )
+    early = (kept[0] + early_arrived.astype(F32)).astype(BF16)
+    early_bound = lax.ppermute(early, "seg", onward)
+    early, late_arrived = lax.optimization_barrier((early, late_arrived))
     late = (kept[1] + late_arrived.astype(F32)).astype(BF16)
     late_bound = lax.ppermute(late, "seg", onward)
     late, right_near, right_relay = lax.optimization_barrier((late, right_near, right_relay))

time: 66.7 us -> 64.6 us (0.969)
  blocking collectives: 10.7 us -> 7.4 us
  waiting for transfers between devices: 3.13 us -> 4.2 us
  starting transfers between devices: 22 us -> 22.7 us
    all_to_all x1, blocking collectives: 10.7 us -> 7.4 us  [gathered(): lax.all_to_all(jnp.broadcast_to(value, (count,) + value.shape), axis, 0, 0)]
    ppermute x3, starting transfers between devices: 10.4 us -> 11.9 us  [the longest x1 5.47 us: on_device(): early_arrived = lax.ppermute(outgoing[0], 'sec', up_two)]
    ppermute x1, waiting for transfers between devices: 0.01 us -> 1.45 us  [on_device(): late_bound = lax.ppermute(late, 'seg', onward)]
  transfers between devices with their start and end apart: 9 -> 9, of which waited for: 1 -> 2; matrix products, arithmetic and copies ran while one was open for 0% -> 0% of each run, Pallas kernels for 28% -> 29%
where the time goes in v5:
time: 64.6 us; the launch traced here: 64.3 us
  Pallas kernels  27.7 us (43%)
  starting transfers between devices  22.7 us (35%)
  blocking collectives  7.4 us (11%)
  waiting for transfers between devices  4.2 us (7%)
  local copies, waits for them, and re-layouts  1.28 us (2%)
  between operations  0.9 us (1%)
    pallas_call x11, Pallas kernels, call(): pl.pallas_call(kernel, out_shape=outs, in_specs=[smem()] * len(scalars) +...  27.7 us
    all_to_all x1, blocking collectives, gathered(): lax.all_to_all(jnp.broadcast_to(value, (count,) + value.shape), axis, 0, 0)  7.4 us
    ppermute x1, starting transfers between devices, on_device(): early_arrived = lax.ppermute(outgoing[0], 'sec', up_two)  5.47 us
    ppermute x1, starting transfers between devices, on_device(): late_arrived = lax.ppermute(late_outgoing, 'sec', up_two)  5.04 us
    ppermute x1, starting transfers between devices, on_device(): early_bound = lax.ppermute(early, 'seg', onward)  3.5 us
    ppermute x1, starting transfers between devices, on_device(): late_bound = lax.ppermute(late, 'seg', onward)  3.48 us
    ppermute x1, waiting for transfers between devices, on_device(): right_far = lax.ppermute(right_packed, 'sec', down_two)  2.73 us
    ppermute x1, starting transfers between devices, on_device(): right_relay = lax.ppermute(right_far, 'sec', across)  1.92 us
  transfers between devices with their start and end apart: 9, of which 2 were waited for; matrix products, arithmetic and copies ran while one was open for 0% of the time, Pallas kernels for 29%

profile of v5, /device:TPU:0, one launch (start us, length us, event | category | flops | bytes accessed | tf_op | source)
XLA Modules:
  0.0 64.3 jit_solution(489627761418312983)
XLA Ops:
  0.6 0.5 collective-permute-start
  1.1 0.1 collective-permute-start.1
  1.2 0.0 copy-start
  1.2 0.0 copy-start.1
  1.2 0.0 copy-start.2
  1.2 0.0 copy-start.3
  1.2 1.4 %collective-permute-start.6 = (bf16[4352,128]{1,0:T(8,128)(2,1)}, bf16[4352,128]{1,0:T(8,128)(2,1)S(1)}, u32[]{:S(2)}, u32[]{:S(2)}) collective-permute-start(bf16[4352,128]{1,0:T(8,128)(2,1)} %bitcast.31), channel_id=1, source_target_pairs={{1,0},{3,2},{5,4},{7,6},{9,8},{11,10},{13,12},{15,14},{17,16},{19,... | collective-permute-start | bytes 3342344 | tf_op jit(solution)/shard_map/ppermute | solution.py:522
  2.7 0.0 copy-start.4
  2.7 1.2 %copy-done.4 = bf16[1,1,34,128,128]{4,3,2,1,0:T(8,128)(2,1)S(1)} copy-done((bf16[1,1,34,128,128]{4,3,2,1,0:T(8,128)(2,1)S(1)}, bf16[1,1,34,128,128]{4,3,2,1,0:T(8,128)(2,1)}, u32[]{:S(2)}) %copy-start.4) | copy-done | bytes 1114136
  3.9 0.3 pack_right.1
  4.2 1.3 %collective-permute-start.2 = (bf16[2224,128]{1,0:T(8,128)(2,1)S(1)}, bf16[2224,128]{1,0:T(8,128)(2,1)S(1)}, u32[]{:S(2)}, u32[]{:S(2)}) collective-permute-start(bf16[2224,128]{1,0:T(8,128)(2,1)S(1)} %pack_right.1), channel_id=1, source_target_pairs={{2,0},{3,1},{4,2},{5,3},{6,4},{7,5},{10,8},{11,9},{12,10},{13,11},... | collective-permute-start | bytes 1708040 | tf_op jit(solution)/shard_map/ppermute | solution.py:526
  5.5 0.0 collective-permute-done.1.far_site_ref
  5.5 0.0 collective-permute-done.far_environ_ref
  5.5 0.0 copy-done
  5.5 0.0 copy-done.1
  5.6 0.0 copy-done.2
  5.6 0.0 copy-done.3
  5.6 6.1 %fold_up.1 = (bf16[1184,128]{1,0:T(8,128)(2,1)S(1)}, bf16[1040,128]{1,0:T(8,128)(2,1)S(1)}) custom-call(s32[8]{0:T(128)S(1)} %copy-done.3, bf16[4352,128]{1,0:T(8,128)(2,1)S(1)} %bitcast.22, bf16[4,128,128]{2,1,0:T(8,128)(2,1)S(1)} %bitcast.27, bf16[4352,128]{1,0:T(8,128)(2,1)S(1)} %collective-permute-done.far_environ_ref, ...), custom_call_target="tpu_custom_call" | custom-call | flops 13200000000 | tf_op jit(solution)/shard_map/fold_up/pallas_call | solution.py:456
  11.7 5.5 %collective-permute-start.3 = (bf16[1184,128]{1,0:T(8,128)(2,1)S(1)}, bf16[1184,128]{1,0:T(8,128)(2,1)S(1)}, u32[]{:S(2)}, u32[]{:S(2)}) collective-permute-start(bf16[1184,128]{1,0:T(8,128)(2,1)S(1)} %get-tuple-element.38), channel_id=1, source_target_pairs={{0,2},{1,3},{2,4},{3,5},{4,6},{5,7},{8,10},{9,11},{10,12},{11,13},... | collective-permute-start | bytes 909320 | tf_op jit(solution)/shard_map/ppermute | solution.py:543
  17.2 0.0 copy-start.7
  17.2 2.4 %fold_own.1 = (f32[1184,128]{1,0:T(8,128)S(1)}, f32[1040,128]{1,0:T(8,128)S(1)}) custom-call(s32[8]{0:T(128)S(1)} %copy-done.3, bf16[4352,128]{1,0:T(8,128)(2,1)S(1)} %bitcast.23, bf16[4,128,128]{2,1,0:T(8,128)(2,1)S(1)} %bitcast.28, bf16[4352,128]{1,0:T(8,128)(2,1)S(1)} %collective-permute-done.far_environ_ref, ...), custom_call_target="tpu_custom_call" | custom-call | flops 110000000 | tf_op jit(solution)/shard_map/fold_own/pallas_call | solution.py:456
  19.6 2.7 %collective-permute-done.2.far_ref = bf16[2224,128]{1,0:T(8,128)(2,1)S(1)} collective-permute-done((bf16[2224,128]{1,0:T(8,128)(2,1)S(1)}, bf16[2224,128]{1,0:T(8,128)(2,1)S(1)}, u32[]{:S(2)}, u32[]{:S(2)}) %collective-permute-start.2) | collective-permute-done | bytes 569376 | tf_op jit(solution)/shard_map/ppermute | solution.py:526
  22.3 5.0 %collective-permute-start.5 = (bf16[1040,128]{1,0:T(8,128)(2,1)S(1)}, bf16[1040,128]{1,0:T(8,128)(2,1)S(1)}, u32[]{:S(2)}, u32[]{:S(2)}) collective-permute-start(bf16[1040,128]{1,0:T(8,128)(2,1)S(1)} %get-tuple-element.52), channel_id=1, source_target_pairs={{0,2},{1,3},{2,4},{3,5},{4,6},{5,7},{8,10},{9,11},{10,12},{11,13},... | collective-permute-start | bytes 798728 | tf_op jit(solution)/shard_map/ppermute | solution.py:551
  27.4 1.9 %collective-permute-start.7 = (bf16[2224,128]{1,0:T(8,128)(2,1)S(1)}, bf16[2224,128]{1,0:T(8,128)(2,1)S(1)}, u32[]{:S(2)}, u32[]{:S(2)}) collective-permute-start(bf16[2224,128]{1,0:T(8,128)(2,1)S(1)} %collective-permute-done.2.far_ref), channel_id=1, source_target_pairs={{0,1},{2,3},{4,5},{6,7},{8,9},{10,11},{12,13},{14,15},{16,17},{18,... | collective-permute-start | bytes 1708040 | tf_op jit(solution)/shard_map/ppermute | solution.py:553
  29.3 0.0 copy-done.7
  29.3 0.0 copy-start.5
  29.3 1.8 %mix_after.1.after_ref = bf16[1,128,4352]{2,1,0:T(8,128)(2,1)S(1)} custom-call(bf16[2224,128]{1,0:T(8,128)(2,1)S(1)} %collective-permute-done.2.far_ref, f32[136,34]{1,0:T(8,128)S(1)} %bitcast.35), custom_call_target="tpu_custom_call" | custom-call | flops 2200000000 | tf_op jit(solution)/shard_map/mix_after/pallas_call | solution.py:456
  31.1 0.0 copy-done.5
  31.1 1.3 %mix_own.1.own_ref = bf16[1,128,4352]{2,1,0:T(8,128)(2,1)S(1)} custom-call(bf16[4352,128]{1,0:T(8,128)(2,1)S(1)} %bitcast.33, f32[136,34]{1,0:T(8,128)S(1)} %bitcast.36), custom_call_target="tpu_custom_call" | custom-call | flops 1100000000 | tf_op jit(solution)/shard_map/mix_own/pallas_call | solution.py:456
  32.4 0.0 collective-permute-done.3
  32.4 0.1 add_convert_fusion.early_ref
  32.5 3.5 %collective-permute-start.4 = (bf16[1184,128]{1,0:T(8,128)(2,1)S(1)}, bf16[1184,128]{1,0:T(8,128)(2,1)S(1)}, u32[]{:S(2)}, u32[]{:S(2)}) collective-permute-start(bf16[1184,128]{1,0:T(8,128)(2,1)S(1)} %add_convert_fusion.early_ref), channel_id=1, source_target_pairs={{0,8},{8,16},{16,24},{1,9},{9,17},{17,25},{2,10},{10,18},{18,26},{... | collective-permute-start | bytes 909320 | tf_op jit(solution)/shard_map/ppermute | solution.py:566
  36.0 0.0 collective-permute-done.5
  36.0 0.1 add_convert_fusion.1.late_ref
  36.1 3.5 %collective-permute-start.8 = (bf16[1040,128]{1,0:T(8,128)(2,1)S(1)}, bf16[1040,128]{1,0:T(8,128)(2,1)S(1)}, u32[]{:S(2)}, u32[]{:S(2)}) collective-permute-start(bf16[1040,128]{1,0:T(8,128)(2,1)S(1)} %add_convert_fusion.1.late_ref), channel_id=1, source_target_pairs={{0,8},{8,16},{16,24},{1,9},{9,17},{17,25},{2,10},{10,18},{18,26},{... | collective-permute-start | bytes 798728 | tf_op jit(solution)/shard_map/ppermute | solution.py:569
  39.6 0.0 collective-permute-done.6.near_ref
  39.6 0.0 collective-permute-done.7.relay_ref
  39.6 2.1 %mix_next.1.next_ref = bf16[2,128,4352]{2,1,0:T(8,128)(2,1)S(1)} custom-call(bf16[4352,128]{1,0:T(8,128)(2,1)S(1)} %collective-permute-done.6.near_ref, bf16[2224,128]{1,0:T(8,128)(2,1)S(1)} %collective-permute-done.7.relay_ref, f32[136,34]{1,0:T(8,128)S(1)} %bitcast.37), custom_call_target="tpu_custom_call" | custom-call | flops 3300000000 | tf_op jit(solution)/shard_map/mix_next/pallas_call | solution.py:456
  41.8 0.0 copy-start.6
  41.8 1.8 %unpack_env.1 = bf16[4352,128]{1,0:T(8,128)(2,1)} custom-call(bf16[1184,128]{1,0:T(8,128)(2,1)S(1)} %add_convert_fusion.early_ref, bf16[1040,128]{1,0:T(8,128)(2,1)S(1)} %add_convert_fusion.1.late_ref), custom_call_target="tpu_custom_call" | custom-call | flops 2200000000 | tf_op jit(solution)/shard_map/unpack_env/pallas_call | solution.py:456
  43.6 0.0 copy-done.6
  43.6 2.0 %head.1 = (f32[4,128,128]{2,1,0:T(8,128)S(1)}, f32[16,128]{1,0:T(8,128)S(1)}, bf16[2,4352,256]{2,1,0:T(8,128)(2,1)S(1)}) custom-call(s32[8]{0:T(128)S(1)} %copy-done.3, f32[4,128,128]{2,1,0:T(8,128)S(1)} %bitcast.34, bf16[1,128,4352]{2,1,0:T(8,128)(2,1)S(1)} %mix_own.1.own_ref, bf16[2,128,4352]{2,1,0:T(8,128)(2,1)S(1)} %mix_next.1.next_ref, ...), custom_call_target="tpu_custom_call" | custom-call | flops 2200000000 | tf_op jit(solution)/shard_map/head/pallas_call | solution.py:456
  45.6 0.0 collective-permute-done.4.packed_ref
  45.6 0.6 open.1
  46.2 1.5 %collective-permute-done.8.packed_ref = bf16[1040,128]{1,0:T(8,128)(2,1)S(1)} collective-permute-done((bf16[1040,128]{1,0:T(8,128)(2,1)S(1)}, bf16[1040,128]{1,0:T(8,128)(2,1)S(1)}, u32[]{:S(2)}, u32[]{:S(2)}) %collective-permute-start.8) | collective-permute-done | bytes 266272 | tf_op jit(solution)/shard_map/ppermute | solution.py:569
  47.7 7.5 %lanczos.1 = (f32[4,4,128,128]{3,2,1,0:T(8,128)S(1)}, f32[16,128]{1,0:T(8,128)S(1)}) custom-call(s32[8]{0:T(128)S(1)} %copy-done.3, bf16[1040,128]{1,0:T(8,128)(2,1)S(1)} %collective-permute-done.8.packed_ref, bf16[4352,128]{1,0:T(8,128)(2,1)S(1)} %bitcast.25, bf16[128,2304]{1,0:T(8,128)(2,1)S(1)} %get-tuple-element.65.early_ref, ...), custom_call_target="tpu_custom_call" | custom-call | flops 13200000000 | tf_op jit(solution)/shard_map/lanczos/pallas_call | solution.py:456
  55.2 7.4 %all_to_all.5.stats_ref = f32[8,16,128]{2,1,0:T(8,128)S(1)} all-to-all(f32[8,16,128]{2,1,0:T(8,128)S(1)} %broadcast_in_dim.9), channel_id=1, replica_groups=mesh['seg'=4,'sec'=8] {'sec'}, dimensions={0} | all-to-all | bytes 131072 | tf_op jit(solution)/shard_map/all_to_all | solution.py:476
  62.6 1.7 %finish.1 = (f32[4,128,128]{2,1,0:T(8,128)}, f32[2,4]{1,0:T(2,128)}) custom-call(f32[8,16,128]{2,1,0:T(8,128)S(1)} %all_to_all.5.stats_ref, f32[4,128,128]{2,1,0:T(8,128)S(1)} %get-tuple-element.67.start_ref, f32[4,4,128,128]{3,2,1,0:T(8,128)S(1)} %get-tuple-element.70.basis_ref), custom_call_target="tpu_custom_call" | custom-call | flops 2200000000 | tf_op jit(solution)/shard_map/finish/pallas_call | solution.py:456
  (1 shorter events, 0.0 us)
Async XLA Ops:
  0.6 4.9 %collective-permute-start = (bf16[4352,128]{1,0:T(8,128)(2,1)}, bf16[4352,128]{1,0:T(8,128)(2,1)S(1)}, u32[]{:S(2)}, u32[]{:S(2)}) collective-permute-start(bf16[4352,128]{1,0:T(8,128)(2,1)} %bitcast.21), channel_id=1, source_target_pairs={{0,1},{1,0},{2,3},{3,2},{4,5},{5,4},{6,7},{7,6},{8,9},{9,8},{10,11... | collective-permute-start | bytes 3342344 | tf_op jit(solution)/shard_map/ppermute | solution.py:520
  1.1 4.4 %collective-permute-start.1 = (bf16[4,128,128]{2,1,0:T(8,128)(2,1)}, bf16[4,128,128]{2,1,0:T(8,128)(2,1)S(1)}, u32[]{:S(2)}, u32[]{:S(2)}) collective-permute-start(bf16[4,128,128]{2,1,0:T(8,128)(2,1)} %bitcast.26), channel_id=1, source_target_pairs={{0,1},{1,0},{2,3},{3,2},{4,5},{5,4},{6,7},{7,6},{8,9},{9,8},{10,11... | collective-permute-start | bytes 393224 | tf_op jit(solution)/shard_map/ppermute | solution.py:521
  1.2 4.3 %copy-start = (bf16[1,1,34,128,128]{4,3,2,1,0:T(8,128)(2,1)S(1)}, bf16[1,1,34,128,128]{4,3,2,1,0:T(8,128)(2,1)}, u32[]{:S(2)}) copy-start(bf16[1,1,34,128,128]{4,3,2,1,0:T(8,128)(2,1)} %param.7) | copy-start | bytes 3342340
  1.2 4.3 %copy-start.1 = (bf16[1,1,4,1,128,128]{5,4,3,2,1,0:T(8,128)(2,1)S(1)}, bf16[1,1,4,1,128,128]{5,4,3,2,1,0:T(8,128)(2,1)}, u32[]{:S(2)}) copy-start(bf16[1,1,4,1,128,128]{5,4,3,2,1,0:T(8,128)(2,1)} %param.9) | copy-start | bytes 393220
  1.2 4.3 %copy-start.2 = (f32[1,1,34,34,4]{3,4,2,1,0:T(4,128)S(1)}, f32[1,1,34,34,4]{3,4,2,1,0:T(4,128)}, u32[]{:S(2)}) copy-start(f32[1,1,34,34,4]{3,4,2,1,0:T(4,128)} %param.10) | copy-start | bytes 55492
  1.2 4.3 %copy-start.3 = (s32[8]{0:T(128)S(1)}, s32[8]{0:T(128)}, u32[]{:S(2)}) copy-start(s32[8]{0:T(128)} %dims_ref.7) | copy-start | bytes 100
  1.2 38.4 %collective-permute-start.6 = (bf16[4352,128]{1,0:T(8,128)(2,1)}, bf16[4352,128]{1,0:T(8,128)(2,1)S(1)}, u32[]{:S(2)}, u32[]{:S(2)}) collective-permute-start(bf16[4352,128]{1,0:T(8,128)(2,1)} %bitcast.31), channel_id=1, source_target_pairs={{1,0},{3,2},{5,4},{7,6},{9,8},{11,10},{13,12},{15,14},{17,16},{19,... | collective-permute-start | bytes 3342344 | tf_op jit(solution)/shard_map/ppermute | solution.py:522
  2.7 1.3 %copy-start.4 = (bf16[1,1,34,128,128]{4,3,2,1,0:T(8,128)(2,1)S(1)}, bf16[1,1,34,128,128]{4,3,2,1,0:T(8,128)(2,1)}, u32[]{:S(2)}) copy-start(bf16[1,1,34,128,128]{4,3,2,1,0:T(8,128)(2,1)} %param.8) | copy-start | bytes 3342340
  4.2 18.1 %collective-permute-start.2 = (bf16[2224,128]{1,0:T(8,128)(2,1)S(1)}, bf16[2224,128]{1,0:T(8,128)(2,1)S(1)}, u32[]{:S(2)}, u32[]{:S(2)}) collective-permute-start(bf16[2224,128]{1,0:T(8,128)(2,1)S(1)} %pack_right.1), channel_id=1, source_target_pairs={{2,0},{3,1},{4,2},{5,3},{6,4},{7,5},{10,8},{11,9},{12,10},{13,11},... | collective-permute-start | bytes 1708040 | tf_op jit(solution)/shard_map/ppermute | solution.py:526
  11.7 20.7 %collective-permute-start.3 = (bf16[1184,128]{1,0:T(8,128)(2,1)S(1)}, bf16[1184,128]{1,0:T(8,128)(2,1)S(1)}, u32[]{:S(2)}, u32[]{:S(2)}) collective-permute-start(bf16[1184,128]{1,0:T(8,128)(2,1)S(1)} %get-tuple-element.38), channel_id=1, source_target_pairs={{0,2},{1,3},{2,4},{3,5},{4,6},{5,7},{8,10},{9,11},{10,12},{11,13},... | collective-permute-start | bytes 909320 | tf_op jit(solution)/shard_map/ppermute | solution.py:543
  17.2 12.1 %copy-start.7 = (f32[1,34,34,4]{2,3,1,0:T(4,128)S(1)}, f32[1,34,34,4]{2,3,1,0:T(4,128)}, u32[]{:S(2)}) copy-start(f32[1,34,34,4]{2,3,1,0:T(4,128)} %param.11) | copy-start | bytes 55492
  22.3 13.7 %collective-permute-start.5 = (bf16[1040,128]{1,0:T(8,128)(2,1)S(1)}, bf16[1040,128]{1,0:T(8,128)(2,1)S(1)}, u32[]{:S(2)}, u32[]{:S(2)}) collective-permute-start(bf16[1040,128]{1,0:T(8,128)(2,1)S(1)} %get-tuple-element.52), channel_id=1, source_target_pairs={{0,2},{1,3},{2,4},{3,5},{4,6},{5,7},{8,10},{9,11},{10,12},{11,13},... | collective-permute-start | bytes 798728 | tf_op jit(solution)/shard_map/ppermute | solution.py:551
  27.4 12.2 %collective-permute-start.7 = (bf16[2224,128]{1,0:T(8,128)(2,1)S(1)}, bf16[2224,128]{1,0:T(8,128)(2,1)S(1)}, u32[]{:S(2)}, u32[]{:S(2)}) collective-permute-start(bf16[2224,128]{1,0:T(8,128)(2,1)S(1)} %collective-permute-done.2.far_ref), channel_id=1, source_target_pairs={{0,1},{2,3},{4,5},{6,7},{8,9},{10,11},{12,13},{14,15},{16,17},{18,... | collective-permute-start | bytes 1708040 | tf_op jit(solution)/shard_map/ppermute | solution.py:553
  29.3 1.8 %copy-start.5 = (bf16[1,1,34,128,128]{4,3,2,1,0:T(8,128)(2,1)S(1)}, bf16[1,1,34,128,128]{4,3,2,1,0:T(8,128)(2,1)}, u32[]{:S(2)}) copy-start(bf16[1,1,34,128,128]{4,3,2,1,0:T(8,128)(2,1)} %param.8) | copy-start | bytes 3342340
  32.5 13.1 %collective-permute-start.4 = (bf16[1184,128]{1,0:T(8,128)(2,1)S(1)}, bf16[1184,128]{1,0:T(8,128)(2,1)S(1)}, u32[]{:S(2)}, u32[]{:S(2)}) collective-permute-start(bf16[1184,128]{1,0:T(8,128)(2,1)S(1)} %add_convert_fusion.early_ref), channel_id=1, source_target_pairs={{0,8},{8,16},{16,24},{1,9},{9,17},{17,25},{2,10},{10,18},{18,26},{... | collective-permute-start | bytes 909320 | tf_op jit(solution)/shard_map/ppermute | solution.py:566
  36.1 11.5 %collective-permute-start.8 = (bf16[1040,128]{1,0:T(8,128)(2,1)S(1)}, bf16[1040,128]{1,0:T(8,128)(2,1)S(1)}, u32[]{:S(2)}, u32[]{:S(2)}) collective-permute-start(bf16[1040,128]{1,0:T(8,128)(2,1)S(1)} %add_convert_fusion.1.late_ref), channel_id=1, source_target_pairs={{0,8},{8,16},{16,24},{1,9},{9,17},{17,25},{2,10},{10,18},{18,26},{... | collective-permute-start | bytes 798728 | tf_op jit(solution)/shard_map/ppermute | solution.py:569
  41.8 1.9 %copy-start.6 = (f32[1,4,1,128,128]{4,3,2,1,0:T(8,128)S(1)}, f32[1,4,1,128,128]{4,3,2,1,0:T(8,128)}, u32[]{:S(2)}) copy-start(f32[1,4,1,128,128]{4,3,2,1,0:T(8,128)} %param.12) | copy-start | bytes 786436

commit v6 on v5

--- a/solution.py
+++ b/solution.py
@@ -87,13 +87,22 @@
     return jnp.concatenate([value, value], axis=0).astype(BF16)
 
 
-def pack_kernel(width, tile, source_ref, out_ref, diag):
+def pack_kernel(width, tile, source_ref, out_ref, held, diag, sems):
     half = tile // 2
+    copies = sems.shape[0]
+    edges = [width * k // copies for k in range(copies + 1)]
+    pending = []
+    for k in range(copies):
+        at = pl.ds(edges[k] * tile, (edges[k + 1] - edges[k]) * tile)
+        pending.append(pltpu.make_async_copy(source_ref.at[at, :], held.at[at, :], sems.at[k]))
+        pending[-1].start()
     diag[...] = jnp.zeros_like(diag)
-    for w in range(width):
-        folded, diagonal = pack_block(source_ref[w * tile : (w + 1) * tile, :].astype(F32))
-        out_ref[w * half : (w + 1) * half, :] = folded.astype(BF16)
-        diag[w : w + 1, :] = diagonal
+    for k in range(copies):
+        pending[k].wait()
+        for w in range(edges[k], edges[k + 1]):
+            folded, diagonal = pack_block(held[w * tile : (w + 1) * tile, :].astype(F32))
+            out_ref[w * half : (w + 1) * half, :] = folded.astype(BF16)
+            diag[w : w + 1, :] = diagonal
     out_ref[width * half :, :] = diag[...].astype(BF16)
 
 
@@ -451,12 +460,13 @@
     return pl.BlockSpec(memory_space=pltpu.VMEM)
 
 
-def call(name, kernel, scalars, arrays, outs, scratch, limit, micros):
+def call(name, kernel, scalars, arrays, outs, scratch, limit, micros, space=pltpu.VMEM):
     many = isinstance(outs, (tuple, list))
     return pl.pallas_call(
         kernel,
         out_shape=outs,
-        in_specs=[smem()] * len(scalars) + [vmem()] * len(arrays),
+        in_specs=[smem()] * len(scalars)
+        + [pl.BlockSpec(memory_space=space)] * len(arrays),
         out_specs=[vmem()] * len(outs) if many else vmem(),
         scratch_shapes=scratch,
         compiler_params=pltpu.CompilerParams(vmem_limit_bytes=limit * MIB),
@@ -517,13 +527,13 @@
             pltpu.VMEM((count, wide * (tile + 8), tile), F32),
         ]
 
+    right_packed = call(
+        "pack_right", functools.partial(pack_kernel, width, tile), [], [right], packed,
+        [pltpu.VMEM((width * tile, tile), BF16), diag, pltpu.SemaphoreType.DMA((4,))], 6, 1, pltpu.HBM,
+    )
+    right_far = lax.ppermute(right_packed, "sec", down_two)
     far_environ = lax.ppermute(environ, "sec", swap)
     far_site = lax.ppermute(site, "sec", swap)
-    right_near = lax.ppermute(right, "sec", down)
-    right_packed = call(
-        "pack_right", functools.partial(pack_kernel, width, tile), [], [right], packed, [diag], 6, 1
-    )
-    right_far = lax.ppermute(right_packed, "sec", down_two)
     fold_scratch = [
         pltpu.VMEM((tile, 3 * tile), BF16),
         pltpu.VMEM((3, tile, tile), BF16),
@@ -549,12 +559,14 @@
     )
     kept, late_outgoing = lax.optimization_barrier((kept, outgoing[1]))
     late_arrived = lax.ppermute(late_outgoing, "sec", up_two)
-    kept, right_far, right = lax.optimization_barrier((kept, right_far, right))
-    right_relay = lax.ppermute(right_far, "sec", across)
+    kept, right = lax.optimization_barrier((kept, right))
+    right_near = lax.ppermute(right, "sec", down)
     own_mixed = call(
         "mix_own", functools.partial(mix_own_kernel, width, tile), [], [right, bound_weights],
         mixed(1), mix_scratch(1), 12, 1,
     )
+    own_mixed, right_far = lax.optimization_barrier((own_mixed, right_far))
+    right_relay = lax.ppermute(right_far, "sec", across)
     after_mixed = call(
         "mix_after", functools.partial(mix_after_kernel, width, tile), [],
         [right_far, bound_weights], mixed(1), mix_scratch(1) + [diag], 12, 2,

time: 64.6 us -> 63.1 us (0.977)
  waiting for transfers between devices: 4.2 us -> 1.48 us
  starting transfers between devices: 22.7 us -> 23.6 us
    ppermute x1, waiting for transfers between devices: 2.73 us -> 0.01 us  [on_device(): right_far = lax.ppermute(right_packed, 'sec', down_two)]
    ppermute x1, starting transfers between devices: 1.92 us -> 3.13 us  [on_device(): right_relay = lax.ppermute(right_far, 'sec', across)]
  transfers between devices with their start and end apart: 9 -> 9, of which waited for: 2 -> 1; matrix products, arithmetic and copies ran while one was open for 0% -> 0% of each run, Pallas kernels for 29% -> 30%
where the time goes in v6:
time: 63.1 us; the launch traced here: 62.8 us
  Pallas kernels  28 us (44%)
  starting transfers between devices  23.6 us (37%)
  blocking collectives  7.4 us (12%)
  waiting for transfers between devices  1.48 us (2%)
  local copies, waits for them, and re-layouts  1.29 us (2%)
  between operations  0.91 us (1%)
    pallas_call x11, Pallas kernels, call(): pl.pallas_call(kernel, out_shape=outs, in_specs=[smem()] * len(scalars) +...  28 us
    all_to_all x1, blocking collectives, gathered(): lax.all_to_all(jnp.broadcast_to(value, (count,) + value.shape), axis, 0, 0)  7.4 us
    ppermute x1, starting transfers between devices, on_device(): early_arrived = lax.ppermute(outgoing[0], 'sec', up_two)  5.47 us
    ppermute x1, starting transfers between devices, on_device(): late_arrived = lax.ppermute(late_outgoing, 'sec', up_two)  4.82 us
    ppermute x1, starting transfers between devices, on_device(): early_bound = lax.ppermute(early, 'seg', onward)  3.51 us
    ppermute x1, starting transfers between devices, on_device(): late_bound = lax.ppermute(late, 'seg', onward)  3.48 us
    ppermute x1, starting transfers between devices, on_device(): right_relay = lax.ppermute(right_far, 'sec', across)  3.13 us
    ppermute x1, waiting for transfers between devices, on_device(): late_bound = lax.ppermute(late, 'seg', onward)  1.46 us
  transfers between devices with their start and end apart: 9, of which 1 were waited for; matrix products, arithmetic and copies ran while one was open for 0% of the time, Pallas kernels for 30%

profile of v6, /device:TPU:0, one launch (start us, length us, event | category | flops | bytes accessed | tf_op | source)
XLA Modules:
  0.0 62.8 jit_solution(11241082416996047333)
XLA Ops:
  0.6 0.5 collective-permute-start
  1.1 0.1 collective-permute-start.1
  1.2 0.0 copy-start.4
  1.2 1.2 %copy-done.4 = bf16[1,1,34,128,128]{4,3,2,1,0:T(8,128)(2,1)S(1)} copy-done((bf16[1,1,34,128,128]{4,3,2,1,0:T(8,128)(2,1)S(1)}, bf16[1,1,34,128,128]{4,3,2,1,0:T(8,128)(2,1)}, u32[]{:S(2)}) %copy-start.4) | copy-done | bytes 1114136
  2.5 0.0 copy-start
  2.5 0.0 copy-start.1
  2.5 0.0 copy-start.2
  2.5 0.0 copy-start.3
  2.5 0.6 %pack_right.1 = bf16[2224,128]{1,0:T(8,128)(2,1)S(1)} custom-call(bf16[4352,128]{1,0:T(8,128)(2,1)S(1)} %bitcast.31), custom_call_target="tpu_custom_call" | custom-call | flops 1100000000 | tf_op jit(solution)/shard_map/pack_right/pallas_call | solution.py:465
  3.1 1.3 %collective-permute-start.3 = (bf16[2224,128]{1,0:T(8,128)(2,1)S(1)}, bf16[2224,128]{1,0:T(8,128)(2,1)S(1)}, u32[]{:S(2)}, u32[]{:S(2)}) collective-permute-start(bf16[2224,128]{1,0:T(8,128)(2,1)S(1)} %pack_right.1), channel_id=1, source_target_pairs={{2,0},{3,1},{4,2},{5,3},{6,4},{7,5},{10,8},{11,9},{12,10},{13,11},... | collective-permute-start | bytes 1708040 | tf_op jit(solution)/shard_map/ppermute | solution.py:534
  4.4 0.0 collective-permute-done.1.far_site_ref
  4.4 0.0 collective-permute-done.far_environ_ref
  4.4 0.0 copy-done
  4.5 0.0 copy-done.1
  4.5 0.0 copy-done.2
  4.5 0.0 copy-done.3
  4.5 6.1 %fold_up.1 = (bf16[1184,128]{1,0:T(8,128)(2,1)S(1)}, bf16[1040,128]{1,0:T(8,128)(2,1)S(1)}) custom-call(s32[8]{0:T(128)S(1)} %copy-done.3, bf16[4352,128]{1,0:T(8,128)(2,1)S(1)} %bitcast.22, bf16[4,128,128]{2,1,0:T(8,128)(2,1)S(1)} %bitcast.27, bf16[4352,128]{1,0:T(8,128)(2,1)S(1)} %collective-permute-done.far_environ_ref, ...), custom_call_target="tpu_custom_call" | custom-call | flops 13200000000 | tf_op jit(solution)/shard_map/fold_up/pallas_call | solution.py:465
  10.6 5.5 %collective-permute-start.2 = (bf16[1184,128]{1,0:T(8,128)(2,1)S(1)}, bf16[1184,128]{1,0:T(8,128)(2,1)S(1)}, u32[]{:S(2)}, u32[]{:S(2)}) collective-permute-start(bf16[1184,128]{1,0:T(8,128)(2,1)S(1)} %get-tuple-element.39), channel_id=1, source_target_pairs={{0,2},{1,3},{2,4},{3,5},{4,6},{5,7},{8,10},{9,11},{10,12},{11,13},... | collective-permute-start | bytes 909320 | tf_op jit(solution)/shard_map/ppermute | solution.py:553
  16.1 0.0 copy-start.5
  16.1 0.0 copy-start.7
  16.1 2.4 %fold_own.1 = (f32[1184,128]{1,0:T(8,128)S(1)}, f32[1040,128]{1,0:T(8,128)S(1)}) custom-call(s32[8]{0:T(128)S(1)} %copy-done.3, bf16[4352,128]{1,0:T(8,128)(2,1)S(1)} %bitcast.23, bf16[4,128,128]{2,1,0:T(8,128)(2,1)S(1)} %bitcast.28, bf16[4352,128]{1,0:T(8,128)(2,1)S(1)} %collective-permute-done.far_environ_ref, ...), custom_call_target="tpu_custom_call" | custom-call | flops 110000000 | tf_op jit(solution)/shard_map/fold_own/pallas_call | solution.py:465
  18.5 4.8 %collective-permute-start.5 = (bf16[1040,128]{1,0:T(8,128)(2,1)S(1)}, bf16[1040,128]{1,0:T(8,128)(2,1)S(1)}, u32[]{:S(2)}, u32[]{:S(2)}) collective-permute-start(bf16[1040,128]{1,0:T(8,128)(2,1)S(1)} %get-tuple-element.54), channel_id=1, source_target_pairs={{0,2},{1,3},{2,4},{3,5},{4,6},{5,7},{8,10},{9,11},{10,12},{11,13},... | collective-permute-start | bytes 798728 | tf_op jit(solution)/shard_map/ppermute | solution.py:561
  23.4 0.0 copy-done.5
  23.4 1.3 %collective-permute-start.6 = (bf16[4352,128]{1,0:T(8,128)(2,1)S(1)}, bf16[4352,128]{1,0:T(8,128)(2,1)S(1)}, u32[]{:S(2)}, u32[]{:S(2)}) collective-permute-start(bf16[4352,128]{1,0:T(8,128)(2,1)S(1)} %bitcast.32), channel_id=1, source_target_pairs={{1,0},{3,2},{5,4},{7,6},{9,8},{11,10},{13,12},{15,14},{17,16},{19,... | collective-permute-start | bytes 3342344 | tf_op jit(solution)/shard_map/ppermute | solution.py:563
  24.7 0.0 copy-done.7
  24.7 1.3 %mix_own.1.own_ref = bf16[1,128,4352]{2,1,0:T(8,128)(2,1)S(1)} custom-call(bf16[4352,128]{1,0:T(8,128)(2,1)S(1)} %bitcast.33, f32[136,34]{1,0:T(8,128)S(1)} %bitcast.35), custom_call_target="tpu_custom_call" | custom-call | flops 1100000000 | tf_op jit(solution)/shard_map/mix_own/pallas_call | solution.py:465
  26.0 0.0 collective-permute-done.3.far_ref
  26.0 3.1 %collective-permute-start.7 = (bf16[2224,128]{1,0:T(8,128)(2,1)S(1)}, bf16[2224,128]{1,0:T(8,128)(2,1)S(1)}, u32[]{:S(2)}, u32[]{:S(2)}) collective-permute-start(bf16[2224,128]{1,0:T(8,128)(2,1)S(1)} %collective-permute-done.3.far_ref), channel_id=1, source_target_pairs={{0,1},{2,3},{4,5},{6,7},{8,9},{10,11},{12,13},{14,15},{16,17},{18,... | collective-permute-start | bytes 1708040 | tf_op jit(solution)/shard_map/ppermute | solution.py:569
  29.1 1.8 %mix_after.1.after_ref = bf16[1,128,4352]{2,1,0:T(8,128)(2,1)S(1)} custom-call(bf16[2224,128]{1,0:T(8,128)(2,1)S(1)} %collective-permute-done.3.far_ref, f32[136,34]{1,0:T(8,128)S(1)} %bitcast.36), custom_call_target="tpu_custom_call" | custom-call | flops 2200000000 | tf_op jit(solution)/shard_map/mix_after/pallas_call | solution.py:465
  30.9 0.0 collective-permute-done.2
  30.9 0.1 add_convert_fusion.early_ref
  31.0 3.5 %collective-permute-start.4 = (bf16[1184,128]{1,0:T(8,128)(2,1)S(1)}, bf16[1184,128]{1,0:T(8,128)(2,1)S(1)}, u32[]{:S(2)}, u32[]{:S(2)}) collective-permute-start(bf16[1184,128]{1,0:T(8,128)(2,1)S(1)} %add_convert_fusion.early_ref), channel_id=1, source_target_pairs={{0,8},{8,16},{16,24},{1,9},{9,17},{17,25},{2,10},{10,18},{18,26},{... | collective-permute-start | bytes 909320 | tf_op jit(solution)/shard_map/ppermute | solution.py:578
  34.5 0.0 collective-permute-done.5
  34.5 0.1 add_convert_fusion.1.late_ref
  34.6 3.5 %collective-permute-start.8 = (bf16[1040,128]{1,0:T(8,128)(2,1)S(1)}, bf16[1040,128]{1,0:T(8,128)(2,1)S(1)}, u32[]{:S(2)}, u32[]{:S(2)}) collective-permute-start(bf16[1040,128]{1,0:T(8,128)(2,1)S(1)} %add_convert_fusion.1.late_ref), channel_id=1, source_target_pairs={{0,8},{8,16},{16,24},{1,9},{9,17},{17,25},{2,10},{10,18},{18,26},{... | collective-permute-start | bytes 798728 | tf_op jit(solution)/shard_map/ppermute | solution.py:581
  38.1 0.0 collective-permute-done.7.relay_ref
  38.1 0.0 collective-permute-done.6.near_ref
  38.1 2.1 %mix_next.1.next_ref = bf16[2,128,4352]{2,1,0:T(8,128)(2,1)S(1)} custom-call(bf16[4352,128]{1,0:T(8,128)(2,1)S(1)} %collective-permute-done.6.near_ref, bf16[2224,128]{1,0:T(8,128)(2,1)S(1)} %collective-permute-done.7.relay_ref, f32[136,34]{1,0:T(8,128)S(1)} %bitcast.37), custom_call_target="tpu_custom_call" | custom-call | flops 3300000000 | tf_op jit(solution)/shard_map/mix_next/pallas_call | solution.py:465
  40.2 0.0 copy-start.6
  40.2 1.8 %unpack_env.1 = bf16[4352,128]{1,0:T(8,128)(2,1)} custom-call(bf16[1184,128]{1,0:T(8,128)(2,1)S(1)} %add_convert_fusion.early_ref, bf16[1040,128]{1,0:T(8,128)(2,1)S(1)} %add_convert_fusion.1.late_ref), custom_call_target="tpu_custom_call" | custom-call | flops 2200000000 | tf_op jit(solution)/shard_map/unpack_env/pallas_call | solution.py:465
  42.1 0.0 copy-done.6
  42.1 2.0 %head.1 = (f32[4,128,128]{2,1,0:T(8,128)S(1)}, f32[16,128]{1,0:T(8,128)S(1)}, bf16[2,4352,256]{2,1,0:T(8,128)(2,1)S(1)}) custom-call(s32[8]{0:T(128)S(1)} %copy-done.3, f32[4,128,128]{2,1,0:T(8,128)S(1)} %bitcast.34, bf16[1,128,4352]{2,1,0:T(8,128)(2,1)S(1)} %mix_own.1.own_ref, bf16[2,128,4352]{2,1,0:T(8,128)(2,1)S(1)} %mix_next.1.next_ref, ...), custom_call_target="tpu_custom_call" | custom-call | flops 2200000000 | tf_op jit(solution)/shard_map/head/pallas_call | solution.py:465
  44.1 0.0 collective-permute-done.4.packed_ref
  44.1 0.6 open.1
  44.7 1.5 %collective-permute-done.8.packed_ref = bf16[1040,128]{1,0:T(8,128)(2,1)S(1)} collective-permute-done((bf16[1040,128]{1,0:T(8,128)(2,1)S(1)}, bf16[1040,128]{1,0:T(8,128)(2,1)S(1)}, u32[]{:S(2)}, u32[]{:S(2)}) %collective-permute-start.8) | collective-permute-done | bytes 266272 | tf_op jit(solution)/shard_map/ppermute | solution.py:581
  46.1 7.5 %lanczos.1 = (f32[4,4,128,128]{3,2,1,0:T(8,128)S(1)}, f32[16,128]{1,0:T(8,128)S(1)}) custom-call(s32[8]{0:T(128)S(1)} %copy-done.3, bf16[1040,128]{1,0:T(8,128)(2,1)S(1)} %collective-permute-done.8.packed_ref, bf16[4352,128]{1,0:T(8,128)(2,1)S(1)} %bitcast.25, bf16[128,2304]{1,0:T(8,128)(2,1)S(1)} %get-tuple-element.67.early_ref, ...), custom_call_target="tpu_custom_call" | custom-call | flops 13200000000 | tf_op jit(solution)/shard_map/lanczos/pallas_call | solution.py:465
  53.7 7.4 %all_to_all.5.stats_ref = f32[8,16,128]{2,1,0:T(8,128)S(1)} all-to-all(f32[8,16,128]{2,1,0:T(8,128)S(1)} %broadcast_in_dim.9), channel_id=1, replica_groups=mesh['seg'=4,'sec'=8] {'sec'}, dimensions={0} | all-to-all | bytes 131072 | tf_op jit(solution)/shard_map/all_to_all | solution.py:486
  61.1 1.7 %finish.1 = (f32[4,128,128]{2,1,0:T(8,128)}, f32[2,4]{1,0:T(2,128)}) custom-call(f32[8,16,128]{2,1,0:T(8,128)S(1)} %all_to_all.5.stats_ref, f32[4,128,128]{2,1,0:T(8,128)S(1)} %get-tuple-element.69.start_ref, f32[4,4,128,128]{3,2,1,0:T(8,128)S(1)} %get-tuple-element.72.basis_ref), custom_call_target="tpu_custom_call" | custom-call | flops 2200000000 | tf_op jit(solution)/shard_map/finish/pallas_call | solution.py:465
  (1 shorter events, 0.0 us)
Async XLA Ops:
  0.6 3.8 %collective-permute-start = (bf16[4352,128]{1,0:T(8,128)(2,1)}, bf16[4352,128]{1,0:T(8,128)(2,1)S(1)}, u32[]{:S(2)}, u32[]{:S(2)}) collective-permute-start(bf16[4352,128]{1,0:T(8,128)(2,1)} %bitcast.21), channel_id=1, source_target_pairs={{0,1},{1,0},{2,3},{3,2},{4,5},{5,4},{6,7},{7,6},{8,9},{9,8},{10,11... | collective-permute-start | bytes 3342344 | tf_op jit(solution)/shard_map/ppermute | solution.py:535
  1.1 3.3 %collective-permute-start.1 = (bf16[4,128,128]{2,1,0:T(8,128)(2,1)}, bf16[4,128,128]{2,1,0:T(8,128)(2,1)S(1)}, u32[]{:S(2)}, u32[]{:S(2)}) collective-permute-start(bf16[4,128,128]{2,1,0:T(8,128)(2,1)} %bitcast.26), channel_id=1, source_target_pairs={{0,1},{1,0},{2,3},{3,2},{4,5},{5,4},{6,7},{7,6},{8,9},{9,8},{10,11... | collective-permute-start | bytes 393224 | tf_op jit(solution)/shard_map/ppermute | solution.py:536
  1.2 1.2 %copy-start.4 = (bf16[1,1,34,128,128]{4,3,2,1,0:T(8,128)(2,1)S(1)}, bf16[1,1,34,128,128]{4,3,2,1,0:T(8,128)(2,1)}, u32[]{:S(2)}) copy-start(bf16[1,1,34,128,128]{4,3,2,1,0:T(8,128)(2,1)} %param.8) | copy-start | bytes 3342340
  2.5 2.0 %copy-start = (bf16[1,1,34,128,128]{4,3,2,1,0:T(8,128)(2,1)S(1)}, bf16[1,1,34,128,128]{4,3,2,1,0:T(8,128)(2,1)}, u32[]{:S(2)}) copy-start(bf16[1,1,34,128,128]{4,3,2,1,0:T(8,128)(2,1)} %param.7) | copy-start | bytes 3342340
  2.5 2.0 %copy-start.1 = (bf16[1,1,4,1,128,128]{5,4,3,2,1,0:T(8,128)(2,1)S(1)}, bf16[1,1,4,1,128,128]{5,4,3,2,1,0:T(8,128)(2,1)}, u32[]{:S(2)}) copy-start(bf16[1,1,4,1,128,128]{5,4,3,2,1,0:T(8,128)(2,1)} %param.9) | copy-start | bytes 393220
  2.5 2.0 %copy-start.2 = (f32[1,1,34,34,4]{3,4,2,1,0:T(4,128)S(1)}, f32[1,1,34,34,4]{3,4,2,1,0:T(4,128)}, u32[]{:S(2)}) copy-start(f32[1,1,34,34,4]{3,4,2,1,0:T(4,128)} %param.10) | copy-start | bytes 55492
  2.5 2.0 %copy-start.3 = (s32[8]{0:T(128)S(1)}, s32[8]{0:T(128)}, u32[]{:S(2)}) copy-start(s32[8]{0:T(128)} %dims_ref.7) | copy-start | bytes 100
  3.1 22.9 %collective-permute-start.3 = (bf16[2224,128]{1,0:T(8,128)(2,1)S(1)}, bf16[2224,128]{1,0:T(8,128)(2,1)S(1)}, u32[]{:S(2)}, u32[]{:S(2)}) collective-permute-start(bf16[2224,128]{1,0:T(8,128)(2,1)S(1)} %pack_right.1), channel_id=1, source_target_pairs={{2,0},{3,1},{4,2},{5,3},{6,4},{7,5},{10,8},{11,9},{12,10},{13,11},... | collective-permute-start | bytes 1708040 | tf_op jit(solution)/shard_map/ppermute | solution.py:534
  10.6 20.3 %collective-permute-start.2 = (bf16[1184,128]{1,0:T(8,128)(2,1)S(1)}, bf16[1184,128]{1,0:T(8,128)(2,1)S(1)}, u32[]{:S(2)}, u32[]{:S(2)}) collective-permute-start(bf16[1184,128]{1,0:T(8,128)(2,1)S(1)} %get-tuple-element.39), channel_id=1, source_target_pairs={{0,2},{1,3},{2,4},{3,5},{4,6},{5,7},{8,10},{9,11},{10,12},{11,13},... | collective-permute-start | bytes 909320 | tf_op jit(solution)/shard_map/ppermute | solution.py:553
  16.1 7.3 %copy-start.5 = (bf16[1,1,34,128,128]{4,3,2,1,0:T(8,128)(2,1)S(1)}, bf16[1,1,34,128,128]{4,3,2,1,0:T(8,128)(2,1)}, u32[]{:S(2)}) copy-start(bf16[1,1,34,128,128]{4,3,2,1,0:T(8,128)(2,1)} %param.8) | copy-start | bytes 3342340
  16.1 8.6 %copy-start.7 = (f32[1,34,34,4]{2,3,1,0:T(4,128)S(1)}, f32[1,34,34,4]{2,3,1,0:T(4,128)}, u32[]{:S(2)}) copy-start(f32[1,34,34,4]{2,3,1,0:T(4,128)} %param.11) | copy-start | bytes 55492
  18.5 16.0 %collective-permute-start.5 = (bf16[1040,128]{1,0:T(8,128)(2,1)S(1)}, bf16[1040,128]{1,0:T(8,128)(2,1)S(1)}, u32[]{:S(2)}, u32[]{:S(2)}) collective-permute-start(bf16[1040,128]{1,0:T(8,128)(2,1)S(1)} %get-tuple-element.54), channel_id=1, source_target_pairs={{0,2},{1,3},{2,4},{3,5},{4,6},{5,7},{8,10},{9,11},{10,12},{11,13},... | collective-permute-start | bytes 798728 | tf_op jit(solution)/shard_map/ppermute | solution.py:561
  23.4 14.7 %collective-permute-start.6 = (bf16[4352,128]{1,0:T(8,128)(2,1)S(1)}, bf16[4352,128]{1,0:T(8,128)(2,1)S(1)}, u32[]{:S(2)}, u32[]{:S(2)}) collective-permute-start(bf16[4352,128]{1,0:T(8,128)(2,1)S(1)} %bitcast.32), channel_id=1, source_target_pairs={{1,0},{3,2},{5,4},{7,6},{9,8},{11,10},{13,12},{15,14},{17,16},{19,... | collective-permute-start | bytes 3342344 | tf_op jit(solution)/shard_map/ppermute | solution.py:563
  26.0 12.1 %collective-permute-start.7 = (bf16[2224,128]{1,0:T(8,128)(2,1)S(1)}, bf16[2224,128]{1,0:T(8,128)(2,1)S(1)}, u32[]{:S(2)}, u32[]{:S(2)}) collective-permute-start(bf16[2224,128]{1,0:T(8,128)(2,1)S(1)} %collective-permute-done.3.far_ref), channel_id=1, source_target_pairs={{0,1},{2,3},{4,5},{6,7},{8,9},{10,11},{12,13},{14,15},{16,17},{18,... | collective-permute-start | bytes 1708040 | tf_op jit(solution)/shard_map/ppermute | solution.py:569
  31.0 13.1 %collective-permute-start.4 = (bf16[1184,128]{1,0:T(8,128)(2,1)S(1)}, bf16[1184,128]{1,0:T(8,128)(2,1)S(1)}, u32[]{:S(2)}, u32[]{:S(2)}) collective-permute-start(bf16[1184,128]{1,0:T(8,128)(2,1)S(1)} %add_convert_fusion.early_ref), channel_id=1, source_target_pairs={{0,8},{8,16},{16,24},{1,9},{9,17},{17,25},{2,10},{10,18},{18,26},{... | collective-permute-start | bytes 909320 | tf_op jit(solution)/shard_map/ppermute | solution.py:578
  34.6 11.5 %collective-permute-start.8 = (bf16[1040,128]{1,0:T(8,128)(2,1)S(1)}, bf16[1040,128]{1,0:T(8,128)(2,1)S(1)}, u32[]{:S(2)}, u32[]{:S(2)}) collective-permute-start(bf16[1040,128]{1,0:T(8,128)(2,1)S(1)} %add_convert_fusion.1.late_ref), channel_id=1, source_target_pairs={{0,8},{8,16},{16,24},{1,9},{9,17},{17,25},{2,10},{10,18},{18,26},{... | collective-permute-start | bytes 798728 | tf_op jit(solution)/shard_map/ppermute | solution.py:581
  40.2 1.9 %copy-start.6 = (f32[1,4,1,128,128]{4,3,2,1,0:T(8,128)S(1)}, f32[1,4,1,128,128]{4,3,2,1,0:T(8,128)}, u32[]{:S(2)}) copy-start(f32[1,4,1,128,128]{4,3,2,1,0:T(8,128)} %param.12) | copy-start | bytes 786436

commit v7 on v5

--- a/solution.py
+++ b/solution.py
@@ -87,6 +87,41 @@
     return jnp.concatenate([value, value], axis=0).astype(BF16)
 
 
+def joined_weights(weight_ref, width, states, square, turned):
+    wide = padded(width)
+    tile = square.shape[0]
+    highs = lows = None
+    for n, p in enumerate(states):
+        square[...] = jnp.zeros_like(square)
+        square[:width, :width] = weight_ref[pl.ds(p, width, stride=len(CHARGES)), :]
+        value = square[...]
+        if turned:
+            value = jnp.transpose(value)
+        high = value.astype(BF16).astype(F32)
+        low = value - high
+        if n:
+            high, low = pltpu.roll(high, n * wide, 1), pltpu.roll(low, n * wide, 1)
+        highs = high if highs is None else highs + high
+        lows = low if lows is None else lows + low
+    used = len(states) * wide
+    assert used <= tile
+    if 2 * used <= tile:
+        joined = highs + pltpu.roll(lows, used, 1)
+    else:
+        joined = jnp.concatenate([highs, lows], axis=1)
+    return joined.astype(BF16)[: packed_height(width)]
+
+
+def joined_rows(values, tile):
+    used = sum(value.shape[0] for value in values)
+    if 2 * used <= tile:
+        gap = jnp.zeros((tile - 2 * used, values[0].shape[1]), F32)
+        return jnp.concatenate(list(values) * 2 + [gap], axis=0).astype(BF16)
+    gap = jnp.zeros((tile - used, values[0].shape[1]), F32)
+    value = jnp.concatenate(list(values) + [gap], axis=0).astype(BF16)
+    return jnp.concatenate([value, value], axis=0)
+
+
 def pack_kernel(width, tile, source_ref, out_ref, diag):
     half = tile // 2
     diag[...] = jnp.zeros_like(diag)
@@ -107,15 +142,6 @@
 
 def reader(ref):
     return lambda at, size: ref[at : at + size, :].astype(F32)
-
-
-def unpack_kernel(width, tile, early_ref, late_ref, out_ref, diag):
-    for (first, count), ref in zip(chunks_of(width), (early_ref, late_ref)):
-
-        def write(w, block, first=first):
-            out_ref[(first + w) * tile : (first + w + 1) * tile, :] = block.astype(BF16)
-
-        unpack_into(count, tile, reader(ref), write, diag)
 
 
 def fold_kernel(
@@ -144,24 +170,22 @@
         for n in range(parts):
             joined_s[:, n * tile : (n + 1) * tile] = sites[n].astype(BF16)
             turned_s[n] = jnp.transpose(sites[n]).astype(BF16)
-            weight_s[n] = weight_rows(weight_ref, width, states[n], square_s, True)
             packed_s[n, width * pitch :, :] = jnp.zeros(((wide - width) * pitch, tile), F32)
             diag_s[n] = jnp.zeros_like(diag_s[n])
+        weights = joined_weights(weight_ref, width, states, square_s, True)
+        weight_s[:, : weights.shape[1]] = weights
 
         for pair in range(width // 2):
             at = slice(pair * tile, (pair + 1) * tile)
-            for k in range(2):
-                here = slice((pair * 2 + k) * tile, (pair * 2 + k + 1) * tile)
-                blocks = [
-                    jnp.dot(environ_ref[here, :], joined_s[:, :tile], preferred_element_type=F32)
-                ]
-                if with_partner:
-                    both = jnp.dot(
-                        far_environ_ref[here, :], joined_s[:, tile:], preferred_element_type=F32
-                    )
-                    blocks += [both[:, :tile], both[:, tile:]]
-                for n in range(parts):
-                    half_s[n, at, k * tile : (k + 1) * tile] = blocks[n].astype(BF16)
+            here = slice(pair * 2 * tile, (pair + 1) * 2 * tile)
+            blocks = [jnp.dot(environ_ref[here, :], joined_s[:, :tile], preferred_element_type=F32)]
+            if with_partner:
+                both = jnp.dot(far_environ_ref[here, :], joined_s[:, tile:], preferred_element_type=F32)
+                blocks += [both[:, :tile], both[:, tile:]]
+            for n in range(parts):
+                block = blocks[n].astype(BF16)
+                for k in range(2):
+                    half_s[n, at, k * tile : (k + 1) * tile] = block[k * tile : (k + 1) * tile]
             for n in range(parts):
                 both = jnp.dot(turned_s[n], half_s[n, at, :], preferred_element_type=F32)
                 for k in range(2):
@@ -171,11 +195,8 @@
                     diag_s[n, w : w + 1, :] = diagonal
 
         def mixed(inputs):
-            value = None
-            for n in range(parts):
-                term = jnp.dot(weight_s[n], doubled(inputs[n]), preferred_element_type=F32)
-                value = term if value is None else value + term
-            return value[:wide]
+            value = joined_rows(inputs, tile)
+            return jnp.dot(weight_s[:, : value.shape[0]], value, preferred_element_type=F32)[:wide]
 
         for at in range(0, half, 2):
             value = mixed([
@@ -249,20 +270,11 @@
 
 
 def mix_next_kernel(
-    width, tile, near_ref, relay_ref, weight_ref, out_ref, square_s, weight_s, wide_s, sums_s, diag
+    width, tile, near_ref, weight_ref, out_ref, square_s, weight_s, wide_s, sums_s, diag
 ):
-    even = lax.rem(lax.axis_index("sec"), 2) == 0
     for k in range(2):
         weight_s[k] = weight_rows(weight_ref, width, k + 1, square_s, False)
-
-    @pl.when(even)
-    def _():
-        copy_wide(width, tile, near_ref, wide_s)
-
-    @pl.when(jnp.logical_not(even))
-    def _():
-        unpack_wide(width, tile, reader(relay_ref), wide_s, diag)
-
+    unpack_wide(width, tile, reader(near_ref), wide_s, diag)
     mix_into(width, tile, [weight_s.at[k] for k in range(2)], wide_s, sums_s, out_ref)
 
 
@@ -345,7 +357,8 @@
 
 def lanczos_kernel(
     width, tile, dims_ref, packed_ref, environ_ref, early_ref, image_ref, own_ref, next_ref, after_ref,
-    start_ref, norm_ref, product_ref, basis_ref, stats_ref, late_s, product_s, diag,
+    start_ref, norm_ref, product_ref, fresh_early_ref, fresh_late_ref, basis_ref, stats_ref, env_ref,
+    late_s, product_s, env_s, diag, sem,
 ):
     states = len(CHARGES)
     sector = lax.axis_index("sec")
@@ -357,7 +370,17 @@
     stats = norm_ref[...]
     split = first * tile
     betas = [None] * states
+    copy = pltpu.make_async_copy(env_s, env_ref, sem)
     for j in range(LANCZOS):
+        if j == 1:
+            for (begin, size), ref in zip(chunks_of(width), (fresh_early_ref, fresh_late_ref)):
+
+                def write(w, block, begin=begin):
+                    at = (begin + w) * tile
+                    env_s[at : at + tile, :] = block.astype(BF16)
+
+                unpack_into(size, tile, reader(ref), write, diag)
+            copy.start()
         source = product_ref if j == 0 else product_s
         for group in range(states // 2):
             members = (2 * group, 2 * group + 1)
@@ -386,6 +409,7 @@
                 stats = put(stats, 1 + 2 * j, sector * states + p, alpha)
                 stats = put(stats, 2 + 2 * j, sector * states + p, beta)
     stats_ref[...] = stats
+    copy.wait()
 
 
 def finish_kernel(entries, stats_ref, start_ref, basis_ref, vector_ref, table_ref):
@@ -451,13 +475,13 @@
     return pl.BlockSpec(memory_space=pltpu.VMEM)
 
 
-def call(name, kernel, scalars, arrays, outs, scratch, limit, micros):
+def call(name, kernel, scalars, arrays, outs, scratch, limit, micros, out_specs=None):
     many = isinstance(outs, (tuple, list))
     return pl.pallas_call(
         kernel,
         out_shape=outs,
         in_specs=[smem()] * len(scalars) + [vmem()] * len(arrays),
-        out_specs=[vmem()] * len(outs) if many else vmem(),
+        out_specs=out_specs or ([vmem()] * len(outs) if many else vmem()),
         scratch_shapes=scratch,
         compiler_params=pltpu.CompilerParams(vmem_limit_bytes=limit * MIB),
         name=name,
@@ -469,11 +493,6 @@
 
 def pairs_of(count, pick):
     return [(source, target) for source in range(count) for target in pick(source) if 0 <= target < count]
-
-
-def gathered(value, axis):
-    count = lax.axis_size(axis)
-    return lax.all_to_all(jnp.broadcast_to(value, (count,) + value.shape), axis, 0, 0)
 
 
 def on_device(left_env, right_env, site_tensors, mpo, boundary_mpo, guess, sector_dims):
@@ -502,8 +521,6 @@
     bound_weights = jnp.transpose(boundary_mpo[0], (0, 2, 1)).reshape(width * states, width)
 
     swap = pairs_of(sectors, lambda q: [q ^ 1])
-    across = pairs_of(sectors, lambda q: [q + 1] if q % 2 == 0 else [])
-    down = pairs_of(sectors, lambda q: [q - 1] if q % 2 else [])
     up_two = pairs_of(sectors, lambda q: [q + 2])
     down_two = pairs_of(sectors, lambda q: [q - 2])
     onward = pairs_of(segments, lambda s: [s + 1])
@@ -517,18 +534,18 @@
             pltpu.VMEM((count, wide * (tile + 8), tile), F32),
         ]
 
+    right_packed = call(
+        "pack_right", functools.partial(pack_kernel, width, tile), [], [right], packed,
+        [diag], 6, 1,
+    )
+    right_far = lax.ppermute(right_packed, "sec", down_two)
     far_environ = lax.ppermute(environ, "sec", swap)
     far_site = lax.ppermute(site, "sec", swap)
-    right_near = lax.ppermute(right, "sec", down)
-    right_packed = call(
-        "pack_right", functools.partial(pack_kernel, width, tile), [], [right], packed, [diag], 6, 1
-    )
-    right_far = lax.ppermute(right_packed, "sec", down_two)
     fold_scratch = [
         pltpu.VMEM((tile, 3 * tile), BF16),
         pltpu.VMEM((3, tile, tile), BF16),
         pltpu.VMEM((tile, tile), F32),
-        pltpu.VMEM((3, packed_height(width), 2 * wide), BF16),
+        pltpu.VMEM((packed_height(width), 2 * tile), BF16),
         pltpu.VMEM((3, width // 2 * tile, 2 * tile), BF16),
         pltpu.VMEM((3, wide * (half + 8), tile), F32),
         pltpu.VMEM((3, drows, tile), F32),
@@ -549,12 +566,14 @@
     )
     kept, late_outgoing = lax.optimization_barrier((kept, outgoing[1]))
     late_arrived = lax.ppermute(late_outgoing, "sec", up_two)
-    kept, right_far, right = lax.optimization_barrier((kept, right_far, right))
-    right_relay = lax.ppermute(right_far, "sec", across)
+    kept, right = lax.optimization_barrier((kept, right))
     own_mixed = call(
         "mix_own", functools.partial(mix_own_kernel, width, tile), [], [right, bound_weights],
         mixed(1), mix_scratch(1), 12, 1,
     )
+    own_mixed, right_far = lax.optimization_barrier((own_mixed, right_far))
+    even = lax.rem(lax.axis_index("sec"), 2) == 0
+    right_near = lax.ppermute(jnp.where(even, right_far, right_packed), "sec", swap)
     after_mixed = call(
         "mix_after", functools.partial(mix_after_kernel, width, tile), [],
         [right_far, bound_weights], mixed(1), mix_scratch(1) + [diag], 12, 2,
@@ -567,10 +586,10 @@
     early, late_arrived = lax.optimization_barrier((early, late_arrived))
     late = (kept[1] + late_arrived.astype(F32)).astype(BF16)
     late_bound = lax.ppermute(late, "seg", onward)
-    late, right_near, right_relay = lax.optimization_barrier((late, right_near, right_relay))
+    late, right_near = lax.optimization_barrier((late, right_near))
     next_mixed = call(
         "mix_next", functools.partial(mix_next_kernel, width, tile), [],
-        [right_near, right_relay, bound_weights], mixed(2), mix_scratch(2) + [diag], 16, 3,
+        [right_near, bound_weights], mixed(2), mix_scratch(2) + [diag], 16, 3,
     )
     start, norms, products = call(
         "head", functools.partial(head_kernel, width, tile),
@@ -582,11 +601,7 @@
         ),
         [], 14, 2,
     )
-    new_env = call(
-        "unpack_env", functools.partial(unpack_kernel, width, tile), [], [early, late],
-        jax.ShapeDtypeStruct((width * tile, tile), BF16), [diag], 6, 2,
-    )
-    early_bound, products, new_env = lax.optimization_barrier((early_bound, products, new_env))
+    early_bound, products = lax.optimization_barrier((early_bound, products))
     bound, image = call(
         "open", functools.partial(open_kernel, width, tile), [], [early_bound, environ, products],
         (
@@ -596,22 +611,26 @@
         [diag], 12, 1,
     )
     late_bound, bound = lax.optimization_barrier((late_bound, bound))
-    basis, stats = call(
+    basis, stats, new_env = call(
         "lanczos", functools.partial(lanczos_kernel, width, tile),
         [sector_dims],
-        [late_bound, environ, bound, image, own_mixed, next_mixed, after_mixed, start, norms, products],
+        [late_bound, environ, bound, image, own_mixed, next_mixed, after_mixed, start, norms, products,
+         early, late],
         (
             jax.ShapeDtypeStruct((LANCZOS, states, tile, tile), F32),
             jax.ShapeDtypeStruct((16, 128), F32),
+            jax.ShapeDtypeStruct((width * tile, tile), BF16),
         ),
         [
             pltpu.VMEM((tile, parts[1][1] * tile), BF16),
             pltpu.VMEM((states // 2, width * tile, 2 * tile), BF16),
+            pltpu.VMEM((width * tile, tile), BF16),
             diag,
+            pltpu.SemaphoreType.DMA,
         ],
-        22, 12,
-    )
-    stats = gathered(stats, "sec")
+        24, 12, [vmem(), vmem(), pl.BlockSpec(memory_space=pltpu.HBM)],
+    )
+    stats = lax.all_gather(stats, "sec")
     entries = float(states * sector_count * tile * tile)
     vector, table = call(
         "finish", functools.partial(finish_kernel, entries), [], [stats, start, basis],

time: 64.6 us -> 64 us (level)
  starting transfers between devices: 22.7 us -> 19.7 us
  blocking collectives: 7.4 us -> 8.33 us
  local copies, waits for them, and re-layouts: 1.28 us -> 2.15 us
    all_gather x0 -> x1, blocking collectives: none -> 8.33 us  [on_device(): stats = lax.all_gather(stats, 'sec')]
    all_to_all x1 -> x0, blocking collectives: 7.4 us -> none  [gathered(): lax.all_to_all(jnp.broadcast_to(value, (count,) + value.shape), axis, 0, 0)]
    ppermute x2 -> x1, starting transfers between devices: 3.35 us -> 0.07 us  [on_device(): lax.ppermute(jnp.where(even, right_far, right_packed), 'sec', swap)]
    ppermute x1, waiting for transfers between devices: 2.73 us -> 0.01 us  [on_device(): right_far = lax.ppermute(right_packed, 'sec', down_two)]
    ppermute x1, waiting for transfers between devices: 1.45 us -> 4.05 us  [on_device(): late_bound = lax.ppermute(late, 'seg', onward)]
    unnamed x16, local copies, waits for them, and re-layouts: 1.28 us -> 2.15 us
    pallas_call x11 -> x10, Pallas kernels: 27.7 us -> 28 us  [call(): pl.pallas_call(kernel, out_shape=outs, in_specs=[smem()] * len(scalars) +...]
  transfers between devices with their start and end apart: 9 -> 8, of which waited for: 2 -> 1; matrix products, arithmetic and copies ran while one was open for 0% -> 0% of each run, Pallas kernels for 29% -> 28%
where the time goes in v7:
time: 64 us; the launch traced here: 63.4 us
  Pallas kernels  28 us (44%)
  starting transfers between devices  19.7 us (31%)
  blocking collectives  8.33 us (13%)
  waiting for transfers between devices  4.07 us (6%)
  local copies, waits for them, and re-layouts  2.15 us (3%)
  between operations  0.91 us (1%)
    pallas_call x10, Pallas kernels, call(): pl.pallas_call(kernel, out_shape=outs, in_specs=[smem()] * len(scalars) +...  28 us
    all_gather x1, blocking collectives, on_device(): stats = lax.all_gather(stats, 'sec')  8.33 us
    ppermute x1, starting transfers between devices, on_device(): early_arrived = lax.ppermute(outgoing[0], 'sec', up_two)  5.47 us
    ppermute x1, starting transfers between devices, on_device(): late_arrived = lax.ppermute(late_outgoing, 'sec', up_two)  5 us
    ppermute x1, waiting for transfers between devices, on_device(): late_bound = lax.ppermute(late, 'seg', onward)  4.05 us
    ppermute x1, starting transfers between devices, on_device(): late_bound = lax.ppermute(late, 'seg', onward)  3.62 us
    ppermute x1, starting transfers between devices, on_device(): early_bound = lax.ppermute(early, 'seg', onward)  3.5 us
    unnamed x16, local copies, waits for them, and re-layouts  2.15 us
  transfers between devices with their start and end apart: 8, of which 1 were waited for; matrix products, arithmetic and copies ran while one was open for 0% of the time, Pallas kernels for 28%

profile of v7, /device:TPU:0, one launch (start us, length us, event | category | flops | bytes accessed | tf_op | source)
XLA Modules:
  0.0 63.4 jit_solution(15576791616350789005)
XLA Ops:
  0.6 0.5 collective-permute-start
  1.1 0.1 collective-permute-start.1
  1.2 0.0 copy-start.4
  1.2 1.2 %copy-done.4 = bf16[1,1,34,128,128]{4,3,2,1,0:T(8,128)(2,1)S(1)} copy-done((bf16[1,1,34,128,128]{4,3,2,1,0:T(8,128)(2,1)S(1)}, bf16[1,1,34,128,128]{4,3,2,1,0:T(8,128)(2,1)}, u32[]{:S(2)}) %copy-start.4) | copy-done | bytes 1114136
  2.5 0.0 copy-start
  2.5 0.0 copy-start.1
  2.5 0.0 copy-start.3
  2.5 0.3 pack_right.1
  2.8 1.4 %collective-permute-start.3 = (bf16[2224,128]{1,0:T(8,128)(2,1)S(1)}, bf16[2224,128]{1,0:T(8,128)(2,1)S(1)}, u32[]{:S(2)}, u32[]{:S(2)}) collective-permute-start(bf16[2224,128]{1,0:T(8,128)(2,1)S(1)} %pack_right.1), channel_id=1, source_target_pairs={{2,0},{3,1},{4,2},{5,3},{6,4},{7,5},{10,8},{11,9},{12,10},{13,11},... | collective-permute-start | bytes 1708040 | tf_op jit(solution)/shard_map/ppermute | solution.py:541
  4.2 0.0 collective-permute-done.1.far_site_ref
  4.2 0.0 collective-permute-done.far_environ_ref
  4.2 0.0 copy-done
  4.2 0.0 copy-done.1
  4.3 0.0 copy-done.3
  4.3 0.0 copy-start.2
  4.3 0.9 %copy-done.2 = f32[1,1,34,34,4]{3,4,2,1,0:T(4,128)S(1)} copy-done((f32[1,1,34,34,4]{3,4,2,1,0:T(4,128)S(1)}, f32[1,1,34,34,4]{3,4,2,1,0:T(4,128)}, u32[]{:S(2)}) %copy-start.2) | copy-done | bytes 18520
  5.2 6.5 %fold_up.1 = (bf16[1184,128]{1,0:T(8,128)(2,1)S(1)}, bf16[1040,128]{1,0:T(8,128)(2,1)S(1)}) custom-call(s32[8]{0:T(128)S(1)} %copy-done.3, bf16[4352,128]{1,0:T(8,128)(2,1)S(1)} %bitcast.23, bf16[4,128,128]{2,1,0:T(8,128)(2,1)S(1)} %bitcast.28, bf16[4352,128]{1,0:T(8,128)(2,1)S(1)} %collective-permute-done.far_environ_ref, ...), custom_call_target="tpu_custom_call" | custom-call | flops 13200000000 | tf_op jit(solution)/shard_map/fold_up/pallas_call | solution.py:480
  11.7 5.5 %collective-permute-start.2 = (bf16[1184,128]{1,0:T(8,128)(2,1)S(1)}, bf16[1184,128]{1,0:T(8,128)(2,1)S(1)}, u32[]{:S(2)}, u32[]{:S(2)}) collective-permute-start(bf16[1184,128]{1,0:T(8,128)(2,1)S(1)} %get-tuple-element.38), channel_id=1, source_target_pairs={{0,2},{1,3},{2,4},{3,5},{4,6},{5,7},{8,10},{9,11},{10,12},{11,13},... | collective-permute-start | bytes 909320 | tf_op jit(solution)/shard_map/ppermute | solution.py:560
  17.2 0.0 copy-start.5
  17.2 0.0 copy-start.7
  17.2 2.7 %fold_own.1 = (f32[1184,128]{1,0:T(8,128)S(1)}, f32[1040,128]{1,0:T(8,128)S(1)}) custom-call(s32[8]{0:T(128)S(1)} %copy-done.3, bf16[4352,128]{1,0:T(8,128)(2,1)S(1)} %bitcast.24, bf16[4,128,128]{2,1,0:T(8,128)(2,1)S(1)} %bitcast.29, bf16[4352,128]{1,0:T(8,128)(2,1)S(1)} %collective-permute-done.far_environ_ref, ...), custom_call_target="tpu_custom_call" | custom-call | flops 110000000 | tf_op jit(solution)/shard_map/fold_own/pallas_call | solution.py:480
  19.9 5.0 %collective-permute-start.4 = (bf16[1040,128]{1,0:T(8,128)(2,1)S(1)}, bf16[1040,128]{1,0:T(8,128)(2,1)S(1)}, u32[]{:S(2)}, u32[]{:S(2)}) collective-permute-start(bf16[1040,128]{1,0:T(8,128)(2,1)S(1)} %get-tuple-element.52), channel_id=1, source_target_pairs={{0,2},{1,3},{2,4},{3,5},{4,6},{5,7},{8,10},{9,11},{10,12},{11,13},... | collective-permute-start | bytes 798728 | tf_op jit(solution)/shard_map/ppermute | solution.py:568
  24.9 0.0 copy-done.5
  24.9 0.0 copy-done.7
  24.9 1.3 %mix_own.1.own_ref = bf16[1,128,4352]{2,1,0:T(8,128)(2,1)S(1)} custom-call(bf16[4352,128]{1,0:T(8,128)(2,1)S(1)} %bitcast.34, f32[136,34]{1,0:T(8,128)S(1)} %bitcast.36), custom_call_target="tpu_custom_call" | custom-call | flops 1100000000 | tf_op jit(solution)/shard_map/mix_own/pallas_call | solution.py:480
  26.2 0.0 collective-permute-done.3.far_ref
  26.2 0.1 broadcast_select_fusion
  26.3 0.1 collective-permute-start.7
  26.4 1.8 %mix_after.1.after_ref = bf16[1,128,4352]{2,1,0:T(8,128)(2,1)S(1)} custom-call(bf16[2224,128]{1,0:T(8,128)(2,1)S(1)} %collective-permute-done.3.far_ref, f32[136,34]{1,0:T(8,128)S(1)} %bitcast.37), custom_call_target="tpu_custom_call" | custom-call | flops 2200000000 | tf_op jit(solution)/shard_map/mix_after/pallas_call | solution.py:480
  28.2 0.0 collective-permute-done.2
  28.2 0.1 add_convert_fusion.fresh_early_ref
  28.2 3.5 %collective-permute-start.6 = (bf16[1184,128]{1,0:T(8,128)(2,1)S(1)}, bf16[1184,128]{1,0:T(8,128)(2,1)S(1)}, u32[]{:S(2)}, u32[]{:S(2)}) collective-permute-start(bf16[1184,128]{1,0:T(8,128)(2,1)S(1)} %add_convert_fusion.fresh_early_ref), channel_id=1, source_target_pairs={{0,8},{8,16},{16,24},{1,9},{9,17},{17,25},{2,10},{10,18},{18,26},{... | collective-permute-start | bytes 909320 | tf_op jit(solution)/shard_map/ppermute | solution.py:585
  31.8 0.0 collective-permute-done.4
  31.8 0.1 add_convert_fusion.1.fresh_late_ref
  31.8 0.0 copy-start.6
  31.8 3.6 %collective-permute-start.5 = (bf16[1040,128]{1,0:T(8,128)(2,1)S(1)}, bf16[1040,128]{1,0:T(8,128)(2,1)S(1)}, u32[]{:S(2)}, u32[]{:S(2)}) collective-permute-start(bf16[1040,128]{1,0:T(8,128)(2,1)S(1)} %add_convert_fusion.1.fresh_late_ref), channel_id=1, source_target_pairs={{0,8},{8,16},{16,24},{1,9},{9,17},{17,25},{2,10},{10,18},{18,26},{... | collective-permute-start | bytes 798728 | tf_op jit(solution)/shard_map/ppermute | solution.py:588
  35.5 0.0 collective-permute-done.7.near_ref
  35.5 2.4 %mix_next.1.next_ref = bf16[2,128,4352]{2,1,0:T(8,128)(2,1)S(1)} custom-call(bf16[2224,128]{1,0:T(8,128)(2,1)S(1)} %collective-permute-done.7.near_ref, f32[136,34]{1,0:T(8,128)S(1)} %bitcast.38), custom_call_target="tpu_custom_call" | custom-call | flops 3300000000 | tf_op jit(solution)/shard_map/mix_next/pallas_call | solution.py:480
  37.9 0.0 copy-done.6
  37.9 2.0 %head.1 = (f32[4,128,128]{2,1,0:T(8,128)S(1)}, f32[16,128]{1,0:T(8,128)S(1)}, bf16[2,4352,256]{2,1,0:T(8,128)(2,1)S(1)}) custom-call(s32[8]{0:T(128)S(1)} %copy-done.3, f32[4,128,128]{2,1,0:T(8,128)S(1)} %bitcast.35, bf16[1,128,4352]{2,1,0:T(8,128)(2,1)S(1)} %mix_own.1.own_ref, bf16[2,128,4352]{2,1,0:T(8,128)(2,1)S(1)} %mix_next.1.next_ref, ...), custom_call_target="tpu_custom_call" | custom-call | flops 2200000000 | tf_op jit(solution)/shard_map/head/pallas_call | solution.py:480
  39.9 0.0 collective-permute-done.6.packed_ref
  39.9 0.6 open.1
  40.5 4.1 %collective-permute-done.5.packed_ref = bf16[1040,128]{1,0:T(8,128)(2,1)S(1)} collective-permute-done((bf16[1040,128]{1,0:T(8,128)(2,1)S(1)}, bf16[1040,128]{1,0:T(8,128)(2,1)S(1)}, u32[]{:S(2)}, u32[]{:S(2)}) %collective-permute-start.5) | collective-permute-done | bytes 266272 | tf_op jit(solution)/shard_map/ppermute | solution.py:588
  44.5 8.8 %lanczos.1 = (f32[4,4,128,128]{3,2,1,0:T(8,128)S(1)}, f32[16,128]{1,0:T(8,128)S(1)}, bf16[4352,128]{1,0:T(8,128)(2,1)}) custom-call(s32[8]{0:T(128)S(1)} %copy-done.3, bf16[1040,128]{1,0:T(8,128)(2,1)S(1)} %collective-permute-done.5.packed_ref, bf16[4352,128]{1,0:T(8,128)(2,1)S(1)} %bitcast.26, bf16[128,2304]{1,0:T(8,128)(2,1)S(1)} %get-tuple-element.62.early_ref, ...), custom_call_target="tpu_custom_call" | custom-call | flops 13200000000 | tf_op jit(solution)/shard_map/lanczos/pallas_call | solution.py:480
  53.3 8.3 %all-gather = f32[128,128]{1,0:T(8,128)S(1)} all-gather(f32[16,128]{1,0:T(8,128)S(1)} %get-tuple-element.69), channel_id=2, replica_groups=mesh['seg'=4,'sec'=8] {'sec'}, dimensions={0}, use_global_device_ids=true | all-gather | bytes 73728 | tf_op jit(solution)/shard_map/all_gather | solution.py:633
  61.6 1.7 %finish.1 = (f32[4,128,128]{2,1,0:T(8,128)}, f32[2,4]{1,0:T(2,128)}) custom-call(f32[8,16,128]{2,1,0:T(8,128)S(1)} %bitcast.32, f32[4,128,128]{2,1,0:T(8,128)S(1)} %get-tuple-element.64.start_ref, f32[4,4,128,128]{3,2,1,0:T(8,128)S(1)} %get-tuple-element.70.basis_ref), custom_call_target="tpu_custom_call" | custom-call | flops 2200000000 | tf_op jit(solution)/shard_map/finish/pallas_call | solution.py:480
Async XLA Ops:
  0.6 3.6 %collective-permute-start = (bf16[4352,128]{1,0:T(8,128)(2,1)}, bf16[4352,128]{1,0:T(8,128)(2,1)S(1)}, u32[]{:S(2)}, u32[]{:S(2)}) collective-permute-start(bf16[4352,128]{1,0:T(8,128)(2,1)} %bitcast.22), channel_id=1, source_target_pairs={{0,1},{1,0},{2,3},{3,2},{4,5},{5,4},{6,7},{7,6},{8,9},{9,8},{10,11... | collective-permute-start | bytes 3342344 | tf_op jit(solution)/shard_map/ppermute | solution.py:542
  1.1 3.1 %collective-permute-start.1 = (bf16[4,128,128]{2,1,0:T(8,128)(2,1)}, bf16[4,128,128]{2,1,0:T(8,128)(2,1)}, u32[]{:S(2)}, u32[]{:S(2)}) collective-permute-start(bf16[4,128,128]{2,1,0:T(8,128)(2,1)} %bitcast.27), channel_id=1, source_target_pairs={{0,1},{1,0},{2,3},{3,2},{4,5},{5,4},{6,7},{7,6},{8,9},{9,8},{10,11... | collective-permute-start | bytes 393224 | tf_op jit(solution)/shard_map/ppermute | solution.py:543
  1.2 1.2 %copy-start.4 = (bf16[1,1,34,128,128]{4,3,2,1,0:T(8,128)(2,1)S(1)}, bf16[1,1,34,128,128]{4,3,2,1,0:T(8,128)(2,1)}, u32[]{:S(2)}) copy-start(bf16[1,1,34,128,128]{4,3,2,1,0:T(8,128)(2,1)} %param.8) | copy-start | bytes 3342340
  2.5 1.8 %copy-start = (bf16[1,1,34,128,128]{4,3,2,1,0:T(8,128)(2,1)S(1)}, bf16[1,1,34,128,128]{4,3,2,1,0:T(8,128)(2,1)}, u32[]{:S(2)}) copy-start(bf16[1,1,34,128,128]{4,3,2,1,0:T(8,128)(2,1)} %param.7) | copy-start | bytes 3342340
  2.5 1.8 %copy-start.1 = (bf16[1,1,4,1,128,128]{5,4,3,2,1,0:T(8,128)(2,1)S(1)}, bf16[1,1,4,1,128,128]{5,4,3,2,1,0:T(8,128)(2,1)}, u32[]{:S(2)}) copy-start(bf16[1,1,4,1,128,128]{5,4,3,2,1,0:T(8,128)(2,1)} %param.9) | copy-start | bytes 393220
  2.5 1.8 %copy-start.3 = (s32[8]{0:T(128)S(1)}, s32[8]{0:T(128)}, u32[]{:S(2)}) copy-start(s32[8]{0:T(128)} %dims_ref.7) | copy-start | bytes 100
  2.8 23.4 %collective-permute-start.3 = (bf16[2224,128]{1,0:T(8,128)(2,1)S(1)}, bf16[2224,128]{1,0:T(8,128)(2,1)S(1)}, u32[]{:S(2)}, u32[]{:S(2)}) collective-permute-start(bf16[2224,128]{1,0:T(8,128)(2,1)S(1)} %pack_right.1), channel_id=1, source_target_pairs={{2,0},{3,1},{4,2},{5,3},{6,4},{7,5},{10,8},{11,9},{12,10},{13,11},... | collective-permute-start | bytes 1708040 | tf_op jit(solution)/shard_map/ppermute | solution.py:541
  4.3 0.9 %copy-start.2 = (f32[1,1,34,34,4]{3,4,2,1,0:T(4,128)S(1)}, f32[1,1,34,34,4]{3,4,2,1,0:T(4,128)}, u32[]{:S(2)}) copy-start(f32[1,1,34,34,4]{3,4,2,1,0:T(4,128)} %param.10) | copy-start | bytes 55492
  11.7 16.5 %collective-permute-start.2 = (bf16[1184,128]{1,0:T(8,128)(2,1)S(1)}, bf16[1184,128]{1,0:T(8,128)(2,1)S(1)}, u32[]{:S(2)}, u32[]{:S(2)}) collective-permute-start(bf16[1184,128]{1,0:T(8,128)(2,1)S(1)} %get-tuple-element.38), channel_id=1, source_target_pairs={{0,2},{1,3},{2,4},{3,5},{4,6},{5,7},{8,10},{9,11},{10,12},{11,13},... | collective-permute-start | bytes 909320 | tf_op jit(solution)/shard_map/ppermute | solution.py:560
  17.2 7.7 %copy-start.5 = (bf16[1,1,34,128,128]{4,3,2,1,0:T(8,128)(2,1)S(1)}, bf16[1,1,34,128,128]{4,3,2,1,0:T(8,128)(2,1)}, u32[]{:S(2)}) copy-start(bf16[1,1,34,128,128]{4,3,2,1,0:T(8,128)(2,1)} %param.8) | copy-start | bytes 3342340
  17.2 7.7 %copy-start.7 = (f32[1,34,34,4]{2,3,1,0:T(4,128)S(1)}, f32[1,34,34,4]{2,3,1,0:T(4,128)}, u32[]{:S(2)}) copy-start(f32[1,34,34,4]{2,3,1,0:T(4,128)} %param.11) | copy-start | bytes 55492
  19.9 11.9 %collective-permute-start.4 = (bf16[1040,128]{1,0:T(8,128)(2,1)S(1)}, bf16[1040,128]{1,0:T(8,128)(2,1)S(1)}, u32[]{:S(2)}, u32[]{:S(2)}) collective-permute-start(bf16[1040,128]{1,0:T(8,128)(2,1)S(1)} %get-tuple-element.52), channel_id=1, source_target_pairs={{0,2},{1,3},{2,4},{3,5},{4,6},{5,7},{8,10},{9,11},{10,12},{11,13},... | collective-permute-start | bytes 798728 | tf_op jit(solution)/shard_map/ppermute | solution.py:568
  26.3 9.2 %collective-permute-start.7 = (bf16[2224,128]{1,0:T(8,128)(2,1)S(1)}, bf16[2224,128]{1,0:T(8,128)(2,1)S(1)}, u32[]{:S(2)}, u32[]{:S(2)}) collective-permute-start(bf16[2224,128]{1,0:T(8,128)(2,1)S(1)} %broadcast_select_fusion), channel_id=1, source_target_pairs={{0,1},{1,0},{2,3},{3,2},{4,5},{5,4},{6,7},{7,6},{8,9},{9,8},{10,11... | collective-permute-start | bytes 1708040 | tf_op jit(solution)/shard_map/ppermute | solution.py:576
  28.2 11.6 %collective-permute-start.6 = (bf16[1184,128]{1,0:T(8,128)(2,1)S(1)}, bf16[1184,128]{1,0:T(8,128)(2,1)S(1)}, u32[]{:S(2)}, u32[]{:S(2)}) collective-permute-start(bf16[1184,128]{1,0:T(8,128)(2,1)S(1)} %add_convert_fusion.fresh_early_ref), channel_id=1, source_target_pairs={{0,8},{8,16},{16,24},{1,9},{9,17},{17,25},{2,10},{10,18},{18,26},{... | collective-permute-start | bytes 909320 | tf_op jit(solution)/shard_map/ppermute | solution.py:585
  31.8 6.0 %copy-start.6 = (f32[1,4,1,128,128]{4,3,2,1,0:T(8,128)S(1)}, f32[1,4,1,128,128]{4,3,2,1,0:T(8,128)}, u32[]{:S(2)}) copy-start(f32[1,4,1,128,128]{4,3,2,1,0:T(8,128)} %param.12) | copy-start | bytes 786436
  31.8 12.7 %collective-permute-start.5 = (bf16[1040,128]{1,0:T(8,128)(2,1)S(1)}, bf16[1040,128]{1,0:T(8,128)(2,1)S(1)}, u32[]{:S(2)}, u32[]{:S(2)}) collective-permute-start(bf16[1040,128]{1,0:T(8,128)(2,1)S(1)} %add_convert_fusion.1.fresh_late_ref), channel_id=1, source_target_pairs={{0,8},{8,16},{16,24},{1,9},{9,17},{17,25},{2,10},{10,18},{18,26},{... | collective-permute-start | bytes 798728 | tf_op jit(solution)/shard_map/ppermute | solution.py:588

commit v8 on v5

--- a/solution.py
+++ b/solution.py
@@ -9,6 +9,7 @@
 
 LANCZOS = 4
 CHARGES = (0, 1, 1, 2)
+GROUPS = ((0, 3), (1, 2))
 F32 = jnp.float32
 BF16 = jnp.bfloat16
 MIB = 1024 * 1024
@@ -249,20 +250,11 @@
 
 
 def mix_next_kernel(
-    width, tile, near_ref, relay_ref, weight_ref, out_ref, square_s, weight_s, wide_s, sums_s, diag
+    width, tile, near_ref, weight_ref, out_ref, square_s, weight_s, wide_s, sums_s, diag
 ):
-    even = lax.rem(lax.axis_index("sec"), 2) == 0
     for k in range(2):
         weight_s[k] = weight_rows(weight_ref, width, k + 1, square_s, False)
-
-    @pl.when(even)
-    def _():
-        copy_wide(width, tile, near_ref, wide_s)
-
-    @pl.when(jnp.logical_not(even))
-    def _():
-        unpack_wide(width, tile, reader(relay_ref), wide_s, diag)
-
+    unpack_wide(width, tile, reader(near_ref), wide_s, diag)
     mix_into(width, tile, [weight_s.at[k] for k in range(2)], wide_s, sums_s, out_ref)
 
 
@@ -270,7 +262,12 @@
     width, tile, far_ref, weight_ref, out_ref, square_s, weight_s, wide_s, sums_s, diag
 ):
     weight_s[0] = weight_rows(weight_ref, width, 3, square_s, False)
-    unpack_wide(width, tile, reader(far_ref), wide_s, diag)
+    inside = lax.axis_index("sec") + 2 < lax.axis_size("sec")
+
+    def read(at, size):
+        return jnp.where(inside, far_ref[at : at + size, :].astype(F32), 0.0)
+
+    unpack_wide(width, tile, read, wide_s, diag)
     mix_into(width, tile, [weight_s.at[0]], wide_s, sums_s, out_ref)
 
 
@@ -289,30 +286,28 @@
     return value * inverse, square * inverse
 
 
-def right_products(width, tile, field, right_ref, out_ref, p):
-    group, lanes = p // 2, slice(p % 2 * tile, (p % 2 + 1) * tile)
+def right_products(width, tile, field, right_ref, out_ref, k):
+    lanes = slice(k * tile, (k + 1) * tile)
     for pair in range(width // 2):
         at = pair * 2 * tile
         both = jnp.dot(field, right_ref[:, at : at + 2 * tile], preferred_element_type=F32).astype(BF16)
-        for k in range(2):
-            out_ref[group, at + k * tile : at + (k + 1) * tile, lanes] = both[:, k * tile : (k + 1) * tile]
-
-
-def head_kernel(
-    width, tile, dims_ref, guess_ref, own_ref, next_ref, after_ref, vector_ref, stats_ref, product_ref
-):
-    states = len(CHARGES)
+        for n in range(2):
+            out_ref[at + n * tile : at + (n + 1) * tile, lanes] = both[:, n * tile : (n + 1) * tile]
+
+
+def head_kernel(members, width, tile, dims_ref, guess_ref, *refs):
+    *right_refs, vector_ref, stats_ref, product_ref = refs
+    rights = [ref.at[n] for ref in right_refs for n in range(ref.shape[0])]
     sector = lax.axis_index("sec")
     rows, columns = live_limits(dims_ref, sector)
     row, lane = iotas((tile, tile))
-    rights = [own_ref.at[0], next_ref.at[0], next_ref.at[1], after_ref.at[0]]
     stats = jnp.zeros(stats_ref.shape, F32)
-    for p in range(states):
+    for k, p in enumerate(members):
         live = (row < rows) & (lane < columns[p])
         vector, norm = scaled(jnp.where(live, guess_ref[p], 0.0))
-        vector_ref[p] = vector
-        stats = put(stats, 0, sector * states + p, norm)
-        right_products(width, tile, vector.astype(BF16), rights[p], product_ref, p)
+        vector_ref[k] = vector
+        stats = put(stats, 0, sector * len(CHARGES) + p, norm)
+        right_products(width, tile, vector.astype(BF16), rights[k], product_ref, k)
     stats_ref[...] = stats
 
 
@@ -334,18 +329,20 @@
         unpack_into(count, tile, reader(packed_ref), write, diag)
 
 
-def open_kernel(width, tile, packed_ref, environ_ref, product_ref, bound_ref, image_ref, diag):
+def open_kernel(width, tile, packed_ref, environ_ref, *refs):
+    *product_refs, bound_ref, image_ref, diag = refs
     first, count = chunks_of(width)[0]
     bound_blocks(first, count, tile, packed_ref, environ_ref, bound_ref, diag)
-    for group in range(len(CHARGES) // 2):
+    for group, product_ref in enumerate(product_refs):
         image_ref[group] = jnp.dot(
-            bound_ref[...], product_ref[group, : count * tile, :], preferred_element_type=F32
+            bound_ref[...], product_ref[: count * tile, :], preferred_element_type=F32
         )
 
 
 def lanczos_kernel(
     width, tile, dims_ref, packed_ref, environ_ref, early_ref, image_ref, own_ref, next_ref, after_ref,
-    start_ref, norm_ref, product_ref, basis_ref, stats_ref, late_s, product_s, diag,
+    start_a, start_b, norm_a, norm_b, product_a, product_b, basis_ref, stats_ref,
+    late_s, product_s, diag,
 ):
     states = len(CHARGES)
     sector = lax.axis_index("sec")
@@ -354,31 +351,30 @@
     rows, columns = live_limits(dims_ref, sector)
     row, lane = iotas((tile, tile))
     rights = [own_ref.at[0], next_ref.at[0], next_ref.at[1], after_ref.at[0]]
-    stats = norm_ref[...]
+    stats = norm_a[...] + norm_b[...]
+    starts = (start_a, start_b)
     split = first * tile
     betas = [None] * states
     for j in range(LANCZOS):
-        source = product_ref if j == 0 else product_s
-        for group in range(states // 2):
-            members = (2 * group, 2 * group + 1)
+        for group, members in enumerate(GROUPS):
             if j == 0:
+                source = (product_a, product_b)[group]
                 images = image_ref[group]
             else:
-                for p in members:
+                source = product_s.at[group]
+                for k, p in enumerate(members):
                     field = basis_ref[j - 1, p].astype(BF16)
-                    right_products(width, tile, field, rights[p], product_s, p)
-                images = jnp.dot(early_ref[...], source[group, :split, :], preferred_element_type=F32)
-            images = images + jnp.dot(
-                late_s[...], source[group, split:, :], preferred_element_type=F32
-            )
-            for p in members:
+                    right_products(width, tile, field, rights[p], source, k)
+                images = jnp.dot(early_ref[...], source[:split, :], preferred_element_type=F32)
+            images = images + jnp.dot(late_s[...], source[split:, :], preferred_element_type=F32)
+            for k, p in enumerate(members):
                 live = (row < rows) & (lane < columns[p])
-                image = jnp.where(live, images[:, p % 2 * tile : (p % 2 + 1) * tile], 0.0)
-                vector = start_ref[p] if j == 0 else basis_ref[j - 1, p]
+                image = jnp.where(live, images[:, k * tile : (k + 1) * tile], 0.0)
+                vector = starts[group][k] if j == 0 else basis_ref[j - 1, p]
                 alpha = total(vector * image)
                 image = image - alpha * vector
                 if j > 0:
-                    before = start_ref[p] if j == 1 else basis_ref[j - 2, p]
+                    before = starts[group][k] if j == 1 else basis_ref[j - 2, p]
                     image = image - betas[p] * before
                 following, beta = scaled(image)
                 basis_ref[j, p] = following
@@ -388,7 +384,7 @@
     stats_ref[...] = stats
 
 
-def finish_kernel(entries, stats_ref, start_ref, basis_ref, vector_ref, table_ref):
+def finish_kernel(entries, stats_ref, start_a, start_b, basis_ref, vector_ref, table_ref):
     states = len(CHARGES)
     sector = lax.axis_index("sec")
     stats = stats_ref[0]
@@ -433,12 +429,13 @@
         table = jnp.where((table_row == 1) & (table_column == j), beta, table)
     table_ref[...] = table
     lane = lax.broadcasted_iota(jnp.int32, (1, stats.shape[1]), 1)
+    starts = {p: ref[k] for members, ref in zip(GROUPS, (start_a, start_b)) for k, p in enumerate(members)}
     for p in range(states):
         value = None
         here = lane == sector * states + p
         for k in range(LANCZOS + 1):
             weight = jnp.sum(jnp.where(here, vector[k], 0.0), axis=1, keepdims=True)
-            term = weight * (start_ref[p] if k == 0 else basis_ref[k - 1, p])
+            term = weight * (starts[p] if k == 0 else basis_ref[k - 1, p])
             value = term if value is None else value + term
         vector_ref[p] = value
 
@@ -467,8 +464,8 @@
     )(*scalars, *arrays)
 
 
-def pairs_of(count, pick):
-    return [(source, target) for source in range(count) for target in pick(source) if 0 <= target < count]
+def shift_by(count, steps):
+    return [(source, (source + steps) % count) for source in range(count)]
 
 
 def gathered(value, axis):
@@ -501,12 +498,11 @@
     site_weights = jnp.transpose(mpo[0, 0], (0, 2, 1)).reshape(width * states, width)
     bound_weights = jnp.transpose(boundary_mpo[0], (0, 2, 1)).reshape(width * states, width)
 
-    swap = pairs_of(sectors, lambda q: [q ^ 1])
-    across = pairs_of(sectors, lambda q: [q + 1] if q % 2 == 0 else [])
-    down = pairs_of(sectors, lambda q: [q - 1] if q % 2 else [])
-    up_two = pairs_of(sectors, lambda q: [q + 2])
-    down_two = pairs_of(sectors, lambda q: [q - 2])
-    onward = pairs_of(segments, lambda s: [s + 1])
+    sector = lax.axis_index("sec")
+    swap = [(q, q ^ 1) for q in range(sectors)]
+    up_two = shift_by(sectors, 2)
+    down_two = shift_by(sectors, -2)
+    onward = shift_by(segments, 1)
     diag = pltpu.VMEM((drows, tile), F32)
 
     def mix_scratch(count):
@@ -517,13 +513,13 @@
             pltpu.VMEM((count, wide * (tile + 8), tile), F32),
         ]
 
+    right_packed = call(
+        "pack_right", functools.partial(pack_kernel, width, tile), [], [right], packed,
+        [diag], 6, 1,
+    )
+    right_far = lax.ppermute(right_packed, "sec", down_two)
     far_environ = lax.ppermute(environ, "sec", swap)
     far_site = lax.ppermute(site, "sec", swap)
-    right_near = lax.ppermute(right, "sec", down)
-    right_packed = call(
-        "pack_right", functools.partial(pack_kernel, width, tile), [], [right], packed, [diag], 6, 1
-    )
-    right_far = lax.ppermute(right_packed, "sec", down_two)
     fold_scratch = [
         pltpu.VMEM((tile, 3 * tile), BF16),
         pltpu.VMEM((3, tile, tile), BF16),
@@ -549,49 +545,58 @@
     )
     kept, late_outgoing = lax.optimization_barrier((kept, outgoing[1]))
     late_arrived = lax.ppermute(late_outgoing, "sec", up_two)
-    kept, right_far, right = lax.optimization_barrier((kept, right_far, right))
-    right_relay = lax.ppermute(right_far, "sec", across)
+    kept, right = lax.optimization_barrier((kept, right))
     own_mixed = call(
         "mix_own", functools.partial(mix_own_kernel, width, tile), [], [right, bound_weights],
         mixed(1), mix_scratch(1), 12, 1,
     )
+    own_mixed, right_far = lax.optimization_barrier((own_mixed, right_far))
+    passed_on = jnp.where(sector + 2 < sectors, right_far, jnp.zeros_like(right_far))
+    passed_on = jnp.where(lax.rem(sector, 2) == 0, passed_on, right_packed)
+    right_near = lax.ppermute(passed_on, "sec", swap)
     after_mixed = call(
         "mix_after", functools.partial(mix_after_kernel, width, tile), [],
         [right_far, bound_weights], mixed(1), mix_scratch(1) + [diag], 12, 2,
     )
-    early_arrived, own_mixed, after_mixed = lax.optimization_barrier(
-        (early_arrived, own_mixed, after_mixed)
-    )
-    early = (kept[0] + early_arrived.astype(F32)).astype(BF16)
+    def head(members, rights):
+        return call(
+            "head", functools.partial(head_kernel, members, width, tile),
+            [sector_dims], [guess[0, :, 0]] + rights,
+            (
+                jax.ShapeDtypeStruct((2, tile, tile), F32),
+                jax.ShapeDtypeStruct((16, 128), F32),
+                jax.ShapeDtypeStruct((width * tile, 2 * tile), BF16),
+            ),
+            [], 9, 0.5,
+        )
+
+    start_a, norms_a, products_a = head(GROUPS[0], [own_mixed, after_mixed])
+    early_arrived, products_a = lax.optimization_barrier((early_arrived, products_a))
+
+    def carried(stays, comes):
+        return (stays + jnp.where(sector >= 2, comes.astype(F32), 0.0)).astype(BF16)
+
+    early = carried(kept[0], early_arrived)
     early_bound = lax.ppermute(early, "seg", onward)
     early, late_arrived = lax.optimization_barrier((early, late_arrived))
-    late = (kept[1] + late_arrived.astype(F32)).astype(BF16)
+    late = carried(kept[1], late_arrived)
     late_bound = lax.ppermute(late, "seg", onward)
-    late, right_near, right_relay = lax.optimization_barrier((late, right_near, right_relay))
+    late, right_near = lax.optimization_barrier((late, right_near))
     next_mixed = call(
         "mix_next", functools.partial(mix_next_kernel, width, tile), [],
-        [right_near, right_relay, bound_weights], mixed(2), mix_scratch(2) + [diag], 16, 3,
-    )
-    start, norms, products = call(
-        "head", functools.partial(head_kernel, width, tile),
-        [sector_dims], [guess[0, :, 0], own_mixed, next_mixed, after_mixed],
-        (
-            jax.ShapeDtypeStruct((states, tile, tile), F32),
-            jax.ShapeDtypeStruct((16, 128), F32),
-            jax.ShapeDtypeStruct((states // 2, width * tile, 2 * tile), BF16),
-        ),
-        [], 14, 2,
-    )
+        [right_near, bound_weights], mixed(2), mix_scratch(2) + [diag], 16, 3,
+    )
+    start_b, norms_b, products_b = head(GROUPS[1], [next_mixed])
     new_env = call(
         "unpack_env", functools.partial(unpack_kernel, width, tile), [], [early, late],
         jax.ShapeDtypeStruct((width * tile, tile), BF16), [diag], 6, 2,
     )
-    early_bound, products, new_env = lax.optimization_barrier((early_bound, products, new_env))
+    early_bound, products_b, new_env = lax.optimization_barrier((early_bound, products_b, new_env))
     bound, image = call(
-        "open", functools.partial(open_kernel, width, tile), [], [early_bound, environ, products],
+        "open", functools.partial(open_kernel, width, tile), [], [early_bound, environ, products_a, products_b],
         (
             jax.ShapeDtypeStruct((tile, parts[0][1] * tile), BF16),
-            jax.ShapeDtypeStruct((states // 2, tile, 2 * tile), F32),
+            jax.ShapeDtypeStruct((len(GROUPS), tile, 2 * tile), F32),
         ),
         [diag], 12, 1,
     )
@@ -599,14 +604,15 @@
     basis, stats = call(
         "lanczos", functools.partial(lanczos_kernel, width, tile),
         [sector_dims],
-        [late_bound, environ, bound, image, own_mixed, next_mixed, after_mixed, start, norms, products],
+        [late_bound, environ, bound, image, own_mixed, next_mixed, after_mixed, start_a, start_b,
+         norms_a, norms_b, products_a, products_b],
         (
             jax.ShapeDtypeStruct((LANCZOS, states, tile, tile), F32),
             jax.ShapeDtypeStruct((16, 128), F32),
         ),
         [
             pltpu.VMEM((tile, parts[1][1] * tile), BF16),
-            pltpu.VMEM((states // 2, width * tile, 2 * tile), BF16),
+            pltpu.VMEM((len(GROUPS), width * tile, 2 * tile), BF16),
             diag,
         ],
         22, 12,
@@ -614,7 +620,7 @@
     stats = gathered(stats, "sec")
     entries = float(states * sector_count * tile * tile)
     vector, table = call(
-        "finish", functools.partial(finish_kernel, entries), [], [stats, start, basis],
+        "finish", functools.partial(finish_kernel, entries), [], [stats, start_a, start_b, basis],
         (
             jax.ShapeDtypeStruct((states, tile, tile), F32),
             jax.ShapeDtypeStruct((2, LANCZOS), F32),

time: 64.6 us -> 59.7 us (0.924)
  starting transfers between devices: 22.7 us -> 10.1 us
  waiting for transfers between devices: 4.2 us -> 9.03 us
  Pallas kernels: 27.7 us -> 29.5 us
  local copies, waits for them, and re-layouts: 1.28 us -> 2.16 us
    ppermute x1, starting transfers between devices: 5.47 us -> 0.11 us  [on_device(): early_arrived = lax.ppermute(outgoing[0], 'sec', up_two)]
    ppermute x1, waiting for transfers between devices: 0.01 us -> 3.74 us  [on_device(): early_arrived = lax.ppermute(outgoing[0], 'sec', up_two)]
    ppermute x2 -> x1, starting transfers between devices: 3.35 us -> 0.07 us  [on_device(): right_near = lax.ppermute(passed_on, 'sec', swap)]
    ppermute x1, waiting for transfers between devices: 0.01 us -> 3.12 us  [on_device(): late_arrived = lax.ppermute(late_outgoing, 'sec', up_two)]
    ppermute x1, starting transfers between devices: 5.04 us -> 1.96 us  [on_device(): late_arrived = lax.ppermute(late_outgoing, 'sec', up_two)]
    ppermute x1, waiting for transfers between devices: 2.73 us -> 0.01 us  [on_device(): right_far = lax.ppermute(right_packed, 'sec', down_two)]
    ppermute x1, starting transfers between devices: 1.29 us -> 3.93 us  [on_device(): right_far = lax.ppermute(right_packed, 'sec', down_two)]
    ppermute x1, starting transfers between devices: 3.5 us -> 1.63 us  [on_device(): early_bound = lax.ppermute(early, 'seg', onward)]
  transfers between devices with their start and end apart: 9 -> 8, of which waited for: 2 -> 3; matrix products, arithmetic and copies ran while one was open for 0% -> 0% of each run, Pallas kernels for 29% -> 34%
where the time goes in v8:
time: 59.7 us; the launch traced here: 59.4 us
  Pallas kernels  29.5 us (49%)
  starting transfers between devices  10.1 us (17%)
  waiting for transfers between devices  9.03 us (15%)
  blocking collectives  7.58 us (13%)
  local copies, waits for them, and re-layouts  2.16 us (4%)
  between operations  0.8 us (1%)
    pallas_call x12, Pallas kernels, call(): pl.pallas_call(kernel, out_shape=outs, in_specs=[smem()] * len(scalars) +...  29.5 us
    all_to_all x1, blocking collectives, gathered(): lax.all_to_all(jnp.broadcast_to(value, (count,) + value.shape), axis, 0, 0)  7.58 us
    ppermute x1, starting transfers between devices, on_device(): right_far = lax.ppermute(right_packed, 'sec', down_two)  3.93 us
    ppermute x1, waiting for transfers between devices, on_device(): early_arrived = lax.ppermute(outgoing[0], 'sec', up_two)  3.74 us
    ppermute x1, waiting for transfers between devices, on_device(): late_arrived = lax.ppermute(late_outgoing, 'sec', up_two)  3.12 us
    ppermute x1, waiting for transfers between devices, on_device(): late_bound = lax.ppermute(late, 'seg', onward)  2.15 us
    unnamed x16, local copies, waits for them, and re-layouts  2.15 us
    ppermute x1, starting transfers between devices, on_device(): late_arrived = lax.ppermute(late_outgoing, 'sec', up_two)  1.96 us
  transfers between devices with their start and end apart: 8, of which 3 were waited for; matrix products, arithmetic and copies ran while one was open for 0% of the time, Pallas kernels for 34%

profile of v8, /device:TPU:0, one launch (start us, length us, event | category | flops | bytes accessed | tf_op | source)
XLA Modules:
  0.0 59.4 jit_solution(7063909531656322606)
XLA Ops:
  0.6 0.5 collective-permute-start
  1.1 0.1 collective-permute-start.1
  1.2 0.0 copy-start.5
  1.2 1.2 %copy-done.5 = bf16[1,1,34,128,128]{4,3,2,1,0:T(8,128)(2,1)S(1)} copy-done((bf16[1,1,34,128,128]{4,3,2,1,0:T(8,128)(2,1)S(1)}, bf16[1,1,34,128,128]{4,3,2,1,0:T(8,128)(2,1)}, u32[]{:S(2)}) %copy-start.5) | copy-done | bytes 1114136
  2.5 0.0 copy-start
  2.5 0.0 copy-start.2
  2.5 0.0 copy-start.4
  2.5 0.3 pack_right.1
  2.8 3.9 %collective-permute-start.3 = (bf16[2224,128]{1,0:T(8,128)(2,1)S(1)}, bf16[2224,128]{1,0:T(8,128)(2,1)S(1)}, u32[]{:S(2)}, u32[]{:S(2)}) collective-permute-start(bf16[2224,128]{1,0:T(8,128)(2,1)S(1)} %pack_right.1), channel_id=1, source_target_pairs={{0,6},{1,7},{2,0},{3,1},{4,2},{5,3},{6,4},{7,5},{8,14},{9,15},{10,... | collective-permute-start | bytes 1708040 | tf_op jit(solution)/shard_map/ppermute | solution.py:520
  6.7 0.0 collective-permute-done.1.far_site_ref
  6.7 0.0 collective-permute-done.far_environ_ref
  6.7 0.0 copy-done
  6.7 0.0 copy-done.2
  6.7 0.0 copy-done.4
  6.7 0.0 copy-start.3
  6.7 0.9 %copy-done.3 = f32[1,1,34,34,4]{3,4,2,1,0:T(4,128)S(1)} copy-done((f32[1,1,34,34,4]{3,4,2,1,0:T(4,128)S(1)}, f32[1,1,34,34,4]{3,4,2,1,0:T(4,128)}, u32[]{:S(2)}) %copy-start.3) | copy-done | bytes 18520
  7.6 6.5 %fold_up.1 = (bf16[1184,128]{1,0:T(8,128)(2,1)S(1)}, bf16[1040,128]{1,0:T(8,128)(2,1)S(1)}) custom-call(s32[8]{0:T(128)S(1)} %copy-done.4, bf16[4352,128]{1,0:T(8,128)(2,1)S(1)} %bitcast.22, bf16[4,128,128]{2,1,0:T(8,128)(2,1)S(1)} %bitcast.29, bf16[4352,128]{1,0:T(8,128)(2,1)S(1)} %collective-permute-done.far_environ_ref, ...), custom_call_target="tpu_custom_call" | custom-call | flops 13200000000 | tf_op jit(solution)/shard_map/fold_up/pallas_call | solution.py:453
  14.1 0.1 collective-permute-start.2
  14.2 0.0 copy-start.6
  14.2 0.0 copy-start.7
  14.2 2.9 %fold_own.1 = (f32[1184,128]{1,0:T(8,128)S(1)}, f32[1040,128]{1,0:T(8,128)S(1)}) custom-call(s32[8]{0:T(128)S(1)} %copy-done.4, bf16[4352,128]{1,0:T(8,128)(2,1)S(1)} %bitcast.23, bf16[4,128,128]{2,1,0:T(8,128)(2,1)S(1)} %bitcast.30, bf16[4352,128]{1,0:T(8,128)(2,1)S(1)} %collective-permute-done.far_environ_ref, ...), custom_call_target="tpu_custom_call" | custom-call | flops 110000000 | tf_op jit(solution)/shard_map/fold_own/pallas_call | solution.py:453
  17.1 2.0 %collective-permute-start.5 = (bf16[1040,128]{1,0:T(8,128)(2,1)S(1)}, bf16[1040,128]{1,0:T(8,128)(2,1)S(1)}, u32[]{:S(2)}, u32[]{:S(2)}) collective-permute-start(bf16[1040,128]{1,0:T(8,128)(2,1)S(1)} %get-tuple-element.55), channel_id=1, source_target_pairs={{0,2},{1,3},{2,4},{3,5},{4,6},{5,7},{6,0},{7,1},{8,10},{9,11},{10,... | collective-permute-start | bytes 798728 | tf_op jit(solution)/shard_map/ppermute | solution.py:547
  19.1 0.0 copy-done.6
  19.1 0.0 copy-done.7
  19.1 1.3 %mix_own.1.refs_0_.own_ref = bf16[1,128,4352]{2,1,0:T(8,128)(2,1)S(1)} custom-call(bf16[4352,128]{1,0:T(8,128)(2,1)S(1)} %bitcast.34, f32[136,34]{1,0:T(8,128)S(1)} %bitcast.35), custom_call_target="tpu_custom_call" | custom-call | flops 1100000000 | tf_op jit(solution)/shard_map/mix_own/pallas_call | solution.py:453
  20.4 0.0 collective-permute-done.3.far_ref
  20.4 0.1 select_select_fusion
  20.5 0.0 copy-start.1
  20.5 0.1 collective-permute-start.6
  20.5 1.8 %mix_after.1.refs_1_.after_ref = bf16[1,128,4352]{2,1,0:T(8,128)(2,1)S(1)} custom-call(bf16[2224,128]{1,0:T(8,128)(2,1)S(1)} %collective-permute-done.3.far_ref, f32[136,34]{1,0:T(8,128)S(1)} %bitcast.36), custom_call_target="tpu_custom_call" | custom-call | flops 2200000000 | tf_op jit(solution)/shard_map/mix_after/pallas_call | solution.py:453
  22.3 0.0 copy-done.1
  22.3 1.4 %head.2 = (f32[2,128,128]{2,1,0:T(8,128)S(1)}, f32[16,128]{1,0:T(8,128)S(1)}, bf16[4352,256]{1,0:T(8,128)(2,1)S(1)}) custom-call(s32[8]{0:T(128)S(1)} %copy-done.4, f32[4,128,128]{2,1,0:T(8,128)S(1)} %bitcast.26, bf16[1,128,4352]{2,1,0:T(8,128)(2,1)S(1)} %mix_own.1.refs_0_.own_ref, bf16[1,128,4352]{2,1,0:T(8,128)(2,1)S(1)} %mix_after.1.refs_1_.after_ref), custom_call_target="tpu_custom_call" | custom-call | flops 550000000 | tf_op jit(solution)/shard_map/head/pallas_call | solution.py:453
  23.7 3.7 %collective-permute-done.2 = bf16[1184,128]{1,0:T(8,128)(2,1)S(1)} collective-permute-done((bf16[1184,128]{1,0:T(8,128)(2,1)S(1)}, bf16[1184,128]{1,0:T(8,128)(2,1)S(1)}, u32[]{:S(2)}, u32[]{:S(2)}) %collective-permute-start.2) | collective-permute-done | bytes 303136 | tf_op jit(solution)/shard_map/ppermute | solution.py:539
  27.5 0.1 add_convert_fusion.early_ref
  27.5 1.6 %collective-permute-start.4 = (bf16[1184,128]{1,0:T(8,128)(2,1)S(1)}, bf16[1184,128]{1,0:T(8,128)(2,1)S(1)}, u32[]{:S(2)}, u32[]{:S(2)}) collective-permute-start(bf16[1184,128]{1,0:T(8,128)(2,1)S(1)} %add_convert_fusion.early_ref), channel_id=1, source_target_pairs={{0,8},{8,16},{16,24},{24,0},{1,9},{9,17},{17,25},{25,1},{2,10},{10... | collective-permute-start | bytes 909320 | tf_op jit(solution)/shard_map/ppermute | solution.py:580
  29.2 3.1 %collective-permute-done.5 = bf16[1040,128]{1,0:T(8,128)(2,1)S(1)} collective-permute-done((bf16[1040,128]{1,0:T(8,128)(2,1)S(1)}, bf16[1040,128]{1,0:T(8,128)(2,1)S(1)}, u32[]{:S(2)}, u32[]{:S(2)}) %collective-permute-start.5) | collective-permute-done | bytes 266272 | tf_op jit(solution)/shard_map/ppermute | solution.py:547
  32.3 0.1 add_convert_fusion.1.late_ref
  32.4 1.8 %collective-permute-start.7 = (bf16[1040,128]{1,0:T(8,128)(2,1)S(1)}, bf16[1040,128]{1,0:T(8,128)(2,1)S(1)}, u32[]{:S(2)}, u32[]{:S(2)}) collective-permute-start(bf16[1040,128]{1,0:T(8,128)(2,1)S(1)} %add_convert_fusion.1.late_ref), channel_id=1, source_target_pairs={{0,8},{8,16},{16,24},{24,0},{1,9},{9,17},{17,25},{25,1},{2,10},{10... | collective-permute-start | bytes 798728 | tf_op jit(solution)/shard_map/ppermute | solution.py:583
  34.2 0.0 collective-permute-done.6.near_ref
  34.2 2.4 %mix_next.1.refs_0_.next_ref = bf16[2,128,4352]{2,1,0:T(8,128)(2,1)S(1)} custom-call(bf16[2224,128]{1,0:T(8,128)(2,1)S(1)} %collective-permute-done.6.near_ref, f32[136,34]{1,0:T(8,128)S(1)} %bitcast.37), custom_call_target="tpu_custom_call" | custom-call | flops 3300000000 | tf_op jit(solution)/shard_map/mix_next/pallas_call | solution.py:453
  36.6 1.4 %head.3 = (f32[2,128,128]{2,1,0:T(8,128)S(1)}, f32[16,128]{1,0:T(8,128)S(1)}, bf16[4352,256]{1,0:T(8,128)(2,1)S(1)}) custom-call(s32[8]{0:T(128)S(1)} %copy-done.4, f32[4,128,128]{2,1,0:T(8,128)S(1)} %bitcast.27, bf16[2,128,4352]{2,1,0:T(8,128)(2,1)S(1)} %mix_next.1.refs_0_.next_ref), custom_call_target="tpu_custom_call" | custom-call | flops 550000000 | tf_op jit(solution)/shard_map/head/pallas_call | solution.py:453
  38.0 1.8 %unpack_env.1 = bf16[4352,128]{1,0:T(8,128)(2,1)} custom-call(bf16[1184,128]{1,0:T(8,128)(2,1)S(1)} %add_convert_fusion.early_ref, bf16[1040,128]{1,0:T(8,128)(2,1)S(1)} %add_convert_fusion.1.late_ref), custom_call_target="tpu_custom_call" | custom-call | flops 2200000000 | tf_op jit(solution)/shard_map/unpack_env/pallas_call | solution.py:453
  39.9 0.0 collective-permute-done.4.packed_ref
  39.9 0.6 open.1
  40.5 2.2 %collective-permute-done.7.packed_ref = bf16[1040,128]{1,0:T(8,128)(2,1)S(1)} collective-permute-done((bf16[1040,128]{1,0:T(8,128)(2,1)S(1)}, bf16[1040,128]{1,0:T(8,128)(2,1)S(1)}, u32[]{:S(2)}, u32[]{:S(2)}) %collective-permute-start.7) | collective-permute-done | bytes 266272 | tf_op jit(solution)/shard_map/ppermute | solution.py:583
  42.6 7.5 %lanczos.1 = (f32[4,4,128,128]{3,2,1,0:T(8,128)S(1)}, f32[16,128]{1,0:T(8,128)S(1)}) custom-call(s32[8]{0:T(128)S(1)} %copy-done.4, bf16[1040,128]{1,0:T(8,128)(2,1)S(1)} %collective-permute-done.7.packed_ref, bf16[4352,128]{1,0:T(8,128)(2,1)S(1)} %bitcast.25, bf16[128,2304]{1,0:T(8,128)(2,1)S(1)} %get-tuple-element.67.early_ref, ...), custom_call_target="tpu_custom_call" | custom-call | flops 13200000000 | tf_op jit(solution)/shard_map/lanczos/pallas_call | solution.py:453
  50.1 7.6 %all_to_all.5.stats_ref = f32[8,16,128]{2,1,0:T(8,128)S(1)} all-to-all(f32[8,16,128]{2,1,0:T(8,128)S(1)} %broadcast_in_dim.23), channel_id=1, replica_groups=mesh['seg'=4,'sec'=8] {'sec'}, dimensions={0} | all-to-all | bytes 131072 | tf_op jit(solution)/shard_map/all_to_all | solution.py:473
  57.7 1.7 %finish.1 = (f32[4,128,128]{2,1,0:T(8,128)}, f32[2,4]{1,0:T(2,128)}) custom-call(f32[8,16,128]{2,1,0:T(8,128)S(1)} %all_to_all.5.stats_ref, f32[2,128,128]{2,1,0:T(8,128)S(1)} %get-tuple-element.69.start_a, f32[2,128,128]{2,1,0:T(8,128)S(1)} %get-tuple-element.70.start_b, f32[4,4,128,128]{3,2,1,0:T(8,128)S(1)} %get-tuple-element.74.basis_ref), custom_call_target="tpu_custom_call" | custom-call | flops 2200000000 | tf_op jit(solution)/shard_map/finish/pallas_call | solution.py:453
  (1 shorter events, 0.0 us)
Async XLA Ops:
  0.6 6.1 %collective-permute-start = (bf16[4352,128]{1,0:T(8,128)(2,1)}, bf16[4352,128]{1,0:T(8,128)(2,1)S(1)}, u32[]{:S(2)}, u32[]{:S(2)}) collective-permute-start(bf16[4352,128]{1,0:T(8,128)(2,1)} %bitcast.21), channel_id=1, source_target_pairs={{0,1},{1,0},{2,3},{3,2},{4,5},{5,4},{6,7},{7,6},{8,9},{9,8},{10,11... | collective-permute-start | bytes 3342344 | tf_op jit(solution)/shard_map/ppermute | solution.py:521
  1.1 5.6 %collective-permute-start.1 = (bf16[4,128,128]{2,1,0:T(8,128)(2,1)}, bf16[4,128,128]{2,1,0:T(8,128)(2,1)}, u32[]{:S(2)}, u32[]{:S(2)}) collective-permute-start(bf16[4,128,128]{2,1,0:T(8,128)(2,1)} %bitcast.28), channel_id=1, source_target_pairs={{0,1},{1,0},{2,3},{3,2},{4,5},{5,4},{6,7},{7,6},{8,9},{9,8},{10,11... | collective-permute-start | bytes 393224 | tf_op jit(solution)/shard_map/ppermute | solution.py:522
  1.2 1.2 %copy-start.5 = (bf16[1,1,34,128,128]{4,3,2,1,0:T(8,128)(2,1)S(1)}, bf16[1,1,34,128,128]{4,3,2,1,0:T(8,128)(2,1)}, u32[]{:S(2)}) copy-start(bf16[1,1,34,128,128]{4,3,2,1,0:T(8,128)(2,1)} %param.8) | copy-start | bytes 3342340
  2.5 4.2 %copy-start = (bf16[1,1,34,128,128]{4,3,2,1,0:T(8,128)(2,1)S(1)}, bf16[1,1,34,128,128]{4,3,2,1,0:T(8,128)(2,1)}, u32[]{:S(2)}) copy-start(bf16[1,1,34,128,128]{4,3,2,1,0:T(8,128)(2,1)} %param.7) | copy-start | bytes 3342340
  2.5 4.2 %copy-start.2 = (bf16[1,1,4,1,128,128]{5,4,3,2,1,0:T(8,128)(2,1)S(1)}, bf16[1,1,4,1,128,128]{5,4,3,2,1,0:T(8,128)(2,1)}, u32[]{:S(2)}) copy-start(bf16[1,1,4,1,128,128]{5,4,3,2,1,0:T(8,128)(2,1)} %param.9) | copy-start | bytes 393220
  2.5 4.2 %copy-start.4 = (s32[8]{0:T(128)S(1)}, s32[8]{0:T(128)}, u32[]{:S(2)}) copy-start(s32[8]{0:T(128)} %dims_ref.9) | copy-start | bytes 100
  2.8 17.6 %collective-permute-start.3 = (bf16[2224,128]{1,0:T(8,128)(2,1)S(1)}, bf16[2224,128]{1,0:T(8,128)(2,1)S(1)}, u32[]{:S(2)}, u32[]{:S(2)}) collective-permute-start(bf16[2224,128]{1,0:T(8,128)(2,1)S(1)} %pack_right.1), channel_id=1, source_target_pairs={{0,6},{1,7},{2,0},{3,1},{4,2},{5,3},{6,4},{7,5},{8,14},{9,15},{10,... | collective-permute-start | bytes 1708040 | tf_op jit(solution)/shard_map/ppermute | solution.py:520
  6.7 0.9 %copy-start.3 = (f32[1,1,34,34,4]{3,4,2,1,0:T(4,128)S(1)}, f32[1,1,34,34,4]{3,4,2,1,0:T(4,128)}, u32[]{:S(2)}) copy-start(f32[1,1,34,34,4]{3,4,2,1,0:T(4,128)} %param.10) | copy-start | bytes 55492
  14.1 13.3 %collective-permute-start.2 = (bf16[1184,128]{1,0:T(8,128)(2,1)S(1)}, bf16[1184,128]{1,0:T(8,128)(2,1)S(1)}, u32[]{:S(2)}, u32[]{:S(2)}) collective-permute-start(bf16[1184,128]{1,0:T(8,128)(2,1)S(1)} %get-tuple-element.40), channel_id=1, source_target_pairs={{0,2},{1,3},{2,4},{3,5},{4,6},{5,7},{6,0},{7,1},{8,10},{9,11},{10,... | collective-permute-start | bytes 909320 | tf_op jit(solution)/shard_map/ppermute | solution.py:539
  14.2 4.8 %copy-start.6 = (bf16[1,1,34,128,128]{4,3,2,1,0:T(8,128)(2,1)S(1)}, bf16[1,1,34,128,128]{4,3,2,1,0:T(8,128)(2,1)}, u32[]{:S(2)}) copy-start(bf16[1,1,34,128,128]{4,3,2,1,0:T(8,128)(2,1)} %param.8) | copy-start | bytes 3342340
  14.2 4.8 %copy-start.7 = (f32[1,34,34,4]{2,3,1,0:T(4,128)S(1)}, f32[1,34,34,4]{2,3,1,0:T(4,128)}, u32[]{:S(2)}) copy-start(f32[1,34,34,4]{2,3,1,0:T(4,128)} %param.11) | copy-start | bytes 55492
  17.1 15.2 %collective-permute-start.5 = (bf16[1040,128]{1,0:T(8,128)(2,1)S(1)}, bf16[1040,128]{1,0:T(8,128)(2,1)S(1)}, u32[]{:S(2)}, u32[]{:S(2)}) collective-permute-start(bf16[1040,128]{1,0:T(8,128)(2,1)S(1)} %get-tuple-element.55), channel_id=1, source_target_pairs={{0,2},{1,3},{2,4},{3,5},{4,6},{5,7},{6,0},{7,1},{8,10},{9,11},{10,... | collective-permute-start | bytes 798728 | tf_op jit(solution)/shard_map/ppermute | solution.py:547
  20.5 1.9 %copy-start.1 = (f32[1,4,1,128,128]{4,3,2,1,0:T(8,128)S(1)}, f32[1,4,1,128,128]{4,3,2,1,0:T(8,128)}, u32[]{:S(2)}) copy-start(f32[1,4,1,128,128]{4,3,2,1,0:T(8,128)} %param.12) | copy-start | bytes 786436
  20.5 13.8 %collective-permute-start.6 = (bf16[2224,128]{1,0:T(8,128)(2,1)S(1)}, bf16[2224,128]{1,0:T(8,128)(2,1)S(1)}, u32[]{:S(2)}, u32[]{:S(2)}) collective-permute-start(bf16[2224,128]{1,0:T(8,128)(2,1)S(1)} %select_select_fusion), channel_id=1, source_target_pairs={{0,1},{1,0},{2,3},{3,2},{4,5},{5,4},{6,7},{7,6},{8,9},{9,8},{10,11... | collective-permute-start | bytes 1708040 | tf_op jit(solution)/shard_map/ppermute | solution.py:556
  27.5 12.3 %collective-permute-start.4 = (bf16[1184,128]{1,0:T(8,128)(2,1)S(1)}, bf16[1184,128]{1,0:T(8,128)(2,1)S(1)}, u32[]{:S(2)}, u32[]{:S(2)}) collective-permute-start(bf16[1184,128]{1,0:T(8,128)(2,1)S(1)} %add_convert_fusion.early_ref), channel_id=1, source_target_pairs={{0,8},{8,16},{16,24},{24,0},{1,9},{9,17},{17,25},{25,1},{2,10},{10... | collective-permute-start | bytes 909320 | tf_op jit(solution)/shard_map/ppermute | solution.py:580
  32.4 10.2 %collective-permute-start.7 = (bf16[1040,128]{1,0:T(8,128)(2,1)S(1)}, bf16[1040,128]{1,0:T(8,128)(2,1)S(1)}, u32[]{:S(2)}, u32[]{:S(2)}) collective-permute-start(bf16[1040,128]{1,0:T(8,128)(2,1)S(1)} %add_convert_fusion.1.late_ref), channel_id=1, source_target_pairs={{0,8},{8,16},{16,24},{24,0},{1,9},{9,17},{17,25},{25,1},{2,10},{10... | collective-permute-start | bytes 798728 | tf_op jit(solution)/shard_map/ppermute | solution.py:583

commit v9 on v8

--- a/solution.py
+++ b/solution.py
@@ -28,8 +28,9 @@
 
 
 def chunks_of(width):
-    first = -(-width // 4) * 2
-    return (0, first), (first, width - first)
+    one = width // 6 * 2
+    two = (width - one) // 4 * 2
+    return (0, one), (one, two), (one + two, width - one - two)
 
 
 def iotas(shape):
@@ -110,8 +111,9 @@
     return lambda at, size: ref[at : at + size, :].astype(F32)
 
 
-def unpack_kernel(width, tile, early_ref, late_ref, out_ref, diag):
-    for (first, count), ref in zip(chunks_of(width), (early_ref, late_ref)):
+def unpack_kernel(width, tile, *refs):
+    *part_refs, out_ref, diag = refs
+    for (first, count), ref in zip(chunks_of(width), part_refs):
 
         def write(w, block, first=first):
             out_ref[(first + w) * tile : (first + w + 1) * tile, :] = block.astype(BF16)
@@ -120,9 +122,12 @@
 
 
 def fold_kernel(
-    width, tile, travels, dims_ref, environ_ref, site_ref, far_environ_ref, far_site_ref, weight_ref, early_ref, late_ref,
-    joined_s, turned_s, square_s, weight_s, half_s, packed_s, diag_s, sums_s, diag_sums_s,
+    width, tile, travels, dims_ref, environ_ref, site_ref, far_environ_ref, far_site_ref, weight_ref, *refs
 ):
+    part_refs = refs[: len(chunks_of(width))]
+    joined_s, turned_s, square_s, weight_s, half_s, packed_s, diag_s, sums_s, diag_sums_s = refs[
+        len(part_refs) :
+    ]
     half = tile // 2
     pitch = half + 8
     wide = padded(width)
@@ -189,7 +194,7 @@
                 sums_s[pl.ds(at + k, wide, stride=pitch), :] = value[:, k * tile : (k + 1) * tile]
         diag_sums_s[...] = jnp.zeros_like(diag_sums_s)
         diag_sums_s[:wide, :] = mixed([diag_s[n, :wide] for n in range(parts)])
-        for (first, count), ref in zip(chunks_of(width), (early_ref, late_ref)):
+        for (first, count), ref in zip(chunks_of(width), part_refs):
             for w in range(count):
                 at = (first + w) * pitch
                 ref[w * half : (w + 1) * half, :] = sums_s[at : at + half, :].astype(ref.dtype)
@@ -311,32 +316,34 @@
     stats_ref[...] = stats
 
 
-def bound_blocks(first, count, tile, packed_ref, environ_ref, out_ref, diag):
+def bound_blocks(chunks, tile, packed_refs, environ_ref, out_ref, diag):
     segment = lax.axis_index("seg")
+    start = chunks[0][0]
 
     @pl.when(segment == 0)
     def _():
-        for w in range(count):
+        for w in range(sum(count for _, count in chunks)):
             out_ref[:, w * tile : (w + 1) * tile] = environ_ref[
-                (first + w) * tile : (first + w + 1) * tile, :
+                (start + w) * tile : (start + w + 1) * tile, :
             ]
 
     @pl.when(segment != 0)
     def _():
-        def write(w, block):
-            out_ref[:, w * tile : (w + 1) * tile] = block.astype(BF16)
-
-        unpack_into(count, tile, reader(packed_ref), write, diag)
-
-
-def open_kernel(width, tile, packed_ref, environ_ref, *refs):
-    *product_refs, bound_ref, image_ref, diag = refs
-    first, count = chunks_of(width)[0]
-    bound_blocks(first, count, tile, packed_ref, environ_ref, bound_ref, diag)
+        for (first, count), ref in zip(chunks, packed_refs):
+
+            def write(w, block, base=first - start):
+                out_ref[:, (base + w) * tile : (base + w + 1) * tile] = block.astype(BF16)
+
+            unpack_into(count, tile, reader(ref), write, diag)
+
+
+def open_kernel(width, tile, environ_ref, *refs):
+    chunks = chunks_of(width)[:-1]
+    packed_refs, (*product_refs, bound_ref, image_ref, diag) = refs[: len(chunks)], refs[len(chunks) :]
+    bound_blocks(chunks, tile, packed_refs, environ_ref, bound_ref, diag)
+    rows = bound_ref.shape[1]
     for group, product_ref in enumerate(product_refs):
-        image_ref[group] = jnp.dot(
-            bound_ref[...], product_ref[: count * tile, :], preferred_element_type=F32
-        )
+        image_ref[group] = jnp.dot(bound_ref[...], product_ref[:rows, :], preferred_element_type=F32)
 
 
 def lanczos_kernel(
@@ -346,14 +353,14 @@
 ):
     states = len(CHARGES)
     sector = lax.axis_index("sec")
-    first, count = chunks_of(width)[1]
-    bound_blocks(first, count, tile, packed_ref, environ_ref, late_s, diag)
+    last = chunks_of(width)[-1:]
+    bound_blocks(last, tile, [packed_ref], environ_ref, late_s, diag)
     rows, columns = live_limits(dims_ref, sector)
     row, lane = iotas((tile, tile))
     rights = [own_ref.at[0], next_ref.at[0], next_ref.at[1], after_ref.at[0]]
     stats = norm_a[...] + norm_b[...]
     starts = (start_a, start_b)
-    split = first * tile
+    split = last[0][0] * tile
     betas = [None] * states
     for j in range(LANCZOS):
         for group, members in enumerate(GROUPS):
@@ -543,17 +550,25 @@
         [sector_dims], [environ, site, far_environ, far_site, site_weights], packed_parts(F32),
         fold_scratch, 20, 0.1,
     )
-    kept, late_outgoing = lax.optimization_barrier((kept, outgoing[1]))
-    late_arrived = lax.ppermute(late_outgoing, "sec", up_two)
+    kept, middle_outgoing = lax.optimization_barrier((kept, outgoing[1]))
+    middle_arrived = lax.ppermute(middle_outgoing, "sec", up_two)
     kept, right = lax.optimization_barrier((kept, right))
     own_mixed = call(
         "mix_own", functools.partial(mix_own_kernel, width, tile), [], [right, bound_weights],
         mixed(1), mix_scratch(1), 12, 1,
     )
-    own_mixed, right_far = lax.optimization_barrier((own_mixed, right_far))
+    own_mixed, right_far, late_outgoing = lax.optimization_barrier((own_mixed, right_far, outgoing[2]))
+    late_arrived = lax.ppermute(late_outgoing, "sec", up_two)
     passed_on = jnp.where(sector + 2 < sectors, right_far, jnp.zeros_like(right_far))
     passed_on = jnp.where(lax.rem(sector, 2) == 0, passed_on, right_packed)
     right_near = lax.ppermute(passed_on, "sec", swap)
+
+    def carried(stays, comes):
+        return (stays + jnp.where(sector >= 2, comes.astype(F32), 0.0)).astype(BF16)
+
+    early = carried(kept[0], early_arrived)
+    early_bound = lax.ppermute(early, "seg", onward)
+    early, right_far = lax.optimization_barrier((early, right_far))
     after_mixed = call(
         "mix_after", functools.partial(mix_after_kernel, width, tile), [],
         [right_far, bound_weights], mixed(1), mix_scratch(1) + [diag], 12, 2,
@@ -571,31 +586,28 @@
         )
 
     start_a, norms_a, products_a = head(GROUPS[0], [own_mixed, after_mixed])
-    early_arrived, products_a = lax.optimization_barrier((early_arrived, products_a))
-
-    def carried(stays, comes):
-        return (stays + jnp.where(sector >= 2, comes.astype(F32), 0.0)).astype(BF16)
-
-    early = carried(kept[0], early_arrived)
-    early_bound = lax.ppermute(early, "seg", onward)
-    early, late_arrived = lax.optimization_barrier((early, late_arrived))
-    late = carried(kept[1], late_arrived)
-    late_bound = lax.ppermute(late, "seg", onward)
-    late, right_near = lax.optimization_barrier((late, right_near))
+    middle_arrived, products_a = lax.optimization_barrier((middle_arrived, products_a))
+    middle = carried(kept[1], middle_arrived)
+    middle_bound = lax.ppermute(middle, "seg", onward)
+    middle, right_near = lax.optimization_barrier((middle, right_near))
     next_mixed = call(
         "mix_next", functools.partial(mix_next_kernel, width, tile), [],
         [right_near, bound_weights], mixed(2), mix_scratch(2) + [diag], 16, 3,
     )
     start_b, norms_b, products_b = head(GROUPS[1], [next_mixed])
+    late_arrived, products_b = lax.optimization_barrier((late_arrived, products_b))
+    late = carried(kept[2], late_arrived)
+    late_bound = lax.ppermute(late, "seg", onward)
     new_env = call(
-        "unpack_env", functools.partial(unpack_kernel, width, tile), [], [early, late],
+        "unpack_env", functools.partial(unpack_kernel, width, tile), [], [early, middle, late],
         jax.ShapeDtypeStruct((width * tile, tile), BF16), [diag], 6, 2,
     )
-    early_bound, products_b, new_env = lax.optimization_barrier((early_bound, products_b, new_env))
+    middle_bound, new_env = lax.optimization_barrier((middle_bound, new_env))
     bound, image = call(
-        "open", functools.partial(open_kernel, width, tile), [], [early_bound, environ, products_a, products_b],
+        "open", functools.partial(open_kernel, width, tile), [],
+        [environ, early_bound, middle_bound, products_a, products_b],
         (
-            jax.ShapeDtypeStruct((tile, parts[0][1] * tile), BF16),
+            jax.ShapeDtypeStruct((tile, parts[-1][0] * tile), BF16),
             jax.ShapeDtypeStruct((len(GROUPS), tile, 2 * tile), F32),
         ),
         [diag], 12, 1,
@@ -611,7 +623,7 @@
             jax.ShapeDtypeStruct((16, 128), F32),
         ),
         [
-            pltpu.VMEM((tile, parts[1][1] * tile), BF16),
+            pltpu.VMEM((tile, parts[-1][1] * tile), BF16),
             pltpu.VMEM((len(GROUPS), width * tile, 2 * tile), BF16),
             diag,
         ],

time: 59.7 us -> 60 us (level)
  starting transfers between devices: 10.1 us -> 13.8 us
  waiting for transfers between devices: 9.03 us -> 5.44 us
    ppermute x0 -> x2, starting transfers between devices: none -> 3.59 us  [the longest x1 1.96 us: on_device(): middle_arrived = lax.ppermute(middle_outgoing, 'sec', up_two)]
    ppermute x1, waiting for transfers between devices: 3.12 us -> 0.01 us  [on_device(): late_arrived = lax.ppermute(late_outgoing, 'sec', up_two)]
    ppermute x1, waiting for transfers between devices: 3.74 us -> 2.02 us  [on_device(): early_arrived = lax.ppermute(outgoing[0], 'sec', up_two)]
    ppermute x1, waiting for transfers between devices: 2.15 us -> 3.4 us  [on_device(): late_bound = lax.ppermute(late, 'seg', onward)]
  transfers between devices with their start and end apart: 8 -> 10, of which waited for: 3 -> 2; matrix products, arithmetic and copies ran while one was open for 0% -> 0% of each run, Pallas kernels for 34% -> 34%
where the time goes in v9:
time: 60 us; the launch traced here: 59.7 us
  Pallas kernels  29.6 us (49%)
  starting transfers between devices  13.8 us (23%)
  blocking collectives  7.59 us (13%)
  waiting for transfers between devices  5.44 us (9%)
  local copies, waits for them, and re-layouts  2.16 us (4%)
  between operations  0.81 us (1%)
    pallas_call x12, Pallas kernels, call(): pl.pallas_call(kernel, out_shape=outs, in_specs=[smem()] * len(scalars) +...  29.6 us
    all_to_all x1, blocking collectives, gathered(): lax.all_to_all(jnp.broadcast_to(value, (count,) + value.shape), axis, 0, 0)  7.59 us
    ppermute x1, starting transfers between devices, on_device(): right_far = lax.ppermute(right_packed, 'sec', down_two)  3.93 us
    ppermute x1, waiting for transfers between devices, on_device(): late_bound = lax.ppermute(late, 'seg', onward)  3.4 us
    unnamed x16, local copies, waits for them, and re-layouts  2.15 us
    ppermute x1, starting transfers between devices, on_device(): late_arrived = lax.ppermute(late_outgoing, 'sec', up_two)  2.04 us
    ppermute x1, waiting for transfers between devices, on_device(): early_arrived = lax.ppermute(outgoing[0], 'sec', up_two)  2.02 us
    ppermute x1, starting transfers between devices, on_device(): middle_arrived = lax.ppermute(middle_outgoing, 'sec', up_two)  1.96 us
  transfers between devices with their start and end apart: 10, of which 2 were waited for; matrix products, arithmetic and copies ran while one was open for 0% of the time, Pallas kernels for 34%

profile of v9, /device:TPU:0, one launch (start us, length us, event | category | flops | bytes accessed | tf_op | source)
XLA Modules:
  0.0 59.7 jit_solution(2511666912006698096)
XLA Ops:
  0.6 0.5 collective-permute-start
  1.1 0.1 collective-permute-start.1
  1.2 0.0 copy-start.5
  1.2 1.2 %copy-done.5 = bf16[1,1,34,128,128]{4,3,2,1,0:T(8,128)(2,1)S(1)} copy-done((bf16[1,1,34,128,128]{4,3,2,1,0:T(8,128)(2,1)S(1)}, bf16[1,1,34,128,128]{4,3,2,1,0:T(8,128)(2,1)}, u32[]{:S(2)}) %copy-start.5) | copy-done | bytes 1114136
  2.5 0.0 copy-start
  2.5 0.0 copy-start.2
  2.5 0.0 copy-start.4
  2.5 0.3 pack_right.1
  2.8 3.9 %collective-permute-start.3 = (bf16[2224,128]{1,0:T(8,128)(2,1)S(1)}, bf16[2224,128]{1,0:T(8,128)(2,1)S(1)}, u32[]{:S(2)}, u32[]{:S(2)}) collective-permute-start(bf16[2224,128]{1,0:T(8,128)(2,1)S(1)} %pack_right.1), channel_id=1, source_target_pairs={{0,6},{1,7},{2,0},{3,1},{4,2},{5,3},{6,4},{7,5},{8,14},{9,15},{10,... | collective-permute-start | bytes 1708040 | tf_op jit(solution)/shard_map/ppermute | solution.py:527
  6.7 0.0 collective-permute-done.1.far_site_ref
  6.7 0.0 collective-permute-done.far_environ_ref
  6.7 0.0 copy-done
  6.7 0.0 copy-done.2
  6.7 0.0 copy-done.4
  6.7 0.0 copy-start.3
  6.7 0.9 %copy-done.3 = f32[1,1,34,34,4]{3,4,2,1,0:T(4,128)S(1)} copy-done((f32[1,1,34,34,4]{3,4,2,1,0:T(4,128)S(1)}, f32[1,1,34,34,4]{3,4,2,1,0:T(4,128)}, u32[]{:S(2)}) %copy-start.3) | copy-done | bytes 18520
  7.6 6.5 %fold_up.1 = (bf16[656,128]{1,0:T(8,128)(2,1)S(1)}, bf16[784,128]{1,0:T(8,128)(2,1)S(1)}, bf16[784,128]{1,0:T(8,128)(2,1)S(1)}) custom-call(s32[8]{0:T(128)S(1)} %copy-done.4, bf16[4352,128]{1,0:T(8,128)(2,1)S(1)} %bitcast.22, bf16[4,128,128]{2,1,0:T(8,128)(2,1)S(1)} %bitcast.29, bf16[4352,128]{1,0:T(8,128)(2,1)S(1)} %collective-permute-done.far_environ_ref, ...), custom_call_target="tpu_custom_call" | custom-call | flops 13200000000 | tf_op jit(solution)/shard_map/fold_up/pallas_call | solution.py:460
  14.1 0.1 collective-permute-start.4
  14.2 0.0 copy-start.6
  14.2 0.0 copy-start.7
  14.2 2.8 %fold_own.1 = (f32[656,128]{1,0:T(8,128)S(1)}, f32[784,128]{1,0:T(8,128)S(1)}, f32[784,128]{1,0:T(8,128)S(1)}) custom-call(s32[8]{0:T(128)S(1)} %copy-done.4, bf16[4352,128]{1,0:T(8,128)(2,1)S(1)} %bitcast.23, bf16[4,128,128]{2,1,0:T(8,128)(2,1)S(1)} %bitcast.30, bf16[4352,128]{1,0:T(8,128)(2,1)S(1)} %collective-permute-done.far_environ_ref, ...), custom_call_target="tpu_custom_call" | custom-call | flops 110000000 | tf_op jit(solution)/shard_map/fold_own/pallas_call | solution.py:460
  17.1 2.0 %collective-permute-start.2 = (bf16[784,128]{1,0:T(8,128)(2,1)S(1)}, bf16[784,128]{1,0:T(8,128)(2,1)S(1)}, u32[]{:S(2)}, u32[]{:S(2)}) collective-permute-start(bf16[784,128]{1,0:T(8,128)(2,1)S(1)} %get-tuple-element.59), channel_id=1, source_target_pairs={{0,2},{1,3},{2,4},{3,5},{4,6},{5,7},{6,0},{7,1},{8,10},{9,11},{10,... | collective-permute-start | bytes 602120 | tf_op jit(solution)/shard_map/ppermute | solution.py:554
  19.0 0.0 copy-done.6
  19.0 0.0 copy-done.7
  19.0 1.3 %mix_own.1.refs_0_.own_ref = bf16[1,128,4352]{2,1,0:T(8,128)(2,1)S(1)} custom-call(bf16[4352,128]{1,0:T(8,128)(2,1)S(1)} %bitcast.34, f32[136,34]{1,0:T(8,128)S(1)} %bitcast.35), custom_call_target="tpu_custom_call" | custom-call | flops 1100000000 | tf_op jit(solution)/shard_map/mix_own/pallas_call | solution.py:460
  20.3 0.0 collective-permute-done.3.far_ref
  20.4 2.0 %collective-permute-start.7 = (bf16[784,128]{1,0:T(8,128)(2,1)S(1)}, bf16[784,128]{1,0:T(8,128)(2,1)S(1)}, u32[]{:S(2)}, u32[]{:S(2)}) collective-permute-start(bf16[784,128]{1,0:T(8,128)(2,1)S(1)} %get-tuple-element.71), channel_id=1, source_target_pairs={{0,2},{1,3},{2,4},{3,5},{4,6},{5,7},{6,0},{7,1},{8,10},{9,11},{10,... | collective-permute-start | bytes 602120 | tf_op jit(solution)/shard_map/ppermute | solution.py:561
  22.4 0.1 select_select_fusion
  22.5 0.1 collective-permute-start.6
  22.5 2.0 %collective-permute-done.4 = bf16[656,128]{1,0:T(8,128)(2,1)S(1)} collective-permute-done((bf16[656,128]{1,0:T(8,128)(2,1)S(1)}, bf16[656,128]{1,0:T(8,128)(2,1)S(1)}, u32[]{:S(2)}, u32[]{:S(2)}) %collective-permute-start.4) | collective-permute-done | bytes 167968 | tf_op jit(solution)/shard_map/ppermute | solution.py:546
  24.6 0.0 copy-start.1
  24.6 1.6 %collective-permute-start.9 = (bf16[656,128]{1,0:T(8,128)(2,1)S(1)}, bf16[656,128]{1,0:T(8,128)(2,1)S(1)}, u32[]{:S(2)}, u32[]{:S(2)}) collective-permute-start(bf16[656,128]{1,0:T(8,128)(2,1)S(1)} %add_convert_fusion.2.refs_0_), channel_id=1, source_target_pairs={{0,8},{8,16},{16,24},{24,0},{1,9},{9,17},{17,25},{25,1},{2,10},{10... | collective-permute-start | bytes 503816 | tf_op jit(solution)/shard_map/ppermute | solution.py:570
  26.2 1.8 %mix_after.1.refs_1_.after_ref = bf16[1,128,4352]{2,1,0:T(8,128)(2,1)S(1)} custom-call(bf16[2224,128]{1,0:T(8,128)(2,1)S(1)} %collective-permute-done.3.far_ref, f32[136,34]{1,0:T(8,128)S(1)} %bitcast.36), custom_call_target="tpu_custom_call" | custom-call | flops 2200000000 | tf_op jit(solution)/shard_map/mix_after/pallas_call | solution.py:460
  28.0 0.0 copy-done.1
  28.0 1.4 %head.2 = (f32[2,128,128]{2,1,0:T(8,128)S(1)}, f32[16,128]{1,0:T(8,128)S(1)}, bf16[4352,256]{1,0:T(8,128)(2,1)S(1)}) custom-call(s32[8]{0:T(128)S(1)} %copy-done.4, f32[4,128,128]{2,1,0:T(8,128)S(1)} %bitcast.26, bf16[1,128,4352]{2,1,0:T(8,128)(2,1)S(1)} %mix_own.1.refs_0_.own_ref, bf16[1,128,4352]{2,1,0:T(8,128)(2,1)S(1)} %mix_after.1.refs_1_.after_ref), custom_call_target="tpu_custom_call" | custom-call | flops 550000000 | tf_op jit(solution)/shard_map/head/pallas_call | solution.py:460
  29.4 0.0 collective-permute-done.2
  29.4 0.1 add_convert_fusion.1.refs_1_
  29.5 1.6 %collective-permute-start.5 = (bf16[784,128]{1,0:T(8,128)(2,1)S(1)}, bf16[784,128]{1,0:T(8,128)(2,1)S(1)}, u32[]{:S(2)}, u32[]{:S(2)}) collective-permute-start(bf16[784,128]{1,0:T(8,128)(2,1)S(1)} %add_convert_fusion.1.refs_1_), channel_id=1, source_target_pairs={{0,8},{8,16},{16,24},{24,0},{1,9},{9,17},{17,25},{25,1},{2,10},{10... | collective-permute-start | bytes 602120 | tf_op jit(solution)/shard_map/ppermute | solution.py:591
  31.1 0.0 collective-permute-done.6.near_ref
  31.1 2.4 %mix_next.1.refs_0_.next_ref = bf16[2,128,4352]{2,1,0:T(8,128)(2,1)S(1)} custom-call(bf16[2224,128]{1,0:T(8,128)(2,1)S(1)} %collective-permute-done.6.near_ref, f32[136,34]{1,0:T(8,128)S(1)} %bitcast.37), custom_call_target="tpu_custom_call" | custom-call | flops 3300000000 | tf_op jit(solution)/shard_map/mix_next/pallas_call | solution.py:460
  33.5 1.4 %head.3 = (f32[2,128,128]{2,1,0:T(8,128)S(1)}, f32[16,128]{1,0:T(8,128)S(1)}, bf16[4352,256]{1,0:T(8,128)(2,1)S(1)}) custom-call(s32[8]{0:T(128)S(1)} %copy-done.4, f32[4,128,128]{2,1,0:T(8,128)S(1)} %bitcast.27, bf16[2,128,4352]{2,1,0:T(8,128)(2,1)S(1)} %mix_next.1.refs_0_.next_ref), custom_call_target="tpu_custom_call" | custom-call | flops 550000000 | tf_op jit(solution)/shard_map/head/pallas_call | solution.py:460
  34.9 0.0 collective-permute-done.7
  34.9 0.1 add_convert_fusion.refs_2_
  35.0 1.9 %collective-permute-start.8 = (bf16[784,128]{1,0:T(8,128)(2,1)S(1)}, bf16[784,128]{1,0:T(8,128)(2,1)S(1)}, u32[]{:S(2)}, u32[]{:S(2)}) collective-permute-start(bf16[784,128]{1,0:T(8,128)(2,1)S(1)} %add_convert_fusion.refs_2_), channel_id=1, source_target_pairs={{0,8},{8,16},{16,24},{24,0},{1,9},{9,17},{17,25},{25,1},{2,10},{10... | collective-permute-start | bytes 602120 | tf_op jit(solution)/shard_map/ppermute | solution.py:600
  36.8 1.8 %unpack_env.1 = bf16[4352,128]{1,0:T(8,128)(2,1)} custom-call(bf16[656,128]{1,0:T(8,128)(2,1)S(1)} %add_convert_fusion.2.refs_0_, bf16[784,128]{1,0:T(8,128)(2,1)S(1)} %add_convert_fusion.1.refs_1_, bf16[784,128]{1,0:T(8,128)(2,1)S(1)} %add_convert_fusion.refs_2_), custom_call_target="tpu_custom_call" | custom-call | flops 2200000000 | tf_op jit(solution)/shard_map/unpack_env/pallas_call | solution.py:460
  38.7 0.0 collective-permute-done.5.refs_1_
  38.7 0.0 collective-permute-done.9.refs_0_
  38.7 0.7 %open.1 = (bf16[128,2816]{1,0:T(8,128)(2,1)S(1)}, f32[2,128,256]{2,1,0:T(8,128)S(1)}) custom-call(bf16[4352,128]{1,0:T(8,128)(2,1)S(1)} %bitcast.24, bf16[656,128]{1,0:T(8,128)(2,1)S(1)} %collective-permute-done.9.refs_0_, bf16[784,128]{1,0:T(8,128)(2,1)S(1)} %collective-permute-done.5.refs_1_, bf16[4352,256]{1,0:T(8,128)(2,1)S(1)} %get-tuple-element.77.refs_2_.product_a, ...), custom_call_target="tpu_custom_call" | custom-call | flops 1100000000 | tf_op jit(solution)/shard_map/open/pallas_call | solution.py:460
  39.4 3.4 %collective-permute-done.8.packed_ref = bf16[784,128]{1,0:T(8,128)(2,1)S(1)} collective-permute-done((bf16[784,128]{1,0:T(8,128)(2,1)S(1)}, bf16[784,128]{1,0:T(8,128)(2,1)S(1)}, u32[]{:S(2)}, u32[]{:S(2)}) %collective-permute-start.8) | collective-permute-done | bytes 200736 | tf_op jit(solution)/shard_map/ppermute | solution.py:600
  42.8 7.6 %lanczos.1 = (f32[4,4,128,128]{3,2,1,0:T(8,128)S(1)}, f32[16,128]{1,0:T(8,128)S(1)}) custom-call(s32[8]{0:T(128)S(1)} %copy-done.4, bf16[784,128]{1,0:T(8,128)(2,1)S(1)} %collective-permute-done.8.packed_ref, bf16[4352,128]{1,0:T(8,128)(2,1)S(1)} %bitcast.25, bf16[128,2816]{1,0:T(8,128)(2,1)S(1)} %get-tuple-element.81.early_ref, ...), custom_call_target="tpu_custom_call" | custom-call | flops 13200000000 | tf_op jit(solution)/shard_map/lanczos/pallas_call | solution.py:460
  50.4 7.6 %all_to_all.5.stats_ref = f32[8,16,128]{2,1,0:T(8,128)S(1)} all-to-all(f32[8,16,128]{2,1,0:T(8,128)S(1)} %broadcast_in_dim.24), channel_id=1, replica_groups=mesh['seg'=4,'sec'=8] {'sec'}, dimensions={0} | all-to-all | bytes 131072 | tf_op jit(solution)/shard_map/all_to_all | solution.py:480
  58.0 1.7 %finish.1 = (f32[4,128,128]{2,1,0:T(8,128)}, f32[2,4]{1,0:T(2,128)}) custom-call(f32[8,16,128]{2,1,0:T(8,128)S(1)} %all_to_all.5.stats_ref, f32[2,128,128]{2,1,0:T(8,128)S(1)} %get-tuple-element.83.start_a, f32[2,128,128]{2,1,0:T(8,128)S(1)} %get-tuple-element.84.start_b, f32[4,4,128,128]{3,2,1,0:T(8,128)S(1)} %get-tuple-element.88.basis_ref), custom_call_target="tpu_custom_call" | custom-call | flops 2200000000 | tf_op jit(solution)/shard_map/finish/pallas_call | solution.py:460
  (2 shorter events, 0.1 us)
Async XLA Ops:
  0.6 6.1 %collective-permute-start = (bf16[4352,128]{1,0:T(8,128)(2,1)}, bf16[4352,128]{1,0:T(8,128)(2,1)S(1)}, u32[]{:S(2)}, u32[]{:S(2)}) collective-permute-start(bf16[4352,128]{1,0:T(8,128)(2,1)} %bitcast.21), channel_id=1, source_target_pairs={{0,1},{1,0},{2,3},{3,2},{4,5},{5,4},{6,7},{7,6},{8,9},{9,8},{10,11... | collective-permute-start | bytes 3342344 | tf_op jit(solution)/shard_map/ppermute | solution.py:528
  1.1 5.6 %collective-permute-start.1 = (bf16[4,128,128]{2,1,0:T(8,128)(2,1)}, bf16[4,128,128]{2,1,0:T(8,128)(2,1)}, u32[]{:S(2)}, u32[]{:S(2)}) collective-permute-start(bf16[4,128,128]{2,1,0:T(8,128)(2,1)} %bitcast.28), channel_id=1, source_target_pairs={{0,1},{1,0},{2,3},{3,2},{4,5},{5,4},{6,7},{7,6},{8,9},{9,8},{10,11... | collective-permute-start | bytes 393224 | tf_op jit(solution)/shard_map/ppermute | solution.py:529
  1.2 1.2 %copy-start.5 = (bf16[1,1,34,128,128]{4,3,2,1,0:T(8,128)(2,1)S(1)}, bf16[1,1,34,128,128]{4,3,2,1,0:T(8,128)(2,1)}, u32[]{:S(2)}) copy-start(bf16[1,1,34,128,128]{4,3,2,1,0:T(8,128)(2,1)} %param.8) | copy-start | bytes 3342340
  2.5 4.2 %copy-start = (bf16[1,1,34,128,128]{4,3,2,1,0:T(8,128)(2,1)S(1)}, bf16[1,1,34,128,128]{4,3,2,1,0:T(8,128)(2,1)}, u32[]{:S(2)}) copy-start(bf16[1,1,34,128,128]{4,3,2,1,0:T(8,128)(2,1)} %param.7) | copy-start | bytes 3342340
  2.5 4.2 %copy-start.2 = (bf16[1,1,4,1,128,128]{5,4,3,2,1,0:T(8,128)(2,1)S(1)}, bf16[1,1,4,1,128,128]{5,4,3,2,1,0:T(8,128)(2,1)}, u32[]{:S(2)}) copy-start(bf16[1,1,4,1,128,128]{5,4,3,2,1,0:T(8,128)(2,1)} %param.9) | copy-start | bytes 393220
  2.5 4.2 %copy-start.4 = (s32[8]{0:T(128)S(1)}, s32[8]{0:T(128)}, u32[]{:S(2)}) copy-start(s32[8]{0:T(128)} %dims_ref.9) | copy-start | bytes 100
  2.8 17.6 %collective-permute-start.3 = (bf16[2224,128]{1,0:T(8,128)(2,1)S(1)}, bf16[2224,128]{1,0:T(8,128)(2,1)S(1)}, u32[]{:S(2)}, u32[]{:S(2)}) collective-permute-start(bf16[2224,128]{1,0:T(8,128)(2,1)S(1)} %pack_right.1), channel_id=1, source_target_pairs={{0,6},{1,7},{2,0},{3,1},{4,2},{5,3},{6,4},{7,5},{8,14},{9,15},{10,... | collective-permute-start | bytes 1708040 | tf_op jit(solution)/shard_map/ppermute | solution.py:527
  6.7 0.9 %copy-start.3 = (f32[1,1,34,34,4]{3,4,2,1,0:T(4,128)S(1)}, f32[1,1,34,34,4]{3,4,2,1,0:T(4,128)}, u32[]{:S(2)}) copy-start(f32[1,1,34,34,4]{3,4,2,1,0:T(4,128)} %param.10) | copy-start | bytes 55492
  14.1 10.5 %collective-permute-start.4 = (bf16[656,128]{1,0:T(8,128)(2,1)S(1)}, bf16[656,128]{1,0:T(8,128)(2,1)S(1)}, u32[]{:S(2)}, u32[]{:S(2)}) collective-permute-start(bf16[656,128]{1,0:T(8,128)(2,1)S(1)} %get-tuple-element.47), channel_id=1, source_target_pairs={{0,2},{1,3},{2,4},{3,5},{4,6},{5,7},{6,0},{7,1},{8,10},{9,11},{10,... | collective-permute-start | bytes 503816 | tf_op jit(solution)/shard_map/ppermute | solution.py:546
  14.2 4.8 %copy-start.6 = (bf16[1,1,34,128,128]{4,3,2,1,0:T(8,128)(2,1)S(1)}, bf16[1,1,34,128,128]{4,3,2,1,0:T(8,128)(2,1)}, u32[]{:S(2)}) copy-start(bf16[1,1,34,128,128]{4,3,2,1,0:T(8,128)(2,1)} %param.8) | copy-start | bytes 3342340
  14.2 4.8 %copy-start.7 = (f32[1,34,34,4]{2,3,1,0:T(4,128)S(1)}, f32[1,34,34,4]{2,3,1,0:T(4,128)}, u32[]{:S(2)}) copy-start(f32[1,34,34,4]{2,3,1,0:T(4,128)} %param.11) | copy-start | bytes 55492
  17.1 12.3 %collective-permute-start.2 = (bf16[784,128]{1,0:T(8,128)(2,1)S(1)}, bf16[784,128]{1,0:T(8,128)(2,1)S(1)}, u32[]{:S(2)}, u32[]{:S(2)}) collective-permute-start(bf16[784,128]{1,0:T(8,128)(2,1)S(1)} %get-tuple-element.59), channel_id=1, source_target_pairs={{0,2},{1,3},{2,4},{3,5},{4,6},{5,7},{6,0},{7,1},{8,10},{9,11},{10,... | collective-permute-start | bytes 602120 | tf_op jit(solution)/shard_map/ppermute | solution.py:554
  20.4 14.6 %collective-permute-start.7 = (bf16[784,128]{1,0:T(8,128)(2,1)S(1)}, bf16[784,128]{1,0:T(8,128)(2,1)S(1)}, u32[]{:S(2)}, u32[]{:S(2)}) collective-permute-start(bf16[784,128]{1,0:T(8,128)(2,1)S(1)} %get-tuple-element.71), channel_id=1, source_target_pairs={{0,2},{1,3},{2,4},{3,5},{4,6},{5,7},{6,0},{7,1},{8,10},{9,11},{10,... | collective-permute-start | bytes 602120 | tf_op jit(solution)/shard_map/ppermute | solution.py:561
  22.5 8.7 %collective-permute-start.6 = (bf16[2224,128]{1,0:T(8,128)(2,1)S(1)}, bf16[2224,128]{1,0:T(8,128)(2,1)S(1)}, u32[]{:S(2)}, u32[]{:S(2)}) collective-permute-start(bf16[2224,128]{1,0:T(8,128)(2,1)S(1)} %select_select_fusion), channel_id=1, source_target_pairs={{0,1},{1,0},{2,3},{3,2},{4,5},{5,4},{6,7},{7,6},{8,9},{9,8},{10,11... | collective-permute-start | bytes 1708040 | tf_op jit(solution)/shard_map/ppermute | solution.py:564
  24.6 3.4 %copy-start.1 = (f32[1,4,1,128,128]{4,3,2,1,0:T(8,128)S(1)}, f32[1,4,1,128,128]{4,3,2,1,0:T(8,128)}, u32[]{:S(2)}) copy-start(f32[1,4,1,128,128]{4,3,2,1,0:T(8,128)} %param.12) | copy-start | bytes 786436
  24.6 14.1 %collective-permute-start.9 = (bf16[656,128]{1,0:T(8,128)(2,1)S(1)}, bf16[656,128]{1,0:T(8,128)(2,1)S(1)}, u32[]{:S(2)}, u32[]{:S(2)}) collective-permute-start(bf16[656,128]{1,0:T(8,128)(2,1)S(1)} %add_convert_fusion.2.refs_0_), channel_id=1, source_target_pairs={{0,8},{8,16},{16,24},{24,0},{1,9},{9,17},{17,25},{25,1},{2,10},{10... | collective-permute-start | bytes 503816 | tf_op jit(solution)/shard_map/ppermute | solution.py:570
  29.5 9.2 %collective-permute-start.5 = (bf16[784,128]{1,0:T(8,128)(2,1)S(1)}, bf16[784,128]{1,0:T(8,128)(2,1)S(1)}, u32[]{:S(2)}, u32[]{:S(2)}) collective-permute-start(bf16[784,128]{1,0:T(8,128)(2,1)S(1)} %add_convert_fusion.1.refs_1_), channel_id=1, source_target_pairs={{0,8},{8,16},{16,24},{24,0},{1,9},{9,17},{17,25},{25,1},{2,10},{10... | collective-permute-start | bytes 602120 | tf_op jit(solution)/shard_map/ppermute | solution.py:591
  35.0 7.8 %collective-permute-start.8 = (bf16[784,128]{1,0:T(8,128)(2,1)S(1)}, bf16[784,128]{1,0:T(8,128)(2,1)S(1)}, u32[]{:S(2)}, u32[]{:S(2)}) collective-permute-start(bf16[784,128]{1,0:T(8,128)(2,1)S(1)} %add_convert_fusion.refs_2_), channel_id=1, source_target_pairs={{0,8},{8,16},{16,24},{24,0},{1,9},{9,17},{17,25},{25,1},{2,10},{10... | collective-permute-start | bytes 602120 | tf_op jit(solution)/shard_map/ppermute | solution.py:600

commit v10 on v9

--- a/solution.py
+++ b/solution.py
@@ -391,12 +391,13 @@
     stats_ref[...] = stats
 
 
-def finish_kernel(entries, stats_ref, start_a, start_b, basis_ref, vector_ref, table_ref):
+def finish_kernel(entries, start_a, start_b, basis_ref, *refs):
     states = len(CHARGES)
     sector = lax.axis_index("sec")
-    stats = stats_ref[0]
-    for q in range(1, stats_ref.shape[0]):
-        stats = stats + stats_ref[q]
+    *share_refs, vector_ref, table_ref = refs
+    stats = share_refs[0][...]
+    for ref in share_refs[1:]:
+        stats = stats + ref[...]
     alphas = [stats[1 + 2 * j : 2 + 2 * j, :] for j in range(LANCZOS)]
     betas = [stats[2 + 2 * j : 3 + 2 * j, :] for j in range(LANCZOS)]
 
@@ -475,9 +476,12 @@
     return [(source, (source + steps) % count) for source in range(count)]
 
 
-def gathered(value, axis):
+def shares(value, axis):
     count = lax.axis_size(axis)
-    return lax.all_to_all(jnp.broadcast_to(value, (count,) + value.shape), axis, 0, 0)
+    value = value + lax.ppermute(value, axis, [(q, q ^ 1) for q in range(count)])
+    return [value] + [
+        lax.ppermute(value, axis, shift_by(count, steps)) for steps in range(2, count, 2)
+    ]
 
 
 def on_device(left_env, right_env, site_tensors, mpo, boundary_mpo, guess, sector_dims):
@@ -585,19 +589,22 @@
             [], 9, 0.5,
         )
 
-    start_a, norms_a, products_a = head(GROUPS[0], [own_mixed, after_mixed])
-    middle_arrived, products_a = lax.optimization_barrier((middle_arrived, products_a))
+    middle_arrived, after_mixed = lax.optimization_barrier((middle_arrived, after_mixed))
     middle = carried(kept[1], middle_arrived)
     middle_bound = lax.ppermute(middle, "seg", onward)
-    middle, right_near = lax.optimization_barrier((middle, right_near))
+    middle, right_near, after_mixed = lax.optimization_barrier((middle, right_near, after_mixed))
+    start_a, norms_a, products_a = head(GROUPS[0], [own_mixed, after_mixed])
     next_mixed = call(
         "mix_next", functools.partial(mix_next_kernel, width, tile), [],
         [right_near, bound_weights], mixed(2), mix_scratch(2) + [diag], 16, 3,
     )
-    start_b, norms_b, products_b = head(GROUPS[1], [next_mixed])
-    late_arrived, products_b = lax.optimization_barrier((late_arrived, products_b))
+    late_arrived, next_mixed, products_a = lax.optimization_barrier(
+        (late_arrived, next_mixed, products_a)
+    )
     late = carried(kept[2], late_arrived)
     late_bound = lax.ppermute(late, "seg", onward)
+    late, next_mixed = lax.optimization_barrier((late, next_mixed))
+    start_b, norms_b, products_b = head(GROUPS[1], [next_mixed])
     new_env = call(
         "unpack_env", functools.partial(unpack_kernel, width, tile), [], [early, middle, late],
         jax.ShapeDtypeStruct((width * tile, tile), BF16), [diag], 6, 2,
@@ -629,10 +636,10 @@
         ],
         22, 12,
     )
-    stats = gathered(stats, "sec")
+    stats = shares(stats, "sec")
     entries = float(states * sector_count * tile * tile)
     vector, table = call(
-        "finish", functools.partial(finish_kernel, entries), [], [stats, start_a, start_b, basis],
+        "finish", functools.partial(finish_kernel, entries), [], [start_a, start_b, basis] + stats,
         (
             jax.ShapeDtypeStruct((states, tile, tile), F32),
             jax.ShapeDtypeStruct((2, LANCZOS), F32),

time: 60 us -> 60.5 us (level)
  blocking collectives: 7.59 us -> 0 us
  waiting for transfers between devices: 5.44 us -> 10.6 us
  starting transfers between devices: 13.8 us -> 16.8 us
    all_to_all x1 -> x0, blocking collectives: 7.59 us -> none  [gathered(): lax.all_to_all(jnp.broadcast_to(value, (count,) + value.shape), axis, 0, 0)]
    ppermute x0 -> x4, waiting for transfers between devices: none -> 5.7 us  [the longest x3 4.55 us: shares(): lax.ppermute(value, axis, shift_by(count, steps))]
    ppermute x0 -> x4, starting transfers between devices: none -> 3.03 us  [the longest x3 2.96 us: shares(): lax.ppermute(value, axis, shift_by(count, steps))]
    ppermute x1, waiting for transfers between devices: 3.4 us -> 1.99 us  [on_device(): late_bound = lax.ppermute(late, 'seg', onward)]
    ppermute x1, waiting for transfers between devices: 0.01 us -> 0.83 us  [on_device(): middle_arrived = lax.ppermute(middle_outgoing, 'sec', up_two)]
  transfers between devices with their start and end apart: 10 -> 14, of which waited for: 2 -> 7; matrix products, arithmetic and copies ran while one was open for 0% -> 0% of each run, Pallas kernels for 34% -> 34%
where the time goes in v10:
time: 60.5 us; the launch traced here: 60.3 us
  Pallas kernels  29.7 us (49%)
  starting transfers between devices  16.8 us (28%)
  waiting for transfers between devices  10.6 us (18%)
  local copies, waits for them, and re-layouts  2.15 us (4%)
  between operations  0.8 us (1%)
    pallas_call x12, Pallas kernels, call(): pl.pallas_call(kernel, out_shape=outs, in_specs=[smem()] * len(scalars) +...  29.7 us
    ppermute x3, waiting for transfers between devices, shares(): lax.ppermute(value, axis, shift_by(count, steps))  4.55 us
    ppermute x1, starting transfers between devices, on_device(): right_far = lax.ppermute(right_packed, 'sec', down_two)  3.93 us
    ppermute x3, starting transfers between devices, shares(): lax.ppermute(value, axis, shift_by(count, steps))  2.96 us
    unnamed x16, local copies, waits for them, and re-layouts  2.15 us
    ppermute x1, starting transfers between devices, on_device(): late_arrived = lax.ppermute(late_outgoing, 'sec', up_two)  2.03 us
    ppermute x1, waiting for transfers between devices, on_device(): early_arrived = lax.ppermute(outgoing[0], 'sec', up_two)  2.02 us
    ppermute x1, waiting for transfers between devices, on_device(): late_bound = lax.ppermute(late, 'seg', onward)  1.99 us
  transfers between devices with their start and end apart: 14, of which 7 were waited for; matrix products, arithmetic and copies ran while one was open for 0% of the time, Pallas kernels for 34%

profile of v10, /device:TPU:0, one launch (start us, length us, event | category | flops | bytes accessed | tf_op | source)
XLA Modules:
  0.0 60.3 jit_solution(10639722310360535197)
XLA Ops:
  0.6 0.5 collective-permute-start
  1.1 0.1 collective-permute-start.1
  1.2 0.0 copy-start.5
  1.2 1.2 %copy-done.5 = bf16[1,1,34,128,128]{4,3,2,1,0:T(8,128)(2,1)S(1)} copy-done((bf16[1,1,34,128,128]{4,3,2,1,0:T(8,128)(2,1)S(1)}, bf16[1,1,34,128,128]{4,3,2,1,0:T(8,128)(2,1)}, u32[]{:S(2)}) %copy-start.5) | copy-done | bytes 1114136
  2.5 0.0 copy-start
  2.5 0.0 copy-start.2
  2.5 0.0 copy-start.4
  2.5 0.3 pack_right.1
  2.8 3.9 %collective-permute-start.4 = (bf16[2224,128]{1,0:T(8,128)(2,1)S(1)}, bf16[2224,128]{1,0:T(8,128)(2,1)S(1)}, u32[]{:S(2)}, u32[]{:S(2)}) collective-permute-start(bf16[2224,128]{1,0:T(8,128)(2,1)S(1)} %pack_right.1), channel_id=1, source_target_pairs={{0,6},{1,7},{2,0},{3,1},{4,2},{5,3},{6,4},{7,5},{8,14},{9,15},{10,... | collective-permute-start | bytes 1708040 | tf_op jit(solution)/shard_map/ppermute | solution.py:531
  6.7 0.0 collective-permute-done.1.far_site_ref
  6.7 0.0 collective-permute-done.far_environ_ref
  6.7 0.0 copy-done
  6.7 0.0 copy-done.2
  6.7 0.0 copy-done.4
  6.7 0.0 copy-start.3
  6.7 0.9 %copy-done.3 = f32[1,1,34,34,4]{3,4,2,1,0:T(4,128)S(1)} copy-done((f32[1,1,34,34,4]{3,4,2,1,0:T(4,128)S(1)}, f32[1,1,34,34,4]{3,4,2,1,0:T(4,128)}, u32[]{:S(2)}) %copy-start.3) | copy-done | bytes 18520
  7.6 6.5 %fold_up.1 = (bf16[656,128]{1,0:T(8,128)(2,1)S(1)}, bf16[784,128]{1,0:T(8,128)(2,1)S(1)}, bf16[784,128]{1,0:T(8,128)(2,1)S(1)}) custom-call(s32[8]{0:T(128)S(1)} %copy-done.4, bf16[4352,128]{1,0:T(8,128)(2,1)S(1)} %bitcast.22, bf16[4,128,128]{2,1,0:T(8,128)(2,1)S(1)} %bitcast.29, bf16[4352,128]{1,0:T(8,128)(2,1)S(1)} %collective-permute-done.far_environ_ref, ...), custom_call_target="tpu_custom_call" | custom-call | flops 13200000000 | tf_op jit(solution)/shard_map/fold_up/pallas_call | solution.py:461
  14.1 0.1 collective-permute-start.3
  14.2 0.0 copy-start.6
  14.2 0.0 copy-start.7
  14.2 2.8 %fold_own.1 = (f32[656,128]{1,0:T(8,128)S(1)}, f32[784,128]{1,0:T(8,128)S(1)}, f32[784,128]{1,0:T(8,128)S(1)}) custom-call(s32[8]{0:T(128)S(1)} %copy-done.4, bf16[4352,128]{1,0:T(8,128)(2,1)S(1)} %bitcast.23, bf16[4,128,128]{2,1,0:T(8,128)(2,1)S(1)} %bitcast.30, bf16[4352,128]{1,0:T(8,128)(2,1)S(1)} %collective-permute-done.far_environ_ref, ...), custom_call_target="tpu_custom_call" | custom-call | flops 110000000 | tf_op jit(solution)/shard_map/fold_own/pallas_call | solution.py:461
  17.1 2.0 %collective-permute-start.2 = (bf16[784,128]{1,0:T(8,128)(2,1)S(1)}, bf16[784,128]{1,0:T(8,128)(2,1)S(1)}, u32[]{:S(2)}, u32[]{:S(2)}) collective-permute-start(bf16[784,128]{1,0:T(8,128)(2,1)S(1)} %get-tuple-element.63), channel_id=1, source_target_pairs={{0,2},{1,3},{2,4},{3,5},{4,6},{5,7},{6,0},{7,1},{8,10},{9,11},{10,... | collective-permute-start | bytes 602120 | tf_op jit(solution)/shard_map/ppermute | solution.py:558
  19.0 0.0 copy-done.6
  19.0 0.0 copy-done.7
  19.0 1.3 %mix_own.1.refs_0_.own_ref = bf16[1,128,4352]{2,1,0:T(8,128)(2,1)S(1)} custom-call(bf16[4352,128]{1,0:T(8,128)(2,1)S(1)} %bitcast.34, f32[136,34]{1,0:T(8,128)S(1)} %bitcast.35), custom_call_target="tpu_custom_call" | custom-call | flops 1100000000 | tf_op jit(solution)/shard_map/mix_own/pallas_call | solution.py:461
  20.4 0.0 collective-permute-done.4.far_ref
  20.4 2.0 %collective-permute-start.7 = (bf16[784,128]{1,0:T(8,128)(2,1)S(1)}, bf16[784,128]{1,0:T(8,128)(2,1)S(1)}, u32[]{:S(2)}, u32[]{:S(2)}) collective-permute-start(bf16[784,128]{1,0:T(8,128)(2,1)S(1)} %get-tuple-element.74), channel_id=1, source_target_pairs={{0,2},{1,3},{2,4},{3,5},{4,6},{5,7},{6,0},{7,1},{8,10},{9,11},{10,... | collective-permute-start | bytes 602120 | tf_op jit(solution)/shard_map/ppermute | solution.py:565
  22.4 0.1 select_select_fusion
  22.5 0.1 collective-permute-start.6
  22.5 2.0 %collective-permute-done.3 = bf16[656,128]{1,0:T(8,128)(2,1)S(1)} collective-permute-done((bf16[656,128]{1,0:T(8,128)(2,1)S(1)}, bf16[656,128]{1,0:T(8,128)(2,1)S(1)}, u32[]{:S(2)}, u32[]{:S(2)}) %collective-permute-start.3) | collective-permute-done | bytes 167968 | tf_op jit(solution)/shard_map/ppermute | solution.py:550
  24.6 0.1 add_convert_fusion.2.refs_0_
  24.6 0.0 copy-start.1
  24.6 1.6 %collective-permute-start.9 = (bf16[656,128]{1,0:T(8,128)(2,1)S(1)}, bf16[656,128]{1,0:T(8,128)(2,1)S(1)}, u32[]{:S(2)}, u32[]{:S(2)}) collective-permute-start(bf16[656,128]{1,0:T(8,128)(2,1)S(1)} %add_convert_fusion.2.refs_0_), channel_id=1, source_target_pairs={{0,8},{8,16},{16,24},{24,0},{1,9},{9,17},{17,25},{25,1},{2,10},{10... | collective-permute-start | bytes 503816 | tf_op jit(solution)/shard_map/ppermute | solution.py:574
  26.3 1.8 %mix_after.1.refs_1_.after_ref = bf16[1,128,4352]{2,1,0:T(8,128)(2,1)S(1)} custom-call(bf16[2224,128]{1,0:T(8,128)(2,1)S(1)} %collective-permute-done.4.far_ref, f32[136,34]{1,0:T(8,128)S(1)} %bitcast.36), custom_call_target="tpu_custom_call" | custom-call | flops 2200000000 | tf_op jit(solution)/shard_map/mix_after/pallas_call | solution.py:461
  28.0 0.8 %collective-permute-done.2 = bf16[784,128]{1,0:T(8,128)(2,1)S(1)} collective-permute-done((bf16[784,128]{1,0:T(8,128)(2,1)S(1)}, bf16[784,128]{1,0:T(8,128)(2,1)S(1)}, u32[]{:S(2)}, u32[]{:S(2)}) %collective-permute-start.2) | collective-permute-done | bytes 200736 | tf_op jit(solution)/shard_map/ppermute | solution.py:558
  28.9 0.1 add_convert_fusion.1.refs_1_
  28.9 1.6 %collective-permute-start.5 = (bf16[784,128]{1,0:T(8,128)(2,1)S(1)}, bf16[784,128]{1,0:T(8,128)(2,1)S(1)}, u32[]{:S(2)}, u32[]{:S(2)}) collective-permute-start(bf16[784,128]{1,0:T(8,128)(2,1)S(1)} %add_convert_fusion.1.refs_1_), channel_id=1, source_target_pairs={{0,8},{8,16},{16,24},{24,0},{1,9},{9,17},{17,25},{25,1},{2,10},{10... | collective-permute-start | bytes 602120 | tf_op jit(solution)/shard_map/ppermute | solution.py:594
  30.6 0.0 collective-permute-done.6.near_ref
  30.6 0.0 copy-done.1
  30.6 1.4 %head.2 = (f32[2,128,128]{2,1,0:T(8,128)S(1)}, f32[16,128]{1,0:T(8,128)S(1)}, bf16[4352,256]{1,0:T(8,128)(2,1)S(1)}) custom-call(s32[8]{0:T(128)S(1)} %copy-done.4, f32[4,128,128]{2,1,0:T(8,128)S(1)} %bitcast.26, bf16[1,128,4352]{2,1,0:T(8,128)(2,1)S(1)} %mix_own.1.refs_0_.own_ref, bf16[1,128,4352]{2,1,0:T(8,128)(2,1)S(1)} %mix_after.1.refs_1_.after_ref), custom_call_target="tpu_custom_call" | custom-call | flops 550000000 | tf_op jit(solution)/shard_map/head/pallas_call | solution.py:461
  31.9 2.4 %mix_next.1.refs_0_.next_ref = bf16[2,128,4352]{2,1,0:T(8,128)(2,1)S(1)} custom-call(bf16[2224,128]{1,0:T(8,128)(2,1)S(1)} %collective-permute-done.6.near_ref, f32[136,34]{1,0:T(8,128)S(1)} %bitcast.37), custom_call_target="tpu_custom_call" | custom-call | flops 3300000000 | tf_op jit(solution)/shard_map/mix_next/pallas_call | solution.py:461
  34.3 0.0 collective-permute-done.7
  34.3 0.1 add_convert_fusion.refs_2_
  34.4 1.9 %collective-permute-start.8 = (bf16[784,128]{1,0:T(8,128)(2,1)S(1)}, bf16[784,128]{1,0:T(8,128)(2,1)S(1)}, u32[]{:S(2)}, u32[]{:S(2)}) collective-permute-start(bf16[784,128]{1,0:T(8,128)(2,1)S(1)} %add_convert_fusion.refs_2_), channel_id=1, source_target_pairs={{0,8},{8,16},{16,24},{24,0},{1,9},{9,17},{17,25},{25,1},{2,10},{10... | collective-permute-start | bytes 602120 | tf_op jit(solution)/shard_map/ppermute | solution.py:605
  36.3 1.8 %unpack_env.1 = bf16[4352,128]{1,0:T(8,128)(2,1)} custom-call(bf16[656,128]{1,0:T(8,128)(2,1)S(1)} %add_convert_fusion.2.refs_0_, bf16[784,128]{1,0:T(8,128)(2,1)S(1)} %add_convert_fusion.1.refs_1_, bf16[784,128]{1,0:T(8,128)(2,1)S(1)} %add_convert_fusion.refs_2_), custom_call_target="tpu_custom_call" | custom-call | flops 2200000000 | tf_op jit(solution)/shard_map/unpack_env/pallas_call | solution.py:461
  38.1 0.0 collective-permute-done.5.refs_1_
  38.1 1.4 %head.3 = (f32[2,128,128]{2,1,0:T(8,128)S(1)}, f32[16,128]{1,0:T(8,128)S(1)}, bf16[4352,256]{1,0:T(8,128)(2,1)S(1)}) custom-call(s32[8]{0:T(128)S(1)} %copy-done.4, f32[4,128,128]{2,1,0:T(8,128)S(1)} %bitcast.27, bf16[2,128,4352]{2,1,0:T(8,128)(2,1)S(1)} %mix_next.1.refs_0_.next_ref), custom_call_target="tpu_custom_call" | custom-call | flops 550000000 | tf_op jit(solution)/shard_map/head/pallas_call | solution.py:461
  39.5 0.0 collective-permute-done.9.refs_0_
  39.5 0.7 %open.1 = (bf16[128,2816]{1,0:T(8,128)(2,1)S(1)}, f32[2,128,256]{2,1,0:T(8,128)S(1)}) custom-call(bf16[4352,128]{1,0:T(8,128)(2,1)S(1)} %bitcast.24, bf16[656,128]{1,0:T(8,128)(2,1)S(1)} %collective-permute-done.9.refs_0_, bf16[784,128]{1,0:T(8,128)(2,1)S(1)} %collective-permute-done.5.refs_1_, bf16[4352,256]{1,0:T(8,128)(2,1)S(1)} %get-tuple-element.87.refs_2_.product_a, ...), custom_call_target="tpu_custom_call" | custom-call | flops 1100000000 | tf_op jit(solution)/shard_map/open/pallas_call | solution.py:461
  40.2 2.0 %collective-permute-done.8.packed_ref = bf16[784,128]{1,0:T(8,128)(2,1)S(1)} collective-permute-done((bf16[784,128]{1,0:T(8,128)(2,1)S(1)}, bf16[784,128]{1,0:T(8,128)(2,1)S(1)}, u32[]{:S(2)}, u32[]{:S(2)}) %collective-permute-start.8) | collective-permute-done | bytes 200736 | tf_op jit(solution)/shard_map/ppermute | solution.py:605
  42.2 7.6 %lanczos.1 = (f32[4,4,128,128]{3,2,1,0:T(8,128)S(1)}, f32[16,128]{1,0:T(8,128)S(1)}) custom-call(s32[8]{0:T(128)S(1)} %copy-done.4, bf16[784,128]{1,0:T(8,128)(2,1)S(1)} %collective-permute-done.8.packed_ref, bf16[4352,128]{1,0:T(8,128)(2,1)S(1)} %bitcast.25, bf16[128,2816]{1,0:T(8,128)(2,1)S(1)} %get-tuple-element.91.early_ref, ...), custom_call_target="tpu_custom_call" | custom-call | flops 13200000000 | tf_op jit(solution)/shard_map/lanczos/pallas_call | solution.py:461
  49.8 0.1 collective-permute-start.10
  49.9 1.2 %collective-permute-done.10 = f32[16,128]{1,0:T(8,128)S(1)} collective-permute-done((f32[16,128]{1,0:T(8,128)S(1)}, f32[16,128]{1,0:T(8,128)S(1)}, u32[]{:S(2)}, u32[]{:S(2)}) %collective-permute-start.10) | collective-permute-done | bytes 8224 | tf_op jit(solution)/shard_map/ppermute | solution.py:481
  51.0 1.4 %collective-permute-start.13 = (f32[16,128]{1,0:T(8,128)S(1)}, f32[16,128]{1,0:T(8,128)S(1)}, u32[]{:S(2)}, u32[]{:S(2)}) collective-permute-start(f32[16,128]{1,0:T(8,128)S(1)} %add.19.refs_0_), channel_id=1, source_target_pairs={{0,6},{1,7},{2,0},{3,1},{4,2},{5,3},{6,4},{7,5},{8,14},{9,15},{10,... | collective-permute-start | bytes 24584 | tf_op jit(solution)/shard_map/ppermute | solution.py:483
  52.5 1.5 %collective-permute-start.12 = (f32[16,128]{1,0:T(8,128)S(1)}, f32[16,128]{1,0:T(8,128)S(1)}, u32[]{:S(2)}, u32[]{:S(2)}) collective-permute-start(f32[16,128]{1,0:T(8,128)S(1)} %add.19.refs_0_), channel_id=1, source_target_pairs={{0,4},{1,5},{2,6},{3,7},{4,0},{5,1},{6,2},{7,3},{8,12},{9,13},{10,... | collective-permute-start | bytes 24584 | tf_op jit(solution)/shard_map/ppermute | solution.py:483
  54.0 0.0 collective-permute-start.11
  54.0 0.7 %collective-permute-done.13.refs_3_ = f32[16,128]{1,0:T(8,128)S(1)} collective-permute-done((f32[16,128]{1,0:T(8,128)S(1)}, f32[16,128]{1,0:T(8,128)S(1)}, u32[]{:S(2)}, u32[]{:S(2)}) %collective-permute-start.13) | collective-permute-done | bytes 8224 | tf_op jit(solution)/shard_map/ppermute | solution.py:483
  54.7 1.4 %collective-permute-done.12.refs_2_ = f32[16,128]{1,0:T(8,128)S(1)} collective-permute-done((f32[16,128]{1,0:T(8,128)S(1)}, f32[16,128]{1,0:T(8,128)S(1)}, u32[]{:S(2)}, u32[]{:S(2)}) %collective-permute-start.12) | collective-permute-done | bytes 8224 | tf_op jit(solution)/shard_map/ppermute | solution.py:483
  56.1 2.4 %collective-permute-done.11.refs_1_ = f32[16,128]{1,0:T(8,128)S(1)} collective-permute-done((f32[16,128]{1,0:T(8,128)S(1)}, f32[16,128]{1,0:T(8,128)S(1)}, u32[]{:S(2)}, u32[]{:S(2)}) %collective-permute-start.11) | collective-permute-done | bytes 8224 | tf_op jit(solution)/shard_map/ppermute | solution.py:483
  58.5 1.7 %finish.1 = (f32[4,128,128]{2,1,0:T(8,128)}, f32[2,4]{1,0:T(2,128)}) custom-call(f32[2,128,128]{2,1,0:T(8,128)S(1)} %get-tuple-element.83.start_a, f32[2,128,128]{2,1,0:T(8,128)S(1)} %get-tuple-element.85.start_b, f32[4,4,128,128]{3,2,1,0:T(8,128)S(1)} %get-tuple-element.95.basis_ref, f32[16,128]{1,0:T(8,128)S(1)} %add.19.refs_0_, ...), custom_call_target="tpu_custom_call" | custom-call | flops 2200000000 | tf_op jit(solution)/shard_map/finish/pallas_call | solution.py:461
  (1 shorter events, 0.0 us)
Async XLA Ops:
  0.6 6.1 %collective-permute-start = (bf16[4352,128]{1,0:T(8,128)(2,1)}, bf16[4352,128]{1,0:T(8,128)(2,1)S(1)}, u32[]{:S(2)}, u32[]{:S(2)}) collective-permute-start(bf16[4352,128]{1,0:T(8,128)(2,1)} %bitcast.21), channel_id=1, source_target_pairs={{0,1},{1,0},{2,3},{3,2},{4,5},{5,4},{6,7},{7,6},{8,9},{9,8},{10,11... | collective-permute-start | bytes 3342344 | tf_op jit(solution)/shard_map/ppermute | solution.py:532
  1.1 5.6 %collective-permute-start.1 = (bf16[4,128,128]{2,1,0:T(8,128)(2,1)}, bf16[4,128,128]{2,1,0:T(8,128)(2,1)}, u32[]{:S(2)}, u32[]{:S(2)}) collective-permute-start(bf16[4,128,128]{2,1,0:T(8,128)(2,1)} %bitcast.28), channel_id=1, source_target_pairs={{0,1},{1,0},{2,3},{3,2},{4,5},{5,4},{6,7},{7,6},{8,9},{9,8},{10,11... | collective-permute-start | bytes 393224 | tf_op jit(solution)/shard_map/ppermute | solution.py:533
  1.2 1.2 %copy-start.5 = (bf16[1,1,34,128,128]{4,3,2,1,0:T(8,128)(2,1)S(1)}, bf16[1,1,34,128,128]{4,3,2,1,0:T(8,128)(2,1)}, u32[]{:S(2)}) copy-start(bf16[1,1,34,128,128]{4,3,2,1,0:T(8,128)(2,1)} %param.8) | copy-start | bytes 3342340
  2.5 4.2 %copy-start = (bf16[1,1,34,128,128]{4,3,2,1,0:T(8,128)(2,1)S(1)}, bf16[1,1,34,128,128]{4,3,2,1,0:T(8,128)(2,1)}, u32[]{:S(2)}) copy-start(bf16[1,1,34,128,128]{4,3,2,1,0:T(8,128)(2,1)} %param.7) | copy-start | bytes 3342340
  2.5 4.2 %copy-start.2 = (bf16[1,1,4,1,128,128]{5,4,3,2,1,0:T(8,128)(2,1)S(1)}, bf16[1,1,4,1,128,128]{5,4,3,2,1,0:T(8,128)(2,1)}, u32[]{:S(2)}) copy-start(bf16[1,1,4,1,128,128]{5,4,3,2,1,0:T(8,128)(2,1)} %param.9) | copy-start | bytes 393220
  2.5 4.2 %copy-start.4 = (s32[8]{0:T(128)S(1)}, s32[8]{0:T(128)}, u32[]{:S(2)}) copy-start(s32[8]{0:T(128)} %dims_ref.9) | copy-start | bytes 100
  2.8 17.6 %collective-permute-start.4 = (bf16[2224,128]{1,0:T(8,128)(2,1)S(1)}, bf16[2224,128]{1,0:T(8,128)(2,1)S(1)}, u32[]{:S(2)}, u32[]{:S(2)}) collective-permute-start(bf16[2224,128]{1,0:T(8,128)(2,1)S(1)} %pack_right.1), channel_id=1, source_target_pairs={{0,6},{1,7},{2,0},{3,1},{4,2},{5,3},{6,4},{7,5},{8,14},{9,15},{10,... | collective-permute-start | bytes 1708040 | tf_op jit(solution)/shard_map/ppermute | solution.py:531
  6.7 0.9 %copy-start.3 = (f32[1,1,34,34,4]{3,4,2,1,0:T(4,128)S(1)}, f32[1,1,34,34,4]{3,4,2,1,0:T(4,128)}, u32[]{:S(2)}) copy-start(f32[1,1,34,34,4]{3,4,2,1,0:T(4,128)} %param.10) | copy-start | bytes 55492
  14.1 10.4 %collective-permute-start.3 = (bf16[656,128]{1,0:T(8,128)(2,1)S(1)}, bf16[656,128]{1,0:T(8,128)(2,1)S(1)}, u32[]{:S(2)}, u32[]{:S(2)}) collective-permute-start(bf16[656,128]{1,0:T(8,128)(2,1)S(1)} %get-tuple-element.51), channel_id=1, source_target_pairs={{0,2},{1,3},{2,4},{3,5},{4,6},{5,7},{6,0},{7,1},{8,10},{9,11},{10,... | collective-permute-start | bytes 503816 | tf_op jit(solution)/shard_map/ppermute | solution.py:550
  14.2 4.8 %copy-start.6 = (bf16[1,1,34,128,128]{4,3,2,1,0:T(8,128)(2,1)S(1)}, bf16[1,1,34,128,128]{4,3,2,1,0:T(8,128)(2,1)}, u32[]{:S(2)}) copy-start(bf16[1,1,34,128,128]{4,3,2,1,0:T(8,128)(2,1)} %param.8) | copy-start | bytes 3342340
  14.2 4.8 %copy-start.7 = (f32[1,34,34,4]{2,3,1,0:T(4,128)S(1)}, f32[1,34,34,4]{2,3,1,0:T(4,128)}, u32[]{:S(2)}) copy-start(f32[1,34,34,4]{2,3,1,0:T(4,128)} %param.11) | copy-start | bytes 55492
  17.1 11.8 %collective-permute-start.2 = (bf16[784,128]{1,0:T(8,128)(2,1)S(1)}, bf16[784,128]{1,0:T(8,128)(2,1)S(1)}, u32[]{:S(2)}, u32[]{:S(2)}) collective-permute-start(bf16[784,128]{1,0:T(8,128)(2,1)S(1)} %get-tuple-element.63), channel_id=1, source_target_pairs={{0,2},{1,3},{2,4},{3,5},{4,6},{5,7},{6,0},{7,1},{8,10},{9,11},{10,... | collective-permute-start | bytes 602120 | tf_op jit(solution)/shard_map/ppermute | solution.py:558
  20.4 14.0 %collective-permute-start.7 = (bf16[784,128]{1,0:T(8,128)(2,1)S(1)}, bf16[784,128]{1,0:T(8,128)(2,1)S(1)}, u32[]{:S(2)}, u32[]{:S(2)}) collective-permute-start(bf16[784,128]{1,0:T(8,128)(2,1)S(1)} %get-tuple-element.74), channel_id=1, source_target_pairs={{0,2},{1,3},{2,4},{3,5},{4,6},{5,7},{6,0},{7,1},{8,10},{9,11},{10,... | collective-permute-start | bytes 602120 | tf_op jit(solution)/shard_map/ppermute | solution.py:565
  22.5 8.1 %collective-permute-start.6 = (bf16[2224,128]{1,0:T(8,128)(2,1)S(1)}, bf16[2224,128]{1,0:T(8,128)(2,1)S(1)}, u32[]{:S(2)}, u32[]{:S(2)}) collective-permute-start(bf16[2224,128]{1,0:T(8,128)(2,1)S(1)} %select_select_fusion), channel_id=1, source_target_pairs={{0,1},{1,0},{2,3},{3,2},{4,5},{5,4},{6,7},{7,6},{8,9},{9,8},{10,11... | collective-permute-start | bytes 1708040 | tf_op jit(solution)/shard_map/ppermute | solution.py:568
  24.6 5.9 %copy-start.1 = (f32[1,4,1,128,128]{4,3,2,1,0:T(8,128)S(1)}, f32[1,4,1,128,128]{4,3,2,1,0:T(8,128)}, u32[]{:S(2)}) copy-start(f32[1,4,1,128,128]{4,3,2,1,0:T(8,128)} %param.12) | copy-start | bytes 786436
  24.6 14.9 %collective-permute-start.9 = (bf16[656,128]{1,0:T(8,128)(2,1)S(1)}, bf16[656,128]{1,0:T(8,128)(2,1)S(1)}, u32[]{:S(2)}, u32[]{:S(2)}) collective-permute-start(bf16[656,128]{1,0:T(8,128)(2,1)S(1)} %add_convert_fusion.2.refs_0_), channel_id=1, source_target_pairs={{0,8},{8,16},{16,24},{24,0},{1,9},{9,17},{17,25},{25,1},{2,10},{10... | collective-permute-start | bytes 503816 | tf_op jit(solution)/shard_map/ppermute | solution.py:574
  28.9 9.2 %collective-permute-start.5 = (bf16[784,128]{1,0:T(8,128)(2,1)S(1)}, bf16[784,128]{1,0:T(8,128)(2,1)S(1)}, u32[]{:S(2)}, u32[]{:S(2)}) collective-permute-start(bf16[784,128]{1,0:T(8,128)(2,1)S(1)} %add_convert_fusion.1.refs_1_), channel_id=1, source_target_pairs={{0,8},{8,16},{16,24},{24,0},{1,9},{9,17},{17,25},{25,1},{2,10},{10... | collective-permute-start | bytes 602120 | tf_op jit(solution)/shard_map/ppermute | solution.py:594
  34.4 7.8 %collective-permute-start.8 = (bf16[784,128]{1,0:T(8,128)(2,1)S(1)}, bf16[784,128]{1,0:T(8,128)(2,1)S(1)}, u32[]{:S(2)}, u32[]{:S(2)}) collective-permute-start(bf16[784,128]{1,0:T(8,128)(2,1)S(1)} %add_convert_fusion.refs_2_), channel_id=1, source_target_pairs={{0,8},{8,16},{16,24},{24,0},{1,9},{9,17},{17,25},{25,1},{2,10},{10... | collective-permute-start | bytes 602120 | tf_op jit(solution)/shard_map/ppermute | solution.py:605
  49.8 1.2 %collective-permute-start.10 = (f32[16,128]{1,0:T(8,128)S(1)}, f32[16,128]{1,0:T(8,128)S(1)}, u32[]{:S(2)}, u32[]{:S(2)}) collective-permute-start(f32[16,128]{1,0:T(8,128)S(1)} %get-tuple-element.96), channel_id=1, source_target_pairs={{0,1},{1,0},{2,3},{3,2},{4,5},{5,4},{6,7},{7,6},{8,9},{9,8},{10,11... | collective-permute-start | bytes 24584 | tf_op jit(solution)/shard_map/ppermute | solution.py:481
  51.0 3.7 %collective-permute-start.13 = (f32[16,128]{1,0:T(8,128)S(1)}, f32[16,128]{1,0:T(8,128)S(1)}, u32[]{:S(2)}, u32[]{:S(2)}) collective-permute-start(f32[16,128]{1,0:T(8,128)S(1)} %add.19.refs_0_), channel_id=1, source_target_pairs={{0,6},{1,7},{2,0},{3,1},{4,2},{5,3},{6,4},{7,5},{8,14},{9,15},{10,... | collective-permute-start | bytes 24584 | tf_op jit(solution)/shard_map/ppermute | solution.py:483
  52.5 3.7 %collective-permute-start.12 = (f32[16,128]{1,0:T(8,128)S(1)}, f32[16,128]{1,0:T(8,128)S(1)}, u32[]{:S(2)}, u32[]{:S(2)}) collective-permute-start(f32[16,128]{1,0:T(8,128)S(1)} %add.19.refs_0_), channel_id=1, source_target_pairs={{0,4},{1,5},{2,6},{3,7},{4,0},{5,1},{6,2},{7,3},{8,12},{9,13},{10,... | collective-permute-start | bytes 24584 | tf_op jit(solution)/shard_map/ppermute | solution.py:483
  54.0 4.5 %collective-permute-start.11 = (f32[16,128]{1,0:T(8,128)S(1)}, f32[16,128]{1,0:T(8,128)S(1)}, u32[]{:S(2)}, u32[]{:S(2)}) collective-permute-start(f32[16,128]{1,0:T(8,128)S(1)} %add.19.refs_0_), channel_id=1, source_target_pairs={{0,2},{1,3},{2,4},{3,5},{4,6},{5,7},{6,0},{7,1},{8,10},{9,11},{10,... | collective-permute-start | bytes 24584 | tf_op jit(solution)/shard_map/ppermute | solution.py:483

commit v11 on v9

--- a/solution.py
+++ b/solution.py
@@ -391,7 +391,9 @@
     stats_ref[...] = stats
 
 
-def finish_kernel(entries, stats_ref, start_a, start_b, basis_ref, vector_ref, table_ref):
+def finish_kernel(
+    entries, stats_ref, start_a, start_b, basis_ref, vector_ref, table_ref
+):
     states = len(CHARGES)
     sector = lax.axis_index("sec")
     stats = stats_ref[0]
@@ -406,34 +408,42 @@
             products = products + x * y
         return jnp.sum(products, axis=1, keepdims=True) / entries
 
-    start = [stats[0:1, :]]
-    vector = [start[0] / jnp.sqrt(mean(start, start) + 1e-06)]
+    def applied(vector):
+        count = len(vector)
+        image = []
+        for k in range(count + 1):
+            terms = []
+            if k > 0:
+                terms.append(betas[k - 1] * vector[k - 1])
+            if k < count:
+                terms.append(alphas[k] * vector[k])
+            if k + 1 < count:
+                terms.append(betas[k] * vector[k + 1])
+            image.append(sum(terms[1:], terms[0]))
+        return image
+
+    residual = [stats[0:1, :]]
     previous = []
-    beta = jnp.zeros((1, 1), F32)
     table_row, table_column = iotas(table_ref.shape)
     table = jnp.zeros(table_ref.shape, F32)
     for j in range(LANCZOS):
-        image = []
-        for k in range(j + 2):
-            term = None
-            if k > 0:
-                term = betas[k - 1] * vector[k - 1]
-            if k <= j:
-                more = alphas[k] * vector[k]
-                term = more if term is None else term + more
-            if k + 1 <= j:
-                term = term + betas[k] * vector[k + 1]
-            image.append(term)
-        alpha = mean(vector, image[: j + 1])
+        image = applied(residual)
+        square = mean(residual, residual) + 1e-06
+        alpha = mean(residual, image[: j + 1]) / square
+        norm = jnp.sqrt(square)
+        vector = [value / norm for value in residual]
+        residual = [value / norm for value in image]
         for k in range(j + 1):
-            image[k] = image[k] - alpha * vector[k]
+            residual[k] = residual[k] - alpha * vector[k]
         for k in range(j):
-            image[k] = image[k] - beta * previous[k]
-        beta = jnp.sqrt(mean(image, image) + 1e-06)
+            residual[k] = residual[k] - norm * previous[k]
         previous = vector
-        vector = [value / beta for value in image]
+        if j > 0:
+            table = jnp.where((table_row == 1) & (table_column == j - 1), norm, table)
         table = jnp.where((table_row == 0) & (table_column == j), alpha, table)
-        table = jnp.where((table_row == 1) & (table_column == j), beta, table)
+    norm = jnp.sqrt(mean(residual, residual) + 1e-06)
+    vector = [value / norm for value in residual]
+    table = jnp.where((table_row == 1) & (table_column == LANCZOS - 1), norm, table)
     table_ref[...] = table
     lane = lax.broadcasted_iota(jnp.int32, (1, stats.shape[1]), 1)
     starts = {p: ref[k] for members, ref in zip(GROUPS, (start_a, start_b)) for k, p in enumerate(members)}
@@ -585,8 +595,7 @@
             [], 9, 0.5,
         )
 
-    start_a, norms_a, products_a = head(GROUPS[0], [own_mixed, after_mixed])
-    middle_arrived, products_a = lax.optimization_barrier((middle_arrived, products_a))
+    middle_arrived, after_mixed = lax.optimization_barrier((middle_arrived, after_mixed))
     middle = carried(kept[1], middle_arrived)
     middle_bound = lax.ppermute(middle, "seg", onward)
     middle, right_near = lax.optimization_barrier((middle, right_near))
@@ -594,10 +603,12 @@
         "mix_next", functools.partial(mix_next_kernel, width, tile), [],
         [right_near, bound_weights], mixed(2), mix_scratch(2) + [diag], 16, 3,
     )
-    start_b, norms_b, products_b = head(GROUPS[1], [next_mixed])
-    late_arrived, products_b = lax.optimization_barrier((late_arrived, products_b))
+    late_arrived, next_mixed = lax.optimization_barrier((late_arrived, next_mixed))
     late = carried(kept[2], late_arrived)
     late_bound = lax.ppermute(late, "seg", onward)
+    late, next_mixed, after_mixed = lax.optimization_barrier((late, next_mixed, after_mixed))
+    start_a, norms_a, products_a = head(GROUPS[0], [own_mixed, after_mixed])
+    start_b, norms_b, products_b = head(GROUPS[1], [next_mixed])
     new_env = call(
         "unpack_env", functools.partial(unpack_kernel, width, tile), [], [early, middle, late],
         jax.ShapeDtypeStruct((width * tile, tile), BF16), [diag], 6, 2,

time: 60 us -> 57.7 us (0.962)
  waiting for transfers between devices: 5.44 us -> 3.5 us
    ppermute x1, waiting for transfers between devices: 3.4 us -> 0.61 us  [on_device(): late_bound = lax.ppermute(late, 'seg', onward)]
    ppermute x1, waiting for transfers between devices: 0.01 us -> 0.85 us  [on_device(): middle_arrived = lax.ppermute(middle_outgoing, 'sec', up_two)]
  transfers between devices with their start and end apart: 10 -> 10, of which waited for: 2 -> 3; matrix products, arithmetic and copies ran while one was open for 0% -> 0% of each run, Pallas kernels for 34% -> 35%
where the time goes in v11:
time: 57.7 us; the launch traced here: 57.4 us
  Pallas kernels  29.3 us (51%)
  starting transfers between devices  13.8 us (24%)
  blocking collectives  7.59 us (13%)
  waiting for transfers between devices  3.5 us (6%)
  local copies, waits for them, and re-layouts  2.16 us (4%)
  between operations  0.8 us (1%)
    pallas_call x12, Pallas kernels, call(): pl.pallas_call(kernel, out_shape=outs, in_specs=[smem()] * len(scalars) +...  29.3 us
    all_to_all x1, blocking collectives, gathered(): lax.all_to_all(jnp.broadcast_to(value, (count,) + value.shape), axis, 0, 0)  7.59 us
    ppermute x1, starting transfers between devices, on_device(): right_far = lax.ppermute(right_packed, 'sec', down_two)  3.93 us
    unnamed x16, local copies, waits for them, and re-layouts  2.15 us
    ppermute x1, starting transfers between devices, on_device(): late_arrived = lax.ppermute(late_outgoing, 'sec', up_two)  2.03 us
    ppermute x1, waiting for transfers between devices, on_device(): early_arrived = lax.ppermute(outgoing[0], 'sec', up_two)  2.02 us
    ppermute x1, starting transfers between devices, on_device(): middle_arrived = lax.ppermute(middle_outgoing, 'sec', up_two)  1.97 us
    ppermute x1, starting transfers between devices, on_device(): late_bound = lax.ppermute(late, 'seg', onward)  1.85 us
  transfers between devices with their start and end apart: 10, of which 3 were waited for; matrix products, arithmetic and copies ran while one was open for 0% of the time, Pallas kernels for 35%

profile of v11, /device:TPU:0, one launch (start us, length us, event | category | flops | bytes accessed | tf_op | source)
XLA Modules:
  0.0 57.4 jit_solution(5967324969576877315)
XLA Ops:
  0.6 0.5 collective-permute-start
  1.1 0.1 collective-permute-start.1
  1.2 0.0 copy-start.5
  1.2 1.2 %copy-done.5 = bf16[1,1,34,128,128]{4,3,2,1,0:T(8,128)(2,1)S(1)} copy-done((bf16[1,1,34,128,128]{4,3,2,1,0:T(8,128)(2,1)S(1)}, bf16[1,1,34,128,128]{4,3,2,1,0:T(8,128)(2,1)}, u32[]{:S(2)}) %copy-start.5) | copy-done | bytes 1114136
  2.5 0.0 copy-start
  2.5 0.0 copy-start.2
  2.5 0.0 copy-start.4
  2.5 0.3 pack_right.1
  2.8 3.9 %collective-permute-start.4 = (bf16[2224,128]{1,0:T(8,128)(2,1)S(1)}, bf16[2224,128]{1,0:T(8,128)(2,1)S(1)}, u32[]{:S(2)}, u32[]{:S(2)}) collective-permute-start(bf16[2224,128]{1,0:T(8,128)(2,1)S(1)} %pack_right.1), channel_id=1, source_target_pairs={{0,6},{1,7},{2,0},{3,1},{4,2},{5,3},{6,4},{7,5},{8,14},{9,15},{10,... | collective-permute-start | bytes 1708040 | tf_op jit(solution)/shard_map/ppermute | solution.py:537
  6.7 0.0 collective-permute-done.1.far_site_ref
  6.7 0.0 collective-permute-done.far_environ_ref
  6.7 0.0 copy-done
  6.7 0.0 copy-done.2
  6.7 0.0 copy-done.4
  6.7 0.0 copy-start.3
  6.7 0.9 %copy-done.3 = f32[1,1,34,34,4]{3,4,2,1,0:T(4,128)S(1)} copy-done((f32[1,1,34,34,4]{3,4,2,1,0:T(4,128)S(1)}, f32[1,1,34,34,4]{3,4,2,1,0:T(4,128)}, u32[]{:S(2)}) %copy-start.3) | copy-done | bytes 18520
  7.6 6.5 %fold_up.1 = (bf16[656,128]{1,0:T(8,128)(2,1)S(1)}, bf16[784,128]{1,0:T(8,128)(2,1)S(1)}, bf16[784,128]{1,0:T(8,128)(2,1)S(1)}) custom-call(s32[8]{0:T(128)S(1)} %copy-done.4, bf16[4352,128]{1,0:T(8,128)(2,1)S(1)} %bitcast.22, bf16[4,128,128]{2,1,0:T(8,128)(2,1)S(1)} %bitcast.29, bf16[4352,128]{1,0:T(8,128)(2,1)S(1)} %collective-permute-done.far_environ_ref, ...), custom_call_target="tpu_custom_call" | custom-call | flops 13200000000 | tf_op jit(solution)/shard_map/fold_up/pallas_call | solution.py:470
  14.1 0.1 collective-permute-start.3
  14.2 0.0 copy-start.6
  14.2 0.0 copy-start.7
  14.2 2.8 %fold_own.1 = (f32[656,128]{1,0:T(8,128)S(1)}, f32[784,128]{1,0:T(8,128)S(1)}, f32[784,128]{1,0:T(8,128)S(1)}) custom-call(s32[8]{0:T(128)S(1)} %copy-done.4, bf16[4352,128]{1,0:T(8,128)(2,1)S(1)} %bitcast.23, bf16[4,128,128]{2,1,0:T(8,128)(2,1)S(1)} %bitcast.30, bf16[4352,128]{1,0:T(8,128)(2,1)S(1)} %collective-permute-done.far_environ_ref, ...), custom_call_target="tpu_custom_call" | custom-call | flops 110000000 | tf_op jit(solution)/shard_map/fold_own/pallas_call | solution.py:470
  17.1 2.0 %collective-permute-start.2 = (bf16[784,128]{1,0:T(8,128)(2,1)S(1)}, bf16[784,128]{1,0:T(8,128)(2,1)S(1)}, u32[]{:S(2)}, u32[]{:S(2)}) collective-permute-start(bf16[784,128]{1,0:T(8,128)(2,1)S(1)} %get-tuple-element.62), channel_id=1, source_target_pairs={{0,2},{1,3},{2,4},{3,5},{4,6},{5,7},{6,0},{7,1},{8,10},{9,11},{10,... | collective-permute-start | bytes 602120 | tf_op jit(solution)/shard_map/ppermute | solution.py:564
  19.0 0.0 copy-done.6
  19.0 0.0 copy-done.7
  19.0 1.3 %mix_own.1.refs_0_.own_ref = bf16[1,128,4352]{2,1,0:T(8,128)(2,1)S(1)} custom-call(bf16[4352,128]{1,0:T(8,128)(2,1)S(1)} %bitcast.34, f32[136,34]{1,0:T(8,128)S(1)} %bitcast.35), custom_call_target="tpu_custom_call" | custom-call | flops 1100000000 | tf_op jit(solution)/shard_map/mix_own/pallas_call | solution.py:470
  20.3 0.0 collective-permute-done.4.far_ref
  20.4 2.0 %collective-permute-start.7 = (bf16[784,128]{1,0:T(8,128)(2,1)S(1)}, bf16[784,128]{1,0:T(8,128)(2,1)S(1)}, u32[]{:S(2)}, u32[]{:S(2)}) collective-permute-start(bf16[784,128]{1,0:T(8,128)(2,1)S(1)} %get-tuple-element.72), channel_id=1, source_target_pairs={{0,2},{1,3},{2,4},{3,5},{4,6},{5,7},{6,0},{7,1},{8,10},{9,11},{10,... | collective-permute-start | bytes 602120 | tf_op jit(solution)/shard_map/ppermute | solution.py:571
  22.4 0.1 select_select_fusion
  22.5 0.1 collective-permute-start.6
  22.5 2.0 %collective-permute-done.3 = bf16[656,128]{1,0:T(8,128)(2,1)S(1)} collective-permute-done((bf16[656,128]{1,0:T(8,128)(2,1)S(1)}, bf16[656,128]{1,0:T(8,128)(2,1)S(1)}, u32[]{:S(2)}, u32[]{:S(2)}) %collective-permute-start.3) | collective-permute-done | bytes 167968 | tf_op jit(solution)/shard_map/ppermute | solution.py:556
  24.6 1.6 %collective-permute-start.9 = (bf16[656,128]{1,0:T(8,128)(2,1)S(1)}, bf16[656,128]{1,0:T(8,128)(2,1)S(1)}, u32[]{:S(2)}, u32[]{:S(2)}) collective-permute-start(bf16[656,128]{1,0:T(8,128)(2,1)S(1)} %add_convert_fusion.2.refs_0_), channel_id=1, source_target_pairs={{0,8},{8,16},{16,24},{24,0},{1,9},{9,17},{17,25},{25,1},{2,10},{10... | collective-permute-start | bytes 503816 | tf_op jit(solution)/shard_map/ppermute | solution.py:580
  26.2 1.8 %mix_after.1.refs_1_.after_ref = bf16[1,128,4352]{2,1,0:T(8,128)(2,1)S(1)} custom-call(bf16[2224,128]{1,0:T(8,128)(2,1)S(1)} %collective-permute-done.4.far_ref, f32[136,34]{1,0:T(8,128)S(1)} %bitcast.36), custom_call_target="tpu_custom_call" | custom-call | flops 2200000000 | tf_op jit(solution)/shard_map/mix_after/pallas_call | solution.py:470
  28.0 0.8 %collective-permute-done.2 = bf16[784,128]{1,0:T(8,128)(2,1)S(1)} collective-permute-done((bf16[784,128]{1,0:T(8,128)(2,1)S(1)}, bf16[784,128]{1,0:T(8,128)(2,1)S(1)}, u32[]{:S(2)}, u32[]{:S(2)}) %collective-permute-start.2) | collective-permute-done | bytes 200736 | tf_op jit(solution)/shard_map/ppermute | solution.py:564
  28.9 0.1 add_convert_fusion.1.refs_1_
  28.9 1.6 %collective-permute-start.5 = (bf16[784,128]{1,0:T(8,128)(2,1)S(1)}, bf16[784,128]{1,0:T(8,128)(2,1)S(1)}, u32[]{:S(2)}, u32[]{:S(2)}) collective-permute-start(bf16[784,128]{1,0:T(8,128)(2,1)S(1)} %add_convert_fusion.1.refs_1_), channel_id=1, source_target_pairs={{0,8},{8,16},{16,24},{24,0},{1,9},{9,17},{17,25},{25,1},{2,10},{10... | collective-permute-start | bytes 602120 | tf_op jit(solution)/shard_map/ppermute | solution.py:600
  30.6 0.0 collective-permute-done.6.near_ref
  30.6 2.4 %mix_next.1.refs_0_.next_ref = bf16[2,128,4352]{2,1,0:T(8,128)(2,1)S(1)} custom-call(bf16[2224,128]{1,0:T(8,128)(2,1)S(1)} %collective-permute-done.6.near_ref, f32[136,34]{1,0:T(8,128)S(1)} %bitcast.37), custom_call_target="tpu_custom_call" | custom-call | flops 3300000000 | tf_op jit(solution)/shard_map/mix_next/pallas_call | solution.py:470
  33.0 0.0 collective-permute-done.7
  33.0 0.1 add_convert_fusion.refs_2_
  33.0 0.0 copy-start.1
  33.0 1.9 %collective-permute-start.8 = (bf16[784,128]{1,0:T(8,128)(2,1)S(1)}, bf16[784,128]{1,0:T(8,128)(2,1)S(1)}, u32[]{:S(2)}, u32[]{:S(2)}) collective-permute-start(bf16[784,128]{1,0:T(8,128)(2,1)S(1)} %add_convert_fusion.refs_2_), channel_id=1, source_target_pairs={{0,8},{8,16},{16,24},{24,0},{1,9},{9,17},{17,25},{25,1},{2,10},{10... | collective-permute-start | bytes 602120 | tf_op jit(solution)/shard_map/ppermute | solution.py:608
  34.9 1.8 %unpack_env.1 = bf16[4352,128]{1,0:T(8,128)(2,1)} custom-call(bf16[656,128]{1,0:T(8,128)(2,1)S(1)} %add_convert_fusion.2.refs_0_, bf16[784,128]{1,0:T(8,128)(2,1)S(1)} %add_convert_fusion.1.refs_1_, bf16[784,128]{1,0:T(8,128)(2,1)S(1)} %add_convert_fusion.refs_2_), custom_call_target="tpu_custom_call" | custom-call | flops 2200000000 | tf_op jit(solution)/shard_map/unpack_env/pallas_call | solution.py:470
  36.7 0.0 collective-permute-done.5.refs_1_
  36.7 0.0 copy-done.1
  36.7 1.4 %head.3 = (f32[2,128,128]{2,1,0:T(8,128)S(1)}, f32[16,128]{1,0:T(8,128)S(1)}, bf16[4352,256]{1,0:T(8,128)(2,1)S(1)}) custom-call(s32[8]{0:T(128)S(1)} %copy-done.4, f32[4,128,128]{2,1,0:T(8,128)S(1)} %bitcast.26, bf16[2,128,4352]{2,1,0:T(8,128)(2,1)S(1)} %mix_next.1.refs_0_.next_ref), custom_call_target="tpu_custom_call" | custom-call | flops 550000000 | tf_op jit(solution)/shard_map/head/pallas_call | solution.py:470
  38.1 1.4 %head.2 = (f32[2,128,128]{2,1,0:T(8,128)S(1)}, f32[16,128]{1,0:T(8,128)S(1)}, bf16[4352,256]{1,0:T(8,128)(2,1)S(1)}) custom-call(s32[8]{0:T(128)S(1)} %copy-done.4, f32[4,128,128]{2,1,0:T(8,128)S(1)} %bitcast.27, bf16[1,128,4352]{2,1,0:T(8,128)(2,1)S(1)} %mix_own.1.refs_0_.own_ref, bf16[1,128,4352]{2,1,0:T(8,128)(2,1)S(1)} %mix_after.1.refs_1_.after_ref), custom_call_target="tpu_custom_call" | custom-call | flops 550000000 | tf_op jit(solution)/shard_map/head/pallas_call | solution.py:470
  39.5 0.0 collective-permute-done.9.refs_0_
  39.5 0.7 %open.1 = (bf16[128,2816]{1,0:T(8,128)(2,1)S(1)}, f32[2,128,256]{2,1,0:T(8,128)S(1)}) custom-call(bf16[4352,128]{1,0:T(8,128)(2,1)S(1)} %bitcast.24, bf16[656,128]{1,0:T(8,128)(2,1)S(1)} %collective-permute-done.9.refs_0_, bf16[784,128]{1,0:T(8,128)(2,1)S(1)} %collective-permute-done.5.refs_1_, bf16[4352,256]{1,0:T(8,128)(2,1)S(1)} %get-tuple-element.82.refs_2_.product_a, ...), custom_call_target="tpu_custom_call" | custom-call | flops 1100000000 | tf_op jit(solution)/shard_map/open/pallas_call | solution.py:470
  40.2 0.6 %collective-permute-done.8.packed_ref = bf16[784,128]{1,0:T(8,128)(2,1)S(1)} collective-permute-done((bf16[784,128]{1,0:T(8,128)(2,1)S(1)}, bf16[784,128]{1,0:T(8,128)(2,1)S(1)}, u32[]{:S(2)}, u32[]{:S(2)}) %collective-permute-start.8) | collective-permute-done | bytes 200736 | tf_op jit(solution)/shard_map/ppermute | solution.py:608
  40.8 7.6 %lanczos.1 = (f32[4,4,128,128]{3,2,1,0:T(8,128)S(1)}, f32[16,128]{1,0:T(8,128)S(1)}) custom-call(s32[8]{0:T(128)S(1)} %copy-done.4, bf16[784,128]{1,0:T(8,128)(2,1)S(1)} %collective-permute-done.8.packed_ref, bf16[4352,128]{1,0:T(8,128)(2,1)S(1)} %bitcast.25, bf16[128,2816]{1,0:T(8,128)(2,1)S(1)} %get-tuple-element.87.early_ref, ...), custom_call_target="tpu_custom_call" | custom-call | flops 13200000000 | tf_op jit(solution)/shard_map/lanczos/pallas_call | solution.py:470
  48.4 7.6 %all_to_all.5.stats_ref = f32[8,16,128]{2,1,0:T(8,128)S(1)} all-to-all(f32[8,16,128]{2,1,0:T(8,128)S(1)} %broadcast_in_dim.24), channel_id=1, replica_groups=mesh['seg'=4,'sec'=8] {'sec'}, dimensions={0} | all-to-all | bytes 131072 | tf_op jit(solution)/shard_map/all_to_all | solution.py:490
  56.0 1.4 %finish.1 = (f32[4,128,128]{2,1,0:T(8,128)}, f32[2,4]{1,0:T(2,128)}) custom-call(f32[8,16,128]{2,1,0:T(8,128)S(1)} %all_to_all.5.stats_ref, f32[2,128,128]{2,1,0:T(8,128)S(1)} %get-tuple-element.89.start_a, f32[2,128,128]{2,1,0:T(8,128)S(1)} %get-tuple-element.90.start_b, f32[4,4,128,128]{3,2,1,0:T(8,128)S(1)} %get-tuple-element.94.basis_ref), custom_call_target="tpu_custom_call" | custom-call | flops 2200000000 | tf_op jit(solution)/shard_map/finish/pallas_call | solution.py:470
  (2 shorter events, 0.1 us)
Async XLA Ops:
  0.6 6.1 %collective-permute-start = (bf16[4352,128]{1,0:T(8,128)(2,1)}, bf16[4352,128]{1,0:T(8,128)(2,1)S(1)}, u32[]{:S(2)}, u32[]{:S(2)}) collective-permute-start(bf16[4352,128]{1,0:T(8,128)(2,1)} %bitcast.21), channel_id=1, source_target_pairs={{0,1},{1,0},{2,3},{3,2},{4,5},{5,4},{6,7},{7,6},{8,9},{9,8},{10,11... | collective-permute-start | bytes 3342344 | tf_op jit(solution)/shard_map/ppermute | solution.py:538
  1.1 5.6 %collective-permute-start.1 = (bf16[4,128,128]{2,1,0:T(8,128)(2,1)}, bf16[4,128,128]{2,1,0:T(8,128)(2,1)}, u32[]{:S(2)}, u32[]{:S(2)}) collective-permute-start(bf16[4,128,128]{2,1,0:T(8,128)(2,1)} %bitcast.28), channel_id=1, source_target_pairs={{0,1},{1,0},{2,3},{3,2},{4,5},{5,4},{6,7},{7,6},{8,9},{9,8},{10,11... | collective-permute-start | bytes 393224 | tf_op jit(solution)/shard_map/ppermute | solution.py:539
  1.2 1.2 %copy-start.5 = (bf16[1,1,34,128,128]{4,3,2,1,0:T(8,128)(2,1)S(1)}, bf16[1,1,34,128,128]{4,3,2,1,0:T(8,128)(2,1)}, u32[]{:S(2)}) copy-start(bf16[1,1,34,128,128]{4,3,2,1,0:T(8,128)(2,1)} %param.8) | copy-start | bytes 3342340
  2.5 4.2 %copy-start = (bf16[1,1,34,128,128]{4,3,2,1,0:T(8,128)(2,1)S(1)}, bf16[1,1,34,128,128]{4,3,2,1,0:T(8,128)(2,1)}, u32[]{:S(2)}) copy-start(bf16[1,1,34,128,128]{4,3,2,1,0:T(8,128)(2,1)} %param.7) | copy-start | bytes 3342340
  2.5 4.2 %copy-start.2 = (bf16[1,1,4,1,128,128]{5,4,3,2,1,0:T(8,128)(2,1)S(1)}, bf16[1,1,4,1,128,128]{5,4,3,2,1,0:T(8,128)(2,1)}, u32[]{:S(2)}) copy-start(bf16[1,1,4,1,128,128]{5,4,3,2,1,0:T(8,128)(2,1)} %param.9) | copy-start | bytes 393220
  2.5 4.2 %copy-start.4 = (s32[8]{0:T(128)S(1)}, s32[8]{0:T(128)}, u32[]{:S(2)}) copy-start(s32[8]{0:T(128)} %dims_ref.9) | copy-start | bytes 100
  2.8 17.6 %collective-permute-start.4 = (bf16[2224,128]{1,0:T(8,128)(2,1)S(1)}, bf16[2224,128]{1,0:T(8,128)(2,1)S(1)}, u32[]{:S(2)}, u32[]{:S(2)}) collective-permute-start(bf16[2224,128]{1,0:T(8,128)(2,1)S(1)} %pack_right.1), channel_id=1, source_target_pairs={{0,6},{1,7},{2,0},{3,1},{4,2},{5,3},{6,4},{7,5},{8,14},{9,15},{10,... | collective-permute-start | bytes 1708040 | tf_op jit(solution)/shard_map/ppermute | solution.py:537
  6.7 0.9 %copy-start.3 = (f32[1,1,34,34,4]{3,4,2,1,0:T(4,128)S(1)}, f32[1,1,34,34,4]{3,4,2,1,0:T(4,128)}, u32[]{:S(2)}) copy-start(f32[1,1,34,34,4]{3,4,2,1,0:T(4,128)} %param.10) | copy-start | bytes 55492
  14.1 10.5 %collective-permute-start.3 = (bf16[656,128]{1,0:T(8,128)(2,1)S(1)}, bf16[656,128]{1,0:T(8,128)(2,1)S(1)}, u32[]{:S(2)}, u32[]{:S(2)}) collective-permute-start(bf16[656,128]{1,0:T(8,128)(2,1)S(1)} %get-tuple-element.50), channel_id=1, source_target_pairs={{0,2},{1,3},{2,4},{3,5},{4,6},{5,7},{6,0},{7,1},{8,10},{9,11},{10,... | collective-permute-start | bytes 503816 | tf_op jit(solution)/shard_map/ppermute | solution.py:556
  14.2 4.8 %copy-start.6 = (bf16[1,1,34,128,128]{4,3,2,1,0:T(8,128)(2,1)S(1)}, bf16[1,1,34,128,128]{4,3,2,1,0:T(8,128)(2,1)}, u32[]{:S(2)}) copy-start(bf16[1,1,34,128,128]{4,3,2,1,0:T(8,128)(2,1)} %param.8) | copy-start | bytes 3342340
  14.2 4.8 %copy-start.7 = (f32[1,34,34,4]{2,3,1,0:T(4,128)S(1)}, f32[1,34,34,4]{2,3,1,0:T(4,128)}, u32[]{:S(2)}) copy-start(f32[1,34,34,4]{2,3,1,0:T(4,128)} %param.11) | copy-start | bytes 55492
  17.1 11.8 %collective-permute-start.2 = (bf16[784,128]{1,0:T(8,128)(2,1)S(1)}, bf16[784,128]{1,0:T(8,128)(2,1)S(1)}, u32[]{:S(2)}, u32[]{:S(2)}) collective-permute-start(bf16[784,128]{1,0:T(8,128)(2,1)S(1)} %get-tuple-element.62), channel_id=1, source_target_pairs={{0,2},{1,3},{2,4},{3,5},{4,6},{5,7},{6,0},{7,1},{8,10},{9,11},{10,... | collective-permute-start | bytes 602120 | tf_op jit(solution)/shard_map/ppermute | solution.py:564
  20.4 12.6 %collective-permute-start.7 = (bf16[784,128]{1,0:T(8,128)(2,1)S(1)}, bf16[784,128]{1,0:T(8,128)(2,1)S(1)}, u32[]{:S(2)}, u32[]{:S(2)}) collective-permute-start(bf16[784,128]{1,0:T(8,128)(2,1)S(1)} %get-tuple-element.72), channel_id=1, source_target_pairs={{0,2},{1,3},{2,4},{3,5},{4,6},{5,7},{6,0},{7,1},{8,10},{9,11},{10,... | collective-permute-start | bytes 602120 | tf_op jit(solution)/shard_map/ppermute | solution.py:571
  22.5 8.1 %collective-permute-start.6 = (bf16[2224,128]{1,0:T(8,128)(2,1)S(1)}, bf16[2224,128]{1,0:T(8,128)(2,1)S(1)}, u32[]{:S(2)}, u32[]{:S(2)}) collective-permute-start(bf16[2224,128]{1,0:T(8,128)(2,1)S(1)} %select_select_fusion), channel_id=1, source_target_pairs={{0,1},{1,0},{2,3},{3,2},{4,5},{5,4},{6,7},{7,6},{8,9},{9,8},{10,11... | collective-permute-start | bytes 1708040 | tf_op jit(solution)/shard_map/ppermute | solution.py:574
  24.6 14.9 %collective-permute-start.9 = (bf16[656,128]{1,0:T(8,128)(2,1)S(1)}, bf16[656,128]{1,0:T(8,128)(2,1)S(1)}, u32[]{:S(2)}, u32[]{:S(2)}) collective-permute-start(bf16[656,128]{1,0:T(8,128)(2,1)S(1)} %add_convert_fusion.2.refs_0_), channel_id=1, source_target_pairs={{0,8},{8,16},{16,24},{24,0},{1,9},{9,17},{17,25},{25,1},{2,10},{10... | collective-permute-start | bytes 503816 | tf_op jit(solution)/shard_map/ppermute | solution.py:580
  28.9 7.8 %collective-permute-start.5 = (bf16[784,128]{1,0:T(8,128)(2,1)S(1)}, bf16[784,128]{1,0:T(8,128)(2,1)S(1)}, u32[]{:S(2)}, u32[]{:S(2)}) collective-permute-start(bf16[784,128]{1,0:T(8,128)(2,1)S(1)} %add_convert_fusion.1.refs_1_), channel_id=1, source_target_pairs={{0,8},{8,16},{16,24},{24,0},{1,9},{9,17},{17,25},{25,1},{2,10},{10... | collective-permute-start | bytes 602120 | tf_op jit(solution)/shard_map/ppermute | solution.py:600
  33.0 3.7 %copy-start.1 = (f32[1,4,1,128,128]{4,3,2,1,0:T(8,128)S(1)}, f32[1,4,1,128,128]{4,3,2,1,0:T(8,128)}, u32[]{:S(2)}) copy-start(f32[1,4,1,128,128]{4,3,2,1,0:T(8,128)} %param.12) | copy-start | bytes 786436
  33.0 7.8 %collective-permute-start.8 = (bf16[784,128]{1,0:T(8,128)(2,1)S(1)}, bf16[784,128]{1,0:T(8,128)(2,1)S(1)}, u32[]{:S(2)}, u32[]{:S(2)}) collective-permute-start(bf16[784,128]{1,0:T(8,128)(2,1)S(1)} %add_convert_fusion.refs_2_), channel_id=1, source_target_pairs={{0,8},{8,16},{16,24},{24,0},{1,9},{9,17},{17,25},{25,1},{2,10},{10... | collective-permute-start | bytes 602120 | tf_op jit(solution)/shard_map/ppermute | solution.py:608

commit v12 on v11

--- a/solution.py
+++ b/solution.py
@@ -28,9 +28,9 @@
 
 
 def chunks_of(width):
-    one = width // 6 * 2
-    two = (width - one) // 4 * 2
-    return (0, one), (one, two), (one + two, width - one - two)
+    side = width // 6 * 2
+    middle = width - 2 * side
+    return (0, side), (side, middle), (side + middle, side)
 
 
 def iotas(shape):
@@ -109,16 +109,6 @@
 
 def reader(ref):
     return lambda at, size: ref[at : at + size, :].astype(F32)
-
-
-def unpack_kernel(width, tile, *refs):
-    *part_refs, out_ref, diag = refs
-    for (first, count), ref in zip(chunks_of(width), part_refs):
-
-        def write(w, block, first=first):
-            out_ref[(first + w) * tile : (first + w + 1) * tile, :] = block.astype(BF16)
-
-        unpack_into(count, tile, reader(ref), write, diag)
 
 
 def fold_kernel(
@@ -291,9 +281,11 @@
     return value * inverse, square * inverse
 
 
-def right_products(width, tile, field, right_ref, out_ref, k):
+def right_products(width, tile, field, right_ref, out_ref, k, beside=None):
     lanes = slice(k * tile, (k + 1) * tile)
     for pair in range(width // 2):
+        if beside is not None:
+            beside(pair)
         at = pair * 2 * tile
         both = jnp.dot(field, right_ref[:, at : at + 2 * tile], preferred_element_type=F32).astype(BF16)
         for n in range(2):
@@ -348,9 +340,9 @@
 
 def lanczos_kernel(
     width, tile, dims_ref, packed_ref, environ_ref, early_ref, image_ref, own_ref, next_ref, after_ref,
-    start_a, start_b, norm_a, norm_b, product_a, product_b, basis_ref, stats_ref,
-    late_s, product_s, diag,
+    start_a, start_b, norm_a, norm_b, product_a, product_b, *refs
 ):
+    *fresh_refs, basis_ref, stats_ref, env_ref, late_s, product_s, env_s, diag, env_diag, sem = refs
     states = len(CHARGES)
     sector = lax.axis_index("sec")
     last = chunks_of(width)[-1:]
@@ -360,6 +352,23 @@
     rights = [own_ref.at[0], next_ref.at[0], next_ref.at[1], after_ref.at[0]]
     stats = norm_a[...] + norm_b[...]
     starts = (start_a, start_b)
+    half = tile // 2
+    places = [
+        (ref, w, first + w)
+        for (first, count), ref in zip(chunks_of(width), fresh_refs)
+        for w in range(count)
+    ]
+    for (first, count), ref in zip(chunks_of(width), fresh_refs):
+        env_diag[first : first + count, :] = ref[count * half :, :].astype(F32)[:count]
+    copy = pltpu.make_async_copy(env_s, env_ref, sem)
+
+    def unpack_one(n):
+        ref, w, to = places[n]
+        folded = ref[w * half : (w + 1) * half, :].astype(F32)
+        env_s[to * tile : (to + 1) * tile, :] = unpack_block(
+            folded, env_diag[to : to + 1, :]
+        ).astype(BF16)
+
     split = last[0][0] * tile
     betas = [None] * states
     for j in range(LANCZOS):
@@ -371,7 +380,15 @@
                 source = product_s.at[group]
                 for k, p in enumerate(members):
                     field = basis_ref[j - 1, p].astype(BF16)
-                    right_products(width, tile, field, rights[p], source, k)
+                    beside = None
+                    if j == 1 and k == 0:
+
+                        def beside(pair, base=group * width // 2):
+                            unpack_one(base + pair)
+
+                    right_products(width, tile, field, rights[p], source, k, beside)
+                if j == 1 and group + 1 == len(GROUPS):
+                    copy.start()
                 images = jnp.dot(early_ref[...], source[:split, :], preferred_element_type=F32)
             images = images + jnp.dot(late_s[...], source[split:, :], preferred_element_type=F32)
             for k, p in enumerate(members):
@@ -389,6 +406,7 @@
                 stats = put(stats, 1 + 2 * j, sector * states + p, alpha)
                 stats = put(stats, 2 + 2 * j, sector * states + p, beta)
     stats_ref[...] = stats
+    copy.wait()
 
 
 def finish_kernel(
@@ -465,13 +483,13 @@
     return pl.BlockSpec(memory_space=pltpu.VMEM)
 
 
-def call(name, kernel, scalars, arrays, outs, scratch, limit, micros):
+def call(name, kernel, scalars, arrays, outs, scratch, limit, micros, out_specs=None):
     many = isinstance(outs, (tuple, list))
     return pl.pallas_call(
         kernel,
         out_shape=outs,
         in_specs=[smem()] * len(scalars) + [vmem()] * len(arrays),
-        out_specs=[vmem()] * len(outs) if many else vmem(),
+        out_specs=out_specs or ([vmem()] * len(outs) if many else vmem()),
         scratch_shapes=scratch,
         compiler_params=pltpu.CompilerParams(vmem_limit_bytes=limit * MIB),
         name=name,
@@ -595,25 +613,20 @@
             [], 9, 0.5,
         )
 
-    middle_arrived, after_mixed = lax.optimization_barrier((middle_arrived, after_mixed))
+    start_a, norms_a, products_a = head(GROUPS[0], [own_mixed, after_mixed])
+    middle_arrived, products_a = lax.optimization_barrier((middle_arrived, products_a))
     middle = carried(kept[1], middle_arrived)
     middle_bound = lax.ppermute(middle, "seg", onward)
-    middle, right_near = lax.optimization_barrier((middle, right_near))
+    middle, late_arrived = lax.optimization_barrier((middle, late_arrived))
+    late = carried(kept[2], late_arrived)
+    late_bound = lax.ppermute(late, "seg", onward)
+    late, right_near = lax.optimization_barrier((late, right_near))
     next_mixed = call(
         "mix_next", functools.partial(mix_next_kernel, width, tile), [],
         [right_near, bound_weights], mixed(2), mix_scratch(2) + [diag], 16, 3,
     )
-    late_arrived, next_mixed = lax.optimization_barrier((late_arrived, next_mixed))
-    late = carried(kept[2], late_arrived)
-    late_bound = lax.ppermute(late, "seg", onward)
-    late, next_mixed, after_mixed = lax.optimization_barrier((late, next_mixed, after_mixed))
-    start_a, norms_a, products_a = head(GROUPS[0], [own_mixed, after_mixed])
     start_b, norms_b, products_b = head(GROUPS[1], [next_mixed])
-    new_env = call(
-        "unpack_env", functools.partial(unpack_kernel, width, tile), [], [early, middle, late],
-        jax.ShapeDtypeStruct((width * tile, tile), BF16), [diag], 6, 2,
-    )
-    middle_bound, new_env = lax.optimization_barrier((middle_bound, new_env))
+    middle_bound, products_b = lax.optimization_barrier((middle_bound, products_b))
     bound, image = call(
         "open", functools.partial(open_kernel, width, tile), [],
         [environ, early_bound, middle_bound, products_a, products_b],
@@ -624,21 +637,25 @@
         [diag], 12, 1,
     )
     late_bound, bound = lax.optimization_barrier((late_bound, bound))
-    basis, stats = call(
+    basis, stats, new_env = call(
         "lanczos", functools.partial(lanczos_kernel, width, tile),
         [sector_dims],
         [late_bound, environ, bound, image, own_mixed, next_mixed, after_mixed, start_a, start_b,
-         norms_a, norms_b, products_a, products_b],
+         norms_a, norms_b, products_a, products_b, early, middle, late],
         (
             jax.ShapeDtypeStruct((LANCZOS, states, tile, tile), F32),
             jax.ShapeDtypeStruct((16, 128), F32),
+            jax.ShapeDtypeStruct((width * tile, tile), BF16),
         ),
         [
             pltpu.VMEM((tile, parts[-1][1] * tile), BF16),
             pltpu.VMEM((len(GROUPS), width * tile, 2 * tile), BF16),
+            pltpu.VMEM((width * tile, tile), BF16),
             diag,
+            diag,
+            pltpu.SemaphoreType.DMA,
         ],
-        22, 12,
+        24, 12, [vmem(), vmem(), pl.BlockSpec(memory_space=pltpu.HBM)],
     )
     stats = gathered(stats, "sec")
     entries = float(states * sector_count * tile * tile)

time: 57.7 us -> 59.1 us (1.024)
  waiting for transfers between devices: 3.5 us -> 5.57 us
    ppermute x1, waiting for transfers between devices: 0.01 us -> 1.25 us  [on_device(): middle_bound = lax.ppermute(middle, 'seg', onward)]
    ppermute x1, waiting for transfers between devices: 0.01 us -> 1.02 us  [on_device(): late_arrived = lax.ppermute(late_outgoing, 'sec', up_two)]
    ppermute x1, waiting for transfers between devices: 0.85 us -> 0.14 us  [on_device(): middle_arrived = lax.ppermute(middle_outgoing, 'sec', up_two)]
    pallas_call x12 -> x11, Pallas kernels: 29.3 us -> 28.9 us  [call(): pl.pallas_call(kernel, out_shape=outs, in_specs=[smem()] * len(scalars) +...]
  transfers between devices with their start and end apart: 10 -> 10, of which waited for: 3 -> 5; matrix products, arithmetic and copies ran while one was open for 0% -> 0% of each run, Pallas kernels for 35% -> 32%
where the time goes in v12:
time: 59.1 us; the launch traced here: 58.9 us
  Pallas kernels  28.9 us (49%)
  starting transfers between devices  13.6 us (23%)
  blocking collectives  7.58 us (13%)
  waiting for transfers between devices  5.57 us (9%)
  local copies, waits for them, and re-layouts  2.16 us (4%)
  between operations  0.79 us (1%)
    pallas_call x11, Pallas kernels, call(): pl.pallas_call(kernel, out_shape=outs, in_specs=[smem()] * len(scalars) +...  28.9 us
    all_to_all x1, blocking collectives, gathered(): lax.all_to_all(jnp.broadcast_to(value, (count,) + value.shape), axis, 0, 0)  7.58 us
    ppermute x1, starting transfers between devices, on_device(): right_far = lax.ppermute(right_packed, 'sec', down_two)  3.93 us
    unnamed x16, local copies, waits for them, and re-layouts  2.15 us
    ppermute x1, starting transfers between devices, on_device(): late_arrived = lax.ppermute(late_outgoing, 'sec', up_two)  2.05 us
    ppermute x1, waiting for transfers between devices, on_device(): early_arrived = lax.ppermute(outgoing[0], 'sec', up_two)  2.02 us
    ppermute x1, starting transfers between devices, on_device(): middle_arrived = lax.ppermute(middle_outgoing, 'sec', up_two)  1.96 us
    ppermute x1, starting transfers between devices, on_device(): middle_bound = lax.ppermute(middle, 'seg', onward)  1.63 us
  transfers between devices with their start and end apart: 10, of which 5 were waited for; matrix products, arithmetic and copies ran while one was open for 0% of the time, Pallas kernels for 32%

profile of v12, /device:TPU:0, one launch (start us, length us, event | category | flops | bytes accessed | tf_op | source)
XLA Modules:
  0.0 58.9 jit_solution(10324648653897625139)
XLA Ops:
  0.6 0.5 collective-permute-start
  1.1 0.1 collective-permute-start.1
  1.2 0.0 copy-start.5
  1.2 1.2 %copy-done.5 = bf16[1,1,34,128,128]{4,3,2,1,0:T(8,128)(2,1)S(1)} copy-done((bf16[1,1,34,128,128]{4,3,2,1,0:T(8,128)(2,1)S(1)}, bf16[1,1,34,128,128]{4,3,2,1,0:T(8,128)(2,1)}, u32[]{:S(2)}) %copy-start.5) | copy-done | bytes 1114136
  2.5 0.0 copy-start
  2.5 0.0 copy-start.2
  2.5 0.0 copy-start.4
  2.5 0.3 pack_right.1
  2.8 3.9 %collective-permute-start.3 = (bf16[2224,128]{1,0:T(8,128)(2,1)S(1)}, bf16[2224,128]{1,0:T(8,128)(2,1)S(1)}, u32[]{:S(2)}, u32[]{:S(2)}) collective-permute-start(bf16[2224,128]{1,0:T(8,128)(2,1)S(1)} %pack_right.1), channel_id=1, source_target_pairs={{0,6},{1,7},{2,0},{3,1},{4,2},{5,3},{6,4},{7,5},{8,14},{9,15},{10,... | collective-permute-start | bytes 1708040 | tf_op jit(solution)/shard_map/ppermute | solution.py:555
  6.7 0.0 collective-permute-done.1.far_site_ref
  6.7 0.0 collective-permute-done.far_environ_ref
  6.7 0.0 copy-done
  6.7 0.0 copy-done.2
  6.7 0.0 copy-done.4
  6.7 0.0 copy-start.3
  6.7 0.9 %copy-done.3 = f32[1,1,34,34,4]{3,4,2,1,0:T(4,128)S(1)} copy-done((f32[1,1,34,34,4]{3,4,2,1,0:T(4,128)S(1)}, f32[1,1,34,34,4]{3,4,2,1,0:T(4,128)}, u32[]{:S(2)}) %copy-start.3) | copy-done | bytes 18520
  7.6 6.5 %fold_up.1 = (bf16[656,128]{1,0:T(8,128)(2,1)S(1)}, bf16[912,128]{1,0:T(8,128)(2,1)S(1)}, bf16[656,128]{1,0:T(8,128)(2,1)S(1)}) custom-call(s32[8]{0:T(128)S(1)} %copy-done.4, bf16[4352,128]{1,0:T(8,128)(2,1)S(1)} %bitcast.22, bf16[4,128,128]{2,1,0:T(8,128)(2,1)S(1)} %bitcast.29, bf16[4352,128]{1,0:T(8,128)(2,1)S(1)} %collective-permute-done.far_environ_ref, ...), custom_call_target="tpu_custom_call" | custom-call | flops 13200000000 | tf_op jit(solution)/shard_map/fold_up/pallas_call | solution.py:488
  14.1 0.1 collective-permute-start.4
  14.2 0.0 copy-start.6
  14.2 0.0 copy-start.7
  14.2 2.8 %fold_own.1 = (f32[656,128]{1,0:T(8,128)S(1)}, f32[912,128]{1,0:T(8,128)S(1)}, f32[656,128]{1,0:T(8,128)S(1)}) custom-call(s32[8]{0:T(128)S(1)} %copy-done.4, bf16[4352,128]{1,0:T(8,128)(2,1)S(1)} %bitcast.23, bf16[4,128,128]{2,1,0:T(8,128)(2,1)S(1)} %bitcast.30, bf16[4352,128]{1,0:T(8,128)(2,1)S(1)} %collective-permute-done.far_environ_ref, ...), custom_call_target="tpu_custom_call" | custom-call | flops 110000000 | tf_op jit(solution)/shard_map/fold_own/pallas_call | solution.py:488
  17.1 2.0 %collective-permute-start.2 = (bf16[912,128]{1,0:T(8,128)(2,1)S(1)}, bf16[912,128]{1,0:T(8,128)(2,1)S(1)}, u32[]{:S(2)}, u32[]{:S(2)}) collective-permute-start(bf16[912,128]{1,0:T(8,128)(2,1)S(1)} %get-tuple-element.61), channel_id=1, source_target_pairs={{0,2},{1,3},{2,4},{3,5},{4,6},{5,7},{6,0},{7,1},{8,10},{9,11},{10,... | collective-permute-start | bytes 700424 | tf_op jit(solution)/shard_map/ppermute | solution.py:582
  19.0 0.0 copy-done.6
  19.0 0.0 copy-done.7
  19.0 1.3 %mix_own.1.refs_0_.own_ref = bf16[1,128,4352]{2,1,0:T(8,128)(2,1)S(1)} custom-call(bf16[4352,128]{1,0:T(8,128)(2,1)S(1)} %bitcast.34, f32[136,34]{1,0:T(8,128)S(1)} %bitcast.35), custom_call_target="tpu_custom_call" | custom-call | flops 1100000000 | tf_op jit(solution)/shard_map/mix_own/pallas_call | solution.py:488
  20.3 0.0 collective-permute-done.3.far_ref
  20.3 2.0 %collective-permute-start.5 = (bf16[656,128]{1,0:T(8,128)(2,1)S(1)}, bf16[656,128]{1,0:T(8,128)(2,1)S(1)}, u32[]{:S(2)}, u32[]{:S(2)}) collective-permute-start(bf16[656,128]{1,0:T(8,128)(2,1)S(1)} %get-tuple-element.70), channel_id=1, source_target_pairs={{0,2},{1,3},{2,4},{3,5},{4,6},{5,7},{6,0},{7,1},{8,10},{9,11},{10,... | collective-permute-start | bytes 503816 | tf_op jit(solution)/shard_map/ppermute | solution.py:589
  22.4 0.1 select_select_fusion
  22.5 0.1 collective-permute-start.9
  22.5 2.0 %collective-permute-done.4 = bf16[656,128]{1,0:T(8,128)(2,1)S(1)} collective-permute-done((bf16[656,128]{1,0:T(8,128)(2,1)S(1)}, bf16[656,128]{1,0:T(8,128)(2,1)S(1)}, u32[]{:S(2)}, u32[]{:S(2)}) %collective-permute-start.4) | collective-permute-done | bytes 167968 | tf_op jit(solution)/shard_map/ppermute | solution.py:574
  24.6 0.1 add_convert_fusion.2.refs_0_
  24.6 0.0 copy-start.1
  24.6 1.6 %collective-permute-start.7 = (bf16[656,128]{1,0:T(8,128)(2,1)S(1)}, bf16[656,128]{1,0:T(8,128)(2,1)S(1)}, u32[]{:S(2)}, u32[]{:S(2)}) collective-permute-start(bf16[656,128]{1,0:T(8,128)(2,1)S(1)} %add_convert_fusion.2.refs_0_), channel_id=1, source_target_pairs={{0,8},{8,16},{16,24},{24,0},{1,9},{9,17},{17,25},{25,1},{2,10},{10... | collective-permute-start | bytes 503816 | tf_op jit(solution)/shard_map/ppermute | solution.py:598
  26.3 1.8 %mix_after.1.refs_1_.after_ref = bf16[1,128,4352]{2,1,0:T(8,128)(2,1)S(1)} custom-call(bf16[2224,128]{1,0:T(8,128)(2,1)S(1)} %collective-permute-done.3.far_ref, f32[136,34]{1,0:T(8,128)S(1)} %bitcast.36), custom_call_target="tpu_custom_call" | custom-call | flops 2200000000 | tf_op jit(solution)/shard_map/mix_after/pallas_call | solution.py:488
  28.0 0.0 copy-done.1
  28.0 1.4 %head.2 = (f32[2,128,128]{2,1,0:T(8,128)S(1)}, f32[16,128]{1,0:T(8,128)S(1)}, bf16[4352,256]{1,0:T(8,128)(2,1)S(1)}) custom-call(s32[8]{0:T(128)S(1)} %copy-done.4, f32[4,128,128]{2,1,0:T(8,128)S(1)} %bitcast.26, bf16[1,128,4352]{2,1,0:T(8,128)(2,1)S(1)} %mix_own.1.refs_0_.own_ref, bf16[1,128,4352]{2,1,0:T(8,128)(2,1)S(1)} %mix_after.1.refs_1_.after_ref), custom_call_target="tpu_custom_call" | custom-call | flops 550000000 | tf_op jit(solution)/shard_map/head/pallas_call | solution.py:488
  29.4 0.1 collective-permute-done.2
  29.6 0.1 add_convert_fusion.refs_1_
  29.6 1.6 %collective-permute-start.8 = (bf16[912,128]{1,0:T(8,128)(2,1)S(1)}, bf16[912,128]{1,0:T(8,128)(2,1)S(1)}, u32[]{:S(2)}, u32[]{:S(2)}) collective-permute-start(bf16[912,128]{1,0:T(8,128)(2,1)S(1)} %add_convert_fusion.refs_1_), channel_id=1, source_target_pairs={{0,8},{8,16},{16,24},{24,0},{1,9},{9,17},{17,25},{25,1},{2,10},{10... | collective-permute-start | bytes 700424 | tf_op jit(solution)/shard_map/ppermute | solution.py:619
  31.3 1.0 %collective-permute-done.5 = bf16[656,128]{1,0:T(8,128)(2,1)S(1)} collective-permute-done((bf16[656,128]{1,0:T(8,128)(2,1)S(1)}, bf16[656,128]{1,0:T(8,128)(2,1)S(1)}, u32[]{:S(2)}, u32[]{:S(2)}) %collective-permute-start.5) | collective-permute-done | bytes 167968 | tf_op jit(solution)/shard_map/ppermute | solution.py:589
  32.3 0.1 add_convert_fusion.1.refs_2_
  32.3 1.6 %collective-permute-start.6 = (bf16[656,128]{1,0:T(8,128)(2,1)S(1)}, bf16[656,128]{1,0:T(8,128)(2,1)S(1)}, u32[]{:S(2)}, u32[]{:S(2)}) collective-permute-start(bf16[656,128]{1,0:T(8,128)(2,1)S(1)} %add_convert_fusion.1.refs_2_), channel_id=1, source_target_pairs={{0,8},{8,16},{16,24},{24,0},{1,9},{9,17},{17,25},{25,1},{2,10},{10... | collective-permute-start | bytes 503816 | tf_op jit(solution)/shard_map/ppermute | solution.py:622
  34.0 0.0 collective-permute-done.9.near_ref
  34.0 2.4 %mix_next.1.refs_0_.next_ref = bf16[2,128,4352]{2,1,0:T(8,128)(2,1)S(1)} custom-call(bf16[2224,128]{1,0:T(8,128)(2,1)S(1)} %collective-permute-done.9.near_ref, f32[136,34]{1,0:T(8,128)S(1)} %bitcast.37), custom_call_target="tpu_custom_call" | custom-call | flops 3300000000 | tf_op jit(solution)/shard_map/mix_next/pallas_call | solution.py:488
  36.4 1.4 %head.3 = (f32[2,128,128]{2,1,0:T(8,128)S(1)}, f32[16,128]{1,0:T(8,128)S(1)}, bf16[4352,256]{1,0:T(8,128)(2,1)S(1)}) custom-call(s32[8]{0:T(128)S(1)} %copy-done.4, f32[4,128,128]{2,1,0:T(8,128)S(1)} %bitcast.27, bf16[2,128,4352]{2,1,0:T(8,128)(2,1)S(1)} %mix_next.1.refs_0_.next_ref), custom_call_target="tpu_custom_call" | custom-call | flops 550000000 | tf_op jit(solution)/shard_map/head/pallas_call | solution.py:488
  37.8 1.2 %collective-permute-done.8.refs_1_ = bf16[912,128]{1,0:T(8,128)(2,1)S(1)} collective-permute-done((bf16[912,128]{1,0:T(8,128)(2,1)S(1)}, bf16[912,128]{1,0:T(8,128)(2,1)S(1)}, u32[]{:S(2)}, u32[]{:S(2)}) %collective-permute-start.8) | collective-permute-done | bytes 233504 | tf_op jit(solution)/shard_map/ppermute | solution.py:619
  39.0 0.0 collective-permute-done.7.refs_0_
  39.0 1.0 %open.1 = (bf16[128,3072]{1,0:T(8,128)(2,1)S(1)}, f32[2,128,256]{2,1,0:T(8,128)S(1)}) custom-call(bf16[4352,128]{1,0:T(8,128)(2,1)S(1)} %bitcast.24, bf16[656,128]{1,0:T(8,128)(2,1)S(1)} %collective-permute-done.7.refs_0_, bf16[912,128]{1,0:T(8,128)(2,1)S(1)} %collective-permute-done.8.refs_1_, bf16[4352,256]{1,0:T(8,128)(2,1)S(1)} %get-tuple-element.75.refs_2_.product_a, ...), custom_call_target="tpu_custom_call" | custom-call | flops 1100000000 | tf_op jit(solution)/shard_map/open/pallas_call | solution.py:488
  40.0 1.1 %collective-permute-done.6.packed_ref = bf16[656,128]{1,0:T(8,128)(2,1)S(1)} collective-permute-done((bf16[656,128]{1,0:T(8,128)(2,1)S(1)}, bf16[656,128]{1,0:T(8,128)(2,1)S(1)}, u32[]{:S(2)}, u32[]{:S(2)}) %collective-permute-start.6) | collective-permute-done | bytes 167968 | tf_op jit(solution)/shard_map/ppermute | solution.py:622
  41.2 8.7 %lanczos.1 = (f32[4,4,128,128]{3,2,1,0:T(8,128)S(1)}, f32[16,128]{1,0:T(8,128)S(1)}, bf16[4352,128]{1,0:T(8,128)(2,1)}) custom-call(s32[8]{0:T(128)S(1)} %copy-done.4, bf16[656,128]{1,0:T(8,128)(2,1)S(1)} %collective-permute-done.6.packed_ref, bf16[4352,128]{1,0:T(8,128)(2,1)S(1)} %bitcast.25, bf16[128,3072]{1,0:T(8,128)(2,1)S(1)} %get-tuple-element.79.early_ref, ...), custom_call_target="tpu_custom_call" | custom-call | flops 13200000000 | tf_op jit(solution)/shard_map/lanczos/pallas_call | solution.py:488
  49.9 7.6 %all_to_all.5.stats_ref = f32[8,16,128]{2,1,0:T(8,128)S(1)} all-to-all(f32[8,16,128]{2,1,0:T(8,128)S(1)} %broadcast_in_dim.24), channel_id=1, replica_groups=mesh['seg'=4,'sec'=8] {'sec'}, dimensions={0} | all-to-all | bytes 131072 | tf_op jit(solution)/shard_map/all_to_all | solution.py:508
  57.5 1.4 %finish.1 = (f32[4,128,128]{2,1,0:T(8,128)}, f32[2,4]{1,0:T(2,128)}) custom-call(f32[8,16,128]{2,1,0:T(8,128)S(1)} %all_to_all.5.stats_ref, f32[2,128,128]{2,1,0:T(8,128)S(1)} %get-tuple-element.81.start_a, f32[2,128,128]{2,1,0:T(8,128)S(1)} %get-tuple-element.82.start_b, f32[4,4,128,128]{3,2,1,0:T(8,128)S(1)} %get-tuple-element.90.basis_ref), custom_call_target="tpu_custom_call" | custom-call | flops 2200000000 | tf_op jit(solution)/shard_map/finish/pallas_call | solution.py:488
  (1 shorter events, 0.0 us)
Async XLA Ops:
  0.6 6.1 %collective-permute-start = (bf16[4352,128]{1,0:T(8,128)(2,1)}, bf16[4352,128]{1,0:T(8,128)(2,1)S(1)}, u32[]{:S(2)}, u32[]{:S(2)}) collective-permute-start(bf16[4352,128]{1,0:T(8,128)(2,1)} %bitcast.21), channel_id=1, source_target_pairs={{0,1},{1,0},{2,3},{3,2},{4,5},{5,4},{6,7},{7,6},{8,9},{9,8},{10,11... | collective-permute-start | bytes 3342344 | tf_op jit(solution)/shard_map/ppermute | solution.py:556
  1.1 5.6 %collective-permute-start.1 = (bf16[4,128,128]{2,1,0:T(8,128)(2,1)}, bf16[4,128,128]{2,1,0:T(8,128)(2,1)}, u32[]{:S(2)}, u32[]{:S(2)}) collective-permute-start(bf16[4,128,128]{2,1,0:T(8,128)(2,1)} %bitcast.28), channel_id=1, source_target_pairs={{0,1},{1,0},{2,3},{3,2},{4,5},{5,4},{6,7},{7,6},{8,9},{9,8},{10,11... | collective-permute-start | bytes 393224 | tf_op jit(solution)/shard_map/ppermute | solution.py:557
  1.2 1.2 %copy-start.5 = (bf16[1,1,34,128,128]{4,3,2,1,0:T(8,128)(2,1)S(1)}, bf16[1,1,34,128,128]{4,3,2,1,0:T(8,128)(2,1)}, u32[]{:S(2)}) copy-start(bf16[1,1,34,128,128]{4,3,2,1,0:T(8,128)(2,1)} %param.8) | copy-start | bytes 3342340
  2.5 4.2 %copy-start = (bf16[1,1,34,128,128]{4,3,2,1,0:T(8,128)(2,1)S(1)}, bf16[1,1,34,128,128]{4,3,2,1,0:T(8,128)(2,1)}, u32[]{:S(2)}) copy-start(bf16[1,1,34,128,128]{4,3,2,1,0:T(8,128)(2,1)} %param.7) | copy-start | bytes 3342340
  2.5 4.2 %copy-start.2 = (bf16[1,1,4,1,128,128]{5,4,3,2,1,0:T(8,128)(2,1)S(1)}, bf16[1,1,4,1,128,128]{5,4,3,2,1,0:T(8,128)(2,1)}, u32[]{:S(2)}) copy-start(bf16[1,1,4,1,128,128]{5,4,3,2,1,0:T(8,128)(2,1)} %param.9) | copy-start | bytes 393220
  2.5 4.2 %copy-start.4 = (s32[8]{0:T(128)S(1)}, s32[8]{0:T(128)}, u32[]{:S(2)}) copy-start(s32[8]{0:T(128)} %dims_ref.9) | copy-start | bytes 100
  2.8 17.6 %collective-permute-start.3 = (bf16[2224,128]{1,0:T(8,128)(2,1)S(1)}, bf16[2224,128]{1,0:T(8,128)(2,1)S(1)}, u32[]{:S(2)}, u32[]{:S(2)}) collective-permute-start(bf16[2224,128]{1,0:T(8,128)(2,1)S(1)} %pack_right.1), channel_id=1, source_target_pairs={{0,6},{1,7},{2,0},{3,1},{4,2},{5,3},{6,4},{7,5},{8,14},{9,15},{10,... | collective-permute-start | bytes 1708040 | tf_op jit(solution)/shard_map/ppermute | solution.py:555
  6.7 0.9 %copy-start.3 = (f32[1,1,34,34,4]{3,4,2,1,0:T(4,128)S(1)}, f32[1,1,34,34,4]{3,4,2,1,0:T(4,128)}, u32[]{:S(2)}) copy-start(f32[1,1,34,34,4]{3,4,2,1,0:T(4,128)} %param.10) | copy-start | bytes 55492
  14.1 10.4 %collective-permute-start.4 = (bf16[656,128]{1,0:T(8,128)(2,1)S(1)}, bf16[656,128]{1,0:T(8,128)(2,1)S(1)}, u32[]{:S(2)}, u32[]{:S(2)}) collective-permute-start(bf16[656,128]{1,0:T(8,128)(2,1)S(1)} %get-tuple-element.48), channel_id=1, source_target_pairs={{0,2},{1,3},{2,4},{3,5},{4,6},{5,7},{6,0},{7,1},{8,10},{9,11},{10,... | collective-permute-start | bytes 503816 | tf_op jit(solution)/shard_map/ppermute | solution.py:574
  14.2 4.8 %copy-start.6 = (bf16[1,1,34,128,128]{4,3,2,1,0:T(8,128)(2,1)S(1)}, bf16[1,1,34,128,128]{4,3,2,1,0:T(8,128)(2,1)}, u32[]{:S(2)}) copy-start(bf16[1,1,34,128,128]{4,3,2,1,0:T(8,128)(2,1)} %param.8) | copy-start | bytes 3342340
  14.2 4.8 %copy-start.7 = (f32[1,34,34,4]{2,3,1,0:T(4,128)S(1)}, f32[1,34,34,4]{2,3,1,0:T(4,128)}, u32[]{:S(2)}) copy-start(f32[1,34,34,4]{2,3,1,0:T(4,128)} %param.11) | copy-start | bytes 55492
  17.1 12.5 %collective-permute-start.2 = (bf16[912,128]{1,0:T(8,128)(2,1)S(1)}, bf16[912,128]{1,0:T(8,128)(2,1)S(1)}, u32[]{:S(2)}, u32[]{:S(2)}) collective-permute-start(bf16[912,128]{1,0:T(8,128)(2,1)S(1)} %get-tuple-element.61), channel_id=1, source_target_pairs={{0,2},{1,3},{2,4},{3,5},{4,6},{5,7},{6,0},{7,1},{8,10},{9,11},{10,... | collective-permute-start | bytes 700424 | tf_op jit(solution)/shard_map/ppermute | solution.py:582
  20.3 11.9 %collective-permute-start.5 = (bf16[656,128]{1,0:T(8,128)(2,1)S(1)}, bf16[656,128]{1,0:T(8,128)(2,1)S(1)}, u32[]{:S(2)}, u32[]{:S(2)}) collective-permute-start(bf16[656,128]{1,0:T(8,128)(2,1)S(1)} %get-tuple-element.70), channel_id=1, source_target_pairs={{0,2},{1,3},{2,4},{3,5},{4,6},{5,7},{6,0},{7,1},{8,10},{9,11},{10,... | collective-permute-start | bytes 503816 | tf_op jit(solution)/shard_map/ppermute | solution.py:589
  22.5 11.5 %collective-permute-start.9 = (bf16[2224,128]{1,0:T(8,128)(2,1)S(1)}, bf16[2224,128]{1,0:T(8,128)(2,1)S(1)}, u32[]{:S(2)}, u32[]{:S(2)}) collective-permute-start(bf16[2224,128]{1,0:T(8,128)(2,1)S(1)} %select_select_fusion), channel_id=1, source_target_pairs={{0,1},{1,0},{2,3},{3,2},{4,5},{5,4},{6,7},{7,6},{8,9},{9,8},{10,11... | collective-permute-start | bytes 1708040 | tf_op jit(solution)/shard_map/ppermute | solution.py:592
  24.6 3.4 %copy-start.1 = (f32[1,4,1,128,128]{4,3,2,1,0:T(8,128)S(1)}, f32[1,4,1,128,128]{4,3,2,1,0:T(8,128)}, u32[]{:S(2)}) copy-start(f32[1,4,1,128,128]{4,3,2,1,0:T(8,128)} %param.12) | copy-start | bytes 786436
  24.6 14.4 %collective-permute-start.7 = (bf16[656,128]{1,0:T(8,128)(2,1)S(1)}, bf16[656,128]{1,0:T(8,128)(2,1)S(1)}, u32[]{:S(2)}, u32[]{:S(2)}) collective-permute-start(bf16[656,128]{1,0:T(8,128)(2,1)S(1)} %add_convert_fusion.2.refs_0_), channel_id=1, source_target_pairs={{0,8},{8,16},{16,24},{24,0},{1,9},{9,17},{17,25},{25,1},{2,10},{10... | collective-permute-start | bytes 503816 | tf_op jit(solution)/shard_map/ppermute | solution.py:598
  29.6 9.4 %collective-permute-start.8 = (bf16[912,128]{1,0:T(8,128)(2,1)S(1)}, bf16[912,128]{1,0:T(8,128)(2,1)S(1)}, u32[]{:S(2)}, u32[]{:S(2)}) collective-permute-start(bf16[912,128]{1,0:T(8,128)(2,1)S(1)} %add_convert_fusion.refs_1_), channel_id=1, source_target_pairs={{0,8},{8,16},{16,24},{24,0},{1,9},{9,17},{17,25},{25,1},{2,10},{10... | collective-permute-start | bytes 700424 | tf_op jit(solution)/shard_map/ppermute | solution.py:619
  32.3 8.8 %collective-permute-start.6 = (bf16[656,128]{1,0:T(8,128)(2,1)S(1)}, bf16[656,128]{1,0:T(8,128)(2,1)S(1)}, u32[]{:S(2)}, u32[]{:S(2)}) collective-permute-start(bf16[656,128]{1,0:T(8,128)(2,1)S(1)} %add_convert_fusion.1.refs_2_), channel_id=1, source_target_pairs={{0,8},{8,16},{16,24},{24,0},{1,9},{9,17},{17,25},{25,1},{2,10},{10... | collective-permute-start | bytes 503816 | tf_op jit(solution)/shard_map/ppermute | solution.py:622

commit v13 on v11

--- a/solution.py
+++ b/solution.py
@@ -28,9 +28,8 @@
 
 
 def chunks_of(width):
-    one = width // 6 * 2
-    two = (width - one) // 4 * 2
-    return (0, one), (one, two), (one + two, width - one - two)
+    side = width // 6 * 2
+    return (0, side), (side, side), (2 * side, width - 2 * side)
 
 
 def iotas(shape):
@@ -52,7 +51,7 @@
     half, tile = folded.shape
     row, lane = iotas((half, tile))
     rolled = pltpu.roll(folded, half, 1)
-    turned = jnp.transpose(jnp.concatenate([folded, rolled], axis=0))
+    turned = jnp.transpose(jnp.concatenate([folded, rolled], axis=0).astype(BF16)).astype(F32)
     top = jnp.where((lane < half) & (row > lane), turned[:half], folded)
     low = jnp.where((lane >= half) & (row > lane - half), rolled, turned[half:])
     low = jnp.where(lane == row + half, diagonal, low)
@@ -300,19 +299,22 @@
             out_ref[at + n * tile : at + (n + 1) * tile, lanes] = both[:, n * tile : (n + 1) * tile]
 
 
-def head_kernel(members, width, tile, dims_ref, guess_ref, *refs):
-    *right_refs, vector_ref, stats_ref, product_ref = refs
-    rights = [ref.at[n] for ref in right_refs for n in range(ref.shape[0])]
+def head_kernel(
+    width, tile, dims_ref, guess_ref, own_ref, next_ref, after_ref,
+    start_a, start_b, stats_ref, product_a, product_b,
+):
+    rights = [own_ref.at[0], next_ref.at[0], next_ref.at[1], after_ref.at[0]]
     sector = lax.axis_index("sec")
     rows, columns = live_limits(dims_ref, sector)
     row, lane = iotas((tile, tile))
     stats = jnp.zeros(stats_ref.shape, F32)
-    for k, p in enumerate(members):
-        live = (row < rows) & (lane < columns[p])
-        vector, norm = scaled(jnp.where(live, guess_ref[p], 0.0))
-        vector_ref[k] = vector
-        stats = put(stats, 0, sector * len(CHARGES) + p, norm)
-        right_products(width, tile, vector.astype(BF16), rights[k], product_ref, k)
+    for members, start_ref, product_ref in zip(GROUPS, (start_a, start_b), (product_a, product_b)):
+        for k, p in enumerate(members):
+            live = (row < rows) & (lane < columns[p])
+            vector, norm = scaled(jnp.where(live, guess_ref[p], 0.0))
+            start_ref[k] = vector
+            stats = put(stats, 0, sector * len(CHARGES) + p, norm)
+            right_products(width, tile, vector.astype(BF16), rights[p], product_ref, k)
     stats_ref[...] = stats
 
 
@@ -348,7 +350,7 @@
 
 def lanczos_kernel(
     width, tile, dims_ref, packed_ref, environ_ref, early_ref, image_ref, own_ref, next_ref, after_ref,
-    start_a, start_b, norm_a, norm_b, product_a, product_b, basis_ref, stats_ref,
+    start_a, start_b, norm_ref, product_a, product_b, basis_ref, stats_ref,
     late_s, product_s, diag,
 ):
     states = len(CHARGES)
@@ -358,7 +360,7 @@
     rows, columns = live_limits(dims_ref, sector)
     row, lane = iotas((tile, tile))
     rights = [own_ref.at[0], next_ref.at[0], next_ref.at[1], after_ref.at[0]]
-    stats = norm_a[...] + norm_b[...]
+    stats = norm_ref[...]
     starts = (start_a, start_b)
     split = last[0][0] * tile
     betas = [None] * states
@@ -583,18 +585,6 @@
         "mix_after", functools.partial(mix_after_kernel, width, tile), [],
         [right_far, bound_weights], mixed(1), mix_scratch(1) + [diag], 12, 2,
     )
-    def head(members, rights):
-        return call(
-            "head", functools.partial(head_kernel, members, width, tile),
-            [sector_dims], [guess[0, :, 0]] + rights,
-            (
-                jax.ShapeDtypeStruct((2, tile, tile), F32),
-                jax.ShapeDtypeStruct((16, 128), F32),
-                jax.ShapeDtypeStruct((width * tile, 2 * tile), BF16),
-            ),
-            [], 9, 0.5,
-        )
-
     middle_arrived, after_mixed = lax.optimization_barrier((middle_arrived, after_mixed))
     middle = carried(kept[1], middle_arrived)
     middle_bound = lax.ppermute(middle, "seg", onward)
@@ -607,8 +597,14 @@
     late = carried(kept[2], late_arrived)
     late_bound = lax.ppermute(late, "seg", onward)
     late, next_mixed, after_mixed = lax.optimization_barrier((late, next_mixed, after_mixed))
-    start_a, norms_a, products_a = head(GROUPS[0], [own_mixed, after_mixed])
-    start_b, norms_b, products_b = head(GROUPS[1], [next_mixed])
+    start_a, start_b, norms, products_a, products_b = call(
+        "head", functools.partial(head_kernel, width, tile),
+        [sector_dims], [guess[0, :, 0], own_mixed, next_mixed, after_mixed],
+        [jax.ShapeDtypeStruct((2, tile, tile), F32)] * 2
+        + [jax.ShapeDtypeStruct((16, 128), F32)]
+        + [jax.ShapeDtypeStruct((width * tile, 2 * tile), BF16)] * 2,
+        [], 14, 0.2,
+    )
     new_env = call(
         "unpack_env", functools.partial(unpack_kernel, width, tile), [], [early, middle, late],
         jax.ShapeDtypeStruct((width * tile, tile), BF16), [diag], 6, 2,
@@ -628,7 +624,7 @@
         "lanczos", functools.partial(lanczos_kernel, width, tile),
         [sector_dims],
         [late_bound, environ, bound, image, own_mixed, next_mixed, after_mixed, start_a, start_b,
-         norms_a, norms_b, products_a, products_b],
+         norms, products_a, products_b],
         (
             jax.ShapeDtypeStruct((LANCZOS, states, tile, tile), F32),
             jax.ShapeDtypeStruct((16, 128), F32),

time: 57.7 us -> 58.1 us (level)
  waiting for transfers between devices: 3.5 us -> 4.53 us
    ppermute x1, waiting for transfers between devices: 0.61 us -> 2.22 us  [on_device(): late_bound = lax.ppermute(late, 'seg', onward)]
    ppermute x1, waiting for transfers between devices: 0.85 us -> 0.11 us  [on_device(): middle_arrived = lax.ppermute(middle_outgoing, 'sec', up_two)]
    pallas_call x12 -> x11, Pallas kernels: 29.3 us -> 28.8 us  [call(): pl.pallas_call(kernel, out_shape=outs, in_specs=[smem()] * len(scalars) +...]
  transfers between devices with their start and end apart: 10 -> 10, of which waited for: 3 -> 4; matrix products, arithmetic and copies ran while one was open for 0% -> 0% of each run, Pallas kernels for 35% -> 34%
where the time goes in v13:
time: 58.1 us; the launch traced here: 57.9 us
  Pallas kernels  28.8 us (50%)
  starting transfers between devices  13.8 us (24%)
  blocking collectives  7.58 us (13%)
  waiting for transfers between devices  4.53 us (8%)
  local copies, waits for them, and re-layouts  2.16 us (4%)
  between operations  0.78 us (1%)
    pallas_call x11, Pallas kernels, call(): pl.pallas_call(kernel, out_shape=outs, in_specs=[smem()] * len(scalars) +...  28.8 us
    all_to_all x1, blocking collectives, gathered(): lax.all_to_all(jnp.broadcast_to(value, (count,) + value.shape), axis, 0, 0)  7.58 us
    ppermute x1, starting transfers between devices, on_device(): right_far = lax.ppermute(right_packed, 'sec', down_two)  3.93 us
    ppermute x1, waiting for transfers between devices, on_device(): late_bound = lax.ppermute(late, 'seg', onward)  2.22 us
    unnamed x16, local copies, waits for them, and re-layouts  2.15 us
    ppermute x1, starting transfers between devices, on_device(): late_arrived = lax.ppermute(late_outgoing, 'sec', up_two)  2.04 us
    ppermute x1, waiting for transfers between devices, on_device(): early_arrived = lax.ppermute(outgoing[0], 'sec', up_two)  2.02 us
    ppermute x1, starting transfers between devices, on_device(): middle_arrived = lax.ppermute(middle_outgoing, 'sec', up_two)  1.96 us
  transfers between devices with their start and end apart: 10, of which 4 were waited for; matrix products, arithmetic and copies ran while one was open for 0% of the time, Pallas kernels for 34%

profile of v13, /device:TPU:0, one launch (start us, length us, event | category | flops | bytes accessed | tf_op | source)
XLA Modules:
  0.0 57.9 jit_solution(15041544815905071496)
XLA Ops:
  0.6 0.5 collective-permute-start
  1.1 0.1 collective-permute-start.1
  1.2 0.0 copy-start.5
  1.2 1.2 %copy-done.5 = bf16[1,1,34,128,128]{4,3,2,1,0:T(8,128)(2,1)S(1)} copy-done((bf16[1,1,34,128,128]{4,3,2,1,0:T(8,128)(2,1)S(1)}, bf16[1,1,34,128,128]{4,3,2,1,0:T(8,128)(2,1)}, u32[]{:S(2)}) %copy-start.5) | copy-done | bytes 1114136
  2.5 0.0 copy-start
  2.5 0.0 copy-start.2
  2.5 0.0 copy-start.4
  2.5 0.3 pack_right.1
  2.8 3.9 %collective-permute-start.4 = (bf16[2224,128]{1,0:T(8,128)(2,1)S(1)}, bf16[2224,128]{1,0:T(8,128)(2,1)S(1)}, u32[]{:S(2)}, u32[]{:S(2)}) collective-permute-start(bf16[2224,128]{1,0:T(8,128)(2,1)S(1)} %pack_right.1), channel_id=1, source_target_pairs={{0,6},{1,7},{2,0},{3,1},{4,2},{5,3},{6,4},{7,5},{8,14},{9,15},{10,... | collective-permute-start | bytes 1708040 | tf_op jit(solution)/shard_map/ppermute | solution.py:539
  6.7 0.0 collective-permute-done.1.far_site_ref
  6.7 0.0 collective-permute-done.far_environ_ref
  6.7 0.0 copy-done
  6.7 0.0 copy-done.2
  6.7 0.0 copy-done.4
  6.7 0.0 copy-start.3
  6.7 0.9 %copy-done.3 = f32[1,1,34,34,4]{3,4,2,1,0:T(4,128)S(1)} copy-done((f32[1,1,34,34,4]{3,4,2,1,0:T(4,128)S(1)}, f32[1,1,34,34,4]{3,4,2,1,0:T(4,128)}, u32[]{:S(2)}) %copy-start.3) | copy-done | bytes 18520
  7.6 6.5 %fold_up.1 = (bf16[656,128]{1,0:T(8,128)(2,1)S(1)}, bf16[656,128]{1,0:T(8,128)(2,1)S(1)}, bf16[912,128]{1,0:T(8,128)(2,1)S(1)}) custom-call(s32[8]{0:T(128)S(1)} %copy-done.4, bf16[4352,128]{1,0:T(8,128)(2,1)S(1)} %bitcast.22, bf16[4,128,128]{2,1,0:T(8,128)(2,1)S(1)} %bitcast.28, bf16[4352,128]{1,0:T(8,128)(2,1)S(1)} %collective-permute-done.far_environ_ref, ...), custom_call_target="tpu_custom_call" | custom-call | flops 13200000000 | tf_op jit(solution)/shard_map/fold_up/pallas_call | solution.py:472
  14.1 0.1 collective-permute-start.3
  14.2 0.0 copy-start.6
  14.2 0.0 copy-start.7
  14.2 2.8 %fold_own.1 = (f32[656,128]{1,0:T(8,128)S(1)}, f32[656,128]{1,0:T(8,128)S(1)}, f32[912,128]{1,0:T(8,128)S(1)}) custom-call(s32[8]{0:T(128)S(1)} %copy-done.4, bf16[4352,128]{1,0:T(8,128)(2,1)S(1)} %bitcast.23, bf16[4,128,128]{2,1,0:T(8,128)(2,1)S(1)} %bitcast.29, bf16[4352,128]{1,0:T(8,128)(2,1)S(1)} %collective-permute-done.far_environ_ref, ...), custom_call_target="tpu_custom_call" | custom-call | flops 110000000 | tf_op jit(solution)/shard_map/fold_own/pallas_call | solution.py:472
  17.1 2.0 %collective-permute-start.2 = (bf16[656,128]{1,0:T(8,128)(2,1)S(1)}, bf16[656,128]{1,0:T(8,128)(2,1)S(1)}, u32[]{:S(2)}, u32[]{:S(2)}) collective-permute-start(bf16[656,128]{1,0:T(8,128)(2,1)S(1)} %get-tuple-element.61), channel_id=1, source_target_pairs={{0,2},{1,3},{2,4},{3,5},{4,6},{5,7},{6,0},{7,1},{8,10},{9,11},{10,... | collective-permute-start | bytes 503816 | tf_op jit(solution)/shard_map/ppermute | solution.py:566
  19.0 0.0 copy-done.6
  19.0 0.0 copy-done.7
  19.0 1.3 %mix_own.1.own_ref = bf16[1,128,4352]{2,1,0:T(8,128)(2,1)S(1)} custom-call(bf16[4352,128]{1,0:T(8,128)(2,1)S(1)} %bitcast.33, f32[136,34]{1,0:T(8,128)S(1)} %bitcast.34), custom_call_target="tpu_custom_call" | custom-call | flops 1100000000 | tf_op jit(solution)/shard_map/mix_own/pallas_call | solution.py:472
  20.3 0.0 collective-permute-done.4.far_ref
  20.4 2.0 %collective-permute-start.7 = (bf16[912,128]{1,0:T(8,128)(2,1)S(1)}, bf16[912,128]{1,0:T(8,128)(2,1)S(1)}, u32[]{:S(2)}, u32[]{:S(2)}) collective-permute-start(bf16[912,128]{1,0:T(8,128)(2,1)S(1)} %get-tuple-element.71), channel_id=1, source_target_pairs={{0,2},{1,3},{2,4},{3,5},{4,6},{5,7},{6,0},{7,1},{8,10},{9,11},{10,... | collective-permute-start | bytes 700424 | tf_op jit(solution)/shard_map/ppermute | solution.py:573
  22.4 0.1 select_select_fusion
  22.5 0.1 collective-permute-start.6
  22.5 2.0 %collective-permute-done.3 = bf16[656,128]{1,0:T(8,128)(2,1)S(1)} collective-permute-done((bf16[656,128]{1,0:T(8,128)(2,1)S(1)}, bf16[656,128]{1,0:T(8,128)(2,1)S(1)}, u32[]{:S(2)}, u32[]{:S(2)}) %collective-permute-start.3) | collective-permute-done | bytes 167968 | tf_op jit(solution)/shard_map/ppermute | solution.py:558
  24.6 1.6 %collective-permute-start.9 = (bf16[656,128]{1,0:T(8,128)(2,1)S(1)}, bf16[656,128]{1,0:T(8,128)(2,1)S(1)}, u32[]{:S(2)}, u32[]{:S(2)}) collective-permute-start(bf16[656,128]{1,0:T(8,128)(2,1)S(1)} %add_convert_fusion.2.refs_0_), channel_id=1, source_target_pairs={{0,8},{8,16},{16,24},{24,0},{1,9},{9,17},{17,25},{25,1},{2,10},{10... | collective-permute-start | bytes 503816 | tf_op jit(solution)/shard_map/ppermute | solution.py:582
  26.2 1.8 %mix_after.1.after_ref = bf16[1,128,4352]{2,1,0:T(8,128)(2,1)S(1)} custom-call(bf16[2224,128]{1,0:T(8,128)(2,1)S(1)} %collective-permute-done.4.far_ref, f32[136,34]{1,0:T(8,128)S(1)} %bitcast.35), custom_call_target="tpu_custom_call" | custom-call | flops 2200000000 | tf_op jit(solution)/shard_map/mix_after/pallas_call | solution.py:472
  28.0 0.1 collective-permute-done.2
  28.2 0.1 add_convert_fusion.1.refs_1_
  28.2 1.6 %collective-permute-start.5 = (bf16[656,128]{1,0:T(8,128)(2,1)S(1)}, bf16[656,128]{1,0:T(8,128)(2,1)S(1)}, u32[]{:S(2)}, u32[]{:S(2)}) collective-permute-start(bf16[656,128]{1,0:T(8,128)(2,1)S(1)} %add_convert_fusion.1.refs_1_), channel_id=1, source_target_pairs={{0,8},{8,16},{16,24},{24,0},{1,9},{9,17},{17,25},{25,1},{2,10},{10... | collective-permute-start | bytes 503816 | tf_op jit(solution)/shard_map/ppermute | solution.py:590
  29.8 0.0 collective-permute-done.6.near_ref
  29.8 2.3 %mix_next.1.next_ref = bf16[2,128,4352]{2,1,0:T(8,128)(2,1)S(1)} custom-call(bf16[2224,128]{1,0:T(8,128)(2,1)S(1)} %collective-permute-done.6.near_ref, f32[136,34]{1,0:T(8,128)S(1)} %bitcast.36), custom_call_target="tpu_custom_call" | custom-call | flops 3300000000 | tf_op jit(solution)/shard_map/mix_next/pallas_call | solution.py:472
  32.1 0.2 collective-permute-done.7
  32.3 0.1 add_convert_fusion.refs_2_
  32.4 0.0 copy-start.1
  32.4 1.8 %collective-permute-start.8 = (bf16[912,128]{1,0:T(8,128)(2,1)S(1)}, bf16[912,128]{1,0:T(8,128)(2,1)S(1)}, u32[]{:S(2)}, u32[]{:S(2)}) collective-permute-start(bf16[912,128]{1,0:T(8,128)(2,1)S(1)} %add_convert_fusion.refs_2_), channel_id=1, source_target_pairs={{0,8},{8,16},{16,24},{24,0},{1,9},{9,17},{17,25},{25,1},{2,10},{10... | collective-permute-start | bytes 700424 | tf_op jit(solution)/shard_map/ppermute | solution.py:598
  34.2 2.3 %unpack_env.1 = bf16[4352,128]{1,0:T(8,128)(2,1)} custom-call(bf16[656,128]{1,0:T(8,128)(2,1)S(1)} %add_convert_fusion.2.refs_0_, bf16[656,128]{1,0:T(8,128)(2,1)S(1)} %add_convert_fusion.1.refs_1_, bf16[912,128]{1,0:T(8,128)(2,1)S(1)} %add_convert_fusion.refs_2_), custom_call_target="tpu_custom_call" | custom-call | flops 2200000000 | tf_op jit(solution)/shard_map/unpack_env/pallas_call | solution.py:472
  36.5 0.0 collective-permute-done.5.refs_1_
  36.5 0.0 copy-done.1
  36.5 2.0 %head.1 = (f32[2,128,128]{2,1,0:T(8,128)S(1)}, f32[2,128,128]{2,1,0:T(8,128)S(1)}, f32[16,128]{1,0:T(8,128)S(1)}, bf16[4352,256]{1,0:T(8,128)(2,1)S(1)}, bf16[4352,256]{1,0:T(8,128)(2,1)S(1)}) custom-call(s32[8]{0:T(128)S(1)} %copy-done.4, f32[4,128,128]{2,1,0:T(8,128)S(1)} %bitcast.26, bf16[1,128,4352]{2,1,0:T(8,128)(2,1)S(1)} %mix_own.1.own_ref, ...), custom_call_target="tpu_custom_call" | custom-call | flops 220000000 | tf_op jit(solution)/shard_map/head/pallas_call | solution.py:472
  38.5 0.0 collective-permute-done.9.refs_0_
  38.5 0.6 %open.1 = (bf16[128,2560]{1,0:T(8,128)(2,1)S(1)}, f32[2,128,256]{2,1,0:T(8,128)S(1)}) custom-call(bf16[4352,128]{1,0:T(8,128)(2,1)S(1)} %bitcast.24, bf16[656,128]{1,0:T(8,128)(2,1)S(1)} %collective-permute-done.9.refs_0_, bf16[656,128]{1,0:T(8,128)(2,1)S(1)} %collective-permute-done.5.refs_1_, bf16[4352,256]{1,0:T(8,128)(2,1)S(1)} %get-tuple-element.82.refs_2_.product_a, ...), custom_call_target="tpu_custom_call" | custom-call | flops 1100000000 | tf_op jit(solution)/shard_map/open/pallas_call | solution.py:472
  39.1 2.2 %collective-permute-done.8.packed_ref = bf16[912,128]{1,0:T(8,128)(2,1)S(1)} collective-permute-done((bf16[912,128]{1,0:T(8,128)(2,1)S(1)}, bf16[912,128]{1,0:T(8,128)(2,1)S(1)}, u32[]{:S(2)}, u32[]{:S(2)}) %collective-permute-start.8) | collective-permute-done | bytes 233504 | tf_op jit(solution)/shard_map/ppermute | solution.py:598
  41.3 7.5 %lanczos.1 = (f32[4,4,128,128]{3,2,1,0:T(8,128)S(1)}, f32[16,128]{1,0:T(8,128)S(1)}) custom-call(s32[8]{0:T(128)S(1)} %copy-done.4, bf16[912,128]{1,0:T(8,128)(2,1)S(1)} %collective-permute-done.8.packed_ref, bf16[4352,128]{1,0:T(8,128)(2,1)S(1)} %bitcast.25, bf16[128,2560]{1,0:T(8,128)(2,1)S(1)} %get-tuple-element.86.early_ref, ...), custom_call_target="tpu_custom_call" | custom-call | flops 13200000000 | tf_op jit(solution)/shard_map/lanczos/pallas_call | solution.py:472
  48.9 7.6 %all_to_all.5.stats_ref = f32[8,16,128]{2,1,0:T(8,128)S(1)} all-to-all(f32[8,16,128]{2,1,0:T(8,128)S(1)} %broadcast_in_dim.24), channel_id=1, replica_groups=mesh['seg'=4,'sec'=8] {'sec'}, dimensions={0} | all-to-all | bytes 131072 | tf_op jit(solution)/shard_map/all_to_all | solution.py:492
  56.5 1.4 %finish.1 = (f32[4,128,128]{2,1,0:T(8,128)}, f32[2,4]{1,0:T(2,128)}) custom-call(f32[8,16,128]{2,1,0:T(8,128)S(1)} %all_to_all.5.stats_ref, f32[2,128,128]{2,1,0:T(8,128)S(1)} %get-tuple-element.88.start_a, f32[2,128,128]{2,1,0:T(8,128)S(1)} %get-tuple-element.89.start_b, f32[4,4,128,128]{3,2,1,0:T(8,128)S(1)} %get-tuple-element.92.basis_ref), custom_call_target="tpu_custom_call" | custom-call | flops 2200000000 | tf_op jit(solution)/shard_map/finish/pallas_call | solution.py:472
  (2 shorter events, 0.1 us)
Async XLA Ops:
  0.6 6.1 %collective-permute-start = (bf16[4352,128]{1,0:T(8,128)(2,1)}, bf16[4352,128]{1,0:T(8,128)(2,1)S(1)}, u32[]{:S(2)}, u32[]{:S(2)}) collective-permute-start(bf16[4352,128]{1,0:T(8,128)(2,1)} %bitcast.21), channel_id=1, source_target_pairs={{0,1},{1,0},{2,3},{3,2},{4,5},{5,4},{6,7},{7,6},{8,9},{9,8},{10,11... | collective-permute-start | bytes 3342344 | tf_op jit(solution)/shard_map/ppermute | solution.py:540
  1.1 5.6 %collective-permute-start.1 = (bf16[4,128,128]{2,1,0:T(8,128)(2,1)}, bf16[4,128,128]{2,1,0:T(8,128)(2,1)}, u32[]{:S(2)}, u32[]{:S(2)}) collective-permute-start(bf16[4,128,128]{2,1,0:T(8,128)(2,1)} %bitcast.27), channel_id=1, source_target_pairs={{0,1},{1,0},{2,3},{3,2},{4,5},{5,4},{6,7},{7,6},{8,9},{9,8},{10,11... | collective-permute-start | bytes 393224 | tf_op jit(solution)/shard_map/ppermute | solution.py:541
  1.2 1.2 %copy-start.5 = (bf16[1,1,34,128,128]{4,3,2,1,0:T(8,128)(2,1)S(1)}, bf16[1,1,34,128,128]{4,3,2,1,0:T(8,128)(2,1)}, u32[]{:S(2)}) copy-start(bf16[1,1,34,128,128]{4,3,2,1,0:T(8,128)(2,1)} %param.8) | copy-start | bytes 3342340
  2.5 4.2 %copy-start = (bf16[1,1,34,128,128]{4,3,2,1,0:T(8,128)(2,1)S(1)}, bf16[1,1,34,128,128]{4,3,2,1,0:T(8,128)(2,1)}, u32[]{:S(2)}) copy-start(bf16[1,1,34,128,128]{4,3,2,1,0:T(8,128)(2,1)} %param.7) | copy-start | bytes 3342340
  2.5 4.2 %copy-start.2 = (bf16[1,1,4,1,128,128]{5,4,3,2,1,0:T(8,128)(2,1)S(1)}, bf16[1,1,4,1,128,128]{5,4,3,2,1,0:T(8,128)(2,1)}, u32[]{:S(2)}) copy-start(bf16[1,1,4,1,128,128]{5,4,3,2,1,0:T(8,128)(2,1)} %param.9) | copy-start | bytes 393220
  2.5 4.2 %copy-start.4 = (s32[8]{0:T(128)S(1)}, s32[8]{0:T(128)}, u32[]{:S(2)}) copy-start(s32[8]{0:T(128)} %dims_ref.7) | copy-start | bytes 100
  2.8 17.6 %collective-permute-start.4 = (bf16[2224,128]{1,0:T(8,128)(2,1)S(1)}, bf16[2224,128]{1,0:T(8,128)(2,1)S(1)}, u32[]{:S(2)}, u32[]{:S(2)}) collective-permute-start(bf16[2224,128]{1,0:T(8,128)(2,1)S(1)} %pack_right.1), channel_id=1, source_target_pairs={{0,6},{1,7},{2,0},{3,1},{4,2},{5,3},{6,4},{7,5},{8,14},{9,15},{10,... | collective-permute-start | bytes 1708040 | tf_op jit(solution)/shard_map/ppermute | solution.py:539
  6.7 0.9 %copy-start.3 = (f32[1,1,34,34,4]{3,4,2,1,0:T(4,128)S(1)}, f32[1,1,34,34,4]{3,4,2,1,0:T(4,128)}, u32[]{:S(2)}) copy-start(f32[1,1,34,34,4]{3,4,2,1,0:T(4,128)} %param.10) | copy-start | bytes 55492
  14.1 10.5 %collective-permute-start.3 = (bf16[656,128]{1,0:T(8,128)(2,1)S(1)}, bf16[656,128]{1,0:T(8,128)(2,1)S(1)}, u32[]{:S(2)}, u32[]{:S(2)}) collective-permute-start(bf16[656,128]{1,0:T(8,128)(2,1)S(1)} %get-tuple-element.49), channel_id=1, source_target_pairs={{0,2},{1,3},{2,4},{3,5},{4,6},{5,7},{6,0},{7,1},{8,10},{9,11},{10,... | collective-permute-start | bytes 503816 | tf_op jit(solution)/shard_map/ppermute | solution.py:558
  14.2 4.8 %copy-start.6 = (bf16[1,1,34,128,128]{4,3,2,1,0:T(8,128)(2,1)S(1)}, bf16[1,1,34,128,128]{4,3,2,1,0:T(8,128)(2,1)}, u32[]{:S(2)}) copy-start(bf16[1,1,34,128,128]{4,3,2,1,0:T(8,128)(2,1)} %param.8) | copy-start | bytes 3342340
  14.2 4.8 %copy-start.7 = (f32[1,34,34,4]{2,3,1,0:T(4,128)S(1)}, f32[1,34,34,4]{2,3,1,0:T(4,128)}, u32[]{:S(2)}) copy-start(f32[1,34,34,4]{2,3,1,0:T(4,128)} %param.11) | copy-start | bytes 55492
  17.1 11.1 %collective-permute-start.2 = (bf16[656,128]{1,0:T(8,128)(2,1)S(1)}, bf16[656,128]{1,0:T(8,128)(2,1)S(1)}, u32[]{:S(2)}, u32[]{:S(2)}) collective-permute-start(bf16[656,128]{1,0:T(8,128)(2,1)S(1)} %get-tuple-element.61), channel_id=1, source_target_pairs={{0,2},{1,3},{2,4},{3,5},{4,6},{5,7},{6,0},{7,1},{8,10},{9,11},{10,... | collective-permute-start | bytes 503816 | tf_op jit(solution)/shard_map/ppermute | solution.py:566
  20.4 11.9 %collective-permute-start.7 = (bf16[912,128]{1,0:T(8,128)(2,1)S(1)}, bf16[912,128]{1,0:T(8,128)(2,1)S(1)}, u32[]{:S(2)}, u32[]{:S(2)}) collective-permute-start(bf16[912,128]{1,0:T(8,128)(2,1)S(1)} %get-tuple-element.71), channel_id=1, source_target_pairs={{0,2},{1,3},{2,4},{3,5},{4,6},{5,7},{6,0},{7,1},{8,10},{9,11},{10,... | collective-permute-start | bytes 700424 | tf_op jit(solution)/shard_map/ppermute | solution.py:573
  22.5 7.4 %collective-permute-start.6 = (bf16[2224,128]{1,0:T(8,128)(2,1)S(1)}, bf16[2224,128]{1,0:T(8,128)(2,1)S(1)}, u32[]{:S(2)}, u32[]{:S(2)}) collective-permute-start(bf16[2224,128]{1,0:T(8,128)(2,1)S(1)} %select_select_fusion), channel_id=1, source_target_pairs={{0,1},{1,0},{2,3},{3,2},{4,5},{5,4},{6,7},{7,6},{8,9},{9,8},{10,11... | collective-permute-start | bytes 1708040 | tf_op jit(solution)/shard_map/ppermute | solution.py:576
  24.6 13.9 %collective-permute-start.9 = (bf16[656,128]{1,0:T(8,128)(2,1)S(1)}, bf16[656,128]{1,0:T(8,128)(2,1)S(1)}, u32[]{:S(2)}, u32[]{:S(2)}) collective-permute-start(bf16[656,128]{1,0:T(8,128)(2,1)S(1)} %add_convert_fusion.2.refs_0_), channel_id=1, source_target_pairs={{0,8},{8,16},{16,24},{24,0},{1,9},{9,17},{17,25},{25,1},{2,10},{10... | collective-permute-start | bytes 503816 | tf_op jit(solution)/shard_map/ppermute | solution.py:582
  28.2 8.3 %collective-permute-start.5 = (bf16[656,128]{1,0:T(8,128)(2,1)S(1)}, bf16[656,128]{1,0:T(8,128)(2,1)S(1)}, u32[]{:S(2)}, u32[]{:S(2)}) collective-permute-start(bf16[656,128]{1,0:T(8,128)(2,1)S(1)} %add_convert_fusion.1.refs_1_), channel_id=1, source_target_pairs={{0,8},{8,16},{16,24},{24,0},{1,9},{9,17},{17,25},{25,1},{2,10},{10... | collective-permute-start | bytes 503816 | tf_op jit(solution)/shard_map/ppermute | solution.py:590
  32.4 4.1 %copy-start.1 = (f32[1,4,1,128,128]{4,3,2,1,0:T(8,128)S(1)}, f32[1,4,1,128,128]{4,3,2,1,0:T(8,128)}, u32[]{:S(2)}) copy-start(f32[1,4,1,128,128]{4,3,2,1,0:T(8,128)} %param.12) | copy-start | bytes 786436
  32.4 9.0 %collective-permute-start.8 = (bf16[912,128]{1,0:T(8,128)(2,1)S(1)}, bf16[912,128]{1,0:T(8,128)(2,1)S(1)}, u32[]{:S(2)}, u32[]{:S(2)}) collective-permute-start(bf16[912,128]{1,0:T(8,128)(2,1)S(1)} %add_convert_fusion.refs_2_), channel_id=1, source_target_pairs={{0,8},{8,16},{16,24},{24,0},{1,9},{9,17},{17,25},{25,1},{2,10},{10... | collective-permute-start | bytes 700424 | tf_op jit(solution)/shard_map/ppermute | solution.py:598

commit v14 on v13

--- a/solution.py
+++ b/solution.py
@@ -28,8 +28,9 @@
 
 
 def chunks_of(width):
-    side = width // 6 * 2
-    return (0, side), (side, side), (2 * side, width - 2 * side)
+    one = width // 6 * 2
+    two = (width - one) // 4 * 2
+    return (0, one), (one, two), (one + two, width - one - two)
 
 
 def iotas(shape):
@@ -47,11 +48,11 @@
     return folded, diagonal
 
 
-def unpack_block(folded, diagonal):
+def unpack_block(folded, diagonal, kind=BF16):
     half, tile = folded.shape
     row, lane = iotas((half, tile))
     rolled = pltpu.roll(folded, half, 1)
-    turned = jnp.transpose(jnp.concatenate([folded, rolled], axis=0).astype(BF16)).astype(F32)
+    turned = jnp.transpose(jnp.concatenate([folded, rolled], axis=0).astype(kind)).astype(F32)
     top = jnp.where((lane < half) & (row > lane), turned[:half], folded)
     low = jnp.where((lane >= half) & (row > lane - half), rolled, turned[half:])
     low = jnp.where(lane == row + half, diagonal, low)
@@ -98,12 +99,12 @@
     out_ref[width * half :, :] = diag[...].astype(BF16)
 
 
-def unpack_into(count, tile, read, write, diag):
+def unpack_into(count, tile, read, write, diag, kind=BF16):
     half = tile // 2
     size = packed_height(count)
     diag[:size, :] = read(count * half, size)
     for w in range(count):
-        write(w, unpack_block(read(w * half, half), diag[w : w + 1, :]))
+        write(w, unpack_block(read(w * half, half), diag[w : w + 1, :], kind))
 
 
 def reader(ref):
@@ -117,7 +118,7 @@
         def write(w, block, first=first):
             out_ref[(first + w) * tile : (first + w + 1) * tile, :] = block.astype(BF16)
 
-        unpack_into(count, tile, reader(ref), write, diag)
+        unpack_into(count, tile, reader(ref), write, diag, F32)
 
 
 def fold_kernel(
@@ -595,7 +596,7 @@
     )
     late_arrived, next_mixed = lax.optimization_barrier((late_arrived, next_mixed))
     late = carried(kept[2], late_arrived)
-    late_bound = lax.ppermute(late, "seg", onward)
+    late_bound = lax.ppermute(late, "seg", onward[:-1])
     late, next_mixed, after_mixed = lax.optimization_barrier((late, next_mixed, after_mixed))
     start_a, start_b, norms, products_a, products_b = call(
         "head", functools.partial(head_kernel, width, tile),

time: 58.1 us -> 58.2 us (level)
  starting transfers between devices: 13.8 us -> 15.8 us
  waiting for transfers between devices: 4.53 us -> 2.86 us
    ppermute x1, waiting for transfers between devices: 2.22 us -> 0.01 us  [on_device(): late_bound = lax.ppermute(late, 'seg', onward[:-1])]
    ppermute x1, starting transfers between devices: 1.85 us -> 3.84 us  [on_device(): late_bound = lax.ppermute(late, 'seg', onward[:-1])]
    ppermute x1, waiting for transfers between devices: 0.11 us -> 0.81 us  [on_device(): middle_arrived = lax.ppermute(middle_outgoing, 'sec', up_two)]
  transfers between devices with their start and end apart: 10 -> 10, of which waited for: 4 -> 2; matrix products, arithmetic and copies ran while one was open for 0% -> 0% of each run, Pallas kernels for 34% -> 34%
where the time goes in v14:
time: 58.2 us; the launch traced here: 57.9 us
  Pallas kernels  28.5 us (49%)
  starting transfers between devices  15.8 us (27%)
  blocking collectives  7.58 us (13%)
  waiting for transfers between devices  2.86 us (5%)
  local copies, waits for them, and re-layouts  2.16 us (4%)
  between operations  0.8 us (1%)
    pallas_call x11, Pallas kernels, call(): pl.pallas_call(kernel, out_shape=outs, in_specs=[smem()] * len(scalars) +...  28.5 us
    all_to_all x1, blocking collectives, gathered(): lax.all_to_all(jnp.broadcast_to(value, (count,) + value.shape), axis, 0, 0)  7.58 us
    ppermute x1, starting transfers between devices, on_device(): right_far = lax.ppermute(right_packed, 'sec', down_two)  3.93 us
    ppermute x1, starting transfers between devices, on_device(): late_bound = lax.ppermute(late, 'seg', onward[:-1])  3.84 us
    unnamed x16, local copies, waits for them, and re-layouts  2.15 us
    ppermute x1, starting transfers between devices, on_device(): late_arrived = lax.ppermute(late_outgoing, 'sec', up_two)  2.03 us
    ppermute x1, waiting for transfers between devices, on_device(): early_arrived = lax.ppermute(outgoing[0], 'sec', up_two)  2.02 us
    ppermute x1, starting transfers between devices, on_device(): middle_arrived = lax.ppermute(middle_outgoing, 'sec', up_two)  1.97 us
  transfers between devices with their start and end apart: 10, of which 2 were waited for; matrix products, arithmetic and copies ran while one was open for 0% of the time, Pallas kernels for 34%

profile of v14, /device:TPU:0, one launch (start us, length us, event | category | flops | bytes accessed | tf_op | source)
XLA Modules:
  0.0 57.9 jit_solution(12861619296235041669)
XLA Ops:
  0.6 0.5 collective-permute-start
  1.1 0.1 collective-permute-start.1
  1.2 0.0 copy-start.5
  1.2 1.2 %copy-done.5 = bf16[1,1,34,128,128]{4,3,2,1,0:T(8,128)(2,1)S(1)} copy-done((bf16[1,1,34,128,128]{4,3,2,1,0:T(8,128)(2,1)S(1)}, bf16[1,1,34,128,128]{4,3,2,1,0:T(8,128)(2,1)}, u32[]{:S(2)}) %copy-start.5) | copy-done | bytes 1114136
  2.5 0.0 copy-start
  2.5 0.0 copy-start.2
  2.5 0.0 copy-start.4
  2.5 0.3 pack_right.1
  2.8 3.9 %collective-permute-start.4 = (bf16[2224,128]{1,0:T(8,128)(2,1)S(1)}, bf16[2224,128]{1,0:T(8,128)(2,1)S(1)}, u32[]{:S(2)}, u32[]{:S(2)}) collective-permute-start(bf16[2224,128]{1,0:T(8,128)(2,1)S(1)} %pack_right.1), channel_id=1, source_target_pairs={{0,6},{1,7},{2,0},{3,1},{4,2},{5,3},{6,4},{7,5},{8,14},{9,15},{10,... | collective-permute-start | bytes 1708040 | tf_op jit(solution)/shard_map/ppermute | solution.py:540
  6.7 0.0 collective-permute-done.1.far_site_ref
  6.7 0.0 collective-permute-done.far_environ_ref
  6.7 0.0 copy-done
  6.7 0.0 copy-done.2
  6.7 0.0 copy-done.4
  6.7 0.0 copy-start.3
  6.7 0.9 %copy-done.3 = f32[1,1,34,34,4]{3,4,2,1,0:T(4,128)S(1)} copy-done((f32[1,1,34,34,4]{3,4,2,1,0:T(4,128)S(1)}, f32[1,1,34,34,4]{3,4,2,1,0:T(4,128)}, u32[]{:S(2)}) %copy-start.3) | copy-done | bytes 18520
  7.6 6.5 %fold_up.1 = (bf16[656,128]{1,0:T(8,128)(2,1)S(1)}, bf16[784,128]{1,0:T(8,128)(2,1)S(1)}, bf16[784,128]{1,0:T(8,128)(2,1)S(1)}) custom-call(s32[8]{0:T(128)S(1)} %copy-done.4, bf16[4352,128]{1,0:T(8,128)(2,1)S(1)} %bitcast.22, bf16[4,128,128]{2,1,0:T(8,128)(2,1)S(1)} %bitcast.28, bf16[4352,128]{1,0:T(8,128)(2,1)S(1)} %collective-permute-done.far_environ_ref, ...), custom_call_target="tpu_custom_call" | custom-call | flops 13200000000 | tf_op jit(solution)/shard_map/fold_up/pallas_call | solution.py:473
  14.1 0.1 collective-permute-start.3
  14.2 0.0 copy-start.6
  14.2 0.0 copy-start.7
  14.2 2.8 %fold_own.1 = (f32[656,128]{1,0:T(8,128)S(1)}, f32[784,128]{1,0:T(8,128)S(1)}, f32[784,128]{1,0:T(8,128)S(1)}) custom-call(s32[8]{0:T(128)S(1)} %copy-done.4, bf16[4352,128]{1,0:T(8,128)(2,1)S(1)} %bitcast.23, bf16[4,128,128]{2,1,0:T(8,128)(2,1)S(1)} %bitcast.29, bf16[4352,128]{1,0:T(8,128)(2,1)S(1)} %collective-permute-done.far_environ_ref, ...), custom_call_target="tpu_custom_call" | custom-call | flops 110000000 | tf_op jit(solution)/shard_map/fold_own/pallas_call | solution.py:473
  17.1 2.0 %collective-permute-start.2 = (bf16[784,128]{1,0:T(8,128)(2,1)S(1)}, bf16[784,128]{1,0:T(8,128)(2,1)S(1)}, u32[]{:S(2)}, u32[]{:S(2)}) collective-permute-start(bf16[784,128]{1,0:T(8,128)(2,1)S(1)} %get-tuple-element.61), channel_id=1, source_target_pairs={{0,2},{1,3},{2,4},{3,5},{4,6},{5,7},{6,0},{7,1},{8,10},{9,11},{10,... | collective-permute-start | bytes 602120 | tf_op jit(solution)/shard_map/ppermute | solution.py:567
  19.0 0.0 copy-done.6
  19.0 0.0 copy-done.7
  19.0 1.3 %mix_own.1.own_ref = bf16[1,128,4352]{2,1,0:T(8,128)(2,1)S(1)} custom-call(bf16[4352,128]{1,0:T(8,128)(2,1)S(1)} %bitcast.33, f32[136,34]{1,0:T(8,128)S(1)} %bitcast.34), custom_call_target="tpu_custom_call" | custom-call | flops 1100000000 | tf_op jit(solution)/shard_map/mix_own/pallas_call | solution.py:473
  20.3 0.0 collective-permute-done.4.far_ref
  20.4 2.0 %collective-permute-start.7 = (bf16[784,128]{1,0:T(8,128)(2,1)S(1)}, bf16[784,128]{1,0:T(8,128)(2,1)S(1)}, u32[]{:S(2)}, u32[]{:S(2)}) collective-permute-start(bf16[784,128]{1,0:T(8,128)(2,1)S(1)} %get-tuple-element.71), channel_id=1, source_target_pairs={{0,2},{1,3},{2,4},{3,5},{4,6},{5,7},{6,0},{7,1},{8,10},{9,11},{10,... | collective-permute-start | bytes 602120 | tf_op jit(solution)/shard_map/ppermute | solution.py:574
  22.4 0.1 select_select_fusion
  22.5 0.1 collective-permute-start.6
  22.5 2.0 %collective-permute-done.3 = bf16[656,128]{1,0:T(8,128)(2,1)S(1)} collective-permute-done((bf16[656,128]{1,0:T(8,128)(2,1)S(1)}, bf16[656,128]{1,0:T(8,128)(2,1)S(1)}, u32[]{:S(2)}, u32[]{:S(2)}) %collective-permute-start.3) | collective-permute-done | bytes 167968 | tf_op jit(solution)/shard_map/ppermute | solution.py:559
  24.6 1.6 %collective-permute-start.9 = (bf16[656,128]{1,0:T(8,128)(2,1)S(1)}, bf16[656,128]{1,0:T(8,128)(2,1)S(1)}, u32[]{:S(2)}, u32[]{:S(2)}) collective-permute-start(bf16[656,128]{1,0:T(8,128)(2,1)S(1)} %add_convert_fusion.2.refs_0_), channel_id=1, source_target_pairs={{0,8},{8,16},{16,24},{24,0},{1,9},{9,17},{17,25},{25,1},{2,10},{10... | collective-permute-start | bytes 503816 | tf_op jit(solution)/shard_map/ppermute | solution.py:583
  26.2 1.8 %mix_after.1.after_ref = bf16[1,128,4352]{2,1,0:T(8,128)(2,1)S(1)} custom-call(bf16[2224,128]{1,0:T(8,128)(2,1)S(1)} %collective-permute-done.4.far_ref, f32[136,34]{1,0:T(8,128)S(1)} %bitcast.35), custom_call_target="tpu_custom_call" | custom-call | flops 2200000000 | tf_op jit(solution)/shard_map/mix_after/pallas_call | solution.py:473
  28.0 0.8 %collective-permute-done.2 = bf16[784,128]{1,0:T(8,128)(2,1)S(1)} collective-permute-done((bf16[784,128]{1,0:T(8,128)(2,1)S(1)}, bf16[784,128]{1,0:T(8,128)(2,1)S(1)}, u32[]{:S(2)}, u32[]{:S(2)}) %collective-permute-start.2) | collective-permute-done | bytes 200736 | tf_op jit(solution)/shard_map/ppermute | solution.py:567
  28.9 0.1 add_convert_fusion.1.refs_1_
  28.9 1.6 %collective-permute-start.5 = (bf16[784,128]{1,0:T(8,128)(2,1)S(1)}, bf16[784,128]{1,0:T(8,128)(2,1)S(1)}, u32[]{:S(2)}, u32[]{:S(2)}) collective-permute-start(bf16[784,128]{1,0:T(8,128)(2,1)S(1)} %add_convert_fusion.1.refs_1_), channel_id=1, source_target_pairs={{0,8},{8,16},{16,24},{24,0},{1,9},{9,17},{17,25},{25,1},{2,10},{10... | collective-permute-start | bytes 602120 | tf_op jit(solution)/shard_map/ppermute | solution.py:591
  30.5 0.0 collective-permute-done.6.near_ref
  30.6 2.3 %mix_next.1.next_ref = bf16[2,128,4352]{2,1,0:T(8,128)(2,1)S(1)} custom-call(bf16[2224,128]{1,0:T(8,128)(2,1)S(1)} %collective-permute-done.6.near_ref, f32[136,34]{1,0:T(8,128)S(1)} %bitcast.36), custom_call_target="tpu_custom_call" | custom-call | flops 3300000000 | tf_op jit(solution)/shard_map/mix_next/pallas_call | solution.py:473
  32.8 0.0 collective-permute-done.7
  32.8 0.1 add_convert_fusion.refs_2_
  32.9 0.0 copy-start.1
  32.9 3.8 %collective-permute-start.8 = (bf16[784,128]{1,0:T(8,128)(2,1)S(1)}, bf16[784,128]{1,0:T(8,128)(2,1)S(1)}, u32[]{:S(2)}, u32[]{:S(2)}) collective-permute-start(bf16[784,128]{1,0:T(8,128)(2,1)S(1)} %add_convert_fusion.refs_2_), channel_id=1, source_target_pairs={{0,8},{8,16},{16,24},{1,9},{9,17},{17,25},{2,10},{10,18},{18,26},{... | collective-permute-start | bytes 602120 | tf_op jit(solution)/shard_map/ppermute | solution.py:599
  36.8 1.8 %unpack_env.1 = bf16[4352,128]{1,0:T(8,128)(2,1)} custom-call(bf16[656,128]{1,0:T(8,128)(2,1)S(1)} %add_convert_fusion.2.refs_0_, bf16[784,128]{1,0:T(8,128)(2,1)S(1)} %add_convert_fusion.1.refs_1_, bf16[784,128]{1,0:T(8,128)(2,1)S(1)} %add_convert_fusion.refs_2_), custom_call_target="tpu_custom_call" | custom-call | flops 2200000000 | tf_op jit(solution)/shard_map/unpack_env/pallas_call | solution.py:473
  38.6 0.0 collective-permute-done.5.refs_1_
  38.6 0.0 copy-done.1
  38.6 2.0 %head.1 = (f32[2,128,128]{2,1,0:T(8,128)S(1)}, f32[2,128,128]{2,1,0:T(8,128)S(1)}, f32[16,128]{1,0:T(8,128)S(1)}, bf16[4352,256]{1,0:T(8,128)(2,1)S(1)}, bf16[4352,256]{1,0:T(8,128)(2,1)S(1)}) custom-call(s32[8]{0:T(128)S(1)} %copy-done.4, f32[4,128,128]{2,1,0:T(8,128)S(1)} %bitcast.26, bf16[1,128,4352]{2,1,0:T(8,128)(2,1)S(1)} %mix_own.1.own_ref, ...), custom_call_target="tpu_custom_call" | custom-call | flops 220000000 | tf_op jit(solution)/shard_map/head/pallas_call | solution.py:473
  40.6 0.0 collective-permute-done.9.refs_0_
  40.6 0.7 %open.1 = (bf16[128,2816]{1,0:T(8,128)(2,1)S(1)}, f32[2,128,256]{2,1,0:T(8,128)S(1)}) custom-call(bf16[4352,128]{1,0:T(8,128)(2,1)S(1)} %bitcast.24, bf16[656,128]{1,0:T(8,128)(2,1)S(1)} %collective-permute-done.9.refs_0_, bf16[784,128]{1,0:T(8,128)(2,1)S(1)} %collective-permute-done.5.refs_1_, bf16[4352,256]{1,0:T(8,128)(2,1)S(1)} %get-tuple-element.82.refs_2_.product_a, ...), custom_call_target="tpu_custom_call" | custom-call | flops 1100000000 | tf_op jit(solution)/shard_map/open/pallas_call | solution.py:473
  41.3 0.0 collective-permute-done.8.packed_ref
  41.3 7.6 %lanczos.1 = (f32[4,4,128,128]{3,2,1,0:T(8,128)S(1)}, f32[16,128]{1,0:T(8,128)S(1)}) custom-call(s32[8]{0:T(128)S(1)} %copy-done.4, bf16[784,128]{1,0:T(8,128)(2,1)S(1)} %collective-permute-done.8.packed_ref, bf16[4352,128]{1,0:T(8,128)(2,1)S(1)} %bitcast.25, bf16[128,2816]{1,0:T(8,128)(2,1)S(1)} %get-tuple-element.86.early_ref, ...), custom_call_target="tpu_custom_call" | custom-call | flops 13200000000 | tf_op jit(solution)/shard_map/lanczos/pallas_call | solution.py:473
  48.9 7.6 %all_to_all.5.stats_ref = f32[8,16,128]{2,1,0:T(8,128)S(1)} all-to-all(f32[8,16,128]{2,1,0:T(8,128)S(1)} %broadcast_in_dim.24), channel_id=1, replica_groups=mesh['seg'=4,'sec'=8] {'sec'}, dimensions={0} | all-to-all | bytes 131072 | tf_op jit(solution)/shard_map/all_to_all | solution.py:493
  56.5 1.4 %finish.1 = (f32[4,128,128]{2,1,0:T(8,128)}, f32[2,4]{1,0:T(2,128)}) custom-call(f32[8,16,128]{2,1,0:T(8,128)S(1)} %all_to_all.5.stats_ref, f32[2,128,128]{2,1,0:T(8,128)S(1)} %get-tuple-element.88.start_a, f32[2,128,128]{2,1,0:T(8,128)S(1)} %get-tuple-element.89.start_b, f32[4,4,128,128]{3,2,1,0:T(8,128)S(1)} %get-tuple-element.92.basis_ref), custom_call_target="tpu_custom_call" | custom-call | flops 2200000000 | tf_op jit(solution)/shard_map/finish/pallas_call | solution.py:473
  (2 shorter events, 0.1 us)
Async XLA Ops:
  0.6 6.1 %collective-permute-start = (bf16[4352,128]{1,0:T(8,128)(2,1)}, bf16[4352,128]{1,0:T(8,128)(2,1)S(1)}, u32[]{:S(2)}, u32[]{:S(2)}) collective-permute-start(bf16[4352,128]{1,0:T(8,128)(2,1)} %bitcast.21), channel_id=1, source_target_pairs={{0,1},{1,0},{2,3},{3,2},{4,5},{5,4},{6,7},{7,6},{8,9},{9,8},{10,11... | collective-permute-start | bytes 3342344 | tf_op jit(solution)/shard_map/ppermute | solution.py:541
  1.1 5.6 %collective-permute-start.1 = (bf16[4,128,128]{2,1,0:T(8,128)(2,1)}, bf16[4,128,128]{2,1,0:T(8,128)(2,1)}, u32[]{:S(2)}, u32[]{:S(2)}) collective-permute-start(bf16[4,128,128]{2,1,0:T(8,128)(2,1)} %bitcast.27), channel_id=1, source_target_pairs={{0,1},{1,0},{2,3},{3,2},{4,5},{5,4},{6,7},{7,6},{8,9},{9,8},{10,11... | collective-permute-start | bytes 393224 | tf_op jit(solution)/shard_map/ppermute | solution.py:542
  1.2 1.2 %copy-start.5 = (bf16[1,1,34,128,128]{4,3,2,1,0:T(8,128)(2,1)S(1)}, bf16[1,1,34,128,128]{4,3,2,1,0:T(8,128)(2,1)}, u32[]{:S(2)}) copy-start(bf16[1,1,34,128,128]{4,3,2,1,0:T(8,128)(2,1)} %param.8) | copy-start | bytes 3342340
  2.5 4.2 %copy-start = (bf16[1,1,34,128,128]{4,3,2,1,0:T(8,128)(2,1)S(1)}, bf16[1,1,34,128,128]{4,3,2,1,0:T(8,128)(2,1)}, u32[]{:S(2)}) copy-start(bf16[1,1,34,128,128]{4,3,2,1,0:T(8,128)(2,1)} %param.7) | copy-start | bytes 3342340
  2.5 4.2 %copy-start.2 = (bf16[1,1,4,1,128,128]{5,4,3,2,1,0:T(8,128)(2,1)S(1)}, bf16[1,1,4,1,128,128]{5,4,3,2,1,0:T(8,128)(2,1)}, u32[]{:S(2)}) copy-start(bf16[1,1,4,1,128,128]{5,4,3,2,1,0:T(8,128)(2,1)} %param.9) | copy-start | bytes 393220
  2.5 4.2 %copy-start.4 = (s32[8]{0:T(128)S(1)}, s32[8]{0:T(128)}, u32[]{:S(2)}) copy-start(s32[8]{0:T(128)} %dims_ref.7) | copy-start | bytes 100
  2.8 17.6 %collective-permute-start.4 = (bf16[2224,128]{1,0:T(8,128)(2,1)S(1)}, bf16[2224,128]{1,0:T(8,128)(2,1)S(1)}, u32[]{:S(2)}, u32[]{:S(2)}) collective-permute-start(bf16[2224,128]{1,0:T(8,128)(2,1)S(1)} %pack_right.1), channel_id=1, source_target_pairs={{0,6},{1,7},{2,0},{3,1},{4,2},{5,3},{6,4},{7,5},{8,14},{9,15},{10,... | collective-permute-start | bytes 1708040 | tf_op jit(solution)/shard_map/ppermute | solution.py:540
  6.7 0.9 %copy-start.3 = (f32[1,1,34,34,4]{3,4,2,1,0:T(4,128)S(1)}, f32[1,1,34,34,4]{3,4,2,1,0:T(4,128)}, u32[]{:S(2)}) copy-start(f32[1,1,34,34,4]{3,4,2,1,0:T(4,128)} %param.10) | copy-start | bytes 55492
  14.1 10.5 %collective-permute-start.3 = (bf16[656,128]{1,0:T(8,128)(2,1)S(1)}, bf16[656,128]{1,0:T(8,128)(2,1)S(1)}, u32[]{:S(2)}, u32[]{:S(2)}) collective-permute-start(bf16[656,128]{1,0:T(8,128)(2,1)S(1)} %get-tuple-element.49), channel_id=1, source_target_pairs={{0,2},{1,3},{2,4},{3,5},{4,6},{5,7},{6,0},{7,1},{8,10},{9,11},{10,... | collective-permute-start | bytes 503816 | tf_op jit(solution)/shard_map/ppermute | solution.py:559
  14.2 4.8 %copy-start.6 = (bf16[1,1,34,128,128]{4,3,2,1,0:T(8,128)(2,1)S(1)}, bf16[1,1,34,128,128]{4,3,2,1,0:T(8,128)(2,1)}, u32[]{:S(2)}) copy-start(bf16[1,1,34,128,128]{4,3,2,1,0:T(8,128)(2,1)} %param.8) | copy-start | bytes 3342340
  14.2 4.8 %copy-start.7 = (f32[1,34,34,4]{2,3,1,0:T(4,128)S(1)}, f32[1,34,34,4]{2,3,1,0:T(4,128)}, u32[]{:S(2)}) copy-start(f32[1,34,34,4]{2,3,1,0:T(4,128)} %param.11) | copy-start | bytes 55492
  17.1 11.8 %collective-permute-start.2 = (bf16[784,128]{1,0:T(8,128)(2,1)S(1)}, bf16[784,128]{1,0:T(8,128)(2,1)S(1)}, u32[]{:S(2)}, u32[]{:S(2)}) collective-permute-start(bf16[784,128]{1,0:T(8,128)(2,1)S(1)} %get-tuple-element.61), channel_id=1, source_target_pairs={{0,2},{1,3},{2,4},{3,5},{4,6},{5,7},{6,0},{7,1},{8,10},{9,11},{10,... | collective-permute-start | bytes 602120 | tf_op jit(solution)/shard_map/ppermute | solution.py:567
  20.4 12.5 %collective-permute-start.7 = (bf16[784,128]{1,0:T(8,128)(2,1)S(1)}, bf16[784,128]{1,0:T(8,128)(2,1)S(1)}, u32[]{:S(2)}, u32[]{:S(2)}) collective-permute-start(bf16[784,128]{1,0:T(8,128)(2,1)S(1)} %get-tuple-element.71), channel_id=1, source_target_pairs={{0,2},{1,3},{2,4},{3,5},{4,6},{5,7},{6,0},{7,1},{8,10},{9,11},{10,... | collective-permute-start | bytes 602120 | tf_op jit(solution)/shard_map/ppermute | solution.py:574
  22.5 8.1 %collective-permute-start.6 = (bf16[2224,128]{1,0:T(8,128)(2,1)S(1)}, bf16[2224,128]{1,0:T(8,128)(2,1)S(1)}, u32[]{:S(2)}, u32[]{:S(2)}) collective-permute-start(bf16[2224,128]{1,0:T(8,128)(2,1)S(1)} %select_select_fusion), channel_id=1, source_target_pairs={{0,1},{1,0},{2,3},{3,2},{4,5},{5,4},{6,7},{7,6},{8,9},{9,8},{10,11... | collective-permute-start | bytes 1708040 | tf_op jit(solution)/shard_map/ppermute | solution.py:577
  24.6 16.0 %collective-permute-start.9 = (bf16[656,128]{1,0:T(8,128)(2,1)S(1)}, bf16[656,128]{1,0:T(8,128)(2,1)S(1)}, u32[]{:S(2)}, u32[]{:S(2)}) collective-permute-start(bf16[656,128]{1,0:T(8,128)(2,1)S(1)} %add_convert_fusion.2.refs_0_), channel_id=1, source_target_pairs={{0,8},{8,16},{16,24},{24,0},{1,9},{9,17},{17,25},{25,1},{2,10},{10... | collective-permute-start | bytes 503816 | tf_op jit(solution)/shard_map/ppermute | solution.py:583
  28.9 9.7 %collective-permute-start.5 = (bf16[784,128]{1,0:T(8,128)(2,1)S(1)}, bf16[784,128]{1,0:T(8,128)(2,1)S(1)}, u32[]{:S(2)}, u32[]{:S(2)}) collective-permute-start(bf16[784,128]{1,0:T(8,128)(2,1)S(1)} %add_convert_fusion.1.refs_1_), channel_id=1, source_target_pairs={{0,8},{8,16},{16,24},{24,0},{1,9},{9,17},{17,25},{25,1},{2,10},{10... | collective-permute-start | bytes 602120 | tf_op jit(solution)/shard_map/ppermute | solution.py:591
  32.9 5.7 %copy-start.1 = (f32[1,4,1,128,128]{4,3,2,1,0:T(8,128)S(1)}, f32[1,4,1,128,128]{4,3,2,1,0:T(8,128)}, u32[]{:S(2)}) copy-start(f32[1,4,1,128,128]{4,3,2,1,0:T(8,128)} %param.12) | copy-start | bytes 786436
  32.9 8.4 %collective-permute-start.8 = (bf16[784,128]{1,0:T(8,128)(2,1)S(1)}, bf16[784,128]{1,0:T(8,128)(2,1)S(1)}, u32[]{:S(2)}, u32[]{:S(2)}) collective-permute-start(bf16[784,128]{1,0:T(8,128)(2,1)S(1)} %add_convert_fusion.refs_2_), channel_id=1, source_target_pairs={{0,8},{8,16},{16,24},{1,9},{9,17},{17,25},{2,10},{10,18},{18,26},{... | collective-permute-start | bytes 602120 | tf_op jit(solution)/shard_map/ppermute | solution.py:599

commit v15 on v13

--- a/solution.py
+++ b/solution.py
@@ -28,8 +28,9 @@
 
 
 def chunks_of(width):
-    side = width // 6 * 2
-    return (0, side), (side, side), (2 * side, width - 2 * side)
+    one = width // 6 * 2
+    two = (width - one) // 4 * 2
+    return (0, one), (one, two), (one + two, width - one - two)
 
 
 def iotas(shape):
@@ -51,7 +52,7 @@
     half, tile = folded.shape
     row, lane = iotas((half, tile))
     rolled = pltpu.roll(folded, half, 1)
-    turned = jnp.transpose(jnp.concatenate([folded, rolled], axis=0).astype(BF16)).astype(F32)
+    turned = jnp.transpose(jnp.concatenate([folded, rolled], axis=0))
     top = jnp.where((lane < half) & (row > lane), turned[:half], folded)
     low = jnp.where((lane >= half) & (row > lane - half), rolled, turned[half:])
     low = jnp.where(lane == row + half, diagonal, low)
@@ -88,8 +89,9 @@
     return jnp.concatenate([value, value], axis=0).astype(BF16)
 
 
-def pack_kernel(width, tile, source_ref, out_ref, diag):
+def pack_kernel(width, tile, source_ref, weight_ref, out_ref, kept_ref, diag):
     half = tile // 2
+    kept_ref[...] = weight_ref[...]
     diag[...] = jnp.zeros_like(diag)
     for w in range(width):
         folded, diagonal = pack_block(source_ref[w * tile : (w + 1) * tile, :].astype(F32))
@@ -532,9 +534,9 @@
             pltpu.VMEM((count, wide * (tile + 8), tile), F32),
         ]
 
-    right_packed = call(
-        "pack_right", functools.partial(pack_kernel, width, tile), [], [right], packed,
-        [diag], 6, 1,
+    right_packed, site_weights = call(
+        "pack_right", functools.partial(pack_kernel, width, tile), [], [right, site_weights],
+        (packed, jax.ShapeDtypeStruct(site_weights.shape, F32)), [diag], 6, 1,
     )
     right_far = lax.ppermute(right_packed, "sec", down_two)
     far_environ = lax.ppermute(environ, "sec", swap)

time: 58.1 us -> 59.2 us (1.019)
  local copies, waits for them, and re-layouts: 2.16 us -> 3.67 us
    unnamed x16 -> x20, local copies, waits for them, and re-layouts: 2.15 us -> 3.66 us
    ppermute x1, waiting for transfers between devices: 2.22 us -> 1.39 us  [on_device(): late_bound = lax.ppermute(late, 'seg', onward)]
    ppermute x1, waiting for transfers between devices: 0.11 us -> 0.84 us  [on_device(): middle_arrived = lax.ppermute(middle_outgoing, 'sec', up_two)]
  transfers between devices with their start and end apart: 10 -> 10, of which waited for: 4 -> 3; matrix products, arithmetic and copies ran while one was open for 0% -> 0% of each run, Pallas kernels for 34% -> 33%
where the time goes in v15:
time: 59.2 us; the launch traced here: 58.9 us
  Pallas kernels  28.6 us (48%)
  starting transfers between devices  13.7 us (23%)
  blocking collectives  7.58 us (13%)
  waiting for transfers between devices  4.28 us (7%)
  local copies, waits for them, and re-layouts  3.67 us (6%)
  between operations  0.82 us (1%)
    pallas_call x11, Pallas kernels, call(): pl.pallas_call(kernel, out_shape=outs, in_specs=[smem()] * len(scalars) +...  28.6 us
    all_to_all x1, blocking collectives, gathered(): lax.all_to_all(jnp.broadcast_to(value, (count,) + value.shape), axis, 0, 0)  7.58 us
    ppermute x1, starting transfers between devices, on_device(): right_far = lax.ppermute(right_packed, 'sec', down_two)  3.87 us
    unnamed x20, local copies, waits for them, and re-layouts  3.66 us
    ppermute x1, starting transfers between devices, on_device(): late_arrived = lax.ppermute(late_outgoing, 'sec', up_two)  2.02 us
    ppermute x1, waiting for transfers between devices, on_device(): early_arrived = lax.ppermute(outgoing[0], 'sec', up_two)  2.02 us
    ppermute x1, starting transfers between devices, on_device(): middle_arrived = lax.ppermute(middle_outgoing, 'sec', up_two)  1.99 us
    ppermute x1, starting transfers between devices, on_device(): late_bound = lax.ppermute(late, 'seg', onward)  1.86 us
  transfers between devices with their start and end apart: 10, of which 3 were waited for; matrix products, arithmetic and copies ran while one was open for 0% of the time, Pallas kernels for 33%

profile of v15, /device:TPU:0, one launch (start us, length us, event | category | flops | bytes accessed | tf_op | source)
XLA Modules:
  0.0 58.9 jit_solution(5697142330774799340)
XLA Ops:
  0.6 0.5 collective-permute-start
  1.1 0.1 collective-permute-start.1
  1.2 0.0 copy-start.6
  1.2 1.2 %copy-done.6 = bf16[1,1,34,128,128]{4,3,2,1,0:T(8,128)(2,1)S(1)} copy-done((bf16[1,1,34,128,128]{4,3,2,1,0:T(8,128)(2,1)S(1)}, bf16[1,1,34,128,128]{4,3,2,1,0:T(8,128)(2,1)}, u32[]{:S(2)}) %copy-start.6) | copy-done | bytes 1114136
  2.5 0.0 copy-start.8
  2.5 0.9 %copy-done.8 = f32[1,1,34,34,4]{3,4,2,1,0:T(4,128)S(1)} copy-done((f32[1,1,34,34,4]{3,4,2,1,0:T(4,128)S(1)}, f32[1,1,34,34,4]{3,4,2,1,0:T(4,128)}, u32[]{:S(2)}) %copy-start.8) | copy-done | bytes 18520
  3.4 0.0 copy-start
  3.4 0.0 copy-start.2
  3.4 0.0 copy-start.5
  3.4 0.3 pack_right.1
  3.7 0.0 copy-start.3
  3.7 0.6 %copy-done.3 = f32[136,34]{1,0:T(8,128)} copy-done((f32[136,34]{1,0:T(8,128)}, f32[136,34]{1,0:T(8,128)S(1)}, u32[]{:S(2)}) %copy-start.3) | copy-done | bytes 18520
  4.3 3.9 %collective-permute-start.4 = (bf16[2224,128]{1,0:T(8,128)(2,1)S(1)}, bf16[2224,128]{1,0:T(8,128)(2,1)S(1)}, u32[]{:S(2)}, u32[]{:S(2)}) collective-permute-start(bf16[2224,128]{1,0:T(8,128)(2,1)S(1)} %get-tuple-element.67), channel_id=1, source_target_pairs={{0,6},{1,7},{2,0},{3,1},{4,2},{5,3},{6,4},{7,5},{8,14},{9,15},{10,... | collective-permute-start | bytes 1708040 | tf_op jit(solution)/shard_map/ppermute | solution.py:541
  8.2 0.0 collective-permute-done.1.far_site_ref
  8.2 0.0 collective-permute-done.far_environ_ref
  8.2 0.0 copy-done
  8.2 0.0 copy-done.2
  8.2 0.0 copy-done.5
  8.2 0.0 copy-start.4
  8.2 0.9 %copy-done.4 = f32[136,34]{1,0:T(8,128)S(1)} copy-done((f32[136,34]{1,0:T(8,128)S(1)}, f32[136,34]{1,0:T(8,128)}, u32[]{:S(2)}) %copy-start.4) | copy-done | bytes 18520
  9.1 6.5 %fold_up.1 = (bf16[656,128]{1,0:T(8,128)(2,1)S(1)}, bf16[784,128]{1,0:T(8,128)(2,1)S(1)}, bf16[784,128]{1,0:T(8,128)(2,1)S(1)}) custom-call(s32[8]{0:T(128)S(1)} %copy-done.5, bf16[4352,128]{1,0:T(8,128)(2,1)S(1)} %bitcast.22, bf16[4,128,128]{2,1,0:T(8,128)(2,1)S(1)} %bitcast.28, bf16[4352,128]{1,0:T(8,128)(2,1)S(1)} %collective-permute-done.far_environ_ref, ...), custom_call_target="tpu_custom_call" | custom-call | flops 13200000000 | tf_op jit(solution)/shard_map/fold_up/pallas_call | solution.py:474
  15.6 0.1 collective-permute-start.3
  15.6 0.0 copy-start.7
  15.7 0.0 copy-start.9
  15.7 2.9 %fold_own.1 = (f32[656,128]{1,0:T(8,128)S(1)}, f32[784,128]{1,0:T(8,128)S(1)}, f32[784,128]{1,0:T(8,128)S(1)}) custom-call(s32[8]{0:T(128)S(1)} %copy-done.5, bf16[4352,128]{1,0:T(8,128)(2,1)S(1)} %bitcast.23, bf16[4,128,128]{2,1,0:T(8,128)(2,1)S(1)} %bitcast.29, bf16[4352,128]{1,0:T(8,128)(2,1)S(1)} %collective-permute-done.far_environ_ref, ...), custom_call_target="tpu_custom_call" | custom-call | flops 110000000 | tf_op jit(solution)/shard_map/fold_own/pallas_call | solution.py:474
  18.5 2.0 %collective-permute-start.2 = (bf16[784,128]{1,0:T(8,128)(2,1)S(1)}, bf16[784,128]{1,0:T(8,128)(2,1)S(1)}, u32[]{:S(2)}, u32[]{:S(2)}) collective-permute-start(bf16[784,128]{1,0:T(8,128)(2,1)S(1)} %get-tuple-element.64), channel_id=1, source_target_pairs={{0,2},{1,3},{2,4},{3,5},{4,6},{5,7},{6,0},{7,1},{8,10},{9,11},{10,... | collective-permute-start | bytes 602120 | tf_op jit(solution)/shard_map/ppermute | solution.py:568
  20.5 0.0 copy-done.7
  20.5 0.0 copy-done.9
  20.5 1.3 %mix_own.1.own_ref = bf16[1,128,4352]{2,1,0:T(8,128)(2,1)S(1)} custom-call(bf16[4352,128]{1,0:T(8,128)(2,1)S(1)} %bitcast.31, f32[136,34]{1,0:T(8,128)S(1)} %bitcast.33), custom_call_target="tpu_custom_call" | custom-call | flops 1100000000 | tf_op jit(solution)/shard_map/mix_own/pallas_call | solution.py:474
  21.8 0.0 collective-permute-done.4.far_ref
  21.8 2.0 %collective-permute-start.7 = (bf16[784,128]{1,0:T(8,128)(2,1)S(1)}, bf16[784,128]{1,0:T(8,128)(2,1)S(1)}, u32[]{:S(2)}, u32[]{:S(2)}) collective-permute-start(bf16[784,128]{1,0:T(8,128)(2,1)S(1)} %get-tuple-element.75), channel_id=1, source_target_pairs={{0,2},{1,3},{2,4},{3,5},{4,6},{5,7},{6,0},{7,1},{8,10},{9,11},{10,... | collective-permute-start | bytes 602120 | tf_op jit(solution)/shard_map/ppermute | solution.py:575
  23.9 0.1 select_select_fusion
  23.9 0.1 collective-permute-start.6
  24.0 2.0 %collective-permute-done.3 = bf16[656,128]{1,0:T(8,128)(2,1)S(1)} collective-permute-done((bf16[656,128]{1,0:T(8,128)(2,1)S(1)}, bf16[656,128]{1,0:T(8,128)(2,1)S(1)}, u32[]{:S(2)}, u32[]{:S(2)}) %collective-permute-start.3) | collective-permute-done | bytes 167968 | tf_op jit(solution)/shard_map/ppermute | solution.py:560
  26.0 0.1 add_convert_fusion.2.refs_0_
  26.1 1.6 %collective-permute-start.9 = (bf16[656,128]{1,0:T(8,128)(2,1)S(1)}, bf16[656,128]{1,0:T(8,128)(2,1)S(1)}, u32[]{:S(2)}, u32[]{:S(2)}) collective-permute-start(bf16[656,128]{1,0:T(8,128)(2,1)S(1)} %add_convert_fusion.2.refs_0_), channel_id=1, source_target_pairs={{0,8},{8,16},{16,24},{24,0},{1,9},{9,17},{17,25},{25,1},{2,10},{10... | collective-permute-start | bytes 503816 | tf_op jit(solution)/shard_map/ppermute | solution.py:584
  27.7 1.8 %mix_after.1.after_ref = bf16[1,128,4352]{2,1,0:T(8,128)(2,1)S(1)} custom-call(bf16[2224,128]{1,0:T(8,128)(2,1)S(1)} %collective-permute-done.4.far_ref, f32[136,34]{1,0:T(8,128)S(1)} %bitcast.34), custom_call_target="tpu_custom_call" | custom-call | flops 2200000000 | tf_op jit(solution)/shard_map/mix_after/pallas_call | solution.py:474
  29.5 0.8 %collective-permute-done.2 = bf16[784,128]{1,0:T(8,128)(2,1)S(1)} collective-permute-done((bf16[784,128]{1,0:T(8,128)(2,1)S(1)}, bf16[784,128]{1,0:T(8,128)(2,1)S(1)}, u32[]{:S(2)}, u32[]{:S(2)}) %collective-permute-start.2) | collective-permute-done | bytes 200736 | tf_op jit(solution)/shard_map/ppermute | solution.py:568
  30.3 0.1 add_convert_fusion.1.refs_1_
  30.4 1.6 %collective-permute-start.5 = (bf16[784,128]{1,0:T(8,128)(2,1)S(1)}, bf16[784,128]{1,0:T(8,128)(2,1)S(1)}, u32[]{:S(2)}, u32[]{:S(2)}) collective-permute-start(bf16[784,128]{1,0:T(8,128)(2,1)S(1)} %add_convert_fusion.1.refs_1_), channel_id=1, source_target_pairs={{0,8},{8,16},{16,24},{24,0},{1,9},{9,17},{17,25},{25,1},{2,10},{10... | collective-permute-start | bytes 602120 | tf_op jit(solution)/shard_map/ppermute | solution.py:592
  32.0 0.0 collective-permute-done.6.near_ref
  32.0 2.4 %mix_next.1.next_ref = bf16[2,128,4352]{2,1,0:T(8,128)(2,1)S(1)} custom-call(bf16[2224,128]{1,0:T(8,128)(2,1)S(1)} %collective-permute-done.6.near_ref, f32[136,34]{1,0:T(8,128)S(1)} %bitcast.35), custom_call_target="tpu_custom_call" | custom-call | flops 3300000000 | tf_op jit(solution)/shard_map/mix_next/pallas_call | solution.py:474
  34.4 0.0 collective-permute-done.7
  34.4 0.1 add_convert_fusion.refs_2_
  34.5 0.0 copy-start.1
  34.5 1.9 %collective-permute-start.8 = (bf16[784,128]{1,0:T(8,128)(2,1)S(1)}, bf16[784,128]{1,0:T(8,128)(2,1)S(1)}, u32[]{:S(2)}, u32[]{:S(2)}) collective-permute-start(bf16[784,128]{1,0:T(8,128)(2,1)S(1)} %add_convert_fusion.refs_2_), channel_id=1, source_target_pairs={{0,8},{8,16},{16,24},{24,0},{1,9},{9,17},{17,25},{25,1},{2,10},{10... | collective-permute-start | bytes 602120 | tf_op jit(solution)/shard_map/ppermute | solution.py:600
  36.4 1.8 %unpack_env.1 = bf16[4352,128]{1,0:T(8,128)(2,1)} custom-call(bf16[656,128]{1,0:T(8,128)(2,1)S(1)} %add_convert_fusion.2.refs_0_, bf16[784,128]{1,0:T(8,128)(2,1)S(1)} %add_convert_fusion.1.refs_1_, bf16[784,128]{1,0:T(8,128)(2,1)S(1)} %add_convert_fusion.refs_2_), custom_call_target="tpu_custom_call" | custom-call | flops 2200000000 | tf_op jit(solution)/shard_map/unpack_env/pallas_call | solution.py:474
  38.2 0.0 collective-permute-done.5.refs_1_
  38.2 0.0 copy-done.1
  38.2 2.0 %head.1 = (f32[2,128,128]{2,1,0:T(8,128)S(1)}, f32[2,128,128]{2,1,0:T(8,128)S(1)}, f32[16,128]{1,0:T(8,128)S(1)}, bf16[4352,256]{1,0:T(8,128)(2,1)S(1)}, bf16[4352,256]{1,0:T(8,128)(2,1)S(1)}) custom-call(s32[8]{0:T(128)S(1)} %copy-done.5, f32[4,128,128]{2,1,0:T(8,128)S(1)} %bitcast.26, bf16[1,128,4352]{2,1,0:T(8,128)(2,1)S(1)} %mix_own.1.own_ref, ...), custom_call_target="tpu_custom_call" | custom-call | flops 220000000 | tf_op jit(solution)/shard_map/head/pallas_call | solution.py:474
  40.2 0.0 collective-permute-done.9.refs_0_
  40.2 0.7 %open.1 = (bf16[128,2816]{1,0:T(8,128)(2,1)S(1)}, f32[2,128,256]{2,1,0:T(8,128)S(1)}) custom-call(bf16[4352,128]{1,0:T(8,128)(2,1)S(1)} %bitcast.24, bf16[656,128]{1,0:T(8,128)(2,1)S(1)} %collective-permute-done.9.refs_0_, bf16[784,128]{1,0:T(8,128)(2,1)S(1)} %collective-permute-done.5.refs_1_, bf16[4352,256]{1,0:T(8,128)(2,1)S(1)} %get-tuple-element.86.refs_2_.product_a, ...), custom_call_target="tpu_custom_call" | custom-call | flops 1100000000 | tf_op jit(solution)/shard_map/open/pallas_call | solution.py:474
  40.9 1.4 %collective-permute-done.8.packed_ref = bf16[784,128]{1,0:T(8,128)(2,1)S(1)} collective-permute-done((bf16[784,128]{1,0:T(8,128)(2,1)S(1)}, bf16[784,128]{1,0:T(8,128)(2,1)S(1)}, u32[]{:S(2)}, u32[]{:S(2)}) %collective-permute-start.8) | collective-permute-done | bytes 200736 | tf_op jit(solution)/shard_map/ppermute | solution.py:600
  42.3 7.6 %lanczos.1 = (f32[4,4,128,128]{3,2,1,0:T(8,128)S(1)}, f32[16,128]{1,0:T(8,128)S(1)}) custom-call(s32[8]{0:T(128)S(1)} %copy-done.5, bf16[784,128]{1,0:T(8,128)(2,1)S(1)} %collective-permute-done.8.packed_ref, bf16[4352,128]{1,0:T(8,128)(2,1)S(1)} %bitcast.25, bf16[128,2816]{1,0:T(8,128)(2,1)S(1)} %get-tuple-element.90.early_ref, ...), custom_call_target="tpu_custom_call" | custom-call | flops 13200000000 | tf_op jit(solution)/shard_map/lanczos/pallas_call | solution.py:474
  49.9 7.6 %all_to_all.5.stats_ref = f32[8,16,128]{2,1,0:T(8,128)S(1)} all-to-all(f32[8,16,128]{2,1,0:T(8,128)S(1)} %broadcast_in_dim.24), channel_id=1, replica_groups=mesh['seg'=4,'sec'=8] {'sec'}, dimensions={0} | all-to-all | bytes 131072 | tf_op jit(solution)/shard_map/all_to_all | solution.py:494
  57.5 1.4 %finish.1 = (f32[4,128,128]{2,1,0:T(8,128)}, f32[2,4]{1,0:T(2,128)}) custom-call(f32[8,16,128]{2,1,0:T(8,128)S(1)} %all_to_all.5.stats_ref, f32[2,128,128]{2,1,0:T(8,128)S(1)} %get-tuple-element.92.start_a, f32[2,128,128]{2,1,0:T(8,128)S(1)} %get-tuple-element.93.start_b, f32[4,4,128,128]{3,2,1,0:T(8,128)S(1)} %get-tuple-element.96.basis_ref), custom_call_target="tpu_custom_call" | custom-call | flops 2200000000 | tf_op jit(solution)/shard_map/finish/pallas_call | solution.py:474
  (1 shorter events, 0.0 us)
Async XLA Ops:
  0.6 7.5 %collective-permute-start = (bf16[4352,128]{1,0:T(8,128)(2,1)}, bf16[4352,128]{1,0:T(8,128)(2,1)S(1)}, u32[]{:S(2)}, u32[]{:S(2)}) collective-permute-start(bf16[4352,128]{1,0:T(8,128)(2,1)} %bitcast.21), channel_id=1, source_target_pairs={{0,1},{1,0},{2,3},{3,2},{4,5},{5,4},{6,7},{7,6},{8,9},{9,8},{10,11... | collective-permute-start | bytes 3342344 | tf_op jit(solution)/shard_map/ppermute | solution.py:542
  1.1 7.0 %collective-permute-start.1 = (bf16[4,128,128]{2,1,0:T(8,128)(2,1)}, bf16[4,128,128]{2,1,0:T(8,128)(2,1)}, u32[]{:S(2)}, u32[]{:S(2)}) collective-permute-start(bf16[4,128,128]{2,1,0:T(8,128)(2,1)} %bitcast.27), channel_id=1, source_target_pairs={{0,1},{1,0},{2,3},{3,2},{4,5},{5,4},{6,7},{7,6},{8,9},{9,8},{10,11... | collective-permute-start | bytes 393224 | tf_op jit(solution)/shard_map/ppermute | solution.py:543
  1.2 1.2 %copy-start.6 = (bf16[1,1,34,128,128]{4,3,2,1,0:T(8,128)(2,1)S(1)}, bf16[1,1,34,128,128]{4,3,2,1,0:T(8,128)(2,1)}, u32[]{:S(2)}) copy-start(bf16[1,1,34,128,128]{4,3,2,1,0:T(8,128)(2,1)} %param.8) | copy-start | bytes 3342340
  2.5 0.9 %copy-start.8 = (f32[1,1,34,34,4]{3,4,2,1,0:T(4,128)S(1)}, f32[1,1,34,34,4]{3,4,2,1,0:T(4,128)}, u32[]{:S(2)}) copy-start(f32[1,1,34,34,4]{3,4,2,1,0:T(4,128)} %param.10) | copy-start | bytes 55492
  3.4 4.8 %copy-start = (bf16[1,1,34,128,128]{4,3,2,1,0:T(8,128)(2,1)S(1)}, bf16[1,1,34,128,128]{4,3,2,1,0:T(8,128)(2,1)}, u32[]{:S(2)}) copy-start(bf16[1,1,34,128,128]{4,3,2,1,0:T(8,128)(2,1)} %param.7) | copy-start | bytes 3342340
  3.4 4.8 %copy-start.2 = (bf16[1,1,4,1,128,128]{5,4,3,2,1,0:T(8,128)(2,1)S(1)}, bf16[1,1,4,1,128,128]{5,4,3,2,1,0:T(8,128)(2,1)}, u32[]{:S(2)}) copy-start(bf16[1,1,4,1,128,128]{5,4,3,2,1,0:T(8,128)(2,1)} %param.9) | copy-start | bytes 393220
  3.4 4.8 %copy-start.5 = (s32[8]{0:T(128)S(1)}, s32[8]{0:T(128)}, u32[]{:S(2)}) copy-start(s32[8]{0:T(128)} %dims_ref.7) | copy-start | bytes 100
  3.7 0.6 %copy-start.3 = (f32[136,34]{1,0:T(8,128)}, f32[136,34]{1,0:T(8,128)S(1)}, u32[]{:S(2)}) copy-start(f32[136,34]{1,0:T(8,128)S(1)} %get-tuple-element.51.weight_ref) | copy-start | bytes 55492
  4.3 17.5 %collective-permute-start.4 = (bf16[2224,128]{1,0:T(8,128)(2,1)S(1)}, bf16[2224,128]{1,0:T(8,128)(2,1)S(1)}, u32[]{:S(2)}, u32[]{:S(2)}) collective-permute-start(bf16[2224,128]{1,0:T(8,128)(2,1)S(1)} %get-tuple-element.67), channel_id=1, source_target_pairs={{0,6},{1,7},{2,0},{3,1},{4,2},{5,3},{6,4},{7,5},{8,14},{9,15},{10,... | collective-permute-start | bytes 1708040 | tf_op jit(solution)/shard_map/ppermute | solution.py:541
  8.2 0.9 %copy-start.4 = (f32[136,34]{1,0:T(8,128)S(1)}, f32[136,34]{1,0:T(8,128)}, u32[]{:S(2)}) copy-start(f32[136,34]{1,0:T(8,128)} %copy-done.3) | copy-start | bytes 55492
  15.6 10.5 %collective-permute-start.3 = (bf16[656,128]{1,0:T(8,128)(2,1)S(1)}, bf16[656,128]{1,0:T(8,128)(2,1)S(1)}, u32[]{:S(2)}, u32[]{:S(2)}) collective-permute-start(bf16[656,128]{1,0:T(8,128)(2,1)S(1)} %get-tuple-element.52), channel_id=1, source_target_pairs={{0,2},{1,3},{2,4},{3,5},{4,6},{5,7},{6,0},{7,1},{8,10},{9,11},{10,... | collective-permute-start | bytes 503816 | tf_op jit(solution)/shard_map/ppermute | solution.py:560
  15.6 4.9 %copy-start.7 = (bf16[1,1,34,128,128]{4,3,2,1,0:T(8,128)(2,1)S(1)}, bf16[1,1,34,128,128]{4,3,2,1,0:T(8,128)(2,1)}, u32[]{:S(2)}) copy-start(bf16[1,1,34,128,128]{4,3,2,1,0:T(8,128)(2,1)} %param.8) | copy-start | bytes 3342340
  15.7 4.9 %copy-start.9 = (f32[1,34,34,4]{2,3,1,0:T(4,128)S(1)}, f32[1,34,34,4]{2,3,1,0:T(4,128)}, u32[]{:S(2)}) copy-start(f32[1,34,34,4]{2,3,1,0:T(4,128)} %param.11) | copy-start | bytes 55492
  18.5 11.8 %collective-permute-start.2 = (bf16[784,128]{1,0:T(8,128)(2,1)S(1)}, bf16[784,128]{1,0:T(8,128)(2,1)S(1)}, u32[]{:S(2)}, u32[]{:S(2)}) collective-permute-start(bf16[784,128]{1,0:T(8,128)(2,1)S(1)} %get-tuple-element.64), channel_id=1, source_target_pairs={{0,2},{1,3},{2,4},{3,5},{4,6},{5,7},{6,0},{7,1},{8,10},{9,11},{10,... | collective-permute-start | bytes 602120 | tf_op jit(solution)/shard_map/ppermute | solution.py:568
  21.8 12.6 %collective-permute-start.7 = (bf16[784,128]{1,0:T(8,128)(2,1)S(1)}, bf16[784,128]{1,0:T(8,128)(2,1)S(1)}, u32[]{:S(2)}, u32[]{:S(2)}) collective-permute-start(bf16[784,128]{1,0:T(8,128)(2,1)S(1)} %get-tuple-element.75), channel_id=1, source_target_pairs={{0,2},{1,3},{2,4},{3,5},{4,6},{5,7},{6,0},{7,1},{8,10},{9,11},{10,... | collective-permute-start | bytes 602120 | tf_op jit(solution)/shard_map/ppermute | solution.py:575
  23.9 8.1 %collective-permute-start.6 = (bf16[2224,128]{1,0:T(8,128)(2,1)S(1)}, bf16[2224,128]{1,0:T(8,128)(2,1)S(1)}, u32[]{:S(2)}, u32[]{:S(2)}) collective-permute-start(bf16[2224,128]{1,0:T(8,128)(2,1)S(1)} %select_select_fusion), channel_id=1, source_target_pairs={{0,1},{1,0},{2,3},{3,2},{4,5},{5,4},{6,7},{7,6},{8,9},{9,8},{10,11... | collective-permute-start | bytes 1708040 | tf_op jit(solution)/shard_map/ppermute | solution.py:578
  26.1 14.1 %collective-permute-start.9 = (bf16[656,128]{1,0:T(8,128)(2,1)S(1)}, bf16[656,128]{1,0:T(8,128)(2,1)S(1)}, u32[]{:S(2)}, u32[]{:S(2)}) collective-permute-start(bf16[656,128]{1,0:T(8,128)(2,1)S(1)} %add_convert_fusion.2.refs_0_), channel_id=1, source_target_pairs={{0,8},{8,16},{16,24},{24,0},{1,9},{9,17},{17,25},{25,1},{2,10},{10... | collective-permute-start | bytes 503816 | tf_op jit(solution)/shard_map/ppermute | solution.py:584
  30.4 7.8 %collective-permute-start.5 = (bf16[784,128]{1,0:T(8,128)(2,1)S(1)}, bf16[784,128]{1,0:T(8,128)(2,1)S(1)}, u32[]{:S(2)}, u32[]{:S(2)}) collective-permute-start(bf16[784,128]{1,0:T(8,128)(2,1)S(1)} %add_convert_fusion.1.refs_1_), channel_id=1, source_target_pairs={{0,8},{8,16},{16,24},{24,0},{1,9},{9,17},{17,25},{25,1},{2,10},{10... | collective-permute-start | bytes 602120 | tf_op jit(solution)/shard_map/ppermute | solution.py:592
  34.5 3.7 %copy-start.1 = (f32[1,4,1,128,128]{4,3,2,1,0:T(8,128)S(1)}, f32[1,4,1,128,128]{4,3,2,1,0:T(8,128)}, u32[]{:S(2)}) copy-start(f32[1,4,1,128,128]{4,3,2,1,0:T(8,128)} %param.12) | copy-start | bytes 786436
  34.5 7.8 %collective-permute-start.8 = (bf16[784,128]{1,0:T(8,128)(2,1)S(1)}, bf16[784,128]{1,0:T(8,128)(2,1)S(1)}, u32[]{:S(2)}, u32[]{:S(2)}) collective-permute-start(bf16[784,128]{1,0:T(8,128)(2,1)S(1)} %add_convert_fusion.refs_2_), channel_id=1, source_target_pairs={{0,8},{8,16},{16,24},{24,0},{1,9},{9,17},{17,25},{25,1},{2,10},{10... | collective-permute-start | bytes 602120 | tf_op jit(solution)/shard_map/ppermute | solution.py:600

commit v16 on v13

--- a/solution.py
+++ b/solution.py
@@ -28,8 +28,9 @@
 
 
 def chunks_of(width):
-    side = width // 6 * 2
-    return (0, side), (side, side), (2 * side, width - 2 * side)
+    one = width // 6 * 2
+    two = (width - one) // 4 * 2
+    return (0, one), (one, two), (one + two, width - one - two)
 
 
 def iotas(shape):
@@ -51,7 +52,7 @@
     half, tile = folded.shape
     row, lane = iotas((half, tile))
     rolled = pltpu.roll(folded, half, 1)
-    turned = jnp.transpose(jnp.concatenate([folded, rolled], axis=0).astype(BF16)).astype(F32)
+    turned = jnp.transpose(jnp.concatenate([folded, rolled], axis=0))
     top = jnp.where((lane < half) & (row > lane), turned[:half], folded)
     low = jnp.where((lane >= half) & (row > lane - half), rolled, turned[half:])
     low = jnp.where(lane == row + half, diagonal, low)
@@ -339,24 +340,61 @@
             unpack_into(count, tile, reader(ref), write, diag)
 
 
-def open_kernel(width, tile, environ_ref, *refs):
-    chunks = chunks_of(width)[:-1]
-    packed_refs, (*product_refs, bound_ref, image_ref, diag) = refs[: len(chunks)], refs[len(chunks) :]
-    bound_blocks(chunks, tile, packed_refs, environ_ref, bound_ref, diag)
+def open_kernel(
+    width, tile, dims_ref, environ_ref, early_in, middle_in, own_ref, next_ref, after_ref,
+    start_a, start_b, norm_ref, product_a, product_b,
+    bound_ref, image_ref, basis_ref, stats_ref, late_s, product_s, diag,
+):
+    chunks = chunks_of(width)
+    bound_blocks(chunks[:-1], tile, (early_in, middle_in), environ_ref, bound_ref, diag)
     rows = bound_ref.shape[1]
-    for group, product_ref in enumerate(product_refs):
+    for group, product_ref in enumerate((product_a, product_b)):
         image_ref[group] = jnp.dot(bound_ref[...], product_ref[:rows, :], preferred_element_type=F32)
 
+    @pl.when(lax.axis_index("seg") == 0)
+    def _():
+        first, count = chunks[-1]
+        for w in range(count):
+            late_s[:, w * tile : (w + 1) * tile] = environ_ref[
+                (first + w) * tile : (first + w + 1) * tile, :
+            ]
+        lanczos_steps(
+            width, tile, dims_ref, bound_ref, late_s, image_ref, own_ref, next_ref, after_ref,
+            start_a, start_b, norm_ref, product_a, product_b, basis_ref, stats_ref, product_s,
+        )
+
 
 def lanczos_kernel(
-    width, tile, dims_ref, packed_ref, environ_ref, early_ref, image_ref, own_ref, next_ref, after_ref,
-    start_a, start_b, norm_ref, product_a, product_b, basis_ref, stats_ref,
+    width, tile, dims_ref, packed_ref, early_ref, image_ref, own_ref, next_ref, after_ref,
+    start_a, start_b, norm_ref, product_a, product_b, basis_in, stats_in, basis_ref, stats_ref,
     late_s, product_s, diag,
+):
+    segment = lax.axis_index("seg")
+
+    @pl.when(segment == 0)
+    def _():
+        basis_ref[...] = basis_in[...]
+        stats_ref[...] = stats_in[...]
+
+    @pl.when(segment != 0)
+    def _():
+        def write(w, block):
+            late_s[:, w * tile : (w + 1) * tile] = block.astype(BF16)
+
+        unpack_into(chunks_of(width)[-1][1], tile, reader(packed_ref), write, diag)
+        lanczos_steps(
+            width, tile, dims_ref, early_ref, late_s, image_ref, own_ref, next_ref, after_ref,
+            start_a, start_b, norm_ref, product_a, product_b, basis_ref, stats_ref, product_s,
+        )
+
+
+def lanczos_steps(
+    width, tile, dims_ref, early_ref, late_s, image_ref, own_ref, next_ref, after_ref,
+    start_a, start_b, norm_ref, product_a, product_b, basis_ref, stats_ref, product_s,
 ):
     states = len(CHARGES)
     sector = lax.axis_index("sec")
     last = chunks_of(width)[-1:]
-    bound_blocks(last, tile, [packed_ref], environ_ref, late_s, diag)
     rows, columns = live_limits(dims_ref, sector)
     row, lane = iotas((tile, tile))
     rights = [own_ref.at[0], next_ref.at[0], next_ref.at[1], after_ref.at[0]]
@@ -610,31 +648,31 @@
         jax.ShapeDtypeStruct((width * tile, tile), BF16), [diag], 6, 2,
     )
     middle_bound, new_env = lax.optimization_barrier((middle_bound, new_env))
-    bound, image = call(
-        "open", functools.partial(open_kernel, width, tile), [],
-        [environ, early_bound, middle_bound, products_a, products_b],
-        (
+    steps = [own_mixed, next_mixed, after_mixed, start_a, start_b, norms, products_a, products_b]
+    results = [
+        jax.ShapeDtypeStruct((LANCZOS, states, tile, tile), F32),
+        jax.ShapeDtypeStruct((16, 128), F32),
+    ]
+    steps_scratch = [
+        pltpu.VMEM((tile, parts[-1][1] * tile), BF16),
+        pltpu.VMEM((len(GROUPS), width * tile, 2 * tile), BF16),
+        diag,
+    ]
+    bound, image, basis, stats = call(
+        "open", functools.partial(open_kernel, width, tile),
+        [sector_dims], [environ, early_bound, middle_bound] + steps,
+        [
             jax.ShapeDtypeStruct((tile, parts[-1][0] * tile), BF16),
             jax.ShapeDtypeStruct((len(GROUPS), tile, 2 * tile), F32),
-        ),
-        [diag], 12, 1,
+        ]
+        + results,
+        steps_scratch, 24, 1,
     )
     late_bound, bound = lax.optimization_barrier((late_bound, bound))
     basis, stats = call(
         "lanczos", functools.partial(lanczos_kernel, width, tile),
-        [sector_dims],
-        [late_bound, environ, bound, image, own_mixed, next_mixed, after_mixed, start_a, start_b,
-         norms, products_a, products_b],
-        (
-            jax.ShapeDtypeStruct((LANCZOS, states, tile, tile), F32),
-            jax.ShapeDtypeStruct((16, 128), F32),
-        ),
-        [
-            pltpu.VMEM((tile, parts[-1][1] * tile), BF16),
-            pltpu.VMEM((len(GROUPS), width * tile, 2 * tile), BF16),
-            diag,
-        ],
-        22, 12,
+        [sector_dims], [late_bound, bound, image] + steps + [basis, stats], results,
+        steps_scratch, 24, 12,
     )
     stats = gathered(stats, "sec")
     entries = float(states * sector_count * tile * tile)

time: 58.1 us -> 57.1 us (0.983)
  waiting for transfers between devices: 4.53 us -> 2.89 us
  Pallas kernels: 28.8 us -> 29.4 us
    ppermute x1, waiting for transfers between devices: 2.22 us -> 0.01 us  [on_device(): late_bound = lax.ppermute(late, 'seg', onward)]
    ppermute x1, waiting for transfers between devices: 0.11 us -> 0.84 us  [on_device(): middle_arrived = lax.ppermute(middle_outgoing, 'sec', up_two)]
    pallas_call x11, Pallas kernels: 28.8 us -> 29.4 us  [call(): pl.pallas_call(kernel, out_shape=outs, in_specs=[smem()] * len(scalars) +...]
  transfers between devices with their start and end apart: 10 -> 10, of which waited for: 4 -> 2; matrix products, arithmetic and copies ran while one was open for 0% -> 0% of each run, Pallas kernels for 34% -> 48%
where the time goes in v16:
time: 57.1 us; the launch traced here: 56.8 us
  Pallas kernels  29.4 us (51%)
  starting transfers between devices  13.8 us (24%)
  blocking collectives  7.57 us (13%)
  waiting for transfers between devices  2.89 us (5%)
  local copies, waits for them, and re-layouts  2.16 us (4%)
  between operations  0.8 us (1%)
    pallas_call x11, Pallas kernels, call(): pl.pallas_call(kernel, out_shape=outs, in_specs=[smem()] * len(scalars) +...  29.4 us
    all_to_all x1, blocking collectives, gathered(): lax.all_to_all(jnp.broadcast_to(value, (count,) + value.shape), axis, 0, 0)  7.57 us
    ppermute x1, starting transfers between devices, on_device(): right_far = lax.ppermute(right_packed, 'sec', down_two)  3.93 us
    unnamed x16, local copies, waits for them, and re-layouts  2.15 us
    ppermute x1, starting transfers between devices, on_device(): late_arrived = lax.ppermute(late_outgoing, 'sec', up_two)  2.03 us
    ppermute x1, waiting for transfers between devices, on_device(): early_arrived = lax.ppermute(outgoing[0], 'sec', up_two)  2.02 us
    ppermute x1, starting transfers between devices, on_device(): middle_arrived = lax.ppermute(middle_outgoing, 'sec', up_two)  1.96 us
    ppermute x1, starting transfers between devices, on_device(): late_bound = lax.ppermute(late, 'seg', onward)  1.85 us
  transfers between devices with their start and end apart: 10, of which 2 were waited for; matrix products, arithmetic and copies ran while one was open for 0% of the time, Pallas kernels for 48%

profile of v16, /device:TPU:0, one launch (start us, length us, event | category | flops | bytes accessed | tf_op | source)
XLA Modules:
  0.0 56.8 jit_solution(11173700055798311331)
XLA Ops:
  0.6 0.5 collective-permute-start
  1.1 0.1 collective-permute-start.1
  1.2 0.0 copy-start.5
  1.2 1.2 %copy-done.5 = bf16[1,1,34,128,128]{4,3,2,1,0:T(8,128)(2,1)S(1)} copy-done((bf16[1,1,34,128,128]{4,3,2,1,0:T(8,128)(2,1)S(1)}, bf16[1,1,34,128,128]{4,3,2,1,0:T(8,128)(2,1)}, u32[]{:S(2)}) %copy-start.5) | copy-done | bytes 1114136
  2.5 0.0 copy-start
  2.5 0.0 copy-start.2
  2.5 0.0 copy-start.4
  2.5 0.3 pack_right.1
  2.8 3.9 %collective-permute-start.4 = (bf16[2224,128]{1,0:T(8,128)(2,1)S(1)}, bf16[2224,128]{1,0:T(8,128)(2,1)S(1)}, u32[]{:S(2)}, u32[]{:S(2)}) collective-permute-start(bf16[2224,128]{1,0:T(8,128)(2,1)S(1)} %pack_right.1), channel_id=1, source_target_pairs={{0,6},{1,7},{2,0},{3,1},{4,2},{5,3},{6,4},{7,5},{8,14},{9,15},{10,... | collective-permute-start | bytes 1708040 | tf_op jit(solution)/shard_map/ppermute | solution.py:577
  6.7 0.0 collective-permute-done.1.far_site_ref
  6.7 0.0 collective-permute-done.far_environ_ref
  6.7 0.0 copy-done
  6.7 0.0 copy-done.2
  6.7 0.0 copy-done.4
  6.7 0.0 copy-start.3
  6.7 0.9 %copy-done.3 = f32[1,1,34,34,4]{3,4,2,1,0:T(4,128)S(1)} copy-done((f32[1,1,34,34,4]{3,4,2,1,0:T(4,128)S(1)}, f32[1,1,34,34,4]{3,4,2,1,0:T(4,128)}, u32[]{:S(2)}) %copy-start.3) | copy-done | bytes 18520
  7.6 6.5 %fold_up.1 = (bf16[656,128]{1,0:T(8,128)(2,1)S(1)}, bf16[784,128]{1,0:T(8,128)(2,1)S(1)}, bf16[784,128]{1,0:T(8,128)(2,1)S(1)}) custom-call(s32[8]{0:T(128)S(1)} %copy-done.4, bf16[4352,128]{1,0:T(8,128)(2,1)S(1)} %bitcast.22, bf16[4,128,128]{2,1,0:T(8,128)(2,1)S(1)} %bitcast.27, bf16[4352,128]{1,0:T(8,128)(2,1)S(1)} %collective-permute-done.far_environ_ref, ...), custom_call_target="tpu_custom_call" | custom-call | flops 13200000000 | tf_op jit(solution)/shard_map/fold_up/pallas_call | solution.py:510
  14.1 0.1 collective-permute-start.3
  14.2 0.0 copy-start.6
  14.2 0.0 copy-start.7
  14.2 2.8 %fold_own.1 = (f32[656,128]{1,0:T(8,128)S(1)}, f32[784,128]{1,0:T(8,128)S(1)}, f32[784,128]{1,0:T(8,128)S(1)}) custom-call(s32[8]{0:T(128)S(1)} %copy-done.4, bf16[4352,128]{1,0:T(8,128)(2,1)S(1)} %bitcast.23, bf16[4,128,128]{2,1,0:T(8,128)(2,1)S(1)} %bitcast.28, bf16[4352,128]{1,0:T(8,128)(2,1)S(1)} %collective-permute-done.far_environ_ref, ...), custom_call_target="tpu_custom_call" | custom-call | flops 110000000 | tf_op jit(solution)/shard_map/fold_own/pallas_call | solution.py:510
  17.1 2.0 %collective-permute-start.2 = (bf16[784,128]{1,0:T(8,128)(2,1)S(1)}, bf16[784,128]{1,0:T(8,128)(2,1)S(1)}, u32[]{:S(2)}, u32[]{:S(2)}) collective-permute-start(bf16[784,128]{1,0:T(8,128)(2,1)S(1)} %get-tuple-element.63), channel_id=1, source_target_pairs={{0,2},{1,3},{2,4},{3,5},{4,6},{5,7},{6,0},{7,1},{8,10},{9,11},{10,... | collective-permute-start | bytes 602120 | tf_op jit(solution)/shard_map/ppermute | solution.py:604
  19.0 0.0 copy-done.6
  19.0 0.0 copy-done.7
  19.0 1.3 %mix_own.1.own_ref = bf16[1,128,4352]{2,1,0:T(8,128)(2,1)S(1)} custom-call(bf16[4352,128]{1,0:T(8,128)(2,1)S(1)} %bitcast.32, f32[136,34]{1,0:T(8,128)S(1)} %bitcast.33), custom_call_target="tpu_custom_call" | custom-call | flops 1100000000 | tf_op jit(solution)/shard_map/mix_own/pallas_call | solution.py:510
  20.4 0.0 collective-permute-done.4.far_ref
  20.4 2.0 %collective-permute-start.7 = (bf16[784,128]{1,0:T(8,128)(2,1)S(1)}, bf16[784,128]{1,0:T(8,128)(2,1)S(1)}, u32[]{:S(2)}, u32[]{:S(2)}) collective-permute-start(bf16[784,128]{1,0:T(8,128)(2,1)S(1)} %get-tuple-element.73), channel_id=1, source_target_pairs={{0,2},{1,3},{2,4},{3,5},{4,6},{5,7},{6,0},{7,1},{8,10},{9,11},{10,... | collective-permute-start | bytes 602120 | tf_op jit(solution)/shard_map/ppermute | solution.py:611
  22.4 0.1 select_select_fusion
  22.5 0.1 collective-permute-start.6
  22.5 2.0 %collective-permute-done.3 = bf16[656,128]{1,0:T(8,128)(2,1)S(1)} collective-permute-done((bf16[656,128]{1,0:T(8,128)(2,1)S(1)}, bf16[656,128]{1,0:T(8,128)(2,1)S(1)}, u32[]{:S(2)}, u32[]{:S(2)}) %collective-permute-start.3) | collective-permute-done | bytes 167968 | tf_op jit(solution)/shard_map/ppermute | solution.py:596
  24.6 0.1 add_convert_fusion.2.refs_0_
  24.6 1.6 %collective-permute-start.9 = (bf16[656,128]{1,0:T(8,128)(2,1)S(1)}, bf16[656,128]{1,0:T(8,128)(2,1)S(1)}, u32[]{:S(2)}, u32[]{:S(2)}) collective-permute-start(bf16[656,128]{1,0:T(8,128)(2,1)S(1)} %add_convert_fusion.2.refs_0_), channel_id=1, source_target_pairs={{0,8},{8,16},{16,24},{24,0},{1,9},{9,17},{17,25},{25,1},{2,10},{10... | collective-permute-start | bytes 503816 | tf_op jit(solution)/shard_map/ppermute | solution.py:620
  26.2 1.8 %mix_after.1.after_ref = bf16[1,128,4352]{2,1,0:T(8,128)(2,1)S(1)} custom-call(bf16[2224,128]{1,0:T(8,128)(2,1)S(1)} %collective-permute-done.4.far_ref, f32[136,34]{1,0:T(8,128)S(1)} %bitcast.34), custom_call_target="tpu_custom_call" | custom-call | flops 2200000000 | tf_op jit(solution)/shard_map/mix_after/pallas_call | solution.py:510
  28.0 0.8 %collective-permute-done.2 = bf16[784,128]{1,0:T(8,128)(2,1)S(1)} collective-permute-done((bf16[784,128]{1,0:T(8,128)(2,1)S(1)}, bf16[784,128]{1,0:T(8,128)(2,1)S(1)}, u32[]{:S(2)}, u32[]{:S(2)}) %collective-permute-start.2) | collective-permute-done | bytes 200736 | tf_op jit(solution)/shard_map/ppermute | solution.py:604
  28.9 0.1 add_convert_fusion.1.refs_1_
  28.9 1.6 %collective-permute-start.5 = (bf16[784,128]{1,0:T(8,128)(2,1)S(1)}, bf16[784,128]{1,0:T(8,128)(2,1)S(1)}, u32[]{:S(2)}, u32[]{:S(2)}) collective-permute-start(bf16[784,128]{1,0:T(8,128)(2,1)S(1)} %add_convert_fusion.1.refs_1_), channel_id=1, source_target_pairs={{0,8},{8,16},{16,24},{24,0},{1,9},{9,17},{17,25},{25,1},{2,10},{10... | collective-permute-start | bytes 602120 | tf_op jit(solution)/shard_map/ppermute | solution.py:628
  30.5 0.0 collective-permute-done.6.near_ref
  30.6 2.4 %mix_next.1.next_ref = bf16[2,128,4352]{2,1,0:T(8,128)(2,1)S(1)} custom-call(bf16[2224,128]{1,0:T(8,128)(2,1)S(1)} %collective-permute-done.6.near_ref, f32[136,34]{1,0:T(8,128)S(1)} %bitcast.35), custom_call_target="tpu_custom_call" | custom-call | flops 3300000000 | tf_op jit(solution)/shard_map/mix_next/pallas_call | solution.py:510
  33.0 0.0 collective-permute-done.7
  33.0 0.1 add_convert_fusion.refs_2_
  33.0 0.0 copy-start.1
  33.0 1.9 %collective-permute-start.8 = (bf16[784,128]{1,0:T(8,128)(2,1)S(1)}, bf16[784,128]{1,0:T(8,128)(2,1)S(1)}, u32[]{:S(2)}, u32[]{:S(2)}) collective-permute-start(bf16[784,128]{1,0:T(8,128)(2,1)S(1)} %add_convert_fusion.refs_2_), channel_id=1, source_target_pairs={{0,8},{8,16},{16,24},{24,0},{1,9},{9,17},{17,25},{25,1},{2,10},{10... | collective-permute-start | bytes 602120 | tf_op jit(solution)/shard_map/ppermute | solution.py:636
  34.9 1.8 %unpack_env.1 = bf16[4352,128]{1,0:T(8,128)(2,1)} custom-call(bf16[656,128]{1,0:T(8,128)(2,1)S(1)} %add_convert_fusion.2.refs_0_, bf16[784,128]{1,0:T(8,128)(2,1)S(1)} %add_convert_fusion.1.refs_1_, bf16[784,128]{1,0:T(8,128)(2,1)S(1)} %add_convert_fusion.refs_2_), custom_call_target="tpu_custom_call" | custom-call | flops 2200000000 | tf_op jit(solution)/shard_map/unpack_env/pallas_call | solution.py:510
  36.7 0.0 collective-permute-done.5.middle_in
  36.7 0.0 copy-done.1
  36.7 2.0 %head.1 = (f32[2,128,128]{2,1,0:T(8,128)S(1)}, f32[2,128,128]{2,1,0:T(8,128)S(1)}, f32[16,128]{1,0:T(8,128)S(1)}, bf16[4352,256]{1,0:T(8,128)(2,1)S(1)}, bf16[4352,256]{1,0:T(8,128)(2,1)S(1)}) custom-call(s32[8]{0:T(128)S(1)} %copy-done.4, f32[4,128,128]{2,1,0:T(8,128)S(1)} %bitcast.25, bf16[1,128,4352]{2,1,0:T(8,128)(2,1)S(1)} %mix_own.1.own_ref, ...), custom_call_target="tpu_custom_call" | custom-call | flops 220000000 | tf_op jit(solution)/shard_map/head/pallas_call | solution.py:510
  38.7 0.0 collective-permute-done.9.early_in
  38.7 8.2 %open.1 = (bf16[128,2816]{1,0:T(8,128)(2,1)S(1)}, f32[2,128,256]{2,1,0:T(8,128)S(1)}, f32[4,4,128,128]{3,2,1,0:T(8,128)S(1)}, f32[16,128]{1,0:T(8,128)S(1)}) custom-call(s32[8]{0:T(128)S(1)} %copy-done.4, bf16[4352,128]{1,0:T(8,128)(2,1)S(1)} %bitcast.24, bf16[656,128]{1,0:T(8,128)(2,1)S(1)} %collective-permute-done.9.early_in, ...), custom_call_target="tpu_custom_call" | custom-call | flops 1100000000 | tf_op jit(solution)/shard_map/open/pallas_call | solution.py:510
  46.9 0.0 collective-permute-done.8.packed_ref
  46.9 0.9 %lanczos.1 = (f32[4,4,128,128]{3,2,1,0:T(8,128)S(1)}, f32[16,128]{1,0:T(8,128)S(1)}) custom-call(s32[8]{0:T(128)S(1)} %copy-done.4, bf16[784,128]{1,0:T(8,128)(2,1)S(1)} %collective-permute-done.8.packed_ref, bf16[128,2816]{1,0:T(8,128)(2,1)S(1)} %get-tuple-element.91.early_ref, f32[2,128,256]{2,1,0:T(8,128)S(1)} %get-tuple-element.92.image_ref, ...), custom_call_target="tpu_custom_call" | custom-call | flops 13200000000 | tf_op jit(solution)/shard_map/lanczos/pallas_call | solution.py:510
  47.8 7.6 %all_to_all.5.stats_ref = f32[8,16,128]{2,1,0:T(8,128)S(1)} all-to-all(f32[8,16,128]{2,1,0:T(8,128)S(1)} %broadcast_in_dim.24), channel_id=1, replica_groups=mesh['seg'=4,'sec'=8] {'sec'}, dimensions={0} | all-to-all | bytes 131072 | tf_op jit(solution)/shard_map/all_to_all | solution.py:530
  55.4 1.4 %finish.1 = (f32[4,128,128]{2,1,0:T(8,128)}, f32[2,4]{1,0:T(2,128)}) custom-call(f32[8,16,128]{2,1,0:T(8,128)S(1)} %all_to_all.5.stats_ref, f32[2,128,128]{2,1,0:T(8,128)S(1)} %get-tuple-element.84.start_a, f32[2,128,128]{2,1,0:T(8,128)S(1)} %get-tuple-element.85.start_b, f32[4,4,128,128]{3,2,1,0:T(8,128)S(1)} %get-tuple-element.96.basis_ref), custom_call_target="tpu_custom_call" | custom-call | flops 2200000000 | tf_op jit(solution)/shard_map/finish/pallas_call | solution.py:510
  (1 shorter events, 0.0 us)
Async XLA Ops:
  0.6 6.1 %collective-permute-start = (bf16[4352,128]{1,0:T(8,128)(2,1)}, bf16[4352,128]{1,0:T(8,128)(2,1)S(1)}, u32[]{:S(2)}, u32[]{:S(2)}) collective-permute-start(bf16[4352,128]{1,0:T(8,128)(2,1)} %bitcast.21), channel_id=1, source_target_pairs={{0,1},{1,0},{2,3},{3,2},{4,5},{5,4},{6,7},{7,6},{8,9},{9,8},{10,11... | collective-permute-start | bytes 3342344 | tf_op jit(solution)/shard_map/ppermute | solution.py:578
  1.1 5.6 %collective-permute-start.1 = (bf16[4,128,128]{2,1,0:T(8,128)(2,1)}, bf16[4,128,128]{2,1,0:T(8,128)(2,1)}, u32[]{:S(2)}, u32[]{:S(2)}) collective-permute-start(bf16[4,128,128]{2,1,0:T(8,128)(2,1)} %bitcast.26), channel_id=1, source_target_pairs={{0,1},{1,0},{2,3},{3,2},{4,5},{5,4},{6,7},{7,6},{8,9},{9,8},{10,11... | collective-permute-start | bytes 393224 | tf_op jit(solution)/shard_map/ppermute | solution.py:579
  1.2 1.2 %copy-start.5 = (bf16[1,1,34,128,128]{4,3,2,1,0:T(8,128)(2,1)S(1)}, bf16[1,1,34,128,128]{4,3,2,1,0:T(8,128)(2,1)}, u32[]{:S(2)}) copy-start(bf16[1,1,34,128,128]{4,3,2,1,0:T(8,128)(2,1)} %param.8) | copy-start | bytes 3342340
  2.5 4.2 %copy-start = (bf16[1,1,34,128,128]{4,3,2,1,0:T(8,128)(2,1)S(1)}, bf16[1,1,34,128,128]{4,3,2,1,0:T(8,128)(2,1)}, u32[]{:S(2)}) copy-start(bf16[1,1,34,128,128]{4,3,2,1,0:T(8,128)(2,1)} %param.7) | copy-start | bytes 3342340
  2.5 4.2 %copy-start.2 = (bf16[1,1,4,1,128,128]{5,4,3,2,1,0:T(8,128)(2,1)S(1)}, bf16[1,1,4,1,128,128]{5,4,3,2,1,0:T(8,128)(2,1)}, u32[]{:S(2)}) copy-start(bf16[1,1,4,1,128,128]{5,4,3,2,1,0:T(8,128)(2,1)} %param.9) | copy-start | bytes 393220
  2.5 4.2 %copy-start.4 = (s32[8]{0:T(128)S(1)}, s32[8]{0:T(128)}, u32[]{:S(2)}) copy-start(s32[8]{0:T(128)} %dims_ref.9) | copy-start | bytes 100
  2.8 17.6 %collective-permute-start.4 = (bf16[2224,128]{1,0:T(8,128)(2,1)S(1)}, bf16[2224,128]{1,0:T(8,128)(2,1)S(1)}, u32[]{:S(2)}, u32[]{:S(2)}) collective-permute-start(bf16[2224,128]{1,0:T(8,128)(2,1)S(1)} %pack_right.1), channel_id=1, source_target_pairs={{0,6},{1,7},{2,0},{3,1},{4,2},{5,3},{6,4},{7,5},{8,14},{9,15},{10,... | collective-permute-start | bytes 1708040 | tf_op jit(solution)/shard_map/ppermute | solution.py:577
  6.7 0.9 %copy-start.3 = (f32[1,1,34,34,4]{3,4,2,1,0:T(4,128)S(1)}, f32[1,1,34,34,4]{3,4,2,1,0:T(4,128)}, u32[]{:S(2)}) copy-start(f32[1,1,34,34,4]{3,4,2,1,0:T(4,128)} %param.10) | copy-start | bytes 55492
  14.1 10.4 %collective-permute-start.3 = (bf16[656,128]{1,0:T(8,128)(2,1)S(1)}, bf16[656,128]{1,0:T(8,128)(2,1)S(1)}, u32[]{:S(2)}, u32[]{:S(2)}) collective-permute-start(bf16[656,128]{1,0:T(8,128)(2,1)S(1)} %get-tuple-element.51), channel_id=1, source_target_pairs={{0,2},{1,3},{2,4},{3,5},{4,6},{5,7},{6,0},{7,1},{8,10},{9,11},{10,... | collective-permute-start | bytes 503816 | tf_op jit(solution)/shard_map/ppermute | solution.py:596
  14.2 4.8 %copy-start.6 = (bf16[1,1,34,128,128]{4,3,2,1,0:T(8,128)(2,1)S(1)}, bf16[1,1,34,128,128]{4,3,2,1,0:T(8,128)(2,1)}, u32[]{:S(2)}) copy-start(bf16[1,1,34,128,128]{4,3,2,1,0:T(8,128)(2,1)} %param.8) | copy-start | bytes 3342340
  14.2 4.8 %copy-start.7 = (f32[1,34,34,4]{2,3,1,0:T(4,128)S(1)}, f32[1,34,34,4]{2,3,1,0:T(4,128)}, u32[]{:S(2)}) copy-start(f32[1,34,34,4]{2,3,1,0:T(4,128)} %param.11) | copy-start | bytes 55492
  17.1 11.8 %collective-permute-start.2 = (bf16[784,128]{1,0:T(8,128)(2,1)S(1)}, bf16[784,128]{1,0:T(8,128)(2,1)S(1)}, u32[]{:S(2)}, u32[]{:S(2)}) collective-permute-start(bf16[784,128]{1,0:T(8,128)(2,1)S(1)} %get-tuple-element.63), channel_id=1, source_target_pairs={{0,2},{1,3},{2,4},{3,5},{4,6},{5,7},{6,0},{7,1},{8,10},{9,11},{10,... | collective-permute-start | bytes 602120 | tf_op jit(solution)/shard_map/ppermute | solution.py:604
  20.4 12.6 %collective-permute-start.7 = (bf16[784,128]{1,0:T(8,128)(2,1)S(1)}, bf16[784,128]{1,0:T(8,128)(2,1)S(1)}, u32[]{:S(2)}, u32[]{:S(2)}) collective-permute-start(bf16[784,128]{1,0:T(8,128)(2,1)S(1)} %get-tuple-element.73), channel_id=1, source_target_pairs={{0,2},{1,3},{2,4},{3,5},{4,6},{5,7},{6,0},{7,1},{8,10},{9,11},{10,... | collective-permute-start | bytes 602120 | tf_op jit(solution)/shard_map/ppermute | solution.py:611
  22.5 8.1 %collective-permute-start.6 = (bf16[2224,128]{1,0:T(8,128)(2,1)S(1)}, bf16[2224,128]{1,0:T(8,128)(2,1)S(1)}, u32[]{:S(2)}, u32[]{:S(2)}) collective-permute-start(bf16[2224,128]{1,0:T(8,128)(2,1)S(1)} %select_select_fusion), channel_id=1, source_target_pairs={{0,1},{1,0},{2,3},{3,2},{4,5},{5,4},{6,7},{7,6},{8,9},{9,8},{10,11... | collective-permute-start | bytes 1708040 | tf_op jit(solution)/shard_map/ppermute | solution.py:614
  24.6 14.1 %collective-permute-start.9 = (bf16[656,128]{1,0:T(8,128)(2,1)S(1)}, bf16[656,128]{1,0:T(8,128)(2,1)S(1)}, u32[]{:S(2)}, u32[]{:S(2)}) collective-permute-start(bf16[656,128]{1,0:T(8,128)(2,1)S(1)} %add_convert_fusion.2.refs_0_), channel_id=1, source_target_pairs={{0,8},{8,16},{16,24},{24,0},{1,9},{9,17},{17,25},{25,1},{2,10},{10... | collective-permute-start | bytes 503816 | tf_op jit(solution)/shard_map/ppermute | solution.py:620
  28.9 7.8 %collective-permute-start.5 = (bf16[784,128]{1,0:T(8,128)(2,1)S(1)}, bf16[784,128]{1,0:T(8,128)(2,1)S(1)}, u32[]{:S(2)}, u32[]{:S(2)}) collective-permute-start(bf16[784,128]{1,0:T(8,128)(2,1)S(1)} %add_convert_fusion.1.refs_1_), channel_id=1, source_target_pairs={{0,8},{8,16},{16,24},{24,0},{1,9},{9,17},{17,25},{25,1},{2,10},{10... | collective-permute-start | bytes 602120 | tf_op jit(solution)/shard_map/ppermute | solution.py:628
  33.0 3.7 %copy-start.1 = (f32[1,4,1,128,128]{4,3,2,1,0:T(8,128)S(1)}, f32[1,4,1,128,128]{4,3,2,1,0:T(8,128)}, u32[]{:S(2)}) copy-start(f32[1,4,1,128,128]{4,3,2,1,0:T(8,128)} %param.12) | copy-start | bytes 786436
  33.0 13.9 %collective-permute-start.8 = (bf16[784,128]{1,0:T(8,128)(2,1)S(1)}, bf16[784,128]{1,0:T(8,128)(2,1)S(1)}, u32[]{:S(2)}, u32[]{:S(2)}) collective-permute-start(bf16[784,128]{1,0:T(8,128)(2,1)S(1)} %add_convert_fusion.refs_2_), channel_id=1, source_target_pairs={{0,8},{8,16},{16,24},{24,0},{1,9},{9,17},{17,25},{25,1},{2,10},{10... | collective-permute-start | bytes 602120 | tf_op jit(solution)/shard_map/ppermute | solution.py:636

commit v17 on v16

--- a/solution.py
+++ b/solution.py
@@ -366,14 +366,13 @@
 
 def lanczos_kernel(
     width, tile, dims_ref, packed_ref, early_ref, image_ref, own_ref, next_ref, after_ref,
-    start_a, start_b, norm_ref, product_a, product_b, basis_in, stats_in, basis_ref, stats_ref,
+    start_a, start_b, norm_ref, product_a, product_b, stats_in, basis_ref, stats_ref,
     late_s, product_s, diag,
 ):
     segment = lax.axis_index("seg")
 
     @pl.when(segment == 0)
     def _():
-        basis_ref[...] = basis_in[...]
         stats_ref[...] = stats_in[...]
 
     @pl.when(segment != 0)
@@ -432,7 +431,7 @@
 
 
 def finish_kernel(
-    entries, stats_ref, start_a, start_b, basis_ref, vector_ref, table_ref
+    entries, stats_ref, start_a, start_b, first_basis_ref, basis_ref, vector_ref, table_ref
 ):
     states = len(CHARGES)
     sector = lax.axis_index("sec")
@@ -487,14 +486,28 @@
     table_ref[...] = table
     lane = lax.broadcasted_iota(jnp.int32, (1, stats.shape[1]), 1)
     starts = {p: ref[k] for members, ref in zip(GROUPS, (start_a, start_b)) for k, p in enumerate(members)}
+    weights = {}
     for p in range(states):
-        value = None
         here = lane == sector * states + p
         for k in range(LANCZOS + 1):
-            weight = jnp.sum(jnp.where(here, vector[k], 0.0), axis=1, keepdims=True)
-            term = weight * (starts[p] if k == 0 else basis_ref[k - 1, p])
-            value = term if value is None else value + term
-        vector_ref[p] = value
+            weights[p, k] = jnp.sum(jnp.where(here, vector[k], 0.0), axis=1, keepdims=True)
+
+    def write(source):
+        for p in range(states):
+            value = weights[p, 0] * starts[p]
+            for k in range(1, LANCZOS + 1):
+                value = value + weights[p, k] * source[k - 1, p]
+            vector_ref[p] = value
+
+    segment = lax.axis_index("seg")
+
+    @pl.when(segment == 0)
+    def _():
+        write(first_basis_ref)
+
+    @pl.when(segment != 0)
+    def _():
+        write(basis_ref)
 
 
 def smem():
@@ -669,15 +682,16 @@
         steps_scratch, 24, 1,
     )
     late_bound, bound = lax.optimization_barrier((late_bound, bound))
+    first_basis = basis
     basis, stats = call(
         "lanczos", functools.partial(lanczos_kernel, width, tile),
-        [sector_dims], [late_bound, bound, image] + steps + [basis, stats], results,
+        [sector_dims], [late_bound, bound, image] + steps + [stats], results,
         steps_scratch, 24, 12,
     )
     stats = gathered(stats, "sec")
     entries = float(states * sector_count * tile * tile)
     vector, table = call(
-        "finish", functools.partial(finish_kernel, entries), [], [stats, start_a, start_b, basis],
+        "finish", functools.partial(finish_kernel, entries), [], [stats, start_a, start_b, first_basis, basis],
         (
             jax.ShapeDtypeStruct((states, tile, tile), F32),
             jax.ShapeDtypeStruct((2, LANCZOS), F32),

time: 57.1 us -> 57 us (level)
  no operation moved by 1% of the time
where the time goes in v17:
time: 57 us; the launch traced here: 56.8 us
  Pallas kernels  29.3 us (51%)
  starting transfers between devices  13.8 us (24%)
  blocking collectives  7.58 us (13%)
  waiting for transfers between devices  2.89 us (5%)
  local copies, waits for them, and re-layouts  2.16 us (4%)
  between operations  0.8 us (1%)
    pallas_call x11, Pallas kernels, call(): pl.pallas_call(kernel, out_shape=outs, in_specs=[smem()] * len(scalars) +...  29.3 us
    all_to_all x1, blocking collectives, gathered(): lax.all_to_all(jnp.broadcast_to(value, (count,) + value.shape), axis, 0, 0)  7.58 us
    ppermute x1, starting transfers between devices, on_device(): right_far = lax.ppermute(right_packed, 'sec', down_two)  3.93 us
    unnamed x16, local copies, waits for them, and re-layouts  2.15 us
    ppermute x1, starting transfers between devices, on_device(): late_arrived = lax.ppermute(late_outgoing, 'sec', up_two)  2.03 us
    ppermute x1, waiting for transfers between devices, on_device(): early_arrived = lax.ppermute(outgoing[0], 'sec', up_two)  2.02 us
    ppermute x1, starting transfers between devices, on_device(): middle_arrived = lax.ppermute(middle_outgoing, 'sec', up_two)  1.96 us
    ppermute x1, starting transfers between devices, on_device(): late_bound = lax.ppermute(late, 'seg', onward)  1.85 us
  transfers between devices with their start and end apart: 10, of which 2 were waited for; matrix products, arithmetic and copies ran while one was open for 0% of the time, Pallas kernels for 48%

profile of v17, /device:TPU:0, one launch (start us, length us, event | category | flops | bytes accessed | tf_op | source)
XLA Modules:
  0.0 56.8 jit_solution(13720106387471681452)
XLA Ops:
  0.6 0.5 collective-permute-start
  1.1 0.1 collective-permute-start.1
  1.2 0.0 copy-start.5
  1.2 1.2 %copy-done.5 = bf16[1,1,34,128,128]{4,3,2,1,0:T(8,128)(2,1)S(1)} copy-done((bf16[1,1,34,128,128]{4,3,2,1,0:T(8,128)(2,1)S(1)}, bf16[1,1,34,128,128]{4,3,2,1,0:T(8,128)(2,1)}, u32[]{:S(2)}) %copy-start.5) | copy-done | bytes 1114136
  2.5 0.0 copy-start
  2.5 0.0 copy-start.2
  2.5 0.0 copy-start.4
  2.5 0.3 pack_right.1
  2.8 3.9 %collective-permute-start.4 = (bf16[2224,128]{1,0:T(8,128)(2,1)S(1)}, bf16[2224,128]{1,0:T(8,128)(2,1)S(1)}, u32[]{:S(2)}, u32[]{:S(2)}) collective-permute-start(bf16[2224,128]{1,0:T(8,128)(2,1)S(1)} %pack_right.1), channel_id=1, source_target_pairs={{0,6},{1,7},{2,0},{3,1},{4,2},{5,3},{6,4},{7,5},{8,14},{9,15},{10,... | collective-permute-start | bytes 1708040 | tf_op jit(solution)/shard_map/ppermute | solution.py:590
  6.7 0.0 collective-permute-done.1.far_site_ref
  6.7 0.0 collective-permute-done.far_environ_ref
  6.7 0.0 copy-done
  6.7 0.0 copy-done.2
  6.7 0.0 copy-done.4
  6.7 0.0 copy-start.3
  6.7 0.9 %copy-done.3 = f32[1,1,34,34,4]{3,4,2,1,0:T(4,128)S(1)} copy-done((f32[1,1,34,34,4]{3,4,2,1,0:T(4,128)S(1)}, f32[1,1,34,34,4]{3,4,2,1,0:T(4,128)}, u32[]{:S(2)}) %copy-start.3) | copy-done | bytes 18520
  7.6 6.5 %fold_up.1 = (bf16[656,128]{1,0:T(8,128)(2,1)S(1)}, bf16[784,128]{1,0:T(8,128)(2,1)S(1)}, bf16[784,128]{1,0:T(8,128)(2,1)S(1)}) custom-call(s32[8]{0:T(128)S(1)} %copy-done.4, bf16[4352,128]{1,0:T(8,128)(2,1)S(1)} %bitcast.22, bf16[4,128,128]{2,1,0:T(8,128)(2,1)S(1)} %bitcast.27, bf16[4352,128]{1,0:T(8,128)(2,1)S(1)} %collective-permute-done.far_environ_ref, ...), custom_call_target="tpu_custom_call" | custom-call | flops 13200000000 | tf_op jit(solution)/shard_map/fold_up/pallas_call | solution.py:523
  14.1 0.1 collective-permute-start.3
  14.2 0.0 copy-start.6
  14.2 0.0 copy-start.7
  14.2 2.8 %fold_own.1 = (f32[656,128]{1,0:T(8,128)S(1)}, f32[784,128]{1,0:T(8,128)S(1)}, f32[784,128]{1,0:T(8,128)S(1)}) custom-call(s32[8]{0:T(128)S(1)} %copy-done.4, bf16[4352,128]{1,0:T(8,128)(2,1)S(1)} %bitcast.23, bf16[4,128,128]{2,1,0:T(8,128)(2,1)S(1)} %bitcast.28, bf16[4352,128]{1,0:T(8,128)(2,1)S(1)} %collective-permute-done.far_environ_ref, ...), custom_call_target="tpu_custom_call" | custom-call | flops 110000000 | tf_op jit(solution)/shard_map/fold_own/pallas_call | solution.py:523
  17.1 2.0 %collective-permute-start.2 = (bf16[784,128]{1,0:T(8,128)(2,1)S(1)}, bf16[784,128]{1,0:T(8,128)(2,1)S(1)}, u32[]{:S(2)}, u32[]{:S(2)}) collective-permute-start(bf16[784,128]{1,0:T(8,128)(2,1)S(1)} %get-tuple-element.63), channel_id=1, source_target_pairs={{0,2},{1,3},{2,4},{3,5},{4,6},{5,7},{6,0},{7,1},{8,10},{9,11},{10,... | collective-permute-start | bytes 602120 | tf_op jit(solution)/shard_map/ppermute | solution.py:617
  19.0 0.0 copy-done.6
  19.0 0.0 copy-done.7
  19.0 1.3 %mix_own.1.own_ref = bf16[1,128,4352]{2,1,0:T(8,128)(2,1)S(1)} custom-call(bf16[4352,128]{1,0:T(8,128)(2,1)S(1)} %bitcast.32, f32[136,34]{1,0:T(8,128)S(1)} %bitcast.33), custom_call_target="tpu_custom_call" | custom-call | flops 1100000000 | tf_op jit(solution)/shard_map/mix_own/pallas_call | solution.py:523
  20.4 0.0 collective-permute-done.4.far_ref
  20.4 2.0 %collective-permute-start.7 = (bf16[784,128]{1,0:T(8,128)(2,1)S(1)}, bf16[784,128]{1,0:T(8,128)(2,1)S(1)}, u32[]{:S(2)}, u32[]{:S(2)}) collective-permute-start(bf16[784,128]{1,0:T(8,128)(2,1)S(1)} %get-tuple-element.73), channel_id=1, source_target_pairs={{0,2},{1,3},{2,4},{3,5},{4,6},{5,7},{6,0},{7,1},{8,10},{9,11},{10,... | collective-permute-start | bytes 602120 | tf_op jit(solution)/shard_map/ppermute | solution.py:624
  22.4 0.1 select_select_fusion
  22.5 0.1 collective-permute-start.6
  22.5 2.0 %collective-permute-done.3 = bf16[656,128]{1,0:T(8,128)(2,1)S(1)} collective-permute-done((bf16[656,128]{1,0:T(8,128)(2,1)S(1)}, bf16[656,128]{1,0:T(8,128)(2,1)S(1)}, u32[]{:S(2)}, u32[]{:S(2)}) %collective-permute-start.3) | collective-permute-done | bytes 167968 | tf_op jit(solution)/shard_map/ppermute | solution.py:609
  24.6 0.1 add_convert_fusion.2.refs_0_
  24.6 1.6 %collective-permute-start.9 = (bf16[656,128]{1,0:T(8,128)(2,1)S(1)}, bf16[656,128]{1,0:T(8,128)(2,1)S(1)}, u32[]{:S(2)}, u32[]{:S(2)}) collective-permute-start(bf16[656,128]{1,0:T(8,128)(2,1)S(1)} %add_convert_fusion.2.refs_0_), channel_id=1, source_target_pairs={{0,8},{8,16},{16,24},{24,0},{1,9},{9,17},{17,25},{25,1},{2,10},{10... | collective-permute-start | bytes 503816 | tf_op jit(solution)/shard_map/ppermute | solution.py:633
  26.2 1.8 %mix_after.1.after_ref = bf16[1,128,4352]{2,1,0:T(8,128)(2,1)S(1)} custom-call(bf16[2224,128]{1,0:T(8,128)(2,1)S(1)} %collective-permute-done.4.far_ref, f32[136,34]{1,0:T(8,128)S(1)} %bitcast.34), custom_call_target="tpu_custom_call" | custom-call | flops 2200000000 | tf_op jit(solution)/shard_map/mix_after/pallas_call | solution.py:523
  28.0 0.8 %collective-permute-done.2 = bf16[784,128]{1,0:T(8,128)(2,1)S(1)} collective-permute-done((bf16[784,128]{1,0:T(8,128)(2,1)S(1)}, bf16[784,128]{1,0:T(8,128)(2,1)S(1)}, u32[]{:S(2)}, u32[]{:S(2)}) %collective-permute-start.2) | collective-permute-done | bytes 200736 | tf_op jit(solution)/shard_map/ppermute | solution.py:617
  28.9 0.1 add_convert_fusion.1.refs_1_
  28.9 1.6 %collective-permute-start.5 = (bf16[784,128]{1,0:T(8,128)(2,1)S(1)}, bf16[784,128]{1,0:T(8,128)(2,1)S(1)}, u32[]{:S(2)}, u32[]{:S(2)}) collective-permute-start(bf16[784,128]{1,0:T(8,128)(2,1)S(1)} %add_convert_fusion.1.refs_1_), channel_id=1, source_target_pairs={{0,8},{8,16},{16,24},{24,0},{1,9},{9,17},{17,25},{25,1},{2,10},{10... | collective-permute-start | bytes 602120 | tf_op jit(solution)/shard_map/ppermute | solution.py:641
  30.5 0.0 collective-permute-done.6.near_ref
  30.6 2.4 %mix_next.1.next_ref = bf16[2,128,4352]{2,1,0:T(8,128)(2,1)S(1)} custom-call(bf16[2224,128]{1,0:T(8,128)(2,1)S(1)} %collective-permute-done.6.near_ref, f32[136,34]{1,0:T(8,128)S(1)} %bitcast.35), custom_call_target="tpu_custom_call" | custom-call | flops 3300000000 | tf_op jit(solution)/shard_map/mix_next/pallas_call | solution.py:523
  33.0 0.0 collective-permute-done.7
  33.0 0.1 add_convert_fusion.refs_2_
  33.0 0.0 copy-start.1
  33.0 1.9 %collective-permute-start.8 = (bf16[784,128]{1,0:T(8,128)(2,1)S(1)}, bf16[784,128]{1,0:T(8,128)(2,1)S(1)}, u32[]{:S(2)}, u32[]{:S(2)}) collective-permute-start(bf16[784,128]{1,0:T(8,128)(2,1)S(1)} %add_convert_fusion.refs_2_), channel_id=1, source_target_pairs={{0,8},{8,16},{16,24},{24,0},{1,9},{9,17},{17,25},{25,1},{2,10},{10... | collective-permute-start | bytes 602120 | tf_op jit(solution)/shard_map/ppermute | solution.py:649
  34.9 1.8 %unpack_env.1 = bf16[4352,128]{1,0:T(8,128)(2,1)} custom-call(bf16[656,128]{1,0:T(8,128)(2,1)S(1)} %add_convert_fusion.2.refs_0_, bf16[784,128]{1,0:T(8,128)(2,1)S(1)} %add_convert_fusion.1.refs_1_, bf16[784,128]{1,0:T(8,128)(2,1)S(1)} %add_convert_fusion.refs_2_), custom_call_target="tpu_custom_call" | custom-call | flops 2200000000 | tf_op jit(solution)/shard_map/unpack_env/pallas_call | solution.py:523
  36.7 0.0 collective-permute-done.5.middle_in
  36.7 0.0 copy-done.1
  36.7 2.0 %head.1 = (f32[2,128,128]{2,1,0:T(8,128)S(1)}, f32[2,128,128]{2,1,0:T(8,128)S(1)}, f32[16,128]{1,0:T(8,128)S(1)}, bf16[4352,256]{1,0:T(8,128)(2,1)S(1)}, bf16[4352,256]{1,0:T(8,128)(2,1)S(1)}) custom-call(s32[8]{0:T(128)S(1)} %copy-done.4, f32[4,128,128]{2,1,0:T(8,128)S(1)} %bitcast.25, bf16[1,128,4352]{2,1,0:T(8,128)(2,1)S(1)} %mix_own.1.own_ref, ...), custom_call_target="tpu_custom_call" | custom-call | flops 220000000 | tf_op jit(solution)/shard_map/head/pallas_call | solution.py:523
  38.7 0.0 collective-permute-done.9.early_in
  38.7 8.2 %open.1 = (bf16[128,2816]{1,0:T(8,128)(2,1)S(1)}, f32[2,128,256]{2,1,0:T(8,128)S(1)}, f32[4,4,128,128]{3,2,1,0:T(8,128)S(1)}, f32[16,128]{1,0:T(8,128)S(1)}) custom-call(s32[8]{0:T(128)S(1)} %copy-done.4, bf16[4352,128]{1,0:T(8,128)(2,1)S(1)} %bitcast.24, bf16[656,128]{1,0:T(8,128)(2,1)S(1)} %collective-permute-done.9.early_in, ...), custom_call_target="tpu_custom_call" | custom-call | flops 1100000000 | tf_op jit(solution)/shard_map/open/pallas_call | solution.py:523
  46.9 0.0 collective-permute-done.8.packed_ref
  47.0 0.8 %lanczos.1 = (f32[4,4,128,128]{3,2,1,0:T(8,128)S(1)}, f32[16,128]{1,0:T(8,128)S(1)}) custom-call(s32[8]{0:T(128)S(1)} %copy-done.4, bf16[784,128]{1,0:T(8,128)(2,1)S(1)} %collective-permute-done.8.packed_ref, bf16[128,2816]{1,0:T(8,128)(2,1)S(1)} %get-tuple-element.91.early_ref, f32[2,128,256]{2,1,0:T(8,128)S(1)} %get-tuple-element.92.image_ref, ...), custom_call_target="tpu_custom_call" | custom-call | flops 13200000000 | tf_op jit(solution)/shard_map/lanczos/pallas_call | solution.py:523
  47.8 7.6 %all_to_all.5.stats_ref = f32[8,16,128]{2,1,0:T(8,128)S(1)} all-to-all(f32[8,16,128]{2,1,0:T(8,128)S(1)} %broadcast_in_dim.24), channel_id=1, replica_groups=mesh['seg'=4,'sec'=8] {'sec'}, dimensions={0} | all-to-all | bytes 131072 | tf_op jit(solution)/shard_map/all_to_all | solution.py:543
  55.4 1.4 %finish.1 = (f32[4,128,128]{2,1,0:T(8,128)}, f32[2,4]{1,0:T(2,128)}) custom-call(f32[8,16,128]{2,1,0:T(8,128)S(1)} %all_to_all.5.stats_ref, f32[2,128,128]{2,1,0:T(8,128)S(1)} %get-tuple-element.84.start_a, f32[2,128,128]{2,1,0:T(8,128)S(1)} %get-tuple-element.85.start_b, f32[4,4,128,128]{3,2,1,0:T(8,128)S(1)} %get-tuple-element.95.first_basis_ref, ...), custom_call_target="tpu_custom_call" | custom-call | flops 2200000000 | tf_op jit(solution)/shard_map/finish/pallas_call | solution.py:523
  (1 shorter events, 0.0 us)
Async XLA Ops:
  0.6 6.1 %collective-permute-start = (bf16[4352,128]{1,0:T(8,128)(2,1)}, bf16[4352,128]{1,0:T(8,128)(2,1)S(1)}, u32[]{:S(2)}, u32[]{:S(2)}) collective-permute-start(bf16[4352,128]{1,0:T(8,128)(2,1)} %bitcast.21), channel_id=1, source_target_pairs={{0,1},{1,0},{2,3},{3,2},{4,5},{5,4},{6,7},{7,6},{8,9},{9,8},{10,11... | collective-permute-start | bytes 3342344 | tf_op jit(solution)/shard_map/ppermute | solution.py:591
  1.1 5.6 %collective-permute-start.1 = (bf16[4,128,128]{2,1,0:T(8,128)(2,1)}, bf16[4,128,128]{2,1,0:T(8,128)(2,1)}, u32[]{:S(2)}, u32[]{:S(2)}) collective-permute-start(bf16[4,128,128]{2,1,0:T(8,128)(2,1)} %bitcast.26), channel_id=1, source_target_pairs={{0,1},{1,0},{2,3},{3,2},{4,5},{5,4},{6,7},{7,6},{8,9},{9,8},{10,11... | collective-permute-start | bytes 393224 | tf_op jit(solution)/shard_map/ppermute | solution.py:592
  1.2 1.2 %copy-start.5 = (bf16[1,1,34,128,128]{4,3,2,1,0:T(8,128)(2,1)S(1)}, bf16[1,1,34,128,128]{4,3,2,1,0:T(8,128)(2,1)}, u32[]{:S(2)}) copy-start(bf16[1,1,34,128,128]{4,3,2,1,0:T(8,128)(2,1)} %param.8) | copy-start | bytes 3342340
  2.5 4.2 %copy-start = (bf16[1,1,34,128,128]{4,3,2,1,0:T(8,128)(2,1)S(1)}, bf16[1,1,34,128,128]{4,3,2,1,0:T(8,128)(2,1)}, u32[]{:S(2)}) copy-start(bf16[1,1,34,128,128]{4,3,2,1,0:T(8,128)(2,1)} %param.7) | copy-start | bytes 3342340
  2.5 4.2 %copy-start.2 = (bf16[1,1,4,1,128,128]{5,4,3,2,1,0:T(8,128)(2,1)S(1)}, bf16[1,1,4,1,128,128]{5,4,3,2,1,0:T(8,128)(2,1)}, u32[]{:S(2)}) copy-start(bf16[1,1,4,1,128,128]{5,4,3,2,1,0:T(8,128)(2,1)} %param.9) | copy-start | bytes 393220
  2.5 4.2 %copy-start.4 = (s32[8]{0:T(128)S(1)}, s32[8]{0:T(128)}, u32[]{:S(2)}) copy-start(s32[8]{0:T(128)} %dims_ref.9) | copy-start | bytes 100
  2.8 17.6 %collective-permute-start.4 = (bf16[2224,128]{1,0:T(8,128)(2,1)S(1)}, bf16[2224,128]{1,0:T(8,128)(2,1)S(1)}, u32[]{:S(2)}, u32[]{:S(2)}) collective-permute-start(bf16[2224,128]{1,0:T(8,128)(2,1)S(1)} %pack_right.1), channel_id=1, source_target_pairs={{0,6},{1,7},{2,0},{3,1},{4,2},{5,3},{6,4},{7,5},{8,14},{9,15},{10,... | collective-permute-start | bytes 1708040 | tf_op jit(solution)/shard_map/ppermute | solution.py:590
  6.7 0.9 %copy-start.3 = (f32[1,1,34,34,4]{3,4,2,1,0:T(4,128)S(1)}, f32[1,1,34,34,4]{3,4,2,1,0:T(4,128)}, u32[]{:S(2)}) copy-start(f32[1,1,34,34,4]{3,4,2,1,0:T(4,128)} %param.10) | copy-start | bytes 55492
  14.1 10.4 %collective-permute-start.3 = (bf16[656,128]{1,0:T(8,128)(2,1)S(1)}, bf16[656,128]{1,0:T(8,128)(2,1)S(1)}, u32[]{:S(2)}, u32[]{:S(2)}) collective-permute-start(bf16[656,128]{1,0:T(8,128)(2,1)S(1)} %get-tuple-element.51), channel_id=1, source_target_pairs={{0,2},{1,3},{2,4},{3,5},{4,6},{5,7},{6,0},{7,1},{8,10},{9,11},{10,... | collective-permute-start | bytes 503816 | tf_op jit(solution)/shard_map/ppermute | solution.py:609
  14.2 4.8 %copy-start.6 = (bf16[1,1,34,128,128]{4,3,2,1,0:T(8,128)(2,1)S(1)}, bf16[1,1,34,128,128]{4,3,2,1,0:T(8,128)(2,1)}, u32[]{:S(2)}) copy-start(bf16[1,1,34,128,128]{4,3,2,1,0:T(8,128)(2,1)} %param.8) | copy-start | bytes 3342340
  14.2 4.8 %copy-start.7 = (f32[1,34,34,4]{2,3,1,0:T(4,128)S(1)}, f32[1,34,34,4]{2,3,1,0:T(4,128)}, u32[]{:S(2)}) copy-start(f32[1,34,34,4]{2,3,1,0:T(4,128)} %param.11) | copy-start | bytes 55492
  17.1 11.8 %collective-permute-start.2 = (bf16[784,128]{1,0:T(8,128)(2,1)S(1)}, bf16[784,128]{1,0:T(8,128)(2,1)S(1)}, u32[]{:S(2)}, u32[]{:S(2)}) collective-permute-start(bf16[784,128]{1,0:T(8,128)(2,1)S(1)} %get-tuple-element.63), channel_id=1, source_target_pairs={{0,2},{1,3},{2,4},{3,5},{4,6},{5,7},{6,0},{7,1},{8,10},{9,11},{10,... | collective-permute-start | bytes 602120 | tf_op jit(solution)/shard_map/ppermute | solution.py:617
  20.4 12.6 %collective-permute-start.7 = (bf16[784,128]{1,0:T(8,128)(2,1)S(1)}, bf16[784,128]{1,0:T(8,128)(2,1)S(1)}, u32[]{:S(2)}, u32[]{:S(2)}) collective-permute-start(bf16[784,128]{1,0:T(8,128)(2,1)S(1)} %get-tuple-element.73), channel_id=1, source_target_pairs={{0,2},{1,3},{2,4},{3,5},{4,6},{5,7},{6,0},{7,1},{8,10},{9,11},{10,... | collective-permute-start | bytes 602120 | tf_op jit(solution)/shard_map/ppermute | solution.py:624
  22.5 8.1 %collective-permute-start.6 = (bf16[2224,128]{1,0:T(8,128)(2,1)S(1)}, bf16[2224,128]{1,0:T(8,128)(2,1)S(1)}, u32[]{:S(2)}, u32[]{:S(2)}) collective-permute-start(bf16[2224,128]{1,0:T(8,128)(2,1)S(1)} %select_select_fusion), channel_id=1, source_target_pairs={{0,1},{1,0},{2,3},{3,2},{4,5},{5,4},{6,7},{7,6},{8,9},{9,8},{10,11... | collective-permute-start | bytes 1708040 | tf_op jit(solution)/shard_map/ppermute | solution.py:627
  24.6 14.1 %collective-permute-start.9 = (bf16[656,128]{1,0:T(8,128)(2,1)S(1)}, bf16[656,128]{1,0:T(8,128)(2,1)S(1)}, u32[]{:S(2)}, u32[]{:S(2)}) collective-permute-start(bf16[656,128]{1,0:T(8,128)(2,1)S(1)} %add_convert_fusion.2.refs_0_), channel_id=1, source_target_pairs={{0,8},{8,16},{16,24},{24,0},{1,9},{9,17},{17,25},{25,1},{2,10},{10... | collective-permute-start | bytes 503816 | tf_op jit(solution)/shard_map/ppermute | solution.py:633
  28.9 7.8 %collective-permute-start.5 = (bf16[784,128]{1,0:T(8,128)(2,1)S(1)}, bf16[784,128]{1,0:T(8,128)(2,1)S(1)}, u32[]{:S(2)}, u32[]{:S(2)}) collective-permute-start(bf16[784,128]{1,0:T(8,128)(2,1)S(1)} %add_convert_fusion.1.refs_1_), channel_id=1, source_target_pairs={{0,8},{8,16},{16,24},{24,0},{1,9},{9,17},{17,25},{25,1},{2,10},{10... | collective-permute-start | bytes 602120 | tf_op jit(solution)/shard_map/ppermute | solution.py:641
  33.0 3.7 %copy-start.1 = (f32[1,4,1,128,128]{4,3,2,1,0:T(8,128)S(1)}, f32[1,4,1,128,128]{4,3,2,1,0:T(8,128)}, u32[]{:S(2)}) copy-start(f32[1,4,1,128,128]{4,3,2,1,0:T(8,128)} %param.12) | copy-start | bytes 786436
  33.0 13.9 %collective-permute-start.8 = (bf16[784,128]{1,0:T(8,128)(2,1)S(1)}, bf16[784,128]{1,0:T(8,128)(2,1)S(1)}, u32[]{:S(2)}, u32[]{:S(2)}) collective-permute-start(bf16[784,128]{1,0:T(8,128)(2,1)S(1)} %add_convert_fusion.refs_2_), channel_id=1, source_target_pairs={{0,8},{8,16},{16,24},{24,0},{1,9},{9,17},{17,25},{25,1},{2,10},{10... | collective-permute-start | bytes 602120 | tf_op jit(solution)/shard_map/ppermute | solution.py:649
